TPU v7x, 32 devices: a whole 2x2x4 slice. The times are simulated.
32 devices in a mesh: rows: 8 (over z, y), heads: 4 (over x, core).
Axes of the slice: x: 2, y: 2, z: 4, core: 2. Of those that a mesh axis runs over, the one named last changes fastest.
Arguments:
- alignment_embedding: bfloat16 [128, 768, 128], P('rows', 'heads'), may hold values from -6 to 6
- line_group_label: int32 [128], replicated, may hold values from 0 to 3, never falling along the last dimension, each value on 1 to 80 neighbouring positions
- group_site_tally: int32 [4], replicated, may hold values from 32 to 128, as said below
- horizontal_triple_matrix: bfloat16 [3, 768, 768], P(None, 'heads'), may hold values from -0.25 to 0.25
- horizontal_mixing_matrix: bfloat16 [768, 768], P('heads'), may hold values from -0.21875 to 0.21875
- vertical_triple_matrix: bfloat16 [3, 768, 768], P(None, 'heads'), may hold values from -0.25 to 0.25
- vertical_mixing_matrix: bfloat16 [768, 768], P('heads'), may hold values from -0.21875 to 0.21875
- expand_matrix: bfloat16 [768, 3072], P(None, 'heads'), may hold values from -0.21875 to 0.21875
- contract_matrix: bfloat16 [3072, 768], P('heads'), may hold values from -0.109375 to 0.109375
Outputs:
- layer_out: bfloat16 [128, 768, 128], P('rows', 'heads')
Inputs may be any that keep to these rules, and one draw needn't show every extreme that they name: `line_group_label`: family ids never fall along the rows; each of the 4 families holds 1 to 80 rows, one family exactly 80. `group_site_tally`: positions at or beyond a family's length are padding; some family has exactly 128.
All inputs are finite; a program needn't handle non-finite values.
Results may differ from a plain program's by a relative error of at most 0.015.
Values may be sent and summed in bfloat16 or wider, within the bound.
No kernel may reach another device: no remote copies, remote signals or barrier semaphores. Data moves between devices by JAX's collectives and lax.ppermute only.
A program may use at most 64 MiB of HBM per device.

v0:
```python
import functools

import jax
import jax.numpy as jnp
from jax import lax
from jax.experimental import pallas as pl
from jax.experimental.pallas import tpu as pltpu
from jax.sharding import Mesh, PartitionSpec as P

HEAD_SIZE = 64
SWAP = [(0, 1), (1, 0)]
ROWS = ("plane", "pair")
BF16 = jnp.bfloat16
F32 = jnp.float32


def other_chip(value):
    return lax.ppermute(value, "chip", SWAP)


def other_pair(value):
    return lax.ppermute(value, "pair", SWAP)


def other_core(value):
    return lax.ppermute(value, "core", SWAP)


def in_order(first, second, index, axis):
    forward = jnp.concatenate([first, second], axis=axis)
    backward = jnp.concatenate([second, first], axis=axis)
    return jnp.where(index == 0, forward, backward)


def half_rows(value, index):
    rows = value.shape[0] // 2
    return lax.dynamic_slice_in_dim(value, index * rows, rows)


def own_norm(values, axis):
    values = values.astype(F32)
    average = jnp.mean(values, axis=axis, keepdims=True)
    centred = values - average
    variance = jnp.mean(centred * centred, axis=axis, keepdims=True)
    return (centred * lax.rsqrt(variance + 1e-05)).astype(BF16)


def masked_softmax(tables, tally):
    live = jnp.arange(tables.shape[-1])[None, :] < tally[:, None]
    tables = jnp.where(live[:, None, None, :], tables, -jnp.inf)
    return jax.nn.softmax(tables, axis=-1).astype(BF16)


def tied_weights(shared, label, tally):
    row_groups, _, rows, sites = shared.shape
    lines = label.shape[0] // row_groups
    ends = label.reshape(row_groups, lines)[:, jnp.array([0, lines - 1])]
    parts = lax.all_to_all(shared, ROWS, 0, 0, tiled=True).astype(F32)
    parts = parts.reshape(row_groups, 2, -1, rows, sites)
    families = jnp.arange(tally.shape[0])
    member = (ends[:, :, None] == families).astype(F32)
    totals = jnp.einsum("stf,sthij->fhij", member, parts, precision=lax.Precision.HIGHEST)
    weights = masked_softmax(totals, tally)
    back = lax.all_to_all(weights[ends], ROWS, 0, 0, tiled=True)
    return jnp.transpose(back, (1, 2, 0, 3, 4)).reshape(2, -1, sites, sites)


CONTRACT_FIRST = (((0,), (0,)), ((), ()))
CONTRACT_LAST = (((1,), (1,)), ((), ()))
IN_VMEM = pl.BlockSpec(memory_space=pltpu.VMEM)
IN_SMEM = pl.BlockSpec(memory_space=pltpu.SMEM)
ANYWHERE = pl.BlockSpec(memory_space=pl.ANY)
GRANT = pltpu.CompilerParams(vmem_limit_bytes=40 * 2**20)


def row_front_kernel(
    count, spot_ref, slot_ref, scale_ref, tally_ref, own, near, far, diagonal, triple,
    table_ref, inner_ref, value_ref, tables, normed,
):
    step = pl.program_id(0)
    group, quarter, sites = own.shape
    heads = quarter // HEAD_SIZE

    @pl.when(step == 0)
    def _():
        tables[...] = jnp.zeros_like(tables)

    pieces = []
    for ref in (own, near, far, diagonal):
        lanes = jnp.concatenate([ref[line] for line in range(group)], axis=-1)
        pieces.append(lanes.astype(F32))
    size = 4 * quarter
    average = sum(jnp.sum(piece, axis=0, keepdims=True) for piece in pieces) / size
    pieces = [piece - average for piece in pieces]
    variance = sum(jnp.sum(piece * piece, axis=0, keepdims=True) for piece in pieces) / size
    inverse = lax.rsqrt(variance + 1e-05)
    for index, piece in enumerate(pieces):
        spot = pl.multiple_of(spot_ref[index] * quarter, quarter)
        normed[pl.ds(spot, quarter), :] = (piece * inverse).astype(BF16)
    projected = jnp.dot(triple[...], normed[...], preferred_element_type=F32).astype(BF16)
    for line in range(group):
        part = projected[:, line * sites : (line + 1) * sites]
        value_ref[line] = part[2 * quarter :]
        slot = slot_ref[step * group + line]
        scale = scale_ref[step * group + line]
        for head in range(heads):
            lower = head * HEAD_SIZE
            queries = part[lower : lower + HEAD_SIZE]
            keys = part[quarter + lower : quarter + lower + HEAD_SIZE]
            logits = lax.dot_general(queries, keys, CONTRACT_FIRST, preferred_element_type=F32)
            tables[slot * heads + head] += logits * scale

    @pl.when(step == count - 1)
    def _():
        for index in range(2 * heads):
            table = tables[index].astype(BF16)
            if len(table_ref.shape) == 4:
                groups, _, rows, _ = table_ref.shape
                table_ref[:, index] = table.reshape(groups, rows, sites)
            else:
                table_ref[index] = table
        site = lax.broadcasted_iota(jnp.int32, (sites, sites), 1)

        def inner(index, carry):
            table = tables[2 * heads + index]
            table = jnp.where(site < tally_ref[index // heads], table, -jnp.inf)
            table = jnp.exp(table - jnp.max(table, axis=-1, keepdims=True))
            table = table / jnp.sum(table, axis=-1, keepdims=True)
            inner_ref[index] = table.astype(BF16)
            return carry

        lax.fori_loop(0, inner_ref.shape[0], inner, 0)


def row_front(pieces, triple, spots, slot, scaling, inner_tally, row_groups):
    lines, quarter, sites = pieces[0].shape
    group = 4
    count = lines // group
    heads = quarter // HEAD_SIZE
    inner = inner_tally.shape[0]
    rows = sites // row_groups
    shape = (row_groups, 2 * heads, rows, sites) if rows % 16 == 0 else (2 * heads, sites, sites)
    block = pl.BlockSpec((group, quarter, sites), lambda step: (step, 0, 0))

    def whole(shape):
        return pl.BlockSpec(shape, lambda step: (0,) * len(shape))

    tables, inner_weights, values = pl.pallas_call(
        functools.partial(row_front_kernel, count),
        grid=(count,),
        out_shape=(
            jax.ShapeDtypeStruct(shape, BF16),
            jax.ShapeDtypeStruct((inner * heads, sites, sites), BF16),
            jax.ShapeDtypeStruct((lines, quarter, sites), BF16),
        ),
        in_specs=[IN_SMEM] * 4 + [block] * 4 + [whole((3 * quarter, 4 * quarter))],
        out_specs=(whole(shape), whole((inner * heads, sites, sites)), block),
        scratch_shapes=[
            pltpu.VMEM(((2 + inner) * heads, sites, sites), F32),
            pltpu.VMEM((4 * quarter, group * sites), BF16),
        ],
        compiler_params=GRANT,
        name="row_front",
    )(spots, slot, scaling, inner_tally, *pieces, triple.reshape(3 * quarter, 4 * quarter))
    if rows % 16:
        tables = jnp.transpose(tables.reshape(-1, row_groups, rows, sites), (1, 0, 2, 3))
    return tables, inner_weights.reshape(inner, heads, sites, sites), values


def column_kernel(
    pair_ref, label_row, label_column, own, other, triple, mixing, piece, rest,
    kept, sent, normed, far, projected, mixed, semaphores,
):
    half = piece.shape[0]
    pair = pair_ref[0]
    copies = []
    for index, (source, place) in enumerate(((piece, pair), (rest, 1 - pair))):
        spot = pl.multiple_of(place * half, half)
        target = far.at[pl.ds(spot, half)]
        copies.append(pltpu.make_async_copy(source, target, semaphores.at[index]))
    for copy in copies:
        copy.start()
    places, rows, model = own.shape
    quarter = mixing.shape[0]
    both = 2 * rows
    normed[:, :rows] = own[...]
    normed[:, rows:] = other[...]
    flat = normed[...].reshape(places * both, model)
    same = label_column[...] == label_row[...]
    scale = HEAD_SIZE**-0.5

    def attend(weights, lower):
        projected[...] = lax.dot_general(
            weights, flat, CONTRACT_LAST, preferred_element_type=F32
        ).astype(BF16)
        for place in range(places):
            lanes = slice(place * both, (place + 1) * both)
            for head in range(quarter // HEAD_SIZE):
                features = slice(head * HEAD_SIZE, (head + 1) * HEAD_SIZE)
                queries = projected[:quarter, lanes][features]
                keys = projected[quarter : 2 * quarter, lanes][features]
                values = projected[2 * quarter :, lanes][features]
                scores = lax.dot_general(
                    keys, queries, CONTRACT_FIRST, preferred_element_type=F32
                )
                scores = jnp.where(same, scores * scale, -jnp.inf)
                scores = jnp.exp(scores - jnp.max(scores, axis=0, keepdims=True))
                total = jnp.sum(scores, axis=0, keepdims=True)
                part = jnp.dot(values, scores.astype(BF16), preferred_element_type=F32)
                target = slice(lower + head * HEAD_SIZE, lower + (head + 1) * HEAD_SIZE)
                mixed[target, lanes] = (part / total).astype(BF16)

    attend(triple[...], 0)
    for copy in copies:
        copy.wait()
    attend(far[quarter : 4 * quarter], quarter)
    for place in range(places):
        lanes = slice(place * both, (place + 1) * both)
        partial = lax.dot_general(
            mixed[:quarter, lanes], mixing[...], CONTRACT_FIRST, preferred_element_type=F32
        )
        partial += lax.dot_general(
            mixed[quarter:, lanes], far[4 * quarter :], CONTRACT_FIRST, preferred_element_type=F32
        )
        kept[place] = partial[:rows]
        sent[place] = partial[rows:].astype(BF16)


def column(own, other, label, triple, mixing, piece, rest, pair):
    places, rows, model = own.shape
    quarter = mixing.shape[0]
    tokens = 2 * places * rows
    return pl.pallas_call(
        column_kernel,
        out_shape=(
            jax.ShapeDtypeStruct(own.shape, F32),
            jax.ShapeDtypeStruct(own.shape, BF16),
        ),
        in_specs=[IN_SMEM] + [IN_VMEM] * 6 + [ANYWHERE] * 2,
        out_specs=(IN_VMEM, IN_VMEM),
        scratch_shapes=[
            pltpu.VMEM((places, 2 * rows, model), BF16),
            pltpu.VMEM((2 * piece.shape[0], model), BF16),
            pltpu.VMEM((3 * quarter, tokens), BF16),
            pltpu.VMEM((2 * quarter, tokens), BF16),
            pltpu.SemaphoreType.DMA((2,)),
        ],
        compiler_params=GRANT,
        name="column",
    )(pair, label[None, :], label[:, None], own, other, triple.reshape(-1, model), mixing, piece, rest)


def feed_forward_kernel(
    pair_ref, normed, expand, contract, piece, rest, out,
    near_expand, near_contract, far_piece, far_rest, hidden, semaphores,
):
    moves = (
        (expand, near_expand), (piece, far_piece), (rest, far_rest), (contract, near_contract)
    )
    copies = [
        pltpu.make_async_copy(source, target, semaphores.at[index])
        for index, (source, target) in enumerate(moves)
    ]
    for copy in copies:
        copy.start()
    width = near_expand.shape[1]
    tile = width // 3
    values = normed[...]
    pair = pair_ref[0]

    def raise_by(weights, lower):
        for start in range(0, width, tile):
            up = jnp.dot(values, weights[:, start : start + tile], preferred_element_type=F32)
            up = 0.5 * up * (1.0 + lax.erf(up * 2.0**-0.5))
            hidden[:, lower + start : lower + start + tile] = up.astype(BF16)

    def lower_by(near_weights, far_weights):
        down = jnp.dot(hidden[:, :width], near_weights[...], preferred_element_type=F32)
        down += jnp.dot(hidden[:, width:], far_weights[...], preferred_element_type=F32)
        out[...] = down.astype(out.dtype)

    copies[0].wait()
    raise_by(near_expand, 0)
    copies[1].wait()
    copies[2].wait()

    @pl.when(pair == 0)
    def _():
        raise_by(far_piece, width)

    @pl.when(pair != 0)
    def _():
        raise_by(far_rest, width)

    copies[3].wait()

    @pl.when(pair == 0)
    def _():
        lower_by(near_contract, far_rest)

    @pl.when(pair != 0)
    def _():
        lower_by(near_contract, far_piece)


def feed_forward(normed, expand, contract, piece, rest, pair, kind):
    places, rows, model = normed.shape
    tokens, width = places * rows, expand.shape[1]
    result = pl.pallas_call(
        feed_forward_kernel,
        out_shape=jax.ShapeDtypeStruct((tokens, model), kind),
        in_specs=[IN_SMEM, IN_VMEM] + [ANYWHERE] * 4,
        out_specs=IN_VMEM,
        scratch_shapes=[
            pltpu.VMEM((model, width), BF16),
            pltpu.VMEM((width, model), BF16),
            pltpu.VMEM((model, width), BF16),
            pltpu.VMEM((model, width), BF16),
            pltpu.VMEM((tokens, 2 * width), BF16),
            pltpu.SemaphoreType.DMA((4,)),
        ],
        compiler_params=GRANT,
        name="feed_forward",
    )(pair, normed.reshape(tokens, model), expand, contract, piece, rest)
    return result.reshape(normed.shape)


def core_sum(stream, kept, sent):
    return (stream.astype(F32) + kept + other_core(sent).astype(F32)).astype(BF16)


def shards(
    alignment_embedding,
    line_group_label,
    group_site_tally,
    horizontal_triple_matrix,
    horizontal_mixing_matrix,
    vertical_triple_matrix,
    vertical_mixing_matrix,
    expand_matrix,
    contract_matrix,
):
    lines, quarter, sites = alignment_embedding.shape
    row_groups = lax.axis_size(ROWS)
    chips = 2 * row_groups
    place = sites // chips
    pair = lax.axis_index("pair")
    chip = lax.axis_index("chip")
    core = lax.axis_index("core")
    label = line_group_label
    tally = group_site_tally
    families = tally.shape[0]

    across = other_chip(alignment_embedding)
    near = other_core(alignment_embedding)
    diagonal = other_core(across)
    pieces = (alignment_embedding, near, across, diagonal)
    spots = jnp.stack(
        [2 * chip + core, 2 * chip + 1 - core, 2 * (1 - chip) + core, 2 * (1 - chip) + 1 - core]
    ).astype(jnp.int32)
    first_pack = jnp.concatenate(
        [
            horizontal_mixing_matrix,
            vertical_triple_matrix.reshape(-1, vertical_triple_matrix.shape[-1]),
            vertical_mixing_matrix,
        ]
    )
    second_pack = jnp.concatenate([expand_matrix, contract_matrix])
    across, first_pack, second_pack = lax.optimization_barrier((across, first_pack, second_pack))
    first_piece = other_chip(half_rows(first_pack, pair))
    second_piece = other_chip(half_rows(second_pack, pair))
    first_rest = other_pair(first_piece)
    second_rest = other_pair(second_piece)

    start = lax.axis_index(ROWS) * lines
    label_here = lax.dynamic_slice_in_dim(label, start, lines)
    first, last = label_here[0], label_here[-1]
    counts = jnp.sum((label[:, None] == jnp.arange(families)).astype(F32), axis=0)
    scaling = HEAD_SIZE**-0.5 * lax.rsqrt(counts)[label_here]
    slots = 2 + max(min(families, lines) - 2, 1)
    slot = jnp.where(
        label_here == first, 0, jnp.where(label_here == last, 1, label_here - first + 1)
    )
    inner = jnp.clip(first + 1 + jnp.arange(slots - 2), 0, families - 1)
    tables, inner_weights, values = row_front(
        pieces, horizontal_triple_matrix, spots, slot, scaling, tally[inner], row_groups
    )
    tables, first_piece = lax.optimization_barrier((tables, first_piece))
    weights = jnp.concatenate([tied_weights(tables, label, tally), inner_weights])[slot]
    values = values.reshape(lines, -1, HEAD_SIZE, sites)
    mixed = jnp.einsum("rhdj,rhij->rhdi", values, weights, preferred_element_type=F32)
    mixed = mixed.astype(BF16).reshape(lines, quarter, sites)

    mixed, first_rest, second_piece = lax.optimization_barrier((mixed, first_rest, second_piece))
    far_mixing = jnp.where(pair == 0, first_piece[:quarter], first_rest[:quarter])
    kept = half_rows(mixed, chip)
    got = other_chip(half_rows(mixed, 1 - chip))
    partial = jnp.einsum("rdi,de->rie", kept, horizontal_mixing_matrix, preferred_element_type=F32)
    partial += jnp.einsum("rdi,de->rie", got, far_mixing, preferred_element_type=F32)
    sent = other_core(half_rows(partial, 1 - core).astype(BF16))
    ours = [half_rows(half_rows(piece, chip), core) for piece in pieces]
    stream = in_order(
        in_order(ours[0], ours[1], core, 1), in_order(ours[2], ours[3], core, 1), chip, 1
    )
    residual = jnp.transpose(stream, (0, 2, 1))
    after_row = residual.astype(F32) + half_rows(partial, core) + sent.astype(F32)
    after_row = after_row.astype(BF16)

    after_row, second_rest = lax.optimization_barrier((after_row, second_rest))
    own = lines // 4
    model = after_row.shape[-1]
    after_row = jnp.transpose(after_row.reshape(own, chips, place, model), (1, 0, 2, 3))
    after_row = lax.all_to_all(after_row, ROWS + ("chip",), 0, 0, tiled=True)
    after_row = jnp.transpose(after_row, (2, 0, 1, 3)).reshape(place, chips * own, model)
    rows = chips * own
    label_cores = label.reshape(chips, 2, own)
    label_sites = jnp.concatenate(
        [
            lax.dynamic_index_in_dim(label_cores, index, 1, False).reshape(-1)
            for index in (core, 1 - core)
        ]
    )

    parity = pair.astype(jnp.int32).reshape(1)
    normed = own_norm(after_row, -1)
    kept, sent = column(
        normed,
        other_core(normed),
        label_sites,
        vertical_triple_matrix,
        vertical_mixing_matrix,
        first_piece,
        first_rest,
        parity,
    )
    after_col = core_sum(after_row, kept, sent)

    normed = own_norm(after_col, -1)
    feed = (expand_matrix, contract_matrix, second_piece, second_rest, parity)
    kept = feed_forward(normed, *feed, F32)
    sent = feed_forward(other_core(normed), *feed, BF16)
    finished = core_sum(after_col, kept, sent)

    finished = finished.reshape(place, row_groups, 2 * own, model // quarter, quarter)
    finished = jnp.transpose(finished, (1, 3, 2, 0, 4)).reshape(-1, 2 * own * place, quarter)
    parts, wide = 2 * own * place // 2, quarter // 3 * 2
    finished = jnp.concatenate(
        [
            finished[:, :, :wide],
            jnp.concatenate([finished[:, :parts, wide:], finished[:, parts:, wide:]], axis=2),
        ],
        axis=1,
    )
    finished = lax.all_to_all(finished, ROWS + ("chip", "core"), 0, 0, tiled=True)
    narrow = finished[:, 2 * parts :]
    narrow = jnp.concatenate([narrow[:, :, : wide // 2], narrow[:, :, wide // 2 :]], axis=1)
    finished = jnp.concatenate([finished[:, : 2 * parts], narrow], axis=2)
    finished = finished.reshape(chips, 2, 2, own, place, quarter)
    finished = jnp.transpose(finished, (2, 1, 3, 5, 0, 4))
    return finished.reshape(lines, quarter, sites)


def solution(mesh):
    planes = mesh.shape["rows"] // 2
    split = Mesh(mesh.devices.reshape(planes, 2, 2, 2), ROWS + ("chip", "core"))
    heads = ("chip", "core")
    placed = (
        P(ROWS, heads, None),
        P(),
        P(),
        P(None, heads, None),
        P(heads, None),
        P(None, heads, None),
        P(heads, None),
        P(None, heads),
        P(heads, None),
    )
    return jax.shard_map(
        shards, mesh=split, in_specs=placed, out_specs=P(ROWS, heads, None), check_vma=False
    )
```

profile of v0, /device:TPU:0, one launch (start us, length us, event | category | flops | bytes accessed | tf_op | source)
XLA Modules:
  0.0 217.0 jit_solution(1012650929561609304)
XLA Ops:
  0.5 2.5 %collective-permute-start.1 = (bf16[16,192,128]{2,1,0:T(8,128)(2,1)}, bf16[16,192,128]{2,1,0:T(8,128)(2,1)}, u32[]{:S(2)}, u32[]{:S(2)}) collective-permute-start(bf16[16,192,128]{2,1,0:T(8,128)(2,1)} %own.1), channel_id=1, source_target_pairs={{0,2},{2,0},{1,3},{3,1},{4,6},{6,4},{5,7},{7,5},{8,10},{10,8},{9,1... | collective-permute-start | bytes 2359304 | tf_op jit(solution)/shard_map/ppermute | solution.py:18
  8.5 1.6 pad_maximum_fusion.1
  10.6 1.6 pad_maximum_fusion
  12.2 9.3 %collective-permute-done.1.far = bf16[16,192,128]{2,1,0:T(8,128)(2,1)} collective-permute-done((bf16[16,192,128]{2,1,0:T(8,128)(2,1)}, bf16[16,192,128]{2,1,0:T(8,128)(2,1)}, u32[]{:S(2)}, u32[]{:S(2)}) %collective-permute-start.1) | collective-permute-done | bytes 786464 | tf_op jit(solution)/shard_map/ppermute | solution.py:18
  22.4 1.7 collective-permute-start.3
  28.4 8.3 %row_front.1 = (bf16[8,6,16,128]{3,2,1,0:T(8,128)(2,1)}, bf16[6,128,128]{2,1,0:T(8,128)(2,1)S(1)}, bf16[16,192,128]{2,1,0:T(8,128)(2,1)S(1)}) custom-call(s32[4]{0:T(128)S(1)} %pad_add_fusion.spot_ref, s32[16]{0:T(128)S(1)} %get-tuple-element.38.slot_ref, f32[16]{0:T(128)S(1)} %broadcast_multiply_fusion.2.scale_ref, s32[2]{0:T(128)S(1)} %gather_fusion.1, ...), custom_call_target="tpu_custom_call" | custom-call | tf_op jit(solution)/shard_map/row_front/pallas_call | solution.py:148
  38.2 3.2 %collective-permute-done.3.piece = bf16[480,768]{1,0:T(8,128)(2,1)S(1)} collective-permute-done((bf16[480,768]{1,0:T(8,128)(2,1)}, bf16[480,768]{1,0:T(8,128)(2,1)S(1)}, u32[]{:S(2)}, u32[]{:S(2)}) %collective-permute-start.3) | collective-permute-done | bytes 737312 | tf_op jit(solution)/shard_map/ppermute | solution.py:18
  41.5 6.1 %all-to-all-start = ((bf16[8,6,16,128]{3,2,1,0:T(8,128)(2,1)}), bf16[8,6,16,128]{3,2,1,0:T(8,128)(2,1)}, u32[]{:S(2)}, u32[]{:S(2)}) async-start(bf16[8,6,16,128]{3,2,1,0:T(8,128)(2,1)} %get-tuple-element.22), calls=%async_computation | async-start | bytes 393216 | tf_op jit(solution)/shard_map/all_to_all | solution.py:58
  47.7 2.4 %constant_dynamic-slice_fusion.1 = bf16[768,768]{1,0:T(8,128)(2,1)} fusion(bf16[1536,768]{1,0:T(8,128)(2,1)} %pad_maximum_fusion, s32[]{:T(128)S(6)} %select_n.127), kind=kLoop, calls=%fused_computation.64 | loop fusion | bytes 2359300 | tf_op jit(solution)/shard_map/dynamic_slice | solution.py:37
  51.5 4.0 %all-to-all-done = bf16[8,6,16,128]{3,2,1,0:T(8,128)(2,1)} async-done(((bf16[8,6,16,128]{3,2,1,0:T(8,128)(2,1)}), bf16[8,6,16,128]{3,2,1,0:T(8,128)(2,1)}, u32[]{:S(2)}, u32[]{:S(2)}) %all-to-all-start) | async-done | bytes 196640 | tf_op jit(solution)/shard_map/all_to_all | solution.py:58
  57.7 2.0 gather_fusion.3
  59.7 4.0 %all-to-all-start.1 = ((bf16[8,2,3,16,128]{4,3,2,1,0:T(8,128)(2,1)}), bf16[8,2,3,16,128]{4,3,2,1,0:T(8,128)(2,1)}, u32[]{:S(2)}, u32[]{:S(2)}) async-start(bf16[8,2,3,16,128]{4,3,2,1,0:T(8,128)(2,1)} %bitcast.97), calls=%async_computation.1 | async-start | bytes 393216 | tf_op jit(solution)/shard_map/all_to_all | solution.py:64
  63.7 1.9 collective-permute-start.4
  65.6 6.0 %all-to-all-done.1 = bf16[8,2,3,16,128]{4,3,2,1,0:T(8,128)(2,1)} async-done(((bf16[8,2,3,16,128]{4,3,2,1,0:T(8,128)(2,1)}), bf16[8,2,3,16,128]{4,3,2,1,0:T(8,128)(2,1)}, u32[]{:S(2)}, u32[]{:S(2)}) %all-to-all-start.1) | async-done | bytes 196640 | tf_op jit(solution)/shard_map/all_to_all | solution.py:64
  72.6 1.7 pad_maximum_fusion.2
  74.3 2.9 %gather_fusion.4 = bf16[16,3,128,128]{3,2,1,0:T(8,128)(2,1)} fusion(bf16[4,3,128,128]{3,2,1,0:T(8,128)(2,1)} %pad_maximum_fusion.2, s32[1024]{0:T(1024)S(1)} %pad_clamp_fusion), kind=kCustom, calls=%fused_computation.4 | custom fusion | bytes 3145792 | tf_op jit(solution)/shard_map/gather | solution.py:389
  77.2 2.8 %convolution_convert_fusion = bf16[16,3,64,128]{3,2,1,0:T(8,128)(2,1)S(1)} fusion(bf16[16,3,64,128]{3,2,1,0:T(8,128)(2,1)} %bitcast.86, bf16[16,3,128,128]{3,2,1,0:T(8,128)(2,1)} %gather_fusion.4), kind=kOutput, calls=%fused_computation.28 | convolution fusion | flops 101056512 | bytes 3145728 | tf_op jit(solution)/shard_map/rhdj,rhij->rhdi/dot_general | solution.py:391
  80.1 2.8 %collective-permute-done.4.rest = bf16[480,768]{1,0:T(8,128)(2,1)} collective-permute-done((bf16[480,768]{1,0:T(8,128)(2,1)}, bf16[480,768]{1,0:T(8,128)(2,1)}, u32[]{:S(2)}, u32[]{:S(2)}) %collective-permute-start.4) | collective-permute-done | bytes 737312 | tf_op jit(solution)/shard_map/ppermute | solution.py:22
  86.4 6.7 %collective-permute-done.6 = bf16[8,192,128]{2,1,0:T(8,128)(2,1)} collective-permute-done((bf16[8,192,128]{2,1,0:T(8,128)(2,1)}, bf16[8,192,128]{2,1,0:T(8,128)(2,1)}, u32[]{:S(2)}, u32[]{:S(2)}) %collective-permute-start.6) | collective-permute-done | bytes 393248 | tf_op jit(solution)/shard_map/ppermute | solution.py:18
  93.1 1.8 fusion.15
  95.6 1.6 copy-done.15
  102.4 2.4 %fusion.10 = bf16[4,128,768]{1,2,0:T(8,128)(2,1)} fusion(bf16[4,128,768]{1,2,0:T(8,128)(2,1)} %collective-permute-done.7, f32[8,128,768]{1,2,0:T(8,128)S(1)} %copy-done.16, s32[]{:T(128)S(6)} %select_n.110, bf16[4,384,128]{2,1,0:T(8,128)(2,1)S(1)} %maximum_select_fusion.2, bf16[4,384,128]{2,1,0:T(8,128)(2,1)S(1)} %maximum_select_fusion.1, pred[]{:T(512)S(6)} %eq.48), kind=kLoop, calls=%fused_computation.23 | loop fusion | flops 5505024 | bytes 3932165 | tf_op jit(solution)/shard_map/convert_element_type | solution.py:407
  104.8 6.2 %collective-permute-done.8.rest = bf16[768,768]{1,0:T(8,128)(2,1)} collective-permute-done((bf16[768,768]{1,0:T(8,128)(2,1)S(1)}, bf16[768,768]{1,0:T(8,128)(2,1)}, u32[]{:S(2)}, u32[]{:S(2)}) %collective-permute-start.8) | collective-permute-done | bytes 1179680 | tf_op jit(solution)/shard_map/ppermute | solution.py:22
  111.0 2.3 %copy.84 = bf16[4,128,768]{2,1,0:T(8,128)(2,1)} copy(bf16[4,128,768]{1,2,0:T(8,128)(2,1)} %fusion.10) | data formatting | bytes 1572864 | tf_op jit(solution)/shard_map/optimization_barrier | solution.py:409
  114.5 23.8 %all_to_all.20 = bf16[16,4,8,768]{3,2,1,0:T(8,128)(2,1)S(1)} all-to-all(bf16[16,4,8,768]{3,2,1,0:T(8,128)(2,1)S(1)} %copy.85), channel_id=1, replica_groups=mesh['plane'=4,'pair'=2,'chip'=2,'core'=2] {'plane','pair','chip'}, dimensions={0} | all-to-all | bytes 1572864 | tf_op jit(solution)/shard_map/all_to_all | solution.py:413
  144.2 2.1 fusion.8
  161.7 13.4 %column.1 = (f32[8,64,768]{2,1,0:T(8,128)S(1)}, bf16[8,64,768]{2,1,0:T(8,128)(2,1)S(1)}) custom-call(s32[1]{0:T(128)} %bitcast.30.pair_ref, s32[1,128]{1,0:T(1,128)S(1)} %get-tuple-element.46.label_row, s32[128,1]{1,0:T(8,128)S(1)} %copy-done.9, bf16[8,64,768]{2,1,0:T(8,128)(2,1)} %multiply_convert_fusion.own, ...), custom_call_target="tpu_custom_call" | custom-call | tf_op jit(solution)/shard_map/column/pallas_call | solution.py:233
  175.7 1.9 collective-permute-done.10
  179.5 1.9 collective-permute-done.11
  181.4 4.2 %feed_forward.3 = bf16[512,768]{1,0:T(8,128)(2,1)S(1)} custom-call(s32[1]{0:T(128)} %bitcast.30.pair_ref, bf16[512,768]{1,0:T(8,128)(2,1)S(1)} %bitcast.85, bf16[768,768]{1,0:T(8,128)(2,1)S(1)} %copy-done, bf16[768,768]{1,0:T(8,128)(2,1)S(1)} %copy-done.1, bf16[768,768]{1,0:T(8,128)(2,1)S(1)} %collective-permute-done.5.piece, ...), custom_call_target="tpu_custom_call" | custom-call | tf_op jit(solution)/shard_map/feed_forward/pallas_call | solution.py:309
  186.0 4.0 %feed_forward.2 = f32[512,768]{1,0:T(8,128)S(1)} custom-call(s32[1]{0:T(128)} %bitcast.30.pair_ref, bf16[512,768]{1,0:T(8,128)(2,1)S(1)} %bitcast.82, bf16[768,768]{1,0:T(8,128)(2,1)S(1)} %copy-done, bf16[768,768]{1,0:T(8,128)(2,1)S(1)} %copy-done.1, bf16[768,768]{1,0:T(8,128)(2,1)S(1)} %collective-permute-done.5.piece, ...), custom_call_target="tpu_custom_call" | custom-call | tf_op jit(solution)/shard_map/feed_forward/pallas_call | solution.py:309
  192.3 22.8 %all_to_all.21 = bf16[32,96,128]{2,1,0:T(8,128)(2,1)S(1)} all-to-all(bf16[32,96,128]{2,1,0:T(8,128)(2,1)S(1)} %maximum_maximum_fusion.1), channel_id=1, replica_groups=mesh['plane'=4,'pair'=2,'chip'=2,'core'=2] {'plane','pair','chip','core'}, dimensions={0} | all-to-all | bytes 1572864 | tf_op jit(solution)/shard_map/all_to_all | solution.py:454
  (129 shorter events, 55.9 us)
Async XLA Ops:
  0.0 26.1 %collective-permute-start = (bf16[16,192,128]{2,1,0:T(8,128)(2,1)}, bf16[16,192,128]{2,1,0:T(8,128)(2,1)}, u32[]{:S(2)}, u32[]{:S(2)}) collective-permute-start(bf16[16,192,128]{2,1,0:T(8,128)(2,1)} %own.1), channel_id=1, source_target_pairs={{0,1},{1,0},{2,3},{3,2},{4,5},{5,4},{6,7},{7,6},{8,9},{9,8},{10,11... | collective-permute-start | bytes 2359304 | tf_op jit(solution)/shard_map/ppermute | solution.py:26
  0.5 21.0 %collective-permute-start.1 = (bf16[16,192,128]{2,1,0:T(8,128)(2,1)}, bf16[16,192,128]{2,1,0:T(8,128)(2,1)}, u32[]{:S(2)}, u32[]{:S(2)}) collective-permute-start(bf16[16,192,128]{2,1,0:T(8,128)(2,1)} %own.1), channel_id=1, source_target_pairs={{0,2},{2,0},{1,3},{3,1},{4,6},{6,4},{5,7},{7,5},{8,10},{10,8},{9,1... | collective-permute-start | bytes 2359304 | tf_op jit(solution)/shard_map/ppermute | solution.py:18
  8.5 1.7 copy-start
  8.5 2.1 copy-start.1
  21.5 4.6 %collective-permute-start.2 = (bf16[16,192,128]{2,1,0:T(8,128)(2,1)}, bf16[16,192,128]{2,1,0:T(8,128)(2,1)}, u32[]{:S(2)}, u32[]{:S(2)}) collective-permute-start(bf16[16,192,128]{2,1,0:T(8,128)(2,1)} %collective-permute-done.1.far), channel_id=1, source_target_pairs={{0,1},{1,0},{2,3},{3,2},{4,5},{5,4},{6,7},{7,6},{8,9},{9,8},{10,11... | collective-permute-start | bytes 2359304 | tf_op jit(solution)/shard_map/ppermute | solution.py:26
  22.4 19.1 %collective-permute-start.3 = (bf16[480,768]{1,0:T(8,128)(2,1)}, bf16[480,768]{1,0:T(8,128)(2,1)S(1)}, u32[]{:S(2)}, u32[]{:S(2)}) collective-permute-start(bf16[480,768]{1,0:T(8,128)(2,1)} %constant_dynamic-slice_fusion.2), channel_id=1, source_target_pairs={{0,2},{2,0},{1,3},{3,1},{4,6},{6,4},{5,7},{7,5},{8,10},{10,8},{9,1... | collective-permute-start | bytes 2211848 | tf_op jit(solution)/shard_map/ppermute | solution.py:18
  26.1 1.1 copy-start.5
  27.2 1.2 copy-start.7
  28.4 19.2 %copy-start.11 = (s32[4]{0:T(128)S(1)}, s32[4]{0:T(128)}, u32[]{:S(2)}) copy-start(s32[4]{0:T(128)} %param.12) | copy-start | bytes 52
  41.5 6.2 %copy-start.3 = (bf16[480,768]{1,0:T(8,128)(2,1)}, bf16[480,768]{1,0:T(8,128)(2,1)S(1)}, u32[]{:S(2)}) copy-start(bf16[480,768]{1,0:T(8,128)(2,1)S(1)} %collective-permute-done.3.piece) | copy-start | bytes 2211844
  41.5 14.0 %all-to-all-start = ((bf16[8,6,16,128]{3,2,1,0:T(8,128)(2,1)}), bf16[8,6,16,128]{3,2,1,0:T(8,128)(2,1)}, u32[]{:S(2)}, u32[]{:S(2)}) async-start(bf16[8,6,16,128]{3,2,1,0:T(8,128)(2,1)} %get-tuple-element.22), calls=%async_computation | async-start | bytes 393216 | tf_op jit(solution)/shard_map/all_to_all | solution.py:58
  50.0 30.0 %collective-permute-start.5 = (bf16[768,768]{1,0:T(8,128)(2,1)}, bf16[768,768]{1,0:T(8,128)(2,1)S(1)}, u32[]{:S(2)}, u32[]{:S(2)}) collective-permute-start(bf16[768,768]{1,0:T(8,128)(2,1)} %constant_dynamic-slice_fusion.1), channel_id=1, source_target_pairs={{0,2},{2,0},{1,3},{3,1},{4,6},{6,4},{5,7},{7,5},{8,10},{10,8},{9,1... | collective-permute-start | bytes 3538952 | tf_op jit(solution)/shard_map/ppermute | solution.py:18
  59.7 11.9 %all-to-all-start.1 = ((bf16[8,2,3,16,128]{4,3,2,1,0:T(8,128)(2,1)}), bf16[8,2,3,16,128]{4,3,2,1,0:T(8,128)(2,1)}, u32[]{:S(2)}, u32[]{:S(2)}) async-start(bf16[8,2,3,16,128]{4,3,2,1,0:T(8,128)(2,1)} %bitcast.97), calls=%async_computation.1 | async-start | bytes 393216 | tf_op jit(solution)/shard_map/all_to_all | solution.py:64
  63.7 19.2 %collective-permute-start.4 = (bf16[480,768]{1,0:T(8,128)(2,1)}, bf16[480,768]{1,0:T(8,128)(2,1)}, u32[]{:S(2)}, u32[]{:S(2)}) collective-permute-start(bf16[480,768]{1,0:T(8,128)(2,1)} %copy-done.3), channel_id=1, source_target_pairs={{0,4},{4,0},{1,5},{5,1},{2,6},{6,2},{3,7},{7,3},{8,12},{12,8},{9,1... | collective-permute-start | bytes 2211848 | tf_op jit(solution)/shard_map/ppermute | solution.py:22
  80.0 2.9 %copy-start.17 = (bf16[16,3,64,128]{3,2,1,0:T(8,128)(2,1)}, bf16[16,3,64,128]{3,2,1,0:T(8,128)(2,1)S(1)}, u32[]{:S(2)}) copy-start(bf16[16,3,64,128]{3,2,1,0:T(8,128)(2,1)S(1)} %convolution_convert_fusion) | copy-start | bytes 2359300
  83.7 9.4 %collective-permute-start.6 = (bf16[8,192,128]{2,1,0:T(8,128)(2,1)}, bf16[8,192,128]{2,1,0:T(8,128)(2,1)}, u32[]{:S(2)}, u32[]{:S(2)}) collective-permute-start(bf16[8,192,128]{2,1,0:T(8,128)(2,1)} %constant_dynamic-slice_fusion), channel_id=1, source_target_pairs={{0,2},{2,0},{1,3},{3,1},{4,6},{6,4},{5,7},{7,5},{8,10},{10,8},{9,1... | collective-permute-start | bytes 1179656 | tf_op jit(solution)/shard_map/ppermute | solution.py:18
  85.2 9.7 %copy-start.18 = (bf16[16,3,64,128]{3,2,1,0:T(8,128)(2,1)S(1)}, bf16[16,3,64,128]{3,2,1,0:T(8,128)(2,1)}, u32[]{:S(2)}) copy-start(bf16[16,3,64,128]{3,2,1,0:T(8,128)(2,1)} %copy-done.17) | copy-start | bytes 2359300
  85.2 9.7 %copy-start.19 = (bf16[192,768]{1,0:T(8,128)(2,1)S(1)}, bf16[192,768]{1,0:T(8,128)(2,1)}, u32[]{:S(2)}) copy-start(bf16[192,768]{1,0:T(8,128)(2,1)} %param.14) | copy-start | bytes 884740
  85.2 25.8 %collective-permute-start.8 = (bf16[768,768]{1,0:T(8,128)(2,1)S(1)}, bf16[768,768]{1,0:T(8,128)(2,1)}, u32[]{:S(2)}, u32[]{:S(2)}) collective-permute-start(bf16[768,768]{1,0:T(8,128)(2,1)S(1)} %collective-permute-done.5.piece), channel_id=1, source_target_pairs={{0,4},{4,0},{1,5},{5,1},{2,6},{6,2},{3,7},{7,3},{8,12},{12,8},{9,1... | collective-permute-start | bytes 3538952 | tf_op jit(solution)/shard_map/ppermute | solution.py:22
  95.6 1.6 copy-start.15
  98.2 4.2 %collective-permute-start.7 = (bf16[4,128,768]{1,2,0:T(8,128)(2,1)}, bf16[4,128,768]{1,2,0:T(8,128)(2,1)}, u32[]{:S(2)}, u32[]{:S(2)}) collective-permute-start(bf16[4,128,768]{1,2,0:T(8,128)(2,1)} %dynamic-slice_convert_fusion), channel_id=1, source_target_pairs={{0,1},{1,0},{2,3},{3,2},{4,5},{5,4},{6,7},{7,6},{8,9},{9,8},{10,11... | collective-permute-start | bytes 2359304 | tf_op jit(solution)/shard_map/ppermute | solution.py:26
  98.2 4.2 %copy-start.16 = (f32[8,128,768]{1,2,0:T(8,128)S(1)}, f32[8,128,768]{1,2,0:T(8,128)}, u32[]{:S(2)}) copy-start(f32[8,128,768]{1,2,0:T(8,128)} %copy-done.15) | copy-start | bytes 9437188
  147.7 4.7 %copy-start.20 = (f32[8,64]{1,0:T(8,128)S(1)}, f32[8,64]{1,0:T(8,128)}, u32[]{:S(2)}) copy-start(f32[8,64]{1,0:T(8,128)} %copy.90) | copy-start | bytes 6148
  151.3 1.2 copy-start.12
  153.8 3.8 %collective-permute-start.9 = (bf16[8,64,768]{2,1,0:T(8,128)(2,1)}, bf16[8,64,768]{2,1,0:T(8,128)(2,1)}, u32[]{:S(2)}, u32[]{:S(2)}) collective-permute-start(bf16[8,64,768]{2,1,0:T(8,128)(2,1)} %multiply_convert_fusion.own), channel_id=1, source_target_pairs={{0,1},{1,0},{2,3},{3,2},{4,5},{5,4},{6,7},{7,6},{8,9},{9,8},{10,11... | collective-permute-start | bytes 2359304 | tf_op jit(solution)/shard_map/ppermute | solution.py:26
  157.6 1.2 copy-start.2
  158.8 1.1 copy-start.4
  159.9 1.0 copy-start.6
  161.7 15.9 %copy-start.13 = (f32[16,4,8,768]{3,2,1,0:T(8,128)S(1)}, f32[16,4,8,768]{3,2,1,0:T(8,128)}, u32[]{:S(2)}) copy-start(f32[16,4,8,768]{3,2,1,0:T(8,128)} %copy-done.12) | copy-start | bytes 4718596
  175.2 2.5 %collective-permute-start.10 = (bf16[8,64,768]{2,1,0:T(8,128)(2,1)S(1)}, bf16[8,64,768]{2,1,0:T(8,128)(2,1)S(1)}, u32[]{:S(2)}, u32[]{:S(2)}) collective-permute-start(bf16[8,64,768]{2,1,0:T(8,128)(2,1)S(1)} %get-tuple-element.30), channel_id=1, source_target_pairs={{0,1},{1,0},{2,3},{3,2},{4,5},{5,4},{6,7},{7,6},{8,9},{9,8},{10,11... | collective-permute-start | bytes 2359304 | tf_op jit(solution)/shard_map/ppermute | solution.py:26
  179.0 2.4 %collective-permute-start.11 = (bf16[8,64,768]{2,1,0:T(8,128)(2,1)S(1)}, bf16[8,64,768]{2,1,0:T(8,128)(2,1)S(1)}, u32[]{:S(2)}, u32[]{:S(2)}) collective-permute-start(bf16[8,64,768]{2,1,0:T(8,128)(2,1)S(1)} %fusion.4), channel_id=1, source_target_pairs={{0,1},{1,0},{2,3},{3,2},{4,5},{5,4},{6,7},{7,6},{8,9},{9,8},{10,11... | collective-permute-start | bytes 2359304 | tf_op jit(solution)/shard_map/ppermute | solution.py:26
  185.6 4.5 %collective-permute-start.12 = (bf16[8,64,768]{2,1,0:T(8,128)(2,1)S(1)}, bf16[8,64,768]{2,1,0:T(8,128)(2,1)S(1)}, u32[]{:S(2)}, u32[]{:S(2)}) collective-permute-start(bf16[8,64,768]{2,1,0:T(8,128)(2,1)S(1)} %bitcast.84), channel_id=1, source_target_pairs={{0,1},{1,0},{2,3},{3,2},{4,5},{5,4},{6,7},{7,6},{8,9},{9,8},{10,11... | collective-permute-start | bytes 2359304 | tf_op jit(solution)/shard_map/ppermute | solution.py:26
  (4 other events, 3.3 us)
where the time goes:
time: 219 us; the launch traced here: 217 us
  local copies, waits for them, and re-layouts  48.9 us (22%)
  blocking collectives  46.6 us (21%)
  waiting for transfers between devices  42.1 us (19%)
  Pallas kernels  29.9 us (14%)
  starting transfers between devices  22.4 us (10%)
  other arithmetic  19.7 us (9%)
  matrix products  6.41 us (3%)
    all_to_all x1, blocking collectives, shards(): after_row = lax.all_to_all(after_row, ROWS + ('chip',), 0, 0, tiled=True)  23.8 us
    all_to_all x1, blocking collectives, shards(): lax.all_to_all(finished, ROWS + ('chip', 'core'), 0, 0, tiled=True)  22.8 us
    ppermute x4, waiting for transfers between devices, other_chip(): return lax.ppermute(value, 'chip', SWAP)  19.2 us
    pallas_call x1, Pallas kernels, column(): pl.pallas_call(column_kernel, out_shape=(jax.ShapeDtypeStruct(own.shape,...  13.4 us
    unnamed x42, local copies, waits for them, and re-layouts  12.2 us
    ppermute x2, waiting for transfers between devices, other_pair(): return lax.ppermute(value, 'pair', SWAP)  9.01 us
    pallas_call x1, Pallas kernels, row_front(): pl.pallas_call(functools.partial(row_front_kernel, count), grid=(count,),...  8.26 us
    pallas_call x2, Pallas kernels, feed_forward(): pl.pallas_call(feed_forward_kernel, out_shape=jax.ShapeDtypeStruct((token...  8.24 us
  transfers between devices with their start and end apart: 15, of which 9 were waited for; matrix products, arithmetic and copies ran while one was open for 18% of the time, Pallas kernels for 6%

commit v1 on v0

--- a/solution.py
+++ b/solution.py
@@ -49,20 +49,6 @@
     live = jnp.arange(tables.shape[-1])[None, :] < tally[:, None]
     tables = jnp.where(live[:, None, None, :], tables, -jnp.inf)
     return jax.nn.softmax(tables, axis=-1).astype(BF16)
-
-
-def tied_weights(shared, label, tally):
-    row_groups, _, rows, sites = shared.shape
-    lines = label.shape[0] // row_groups
-    ends = label.reshape(row_groups, lines)[:, jnp.array([0, lines - 1])]
-    parts = lax.all_to_all(shared, ROWS, 0, 0, tiled=True).astype(F32)
-    parts = parts.reshape(row_groups, 2, -1, rows, sites)
-    families = jnp.arange(tally.shape[0])
-    member = (ends[:, :, None] == families).astype(F32)
-    totals = jnp.einsum("stf,sthij->fhij", member, parts, precision=lax.Precision.HIGHEST)
-    weights = masked_softmax(totals, tally)
-    back = lax.all_to_all(weights[ends], ROWS, 0, 0, tiled=True)
-    return jnp.transpose(back, (1, 2, 0, 3, 4)).reshape(2, -1, sites, sites)
 
 
 CONTRACT_FIRST = (((0,), (0,)), ((), ()))
@@ -164,7 +150,219 @@
     )(spots, slot, scaling, inner_tally, *pieces, triple.reshape(3 * quarter, 4 * quarter))
     if rows % 16:
         tables = jnp.transpose(tables.reshape(-1, row_groups, rows, sites), (1, 0, 2, 3))
-    return tables, inner_weights.reshape(inner, heads, sites, sites), values
+    return tables, inner_weights, values
+
+
+def tie_kernel(end_ref, tally_ref, parts, out, weights):
+    groups, pairs, rows, sites = parts.shape
+    heads = pairs // 2
+    site = lax.broadcasted_iota(jnp.int32, (heads, rows, sites), 2)
+    for family in range(weights.shape[0]):
+        total = jnp.zeros((heads, rows, sites), F32)
+        for group in range(groups):
+            for end in range(2):
+                part = parts[group, end * heads : (end + 1) * heads].astype(F32)
+                total += jnp.where(end_ref[2 * group + end] == family, part, 0.0)
+        total = jnp.where(site < tally_ref[family], total, -jnp.inf)
+        total = jnp.exp(total - jnp.max(total, axis=-1, keepdims=True))
+        total = total / jnp.sum(total, axis=-1, keepdims=True)
+        weights[family] = total.astype(BF16)
+    for group in range(groups):
+        for end in range(2):
+            chosen = weights[end_ref[2 * group + end]]
+            out[group, end * heads : (end + 1) * heads] = chosen
+
+
+def tie(parts, ends, tally):
+    groups, pairs, rows, sites = parts.shape
+    if rows % 16 == 0:
+        return pl.pallas_call(
+            tie_kernel,
+            out_shape=jax.ShapeDtypeStruct(parts.shape, BF16),
+            in_specs=[IN_SMEM, IN_SMEM, IN_VMEM],
+            out_specs=IN_VMEM,
+            scratch_shapes=[pltpu.VMEM((tally.shape[0], pairs // 2, rows, sites), BF16)],
+            compiler_params=GRANT,
+            name="tie",
+        )(ends, tally, parts)
+    ends = ends.reshape(groups, 2)
+    parts = parts.astype(F32).reshape(groups, 2, -1, rows, sites)
+    member = (ends[:, :, None] == jnp.arange(tally.shape[0])).astype(F32)
+    totals = jnp.einsum("stf,sthij->fhij", member, parts, precision=lax.Precision.HIGHEST)
+    return masked_softmax(totals, tally)[ends].reshape(groups, pairs, rows, sites)
+
+
+def mix_kernel(spot_ref, slot_ref, shared, inner, values, kept, sent):
+    pairs, sites = shared.shape[1], values.shape[2]
+    heads = pairs // 2
+    half = kept.shape[0]
+
+    def run(weights):
+        weights[: 2 * heads] = jnp.stack(
+            [shared[:, index].reshape(sites, sites) for index in range(2 * heads)]
+        )
+        weights[2 * heads :] = inner[...]
+        for target, chip in ((sent, 1 - spot_ref[0]), (kept, spot_ref[0])):
+            for line in range(half):
+                row = chip * half + line
+                slot = slot_ref[row]
+                value = values[row]
+                for head in range(heads):
+                    features = slice(head * HEAD_SIZE, (head + 1) * HEAD_SIZE)
+                    target[line, features] = lax.dot_general(
+                        value[features],
+                        weights[slot * heads + head],
+                        CONTRACT_LAST,
+                        preferred_element_type=F32,
+                    ).astype(BF16)
+
+    pl.run_scoped(run, pltpu.VMEM((2 * heads + inner.shape[0], sites, sites), BF16))
+
+
+def mix(shared, inner, values, slot, chip):
+    groups, pairs, rows, sites = shared.shape
+    lines, quarter, _ = values.shape
+    if rows % 16 == 0:
+        half = jax.ShapeDtypeStruct((lines // 2, quarter, sites), BF16)
+        return pl.pallas_call(
+            mix_kernel,
+            out_shape=(half, half),
+            in_specs=[IN_SMEM, IN_SMEM] + [IN_VMEM] * 3,
+            out_specs=(IN_VMEM, IN_VMEM),
+            compiler_params=GRANT,
+            name="mix",
+        )(chip.astype(jnp.int32).reshape(1), slot, shared, inner, values)
+    ends = jnp.transpose(shared, (1, 0, 2, 3)).reshape(2, pairs // 2, sites, sites)
+    weights = jnp.concatenate([ends, inner.reshape(-1, *ends.shape[1:])])[slot]
+    values = values.reshape(lines, -1, HEAD_SIZE, sites)
+    mixed = jnp.einsum("rhdj,rhij->rhdi", values, weights, preferred_element_type=F32)
+    mixed = mixed.astype(BF16).reshape(lines, quarter, sites)
+    return half_rows(mixed, chip), half_rows(mixed, 1 - chip)
+
+
+def project_kernel(
+    spot_ref, line_ref, mixed, got, mixing, piece, rest, own, near, across, diagonal,
+    kept, sent, stream, far, semaphores,
+):
+    lines, _, sites = stream.shape
+    quarter = mixing.shape[0]
+    copies = []
+    for index, source in enumerate((own, near, across, diagonal)):
+        spot = pl.multiple_of(spot_ref[index] * quarter, quarter)
+        copies.append(
+            pltpu.make_async_copy(
+                source.at[pl.ds(line_ref[0], lines)],
+                stream.at[:, pl.ds(spot, quarter)],
+                semaphores.at[index],
+            )
+        )
+    for copy in copies:
+        copy.start()
+    pair, core = line_ref[1], line_ref[2]
+
+    @pl.when(pair == 0)
+    def _():
+        far[...] = piece[:quarter]
+
+    @pl.when(pair != 0)
+    def _():
+        far[...] = rest[:quarter]
+
+    def partial(row):
+        near_part = lax.dot_general(
+            mixed[row], mixing[...], CONTRACT_FIRST, preferred_element_type=F32
+        )
+        return near_part + lax.dot_general(
+            got[row], far[...], CONTRACT_FIRST, preferred_element_type=F32
+        )
+
+    for line in range(lines):
+        sent[line] = partial((1 - core) * lines + line).astype(BF16)
+    for copy in copies:
+        copy.wait()
+    for line in range(lines):
+        kept[line] = partial(core * lines + line) + stream[line].astype(F32).T
+
+
+def project(mixed, got, mixing, piece, rest, pieces, spots, place):
+    half, quarter, sites = mixed.shape
+    lines, model = half // 2, mixing.shape[1]
+    out = (lines, sites, model)
+    return pl.pallas_call(
+        project_kernel,
+        out_shape=(jax.ShapeDtypeStruct(out, F32), jax.ShapeDtypeStruct(out, BF16)),
+        in_specs=[IN_SMEM, IN_SMEM] + [IN_VMEM] * 5 + [ANYWHERE] * 4,
+        out_specs=(IN_VMEM, IN_VMEM),
+        scratch_shapes=[
+            pltpu.VMEM((lines, model, sites), BF16),
+            pltpu.VMEM((quarter, model), BF16),
+            pltpu.SemaphoreType.DMA((4,)),
+        ],
+        compiler_params=GRANT,
+        name="project",
+    )(spots, place, mixed, got, mixing, piece, rest, *pieces)
+
+
+def settle_kernel(kept, got, out):
+    lines, sites, model = kept.shape
+    chips = out.shape[0]
+    parts = []
+    for line in range(lines):
+        total = kept[line] + got[line].astype(F32)
+        parts.append(total.reshape(chips, sites // chips, model))
+    out[...] = jnp.concatenate(parts, axis=1).astype(BF16)
+
+
+def settle(kept, got, chips):
+    lines, sites, model = kept.shape
+    place = sites // chips
+    if place % 8 == 0:
+        return pl.pallas_call(
+            settle_kernel,
+            out_shape=jax.ShapeDtypeStruct((chips, lines * place, model), BF16),
+            in_specs=[IN_VMEM, IN_VMEM],
+            out_specs=IN_VMEM,
+            compiler_params=GRANT,
+            name="settle",
+        )(kept, got)
+    total = (kept + got.astype(F32)).astype(BF16).reshape(lines, chips, place, model)
+    return jnp.transpose(total, (1, 0, 2, 3)).reshape(chips, lines * place, model)
+
+
+def arrive_kernel(blocks, normed, stream, tokens):
+    chips, count, model = blocks.shape
+    places, rows, _ = normed.shape
+    lanes = tokens.shape[-1]
+    flat = blocks[...].reshape(chips * count, model).astype(F32)
+    for index in range(tokens.shape[0]):
+        tokens[index] = flat[:, index * lanes : (index + 1) * lanes]
+    for place in range(places):
+        values = [
+            tokens[index, pl.ds(place, rows, stride=places), :] for index in range(tokens.shape[0])
+        ]
+        values = jnp.concatenate(values, axis=-1)
+        stream[place] = values.astype(BF16)
+        centred = values - jnp.mean(values, axis=-1, keepdims=True)
+        variance = jnp.mean(centred * centred, axis=-1, keepdims=True)
+        normed[place] = (centred * lax.rsqrt(variance + 1e-05)).astype(BF16)
+
+
+def arrive(blocks, place):
+    chips, count, model = blocks.shape
+    rows = chips * count // place
+    if place % 8 == 0:
+        shape = jax.ShapeDtypeStruct((place, rows, model), BF16)
+        return pl.pallas_call(
+            arrive_kernel,
+            out_shape=(shape, shape),
+            in_specs=[IN_VMEM],
+            out_specs=(IN_VMEM, IN_VMEM),
+            scratch_shapes=[pltpu.VMEM((model // 128, chips * count, 128), F32)],
+            compiler_params=GRANT,
+            name="arrive",
+        )(blocks)
+    stream = jnp.transpose(blocks.reshape(rows, place, model), (1, 0, 2))
+    return own_norm(stream, -1), stream
 
 
 def column_kernel(
@@ -386,33 +584,30 @@
         pieces, horizontal_triple_matrix, spots, slot, scaling, tally[inner], row_groups
     )
     tables, first_piece = lax.optimization_barrier((tables, first_piece))
-    weights = jnp.concatenate([tied_weights(tables, label, tally), inner_weights])[slot]
-    values = values.reshape(lines, -1, HEAD_SIZE, sites)
-    mixed = jnp.einsum("rhdj,rhij->rhdi", values, weights, preferred_element_type=F32)
-    mixed = mixed.astype(BF16).reshape(lines, quarter, sites)
-
-    mixed, first_rest, second_piece = lax.optimization_barrier((mixed, first_rest, second_piece))
-    far_mixing = jnp.where(pair == 0, first_piece[:quarter], first_rest[:quarter])
-    kept = half_rows(mixed, chip)
-    got = other_chip(half_rows(mixed, 1 - chip))
-    partial = jnp.einsum("rdi,de->rie", kept, horizontal_mixing_matrix, preferred_element_type=F32)
-    partial += jnp.einsum("rdi,de->rie", got, far_mixing, preferred_element_type=F32)
-    sent = other_core(half_rows(partial, 1 - core).astype(BF16))
-    ours = [half_rows(half_rows(piece, chip), core) for piece in pieces]
-    stream = in_order(
-        in_order(ours[0], ours[1], core, 1), in_order(ours[2], ours[3], core, 1), chip, 1
-    )
-    residual = jnp.transpose(stream, (0, 2, 1))
-    after_row = residual.astype(F32) + half_rows(partial, core) + sent.astype(F32)
-    after_row = after_row.astype(BF16)
-
-    after_row, second_rest = lax.optimization_barrier((after_row, second_rest))
+    ends = label.reshape(row_groups, lines)[:, jnp.array([0, lines - 1])].reshape(-1)
+    shared = tie(lax.all_to_all(tables, ROWS, 0, 0, tiled=True), ends, tally)
+    shared = lax.all_to_all(shared, ROWS, 0, 0, tiled=True)
+    mixed, sent = mix(shared, inner_weights, values, slot, chip)
+
+    sent, first_rest, second_piece = lax.optimization_barrier((sent, first_rest, second_piece))
     own = lines // 4
-    model = after_row.shape[-1]
-    after_row = jnp.transpose(after_row.reshape(own, chips, place, model), (1, 0, 2, 3))
-    after_row = lax.all_to_all(after_row, ROWS + ("chip",), 0, 0, tiled=True)
-    after_row = jnp.transpose(after_row, (2, 0, 1, 3)).reshape(place, chips * own, model)
     rows = chips * own
+    here = jnp.stack([(2 * chip + core) * own, pair, core]).astype(jnp.int32)
+    kept, sent = project(
+        mixed,
+        other_chip(sent),
+        horizontal_mixing_matrix,
+        first_piece,
+        first_rest,
+        pieces,
+        spots,
+        here,
+    )
+
+    blocks = settle(kept, other_core(sent), chips)
+    blocks, second_rest = lax.optimization_barrier((blocks, second_rest))
+    blocks = lax.all_to_all(blocks, ROWS + ("chip",), 0, 0, tiled=True)
+    normed, after_row = arrive(blocks, place)
     label_cores = label.reshape(chips, 2, own)
     label_sites = jnp.concatenate(
         [
@@ -422,7 +617,6 @@
     )
 
     parity = pair.astype(jnp.int32).reshape(1)
-    normed = own_norm(after_row, -1)
     kept, sent = column(
         normed,
         other_core(normed),
@@ -441,7 +635,8 @@
     sent = feed_forward(other_core(normed), *feed, BF16)
     finished = core_sum(after_col, kept, sent)
 
-    finished = finished.reshape(place, row_groups, 2 * own, model // quarter, quarter)
+    heads = after_col.shape[-1] // quarter
+    finished = finished.reshape(place, row_groups, 2 * own, heads, quarter)
     finished = jnp.transpose(finished, (1, 3, 2, 0, 4)).reshape(-1, 2 * own * place, quarter)
     parts, wide = 2 * own * place // 2, quarter // 3 * 2
     finished = jnp.concatenate(

time: 219 us -> 193 us (0.88)
  local copies, waits for them, and re-layouts: 48.9 us -> 32.5 us
  other arithmetic: 19.7 us -> 11.2 us
  starting transfers between devices: 22.4 us -> 14.8 us
  Pallas kernels: 29.9 us -> 37.4 us
  matrix products: 6.41 us -> 0 us
  blocking collectives: 46.6 us -> 52.5 us
    ppermute x4, waiting for transfers between devices: 19.2 us -> 27.7 us  [other_chip(): return lax.ppermute(value, 'chip', SWAP)]
    pallas_call x0 -> x5, Pallas kernels: none -> 8.41 us  [the longest x1 3.31 us: project(): pl.pallas_call(project_kernel, out_shape=(jax.ShapeDtypeStruct(out, F32),...]
    all_to_all x2 -> x1, waiting for transfers between devices: 9.99 us -> 3.08 us  [shards(): shared = tie(lax.all_to_all(tables, ROWS, 0, 0, tiled=True), ends, tally)]
    dot_general x4 -> x0, matrix products: 6.41 us -> none  [the longest x1 2.83 us: shards(): jnp.einsum('rhdj,rhij->rhdi', values, weights, preferred_element_type=F32)]
    all_to_all x1 -> x2, blocking collectives: 23.8 us -> 29.7 us  [the longest x1 19.1 us: shards(): blocks = lax.all_to_all(blocks, ROWS + ('chip',), 0, 0, tiled=True)]
    all_to_all x2 -> x1, starting transfers between devices: 10.1 us -> 4.88 us  [shards(): shared = tie(lax.all_to_all(tables, ROWS, 0, 0, tiled=True), ends, tally)]
    dynamic_slice x7 -> x2, local copies, waits for them, and re-layouts: 8.01 us -> 3.28 us  [half_rows(): return lax.dynamic_slice_in_dim(value, index * rows, rows)]
    convert_element_type x3 -> x0, other arithmetic: 3.81 us -> none  [the longest x1 2.4 us: shards(): after_row = after_row.astype(BF16)]
  transfers between devices with their start and end apart: 15 -> 14, of which waited for: 9 -> 8; matrix products, arithmetic and copies ran while one was open for 18% -> 12% of each run, Pallas kernels for 6% -> 10%
where the time goes in v1:
time: 193 us; the launch traced here: 192 us
  blocking collectives  52.5 us (27%)
  waiting for transfers between devices  42.8 us (22%)
  Pallas kernels  37.4 us (19%)
  local copies, waits for them, and re-layouts  32.5 us (17%)
  starting transfers between devices  14.8 us (8%)
  other arithmetic  11.2 us (6%)
    ppermute x4, waiting for transfers between devices, other_chip(): return lax.ppermute(value, 'chip', SWAP)  27.7 us
    all_to_all x1, blocking collectives, shards(): lax.all_to_all(finished, ROWS + ('chip', 'core'), 0, 0, tiled=True)  22.8 us
    all_to_all x1, blocking collectives, shards(): blocks = lax.all_to_all(blocks, ROWS + ('chip',), 0, 0, tiled=True)  19.1 us
    unnamed x42, local copies, waits for them, and re-layouts  14.9 us
    pallas_call x1, Pallas kernels, column(): pl.pallas_call(column_kernel, out_shape=(jax.ShapeDtypeStruct(own.shape,...  13.1 us
    all_to_all x1, blocking collectives, shards(): shared = lax.all_to_all(shared, ROWS, 0, 0, tiled=True)  10.5 us
    pallas_call x2, Pallas kernels, feed_forward(): pl.pallas_call(feed_forward_kernel, out_shape=jax.ShapeDtypeStruct((token...  8.24 us
    pallas_call x1, Pallas kernels, row_front(): pl.pallas_call(functools.partial(row_front_kernel, count), grid=(count,),...  7.62 us
  transfers between devices with their start and end apart: 14, of which 8 were waited for; matrix products, arithmetic and copies ran while one was open for 12% of the time, Pallas kernels for 10%

profile of v1, /device:TPU:0, one launch (start us, length us, event | category | flops | bytes accessed | tf_op | source)
XLA Modules:
  0.0 192.1 jit_solution(13380873193192839951)
XLA Ops:
  0.0 2.9 %collective-permute-start.1 = (bf16[16,192,128]{2,1,0:T(8,128)(2,1)}, bf16[16,192,128]{2,1,0:T(8,128)(2,1)}, u32[]{:S(2)}, u32[]{:S(2)}) collective-permute-start(bf16[16,192,128]{2,1,0:T(8,128)(2,1)} %own.3), channel_id=1, source_target_pairs={{0,2},{2,0},{1,3},{3,1},{4,6},{6,4},{5,7},{7,5},{8,10},{10,8},{9,1... | collective-permute-start | bytes 2359304 | tf_op jit(solution)/shard_map/ppermute | solution.py:18
  4.3 1.4 pad_maximum_fusion.1
  5.7 1.3 compare_select_fusion.4.slot_ref
  7.0 1.6 pad_maximum_fusion
  8.6 12.2 %collective-permute-done.1.far.across = bf16[16,192,128]{2,1,0:T(8,128)(2,1)} collective-permute-done((bf16[16,192,128]{2,1,0:T(8,128)(2,1)}, bf16[16,192,128]{2,1,0:T(8,128)(2,1)}, u32[]{:S(2)}, u32[]{:S(2)}) %collective-permute-start.1) | collective-permute-done | bytes 786464 | tf_op jit(solution)/shard_map/ppermute | solution.py:18
  21.7 1.7 collective-permute-start.3
  24.9 2.4 %constant_dynamic-slice_fusion = bf16[768,768]{1,0:T(8,128)(2,1)} fusion(bf16[1536,768]{1,0:T(8,128)(2,1)} %pad_maximum_fusion, s32[]{:T(128)S(6)} %select_n.46), kind=kLoop, calls=%fused_computation.31 | loop fusion | bytes 2359300 | tf_op jit(solution)/shard_map/dynamic_slice | solution.py:37
  28.8 1.2 gather_fusion.1
  30.0 1.3 pad_clamp_fusion
  32.4 9.0 %collective-permute-done.3.piece = bf16[480,768]{1,0:T(8,128)(2,1)} collective-permute-done((bf16[480,768]{1,0:T(8,128)(2,1)}, bf16[480,768]{1,0:T(8,128)(2,1)}, u32[]{:S(2)}, u32[]{:S(2)}) %collective-permute-start.3) | collective-permute-done | bytes 737312 | tf_op jit(solution)/shard_map/ppermute | solution.py:18
  41.5 1.8 collective-permute-start.4
  47.0 7.6 %row_front.1 = (bf16[8,6,16,128]{3,2,1,0:T(8,128)(2,1)S(1)}, bf16[6,128,128]{2,1,0:T(8,128)(2,1)S(1)}, bf16[16,192,128]{2,1,0:T(8,128)(2,1)S(1)}) custom-call(s32[4]{0:T(128)S(1)} %pad_add_fusion.spot_ref, s32[16]{0:T(128)S(1)} %compare_select_fusion.4.slot_ref, f32[16]{0:T(128)S(1)} %copy-done.19, s32[2]{0:T(128)S(1)} %gather_fusion.2, ...), custom_call_target="tpu_custom_call" | custom-call | tf_op jit(solution)/shard_map/row_front/pallas_call | solution.py:134
  56.8 4.9 %all-to-all-start = ((bf16[8,6,16,128]{3,2,1,0:T(8,128)(2,1)}), bf16[8,6,16,128]{3,2,1,0:T(8,128)(2,1)}, u32[]{:S(2)}, u32[]{:S(2)}) async-start(bf16[8,6,16,128]{3,2,1,0:T(8,128)(2,1)} %copy-done.16), calls=%async_computation | async-start | bytes 393216 | tf_op jit(solution)/shard_map/all_to_all | solution.py:588
  63.7 1.4 gather_fusion
  66.5 3.1 %all-to-all-done.parts = bf16[8,6,16,128]{3,2,1,0:T(8,128)(2,1)} async-done(((bf16[8,6,16,128]{3,2,1,0:T(8,128)(2,1)}), bf16[8,6,16,128]{3,2,1,0:T(8,128)(2,1)}, u32[]{:S(2)}, u32[]{:S(2)}) %all-to-all-start) | async-done | bytes 196640 | tf_op jit(solution)/shard_map/all_to_all | solution.py:588
  69.6 1.3 tie.1
  70.9 10.5 %all_to_all.20.shared = bf16[8,6,16,128]{3,2,1,0:T(8,128)(2,1)S(1)} all-to-all(bf16[8,6,16,128]{3,2,1,0:T(8,128)(2,1)S(1)} %tie.1), channel_id=1, replica_groups=mesh['plane'=4,'pair'=2,'chip'=2,'core'=2] {'plane','pair'}, dimensions={0} | all-to-all | bytes 393216 | tf_op jit(solution)/shard_map/all_to_all | solution.py:589
  83.5 2.0 %mix.1 = (bf16[8,192,128]{2,1,0:T(8,128)(2,1)S(1)}, bf16[8,192,128]{2,1,0:T(8,128)(2,1)}) custom-call(s32[1]{0:T(128)} %bitcast.7.spot_ref, s32[16]{0:T(128)S(1)} %compare_select_fusion.4.slot_ref, bf16[8,6,16,128]{3,2,1,0:T(8,128)(2,1)S(1)} %all_to_all.20.shared, bf16[6,128,128]{2,1,0:T(8,128)(2,1)S(1)} %copy-done.18, bf16[16,192,128]{2,1,0:T(8,128)(2,1)S(1)} %copy-done.12), custom_call_target="tpu_custom_call" | custom-call | tf_op jit(solution)/shard_map/mix/pallas_call | solution.py:227
  86.2 1.5 collective-permute-start.6
  87.8 6.5 %collective-permute-done.6.got = bf16[8,192,128]{2,1,0:T(8,128)(2,1)} collective-permute-done((bf16[8,192,128]{2,1,0:T(8,128)(2,1)}, bf16[8,192,128]{2,1,0:T(8,128)(2,1)}, u32[]{:S(2)}, u32[]{:S(2)}) %collective-permute-start.6) | collective-permute-done | bytes 393248 | tf_op jit(solution)/shard_map/ppermute | solution.py:18
  97.4 3.3 %project.1 = (f32[4,128,768]{2,1,0:T(8,128)S(1)}, bf16[4,128,768]{2,1,0:T(8,128)(2,1)S(1)}) custom-call(s32[4]{0:T(128)S(1)} %pad_add_fusion.spot_ref, s32[3]{0:T(128)S(1)} %pad_add_fusion.1.line_ref, bf16[8,192,128]{2,1,0:T(8,128)(2,1)S(1)} %copy-done.14, bf16[8,192,128]{2,1,0:T(8,128)(2,1)} %collective-permute-done.6.got, bf16[192,768]{1,0:T(8,128)(2,1)S(1)} %copy-done.6, ...), custom_call_target="tpu_custom_call" | custom-call | tf_op jit(solution)/shard_map/project/pallas_call | solution.py:291
  100.8 2.3 %collective-permute-done.7.got = bf16[4,128,768]{2,1,0:T(8,128)(2,1)S(1)} collective-permute-done((bf16[4,128,768]{2,1,0:T(8,128)(2,1)S(1)}, bf16[4,128,768]{2,1,0:T(8,128)(2,1)S(1)}, u32[]{:S(2)}, u32[]{:S(2)}) %collective-permute-start.7) | collective-permute-done | bytes 786464 | tf_op jit(solution)/shard_map/ppermute | solution.py:26
  103.2 5.9 %collective-permute-done.8.rest = bf16[768,768]{1,0:T(8,128)(2,1)} collective-permute-done((bf16[768,768]{1,0:T(8,128)(2,1)S(1)}, bf16[768,768]{1,0:T(8,128)(2,1)}, u32[]{:S(2)}, u32[]{:S(2)}) %collective-permute-start.8) | collective-permute-done | bytes 1179680 | tf_op jit(solution)/shard_map/ppermute | solution.py:22
  109.1 19.1 %all_to_all.21.blocks = bf16[16,32,768]{2,1,0:T(8,128)(2,1)S(1)} all-to-all(bf16[16,32,768]{2,1,0:T(8,128)(2,1)S(1)} %settle.1), channel_id=1, replica_groups=mesh['plane'=4,'pair'=2,'chip'=2,'core'=2] {'plane','pair','chip'}, dimensions={0} | all-to-all | bytes 1572864 | tf_op jit(solution)/shard_map/all_to_all | solution.py:609
  128.3 1.7 arrive.1
  137.6 13.1 %column.1 = (f32[8,64,768]{2,1,0:T(8,128)S(1)}, bf16[8,64,768]{2,1,0:T(8,128)(2,1)S(1)}) custom-call(s32[1]{0:T(128)} %bitcast.5.pair_ref, s32[1,128]{1,0:T(1,128)S(1)} %get-tuple-element.56.label_row, s32[128,1]{1,0:T(8,128)S(1)} %copy-done.15, bf16[8,64,768]{2,1,0:T(8,128)(2,1)} %get-tuple-element.40.own, ...), custom_call_target="tpu_custom_call" | custom-call | tf_op jit(solution)/shard_map/column/pallas_call | solution.py:431
  151.3 1.9 collective-permute-done.10
  154.7 1.9 collective-permute-done.11
  156.6 4.2 %feed_forward.3 = bf16[512,768]{1,0:T(8,128)(2,1)S(1)} custom-call(s32[1]{0:T(128)} %bitcast.5.pair_ref, bf16[512,768]{1,0:T(8,128)(2,1)S(1)} %bitcast.36, bf16[768,768]{1,0:T(8,128)(2,1)S(1)} %copy-done.1, bf16[768,768]{1,0:T(8,128)(2,1)S(1)} %copy-done.2, bf16[768,768]{1,0:T(8,128)(2,1)S(1)} %collective-permute-done.5.piece, ...), custom_call_target="tpu_custom_call" | custom-call | tf_op jit(solution)/shard_map/feed_forward/pallas_call | solution.py:507
  161.3 4.0 %feed_forward.2 = f32[512,768]{1,0:T(8,128)S(1)} custom-call(s32[1]{0:T(128)} %bitcast.5.pair_ref, bf16[512,768]{1,0:T(8,128)(2,1)S(1)} %bitcast.33, bf16[768,768]{1,0:T(8,128)(2,1)S(1)} %copy-done.1, bf16[768,768]{1,0:T(8,128)(2,1)S(1)} %copy-done.2, bf16[768,768]{1,0:T(8,128)(2,1)S(1)} %collective-permute-done.5.piece, ...), custom_call_target="tpu_custom_call" | custom-call | tf_op jit(solution)/shard_map/feed_forward/pallas_call | solution.py:507
  167.5 22.8 %all_to_all.22 = bf16[32,96,128]{2,1,0:T(8,128)(2,1)S(1)} all-to-all(bf16[32,96,128]{2,1,0:T(8,128)(2,1)S(1)} %maximum_maximum_fusion.1), channel_id=1, replica_groups=mesh['plane'=4,'pair'=2,'chip'=2,'core'=2] {'plane','pair','chip','core'}, dimensions={0} | all-to-all | bytes 1572864 | tf_op jit(solution)/shard_map/all_to_all | solution.py:649
  190.9 1.3 copy.25
  (96 shorter events, 34.1 us)
Async XLA Ops:
  0.0 7.0 %copy-start.2 = (bf16[768,768]{1,0:T(8,128)(2,1)S(1)}, bf16[768,768]{1,0:T(8,128)(2,1)}, u32[]{:S(2)}) copy-start(bf16[768,768]{1,0:T(8,128)(2,1)} %contract.3) | copy-start | bytes 3538948
  0.0 7.0 %copy-start.1 = (bf16[768,768]{1,0:T(8,128)(2,1)S(1)}, bf16[768,768]{1,0:T(8,128)(2,1)}, u32[]{:S(2)}) copy-start(bf16[768,768]{1,0:T(8,128)(2,1)} %expand.3) | copy-start | bytes 3538948
  0.0 20.8 %collective-permute-start.1 = (bf16[16,192,128]{2,1,0:T(8,128)(2,1)}, bf16[16,192,128]{2,1,0:T(8,128)(2,1)}, u32[]{:S(2)}, u32[]{:S(2)}) collective-permute-start(bf16[16,192,128]{2,1,0:T(8,128)(2,1)} %own.3), channel_id=1, source_target_pairs={{0,2},{2,0},{1,3},{3,1},{4,6},{6,4},{5,7},{7,5},{8,10},{10,8},{9,1... | collective-permute-start | bytes 2359304 | tf_op jit(solution)/shard_map/ppermute | solution.py:18
  2.9 41.1 %collective-permute-start = (bf16[16,192,128]{2,1,0:T(8,128)(2,1)}, bf16[16,192,128]{2,1,0:T(8,128)(2,1)}, u32[]{:S(2)}, u32[]{:S(2)}) collective-permute-start(bf16[16,192,128]{2,1,0:T(8,128)(2,1)} %own.3), channel_id=1, source_target_pairs={{0,1},{1,0},{2,3},{3,2},{4,5},{5,4},{6,7},{7,6},{8,9},{9,8},{10,11... | collective-permute-start | bytes 2359304 | tf_op jit(solution)/shard_map/ppermute | solution.py:26
  7.0 17.2 %copy-start.20 = (s32[128]{0:T(128)S(1)}, s32[128]{0:T(128)}, u32[]{:S(2)}) copy-start(s32[128]{0:T(128)} %param.11) | copy-start | bytes 1540
  21.7 21.6 %copy-start = (s32[4]{0:T(128)S(1)}, s32[4]{0:T(128)}, u32[]{:S(2)}) copy-start(s32[4]{0:T(128)} %tally_ref.1) | copy-start | bytes 52
  21.7 19.7 %collective-permute-start.3 = (bf16[480,768]{1,0:T(8,128)(2,1)}, bf16[480,768]{1,0:T(8,128)(2,1)}, u32[]{:S(2)}, u32[]{:S(2)}) collective-permute-start(bf16[480,768]{1,0:T(8,128)(2,1)} %constant_dynamic-slice_fusion.1), channel_id=1, source_target_pairs={{0,2},{2,0},{1,3},{3,1},{4,6},{6,4},{5,7},{7,5},{8,10},{10,8},{9,1... | collective-permute-start | bytes 2211848 | tf_op jit(solution)/shard_map/ppermute | solution.py:18
  24.1 19.9 %collective-permute-start.2 = (bf16[16,192,128]{2,1,0:T(8,128)(2,1)}, bf16[16,192,128]{2,1,0:T(8,128)(2,1)}, u32[]{:S(2)}, u32[]{:S(2)}) collective-permute-start(bf16[16,192,128]{2,1,0:T(8,128)(2,1)} %collective-permute-done.1.far.across), channel_id=1, source_target_pairs={{0,1},{1,0},{2,3},{3,2},{4,5},{5,4},{6,7},{7,6},{8,9},{9,8},{10,11... | collective-permute-start | bytes 2359304 | tf_op jit(solution)/shard_map/ppermute | solution.py:26
  27.3 58.9 %collective-permute-start.5 = (bf16[768,768]{1,0:T(8,128)(2,1)}, bf16[768,768]{1,0:T(8,128)(2,1)S(1)}, u32[]{:S(2)}, u32[]{:S(2)}) collective-permute-start(bf16[768,768]{1,0:T(8,128)(2,1)} %constant_dynamic-slice_fusion), channel_id=1, source_target_pairs={{0,2},{2,0},{1,3},{3,1},{4,6},{6,4},{5,7},{7,5},{8,10},{10,8},{9,1... | collective-permute-start | bytes 3538952 | tf_op jit(solution)/shard_map/ppermute | solution.py:18
  41.5 44.8 %collective-permute-start.4 = (bf16[480,768]{1,0:T(8,128)(2,1)}, bf16[480,768]{1,0:T(8,128)(2,1)}, u32[]{:S(2)}, u32[]{:S(2)}) collective-permute-start(bf16[480,768]{1,0:T(8,128)(2,1)} %collective-permute-done.3.piece), channel_id=1, source_target_pairs={{0,4},{4,0},{1,5},{5,1},{2,6},{6,2},{3,7},{7,3},{8,12},{12,8},{9,1... | collective-permute-start | bytes 2211848 | tf_op jit(solution)/shard_map/ppermute | solution.py:22
  44.1 1.1 copy-start.4
  45.2 1.2 copy-start.8
  54.6 0.9 copy-start.11
  56.8 12.8 %all-to-all-start = ((bf16[8,6,16,128]{3,2,1,0:T(8,128)(2,1)}), bf16[8,6,16,128]{3,2,1,0:T(8,128)(2,1)}, u32[]{:S(2)}, u32[]{:S(2)}) async-start(bf16[8,6,16,128]{3,2,1,0:T(8,128)(2,1)} %copy-done.16), calls=%async_computation | async-start | bytes 393216 | tf_op jit(solution)/shard_map/all_to_all | solution.py:588
  81.4 1.1 copy-start.12
  82.6 0.9 copy-start.18
  85.5 0.8 copy-start.13
  86.2 8.1 %collective-permute-start.6 = (bf16[8,192,128]{2,1,0:T(8,128)(2,1)}, bf16[8,192,128]{2,1,0:T(8,128)(2,1)}, u32[]{:S(2)}, u32[]{:S(2)}) collective-permute-start(bf16[8,192,128]{2,1,0:T(8,128)(2,1)} %get-tuple-element.33), channel_id=1, source_target_pairs={{0,2},{2,0},{1,3},{3,1},{4,6},{6,4},{5,7},{7,5},{8,10},{10,8},{9,1... | collective-permute-start | bytes 1179656 | tf_op jit(solution)/shard_map/ppermute | solution.py:18
  87.7 21.4 %collective-permute-start.8 = (bf16[768,768]{1,0:T(8,128)(2,1)S(1)}, bf16[768,768]{1,0:T(8,128)(2,1)}, u32[]{:S(2)}, u32[]{:S(2)}) collective-permute-start(bf16[768,768]{1,0:T(8,128)(2,1)S(1)} %collective-permute-done.5.piece), channel_id=1, source_target_pairs={{0,4},{4,0},{1,5},{5,1},{2,6},{6,2},{3,7},{7,3},{8,12},{12,8},{9,1... | collective-permute-start | bytes 3538952 | tf_op jit(solution)/shard_map/ppermute | solution.py:22
  94.3 1.1 copy-start.5
  95.5 1.0 copy-start.6
  96.4 1.0 copy-start.14
  100.7 2.4 %collective-permute-start.7 = (bf16[4,128,768]{2,1,0:T(8,128)(2,1)S(1)}, bf16[4,128,768]{2,1,0:T(8,128)(2,1)S(1)}, u32[]{:S(2)}, u32[]{:S(2)}) collective-permute-start(bf16[4,128,768]{2,1,0:T(8,128)(2,1)S(1)} %get-tuple-element.37), channel_id=1, source_target_pairs={{0,1},{1,0},{2,3},{3,2},{4,5},{5,4},{6,7},{7,6},{8,9},{9,8},{10,11... | collective-permute-start | bytes 2359304 | tf_op jit(solution)/shard_map/ppermute | solution.py:26
  130.0 0.9 copy-start.9
  130.8 3.8 %collective-permute-start.9 = (bf16[8,64,768]{2,1,0:T(8,128)(2,1)}, bf16[8,64,768]{2,1,0:T(8,128)(2,1)}, u32[]{:S(2)}, u32[]{:S(2)}) collective-permute-start(bf16[8,64,768]{2,1,0:T(8,128)(2,1)} %get-tuple-element.40.own), channel_id=1, source_target_pairs={{0,1},{1,0},{2,3},{3,2},{4,5},{5,4},{6,7},{7,6},{8,9},{9,8},{10,11... | collective-permute-start | bytes 2359304 | tf_op jit(solution)/shard_map/ppermute | solution.py:26
  134.6 1.2 copy-start.3
  135.8 1.0 copy-start.7
  136.8 0.8 copy-start.15
  137.6 15.6 %copy-start.10 = (bf16[8,64,768]{2,1,0:T(8,128)(2,1)S(1)}, bf16[8,64,768]{2,1,0:T(8,128)(2,1)}, u32[]{:S(2)}) copy-start(bf16[8,64,768]{2,1,0:T(8,128)(2,1)} %copy-done.9) | copy-start | bytes 2359300
  150.7 2.5 %collective-permute-start.10 = (bf16[8,64,768]{2,1,0:T(8,128)(2,1)S(1)}, bf16[8,64,768]{2,1,0:T(8,128)(2,1)S(1)}, u32[]{:S(2)}, u32[]{:S(2)}) collective-permute-start(bf16[8,64,768]{2,1,0:T(8,128)(2,1)S(1)} %get-tuple-element.42), channel_id=1, source_target_pairs={{0,1},{1,0},{2,3},{3,2},{4,5},{5,4},{6,7},{7,6},{8,9},{9,8},{10,11... | collective-permute-start | bytes 2359304 | tf_op jit(solution)/shard_map/ppermute | solution.py:26
  154.2 2.4 %collective-permute-start.11 = (bf16[8,64,768]{2,1,0:T(8,128)(2,1)S(1)}, bf16[8,64,768]{2,1,0:T(8,128)(2,1)S(1)}, u32[]{:S(2)}, u32[]{:S(2)}) collective-permute-start(bf16[8,64,768]{2,1,0:T(8,128)(2,1)S(1)} %fusion.3), channel_id=1, source_target_pairs={{0,1},{1,0},{2,3},{3,2},{4,5},{5,4},{6,7},{7,6},{8,9},{9,8},{10,11... | collective-permute-start | bytes 2359304 | tf_op jit(solution)/shard_map/ppermute | solution.py:26
  160.8 4.5 %collective-permute-start.12 = (bf16[8,64,768]{2,1,0:T(8,128)(2,1)S(1)}, bf16[8,64,768]{2,1,0:T(8,128)(2,1)S(1)}, u32[]{:S(2)}, u32[]{:S(2)}) collective-permute-start(bf16[8,64,768]{2,1,0:T(8,128)(2,1)S(1)} %bitcast.35), channel_id=1, source_target_pairs={{0,1},{1,0},{2,3},{3,2},{4,5},{5,4},{6,7},{7,6},{8,9},{9,8},{10,11... | collective-permute-start | bytes 2359304 | tf_op jit(solution)/shard_map/ppermute | solution.py:26
  (3 other events, 2.0 us)

commit v2 on v1

--- a/solution.py
+++ b/solution.py
@@ -59,17 +59,34 @@
 GRANT = pltpu.CompilerParams(vmem_limit_bytes=40 * 2**20)
 
 
+def slot_of(label_ref, start, lines, line):
+    first, last = label_ref[start], label_ref[start + lines - 1]
+    family = label_ref[start + line]
+    return jnp.where(family == first, 0, jnp.where(family == last, 1, family - first + 1))
+
+
+def quarter_spots(me_ref):
+    chip, core = me_ref[1], me_ref[2]
+    return (
+        2 * chip + core, 2 * chip + 1 - core, 2 * (1 - chip) + core, 2 * (1 - chip) + 1 - core
+    )
+
+
 def row_front_kernel(
-    count, spot_ref, slot_ref, scale_ref, tally_ref, own, near, far, diagonal, triple,
-    table_ref, inner_ref, value_ref, tables, normed,
+    start, lines, me_ref, label_ref, starts_ref, tally_ref, own, near, far, diagonal, triple, *refs
 ):
+    if len(refs) == 3:
+        value_ref, tables, normed = refs
+        before = table_ref = None
+    else:
+        before, table_ref, inner_ref, value_ref, tables, normed = refs
     step = pl.program_id(0)
     group, quarter, sites = own.shape
     heads = quarter // HEAD_SIZE
 
     @pl.when(step == 0)
     def _():
-        tables[...] = jnp.zeros_like(tables)
+        tables[...] = jnp.zeros_like(tables) if before is None else before[...]
 
     pieces = []
     for ref in (own, near, far, diagonal):
@@ -80,15 +97,19 @@
     pieces = [piece - average for piece in pieces]
     variance = sum(jnp.sum(piece * piece, axis=0, keepdims=True) for piece in pieces) / size
     inverse = lax.rsqrt(variance + 1e-05)
-    for index, piece in enumerate(pieces):
-        spot = pl.multiple_of(spot_ref[index] * quarter, quarter)
+    for spot, piece in zip(quarter_spots(me_ref), pieces):
+        spot = pl.multiple_of(spot * quarter, quarter)
         normed[pl.ds(spot, quarter), :] = (piece * inverse).astype(BF16)
     projected = jnp.dot(triple[...], normed[...], preferred_element_type=F32).astype(BF16)
+    base = me_ref[0] * lines
     for line in range(group):
         part = projected[:, line * sites : (line + 1) * sites]
         value_ref[line] = part[2 * quarter :]
-        slot = slot_ref[step * group + line]
-        scale = scale_ref[step * group + line]
+        place = start + step * group + line
+        slot = slot_of(label_ref, base, lines, place)
+        family = label_ref[base + place]
+        members = jnp.full((1, sites), starts_ref[family + 1] - starts_ref[family], jnp.int32)
+        scale = HEAD_SIZE**-0.5 * lax.rsqrt(members.astype(F32))
         for head in range(heads):
             lower = head * HEAD_SIZE
             queries = part[lower : lower + HEAD_SIZE]
@@ -96,7 +117,10 @@
             logits = lax.dot_general(queries, keys, CONTRACT_FIRST, preferred_element_type=F32)
             tables[slot * heads + head] += logits * scale
 
-    @pl.when(step == count - 1)
+    if table_ref is None:
+        return
+
+    @pl.when(step == pl.num_programs(0) - 1)
     def _():
         for index in range(2 * heads):
             table = tables[index].astype(BF16)
@@ -109,7 +133,9 @@
 
         def inner(index, carry):
             table = tables[2 * heads + index]
-            table = jnp.where(site < tally_ref[index // heads], table, -jnp.inf)
+            family = label_ref[base] + 1 + index // heads
+            family = jnp.minimum(family, tally_ref.shape[0] - 1)
+            table = jnp.where(site < tally_ref[family], table, -jnp.inf)
             table = jnp.exp(table - jnp.max(table, axis=-1, keepdims=True))
             table = table / jnp.sum(table, axis=-1, keepdims=True)
             inner_ref[index] = table.astype(BF16)
@@ -118,43 +144,60 @@
         lax.fori_loop(0, inner_ref.shape[0], inner, 0)
 
 
-def row_front(pieces, triple, spots, slot, scaling, inner_tally, row_groups):
+def row_front(pieces, triple, plan, slots, row_groups, start, lines_here, before=None):
     lines, quarter, sites = pieces[0].shape
     group = 4
     count = lines // group
     heads = quarter // HEAD_SIZE
-    inner = inner_tally.shape[0]
+    inner = slots - 2
     rows = sites // row_groups
     shape = (row_groups, 2 * heads, rows, sites) if rows % 16 == 0 else (2 * heads, sites, sites)
     block = pl.BlockSpec((group, quarter, sites), lambda step: (step, 0, 0))
+    every = ((2 + inner) * heads, sites, sites)
 
     def whole(shape):
         return pl.BlockSpec(shape, lambda step: (0,) * len(shape))
 
+    operands = (*pieces, triple.reshape(3 * quarter, 4 * quarter))
+    in_specs = [IN_SMEM] * 4 + [block] * 4 + [whole((3 * quarter, 4 * quarter))]
+    values = jax.ShapeDtypeStruct((lines, quarter, sites), BF16)
+    normed = pltpu.VMEM((4 * quarter, group * sites), BF16)
+    name = "row_front"
+    if before is None:
+        values, tables = pl.pallas_call(
+            functools.partial(row_front_kernel, start, lines_here),
+            grid=(count,),
+            out_shape=(values, jax.ShapeDtypeStruct(every, F32)),
+            in_specs=in_specs,
+            out_specs=(block, whole(every)),
+            scratch_shapes=[normed],
+            compiler_params=GRANT,
+            name=name,
+        )(*plan, *operands)
+        return tables, values
     tables, inner_weights, values = pl.pallas_call(
-        functools.partial(row_front_kernel, count),
+        functools.partial(row_front_kernel, start, lines_here),
         grid=(count,),
         out_shape=(
             jax.ShapeDtypeStruct(shape, BF16),
             jax.ShapeDtypeStruct((inner * heads, sites, sites), BF16),
-            jax.ShapeDtypeStruct((lines, quarter, sites), BF16),
+            values,
         ),
-        in_specs=[IN_SMEM] * 4 + [block] * 4 + [whole((3 * quarter, 4 * quarter))],
+        in_specs=in_specs + [whole(every)],
         out_specs=(whole(shape), whole((inner * heads, sites, sites)), block),
-        scratch_shapes=[
-            pltpu.VMEM(((2 + inner) * heads, sites, sites), F32),
-            pltpu.VMEM((4 * quarter, group * sites), BF16),
-        ],
+        scratch_shapes=[pltpu.VMEM(every, F32), normed],
         compiler_params=GRANT,
-        name="row_front",
-    )(spots, slot, scaling, inner_tally, *pieces, triple.reshape(3 * quarter, 4 * quarter))
+        name=name,
+    )(*plan, *operands, before)
     if rows % 16:
         tables = jnp.transpose(tables.reshape(-1, row_groups, rows, sites), (1, 0, 2, 3))
     return tables, inner_weights, values
 
 
-def tie_kernel(end_ref, tally_ref, parts, out, weights):
+def tie_kernel(me_ref, label_ref, starts_ref, tally_ref, parts, out, weights):
     groups, pairs, rows, sites = parts.shape
+    lines = label_ref.shape[0] // groups
+    ends = [label_ref[g * lines + e * (lines - 1)] for g in range(groups) for e in range(2)]
     heads = pairs // 2
     site = lax.broadcasted_iota(jnp.int32, (heads, rows, sites), 2)
     for family in range(weights.shape[0]):
@@ -162,38 +205,39 @@
         for group in range(groups):
             for end in range(2):
                 part = parts[group, end * heads : (end + 1) * heads].astype(F32)
-                total += jnp.where(end_ref[2 * group + end] == family, part, 0.0)
+                total += jnp.where(ends[2 * group + end] == family, part, 0.0)
         total = jnp.where(site < tally_ref[family], total, -jnp.inf)
         total = jnp.exp(total - jnp.max(total, axis=-1, keepdims=True))
         total = total / jnp.sum(total, axis=-1, keepdims=True)
         weights[family] = total.astype(BF16)
     for group in range(groups):
         for end in range(2):
-            chosen = weights[end_ref[2 * group + end]]
+            chosen = weights[ends[2 * group + end]]
             out[group, end * heads : (end + 1) * heads] = chosen
 
 
-def tie(parts, ends, tally):
+def tie(parts, plan):
     groups, pairs, rows, sites = parts.shape
+    _, label, _, tally = plan
     if rows % 16 == 0:
         return pl.pallas_call(
             tie_kernel,
             out_shape=jax.ShapeDtypeStruct(parts.shape, BF16),
-            in_specs=[IN_SMEM, IN_SMEM, IN_VMEM],
+            in_specs=[IN_SMEM] * 4 + [IN_VMEM],
             out_specs=IN_VMEM,
             scratch_shapes=[pltpu.VMEM((tally.shape[0], pairs // 2, rows, sites), BF16)],
             compiler_params=GRANT,
             name="tie",
-        )(ends, tally, parts)
-    ends = ends.reshape(groups, 2)
+        )(*plan, parts)
+    ends = jnp.stack([label.reshape(groups, -1)[:, 0], label.reshape(groups, -1)[:, -1]], axis=1)
     parts = parts.astype(F32).reshape(groups, 2, -1, rows, sites)
     member = (ends[:, :, None] == jnp.arange(tally.shape[0])).astype(F32)
     totals = jnp.einsum("stf,sthij->fhij", member, parts, precision=lax.Precision.HIGHEST)
     return masked_softmax(totals, tally)[ends].reshape(groups, pairs, rows, sites)
 
 
-def mix_kernel(spot_ref, slot_ref, shared, inner, values, kept, sent):
-    pairs, sites = shared.shape[1], values.shape[2]
+def mix_kernel(me_ref, label_ref, starts_ref, tally_ref, shared, inner, first, second, kept, sent):
+    pairs, sites = shared.shape[1], first.shape[2]
     heads = pairs // 2
     half = kept.shape[0]
 
@@ -202,71 +246,90 @@
             [shared[:, index].reshape(sites, sites) for index in range(2 * heads)]
         )
         weights[2 * heads :] = inner[...]
-        for target, chip in ((sent, 1 - spot_ref[0]), (kept, spot_ref[0])):
-            for line in range(half):
-                row = chip * half + line
-                slot = slot_ref[row]
-                value = values[row]
-                for head in range(heads):
-                    features = slice(head * HEAD_SIZE, (head + 1) * HEAD_SIZE)
-                    target[line, features] = lax.dot_general(
-                        value[features],
-                        weights[slot * heads + head],
-                        CONTRACT_LAST,
-                        preferred_element_type=F32,
-                    ).astype(BF16)
+        chip = me_ref[1]
+
+        @pl.when(chip == 0)
+        def _():
+            spread(weights, second, half, sent)
+            spread(weights, first, 0, kept)
+
+        @pl.when(chip != 0)
+        def _():
+            spread(weights, first, 0, sent)
+            spread(weights, second, half, kept)
+
+    def spread(weights, values, start, target):
+        for line in range(half):
+            slot = slot_of(label_ref, me_ref[0] * 2 * half, 2 * half, start + line)
+            value = values[line]
+            for head in range(heads):
+                features = slice(head * HEAD_SIZE, (head + 1) * HEAD_SIZE)
+                target[line, features] = lax.dot_general(
+                    value[features],
+                    weights[slot * heads + head],
+                    CONTRACT_LAST,
+                    preferred_element_type=F32,
+                ).astype(BF16)
 
     pl.run_scoped(run, pltpu.VMEM((2 * heads + inner.shape[0], sites, sites), BF16))
 
 
-def mix(shared, inner, values, slot, chip):
+def mix(shared, inner, first, second, plan):
     groups, pairs, rows, sites = shared.shape
-    lines, quarter, _ = values.shape
+    lines, quarter, _ = first.shape
     if rows % 16 == 0:
-        half = jax.ShapeDtypeStruct((lines // 2, quarter, sites), BF16)
+        half = jax.ShapeDtypeStruct(first.shape, BF16)
         return pl.pallas_call(
             mix_kernel,
             out_shape=(half, half),
-            in_specs=[IN_SMEM, IN_SMEM] + [IN_VMEM] * 3,
+            in_specs=[IN_SMEM] * 4 + [IN_VMEM] * 4,
             out_specs=(IN_VMEM, IN_VMEM),
             compiler_params=GRANT,
             name="mix",
-        )(chip.astype(jnp.int32).reshape(1), slot, shared, inner, values)
+        )(*plan, shared, inner, first, second)
+    me, label = plan[:2]
+    chip = me[1]
+    label = lax.dynamic_slice_in_dim(label, me[0] * 2 * lines, 2 * lines)
+    slot = slot_of(label, 0, 2 * lines, jnp.arange(2 * lines))
     ends = jnp.transpose(shared, (1, 0, 2, 3)).reshape(2, pairs // 2, sites, sites)
     weights = jnp.concatenate([ends, inner.reshape(-1, *ends.shape[1:])])[slot]
-    values = values.reshape(lines, -1, HEAD_SIZE, sites)
+    values = jnp.concatenate([first, second]).reshape(2 * lines, -1, HEAD_SIZE, sites)
     mixed = jnp.einsum("rhdj,rhij->rhdi", values, weights, preferred_element_type=F32)
-    mixed = mixed.astype(BF16).reshape(lines, quarter, sites)
+    mixed = mixed.astype(BF16).reshape(2 * lines, quarter, sites)
     return half_rows(mixed, chip), half_rows(mixed, 1 - chip)
 
 
 def project_kernel(
-    spot_ref, line_ref, mixed, got, mixing, piece, rest, own, near, across, diagonal,
-    kept, sent, stream, far, semaphores,
+    me_ref, mixed, got, mixing, piece, *refs
 ):
+    halves = refs[:4], refs[4:8]
+    kept, sent, stream, far, semaphores = refs[8:]
     lines, _, sites = stream.shape
     quarter = mixing.shape[0]
-    copies = []
-    for index, source in enumerate((own, near, across, diagonal)):
-        spot = pl.multiple_of(spot_ref[index] * quarter, quarter)
-        copies.append(
-            pltpu.make_async_copy(
-                source.at[pl.ds(line_ref[0], lines)],
-                stream.at[:, pl.ds(spot, quarter)],
-                semaphores.at[index],
+    chip, core = me_ref[1], me_ref[2]
+
+    def copies(half):
+        result = []
+        for index, (spot, source) in enumerate(zip(quarter_spots(me_ref), half)):
+            spot = pl.multiple_of(spot * quarter, quarter)
+            result.append(
+                pltpu.make_async_copy(
+                    source.at[pl.ds(core * lines, lines)],
+                    stream.at[:, pl.ds(spot, quarter)],
+                    semaphores.at[index],
+                )
             )
-        )
-    for copy in copies:
-        copy.start()
-    pair, core = line_ref[1], line_ref[2]
-
-    @pl.when(pair == 0)
-    def _():
-        far[...] = piece[:quarter]
-
-    @pl.when(pair != 0)
-    def _():
-        far[...] = rest[:quarter]
+        return result
+
+    for index, half in enumerate(halves):
+
+        @pl.when(chip == index)
+        def _(half=half):
+            for copy in copies(half):
+                copy.start()
+
+    fetch = pltpu.make_async_copy(piece.at[pl.ds(2 * quarter, quarter)], far, semaphores.at[4])
+    fetch.start()
 
     def partial(row):
         near_part = lax.dot_general(
@@ -276,31 +339,32 @@
             got[row], far[...], CONTRACT_FIRST, preferred_element_type=F32
         )
 
+    fetch.wait()
     for line in range(lines):
         sent[line] = partial((1 - core) * lines + line).astype(BF16)
-    for copy in copies:
+    for copy in copies(halves[0]):
         copy.wait()
     for line in range(lines):
         kept[line] = partial(core * lines + line) + stream[line].astype(F32).T
 
 
-def project(mixed, got, mixing, piece, rest, pieces, spots, place):
+def project(mixed, got, mixing, piece, halves, me):
     half, quarter, sites = mixed.shape
     lines, model = half // 2, mixing.shape[1]
     out = (lines, sites, model)
     return pl.pallas_call(
         project_kernel,
         out_shape=(jax.ShapeDtypeStruct(out, F32), jax.ShapeDtypeStruct(out, BF16)),
-        in_specs=[IN_SMEM, IN_SMEM] + [IN_VMEM] * 5 + [ANYWHERE] * 4,
+        in_specs=[IN_SMEM] + [IN_VMEM] * 3 + [ANYWHERE] * 9,
         out_specs=(IN_VMEM, IN_VMEM),
         scratch_shapes=[
             pltpu.VMEM((lines, model, sites), BF16),
             pltpu.VMEM((quarter, model), BF16),
-            pltpu.SemaphoreType.DMA((4,)),
+            pltpu.SemaphoreType.DMA((5,)),
         ],
         compiler_params=GRANT,
         name="project",
-    )(spots, place, mixed, got, mixing, piece, rest, *pieces)
+    )(me, mixed, got, mixing, piece, *halves[0], *halves[1])
 
 
 def settle_kernel(kept, got, out):
@@ -366,16 +430,18 @@
 
 
 def column_kernel(
-    pair_ref, label_row, label_column, own, other, triple, mixing, piece, rest,
+    lines, me_ref, starts_ref, own, other, triple, mixing, piece, rest,
     kept, sent, normed, far, projected, mixed, semaphores,
 ):
-    half = piece.shape[0]
-    pair = pair_ref[0]
+    half = far.shape[0] // 2
+    core, pair = me_ref[2], me_ref[3]
     copies = []
     for index, (source, place) in enumerate(((piece, pair), (rest, 1 - pair))):
         spot = pl.multiple_of(place * half, half)
         target = far.at[pl.ds(spot, half)]
-        copies.append(pltpu.make_async_copy(source, target, semaphores.at[index]))
+        copies.append(
+            pltpu.make_async_copy(source.at[pl.ds(0, half)], target, semaphores.at[index])
+        )
     for copy in copies:
         copy.start()
     places, rows, model = own.shape
@@ -384,7 +450,19 @@
     normed[:, :rows] = own[...]
     normed[:, rows:] = other[...]
     flat = normed[...].reshape(places * both, model)
-    same = label_column[...] == label_row[...]
+
+    def families(axis):
+        shape = (both, 1) if axis == 0 else (1, both)
+        index = lax.broadcasted_iota(jnp.int32, shape, axis)
+        line = jnp.where(index < rows, core * lines, (1 - core) * lines)
+        index = jnp.where(index < rows, index, index - rows)
+        line += index // lines * (2 * lines) + index % lines
+        return sum(
+            (line >= starts_ref[family]).astype(jnp.int32)
+            for family in range(1, starts_ref.shape[0] - 1)
+        )
+
+    same = families(0) == families(1)
     scale = HEAD_SIZE**-0.5
 
     def attend(weights, lower):
@@ -411,60 +489,86 @@
     attend(triple[...], 0)
     for copy in copies:
         copy.wait()
-    attend(far[quarter : 4 * quarter], quarter)
+    attend(far[: 3 * quarter], quarter)
     for place in range(places):
         lanes = slice(place * both, (place + 1) * both)
         partial = lax.dot_general(
             mixed[:quarter, lanes], mixing[...], CONTRACT_FIRST, preferred_element_type=F32
         )
         partial += lax.dot_general(
-            mixed[quarter:, lanes], far[4 * quarter :], CONTRACT_FIRST, preferred_element_type=F32
+            mixed[quarter:, lanes], far[3 * quarter :], CONTRACT_FIRST, preferred_element_type=F32
         )
         kept[place] = partial[:rows]
         sent[place] = partial[rows:].astype(BF16)
 
 
-def column(own, other, label, triple, mixing, piece, rest, pair):
+def column(own, other, triple, mixing, piece, rest, plan, lines):
     places, rows, model = own.shape
     quarter = mixing.shape[0]
     tokens = 2 * places * rows
     return pl.pallas_call(
-        column_kernel,
+        functools.partial(column_kernel, lines),
         out_shape=(
             jax.ShapeDtypeStruct(own.shape, F32),
             jax.ShapeDtypeStruct(own.shape, BF16),
         ),
-        in_specs=[IN_SMEM] + [IN_VMEM] * 6 + [ANYWHERE] * 2,
+        in_specs=[IN_SMEM] * 2 + [IN_VMEM] * 4 + [ANYWHERE] * 2,
         out_specs=(IN_VMEM, IN_VMEM),
         scratch_shapes=[
             pltpu.VMEM((places, 2 * rows, model), BF16),
-            pltpu.VMEM((2 * piece.shape[0], model), BF16),
+            pltpu.VMEM((4 * quarter, model), BF16),
             pltpu.VMEM((3 * quarter, tokens), BF16),
             pltpu.VMEM((2 * quarter, tokens), BF16),
             pltpu.SemaphoreType.DMA((2,)),
         ],
         compiler_params=GRANT,
         name="column",
-    )(pair, label[None, :], label[:, None], own, other, triple.reshape(-1, model), mixing, piece, rest)
+    )(plan[0], plan[2], own, other, triple.reshape(-1, model), mixing, piece, rest)
 
 
 def feed_forward_kernel(
-    pair_ref, normed, expand, contract, piece, rest, out,
+    me_ref, normed, expand, contract, piece, rest, late, out,
     near_expand, near_contract, far_piece, far_rest, hidden, semaphores,
 ):
+    shared, direct = rest.shape[0], late.shape[0] // 2
+    pair = me_ref[3]
     moves = (
-        (expand, near_expand), (piece, far_piece), (rest, far_rest), (contract, near_contract)
+        (expand, near_expand),
+        (contract, near_contract),
+        (piece.at[pl.ds(piece.shape[0] - shared, shared)], far_piece.at[pl.ds(0, shared)]),
+        (rest, far_rest.at[pl.ds(0, shared)]),
     )
     copies = [
         pltpu.make_async_copy(source, target, semaphores.at[index])
         for index, (source, target) in enumerate(moves)
     ]
+
+    def tails(first, second):
+        return [
+            pltpu.make_async_copy(
+                late.at[pl.ds(index * direct, direct)],
+                target.at[pl.ds(shared, direct)],
+                semaphores.at[4 + index],
+            )
+            for index, target in enumerate((first, second))
+        ]
+
     for copy in copies:
         copy.start()
+
+    @pl.when(pair == 0)
+    def _():
+        for copy in tails(far_piece, far_rest):
+            copy.start()
+
+    @pl.when(pair != 0)
+    def _():
+        for copy in tails(far_rest, far_piece):
+            copy.start()
+
     width = near_expand.shape[1]
     tile = width // 3
     values = normed[...]
-    pair = pair_ref[0]
 
     def raise_by(weights, lower):
         for start in range(0, width, tile):
@@ -479,8 +583,8 @@
 
     copies[0].wait()
     raise_by(near_expand, 0)
-    copies[1].wait()
-    copies[2].wait()
+    for copy in copies[2:] + tails(far_piece, far_rest):
+        copy.wait()
 
     @pl.when(pair == 0)
     def _():
@@ -490,7 +594,7 @@
     def _():
         raise_by(far_rest, width)
 
-    copies[3].wait()
+    copies[1].wait()
 
     @pl.when(pair == 0)
     def _():
@@ -501,13 +605,13 @@
         lower_by(near_contract, far_piece)
 
 
-def feed_forward(normed, expand, contract, piece, rest, pair, kind):
+def feed_forward(normed, expand, contract, piece, rest, late, me, kind):
     places, rows, model = normed.shape
     tokens, width = places * rows, expand.shape[1]
     result = pl.pallas_call(
         feed_forward_kernel,
         out_shape=jax.ShapeDtypeStruct((tokens, model), kind),
-        in_specs=[IN_SMEM, IN_VMEM] + [ANYWHERE] * 4,
+        in_specs=[IN_SMEM, IN_VMEM] + [ANYWHERE] * 5,
         out_specs=IN_VMEM,
         scratch_shapes=[
             pltpu.VMEM((model, width), BF16),
@@ -515,11 +619,11 @@
             pltpu.VMEM((model, width), BF16),
             pltpu.VMEM((model, width), BF16),
             pltpu.VMEM((tokens, 2 * width), BF16),
-            pltpu.SemaphoreType.DMA((4,)),
+            pltpu.SemaphoreType.DMA((6,)),
         ],
         compiler_params=GRANT,
         name="feed_forward",
-    )(pair, normed.reshape(tokens, model), expand, contract, piece, rest)
+    )(me, normed.reshape(tokens, model), expand, contract, piece, rest, late)
     return result.reshape(normed.shape)
 
 
@@ -540,6 +644,7 @@
 ):
     lines, quarter, sites = alignment_embedding.shape
     row_groups = lax.axis_size(ROWS)
+    own = lines // 4
     chips = 2 * row_groups
     place = sites // chips
     pair = lax.axis_index("pair")
@@ -549,88 +654,83 @@
     tally = group_site_tally
     families = tally.shape[0]
 
-    across = other_chip(alignment_embedding)
-    near = other_core(alignment_embedding)
-    diagonal = other_core(across)
-    pieces = (alignment_embedding, near, across, diagonal)
-    spots = jnp.stack(
-        [2 * chip + core, 2 * chip + 1 - core, 2 * (1 - chip) + core, 2 * (1 - chip) + 1 - core]
-    ).astype(jnp.int32)
+    starts = jnp.sum(label[:, None] < jnp.arange(families + 1), axis=0, dtype=jnp.int32)
+    me = jnp.stack([lax.axis_index(ROWS), chip, core, pair]).astype(jnp.int32)
+
+    halves = (alignment_embedding[: lines // 2], alignment_embedding[lines // 2 :])
+    across = [other_chip(half) for half in halves]
+    near = [other_core(half) for half in halves]
     first_pack = jnp.concatenate(
         [
-            horizontal_mixing_matrix,
             vertical_triple_matrix.reshape(-1, vertical_triple_matrix.shape[-1]),
             vertical_mixing_matrix,
         ]
     )
     second_pack = jnp.concatenate([expand_matrix, contract_matrix])
-    across, first_pack, second_pack = lax.optimization_barrier((across, first_pack, second_pack))
-    first_piece = other_chip(half_rows(first_pack, pair))
-    second_piece = other_chip(half_rows(second_pack, pair))
-    first_rest = other_pair(first_piece)
-    second_rest = other_pair(second_piece)
-
-    start = lax.axis_index(ROWS) * lines
-    label_here = lax.dynamic_slice_in_dim(label, start, lines)
-    first, last = label_here[0], label_here[-1]
-    counts = jnp.sum((label[:, None] == jnp.arange(families)).astype(F32), axis=0)
-    scaling = HEAD_SIZE**-0.5 * lax.rsqrt(counts)[label_here]
-    slots = 2 + max(min(families, lines) - 2, 1)
-    slot = jnp.where(
-        label_here == first, 0, jnp.where(label_here == last, 1, label_here - first + 1)
-    )
-    inner = jnp.clip(first + 1 + jnp.arange(slots - 2), 0, families - 1)
-    tables, inner_weights, values = row_front(
-        pieces, horizontal_triple_matrix, spots, slot, scaling, tally[inner], row_groups
-    )
-    tables, first_piece = lax.optimization_barrier((tables, first_piece))
-    ends = label.reshape(row_groups, lines)[:, jnp.array([0, lines - 1])].reshape(-1)
-    shared = tie(lax.all_to_all(tables, ROWS, 0, 0, tiled=True), ends, tally)
-    shared = lax.all_to_all(shared, ROWS, 0, 0, tiled=True)
-    mixed, sent = mix(shared, inner_weights, values, slot, chip)
-
-    sent, first_rest, second_piece = lax.optimization_barrier((sent, first_rest, second_piece))
-    own = lines // 4
-    rows = chips * own
-    here = jnp.stack([(2 * chip + core) * own, pair, core]).astype(jnp.int32)
+    column_rows = first_pack.shape[0] // 2
+    shared_rows = expand_matrix.shape[0] * 3 // 4
+    feed_pack = half_rows(second_pack, pair)[:shared_rows]
+    pack = jnp.concatenate([half_rows(first_pack, pair), horizontal_mixing_matrix, feed_pack])
+    late_pack = jnp.concatenate([expand_matrix[shared_rows:], contract_matrix[shared_rows:]])
+    across[0], pack, late_pack, starts, me = lax.optimization_barrier(
+        (across[0], pack, late_pack, starts, me)
+    )
+    plan = (me, label, starts, tally)
+    diagonal = [other_core(across[0])]
+    across[1], pack = lax.optimization_barrier((across[1], pack))
+    diagonal.append(other_core(across[1]))
+    piece = other_chip(pack)
+
+    tables, values = None, []
+    for index in range(2):
+        *tables, value = row_front(
+            (halves[index], near[index], across[index], diagonal[index]),
+            horizontal_triple_matrix,
+            plan,
+            2 + max(min(families, lines) - 2, 1),
+            row_groups,
+            index * lines // 2,
+            lines,
+            before=tables[0] if index else None,
+        )
+        values.append(value)
+    shared, inner_weights = tables
+    parts = lax.all_to_all(shared, ROWS, 0, 0, tiled=True)
+    shared = lax.all_to_all(tie(parts, plan), ROWS, 0, 0, tiled=True)
+    mixed, sent = mix(shared, inner_weights, *values, plan)
+    sent, piece, late_pack = lax.optimization_barrier((sent, piece, late_pack))
+    first_rest = other_pair(piece[:column_rows])
+    second_rest = other_pair(piece[column_rows + quarter :])
+    late_piece = other_chip(late_pack)
+
+    got, first_rest = lax.optimization_barrier((other_chip(sent), first_rest))
     kept, sent = project(
         mixed,
-        other_chip(sent),
+        got,
         horizontal_mixing_matrix,
-        first_piece,
-        first_rest,
-        pieces,
-        spots,
-        here,
+        piece,
+        list(zip(halves, near, across, diagonal)),
+        me,
     )
 
     blocks = settle(kept, other_core(sent), chips)
-    blocks, second_rest = lax.optimization_barrier((blocks, second_rest))
     blocks = lax.all_to_all(blocks, ROWS + ("chip",), 0, 0, tiled=True)
     normed, after_row = arrive(blocks, place)
-    label_cores = label.reshape(chips, 2, own)
-    label_sites = jnp.concatenate(
-        [
-            lax.dynamic_index_in_dim(label_cores, index, 1, False).reshape(-1)
-            for index in (core, 1 - core)
-        ]
-    )
-
-    parity = pair.astype(jnp.int32).reshape(1)
+    normed, second_rest, late_piece = lax.optimization_barrier((normed, second_rest, late_piece))
     kept, sent = column(
         normed,
         other_core(normed),
-        label_sites,
         vertical_triple_matrix,
         vertical_mixing_matrix,
-        first_piece,
+        piece,
         first_rest,
-        parity,
+        plan,
+        lines // 4,
     )
     after_col = core_sum(after_row, kept, sent)
 
     normed = own_norm(after_col, -1)
-    feed = (expand_matrix, contract_matrix, second_piece, second_rest, parity)
+    feed = (expand_matrix, contract_matrix, piece, second_rest, late_piece, me)
     kept = feed_forward(normed, *feed, F32)
     sent = feed_forward(other_core(normed), *feed, BF16)
     finished = core_sum(after_col, kept, sent)

time: 193 us -> 182 us (0.943)
  local copies, waits for them, and re-layouts: 32.5 us -> 11.8 us
  waiting for transfers between devices: 42.8 us -> 59.8 us
  other arithmetic: 11.2 us -> 5.26 us
  blocking collectives: 52.5 us -> 49.2 us
  starting transfers between devices: 14.8 us -> 17.7 us
    all_to_all x1, waiting for transfers between devices: 3.08 us -> 15.7 us  [shards(): blocks = lax.all_to_all(blocks, ROWS + ('chip',), 0, 0, tiled=True)]
    unnamed x42 -> x34, local copies, waits for them, and re-layouts: 14.9 us -> 5.42 us
    ppermute x4 -> x5, waiting for transfers between devices: 27.7 us -> 22.6 us  [other_chip(): return lax.ppermute(value, 'chip', SWAP)]
    all_to_all x2, blocking collectives: 29.7 us -> 24.6 us  [the longest x1 13.9 us: shards(): parts = lax.all_to_all(shared, ROWS, 0, 0, tiled=True)]
    ppermute x7 -> x9, waiting for transfers between devices: 6.11 us -> 10.9 us  [other_core(): return lax.ppermute(value, 'core', SWAP)]
    ppermute x2, waiting for transfers between devices: 5.9 us -> 10.5 us  [other_pair(): return lax.ppermute(value, 'pair', SWAP)]
    reshape x6 -> x0, local copies, waits for them, and re-layouts: 4.48 us -> none  [the longest x3 2.15 us: shards(): label.reshape(row_groups, lines)[:, jnp.array([0, lines - 1])].reshape(-1)]
    gather x4 -> x0, local copies, waits for them, and re-layouts: 3.99 us -> none  [the longest x2 2.05 us: shards(): label.reshape(row_groups, lines)[:, jnp.array([0, lines - 1])].reshape(-1)]
  transfers between devices with their start and end apart: 14 -> 17, of which waited for: 8 -> 12; matrix products, arithmetic and copies ran while one was open for 12% -> 3% of each run, Pallas kernels for 10% -> 10%
where the time goes in v2:
time: 182 us; the launch traced here: 181 us
  waiting for transfers between devices  59.8 us (33%)
  blocking collectives  49.2 us (27%)
  Pallas kernels  37.3 us (20%)
  starting transfers between devices  17.7 us (10%)
  local copies, waits for them, and re-layouts  11.8 us (6%)
  other arithmetic  5.26 us (3%)
    all_to_all x1, blocking collectives, shards(): lax.all_to_all(finished, ROWS + ('chip', 'core'), 0, 0, tiled=True)  24.6 us
    ppermute x5, waiting for transfers between devices, other_chip(): return lax.ppermute(value, 'chip', SWAP)  22.6 us
    all_to_all x1, waiting for transfers between devices, shards(): blocks = lax.all_to_all(blocks, ROWS + ('chip',), 0, 0, tiled=True)  15.7 us
    all_to_all x1, blocking collectives, shards(): parts = lax.all_to_all(shared, ROWS, 0, 0, tiled=True)  13.9 us
    pallas_call x1, Pallas kernels, column(): pl.pallas_call(functools.partial(column_kernel, lines), out_shape=(jax.Sh...  12.5 us
    ppermute x9, waiting for transfers between devices, other_core(): return lax.ppermute(value, 'core', SWAP)  10.9 us
    all_to_all x1, blocking collectives, shards(): shared = lax.all_to_all(tie(parts, plan), ROWS, 0, 0, tiled=True)  10.7 us
    ppermute x2, waiting for transfers between devices, other_pair(): return lax.ppermute(value, 'pair', SWAP)  10.5 us
  transfers between devices with their start and end apart: 17, of which 12 were waited for; matrix products, arithmetic and copies ran while one was open for 3% of the time, Pallas kernels for 10%

profile of v2, /device:TPU:0, one launch (start us, length us, event | category | flops | bytes accessed | tf_op | source)
XLA Modules:
  0.0 181.5 jit_solution(1554451726915064953)
XLA Ops:
  0.0 2.1 %fusion.10 = (bf16[8,192,128]{2,1,0:T(8,128)(2,1)S(1)}, bf16[8,192,128]{2,1,0:T(8,128)(2,1)}) fusion(bf16[16,192,128]{2,1,0:T(8,128)(2,1)} %param.9), kind=kLoop, calls=%fused_computation.27 | loop fusion | bytes 1572864 | tf_op jit(solution)/shard_map/slice | solution.py:660
  2.1 2.9 %collective-permute-start.2 = (bf16[8,192,128]{2,1,0:T(8,128)(2,1)S(1)}, bf16[8,192,128]{2,1,0:T(8,128)(2,1)}, u32[]{:S(2)}, u32[]{:S(2)}) collective-permute-start(bf16[8,192,128]{2,1,0:T(8,128)(2,1)S(1)} %get-tuple-element.67.own.refs_4_), channel_id=1, source_target_pairs={{0,2},{2,0},{1,3},{3,1},{4,6},{6,4},{5,7},{7,5},{8,10},{10,8},{9,1... | collective-permute-start | bytes 1179656 | tf_op jit(solution)/shard_map/ppermute | solution.py:18
  5.2 2.1 %fusion.6 = bf16[576,768]{1,0:T(8,128)(2,1)} fusion(s32[]{:T(128)S(6)} %select_n.7, bf16[768,768]{1,0:T(8,128)(2,1)S(1)} %copy-done, bf16[768,768]{1,0:T(8,128)(2,1)S(1)} %copy-done.1), kind=kLoop, calls=%fused_computation.16 | loop fusion | flops 1769472 | bytes 3244036 | tf_op jit(solution)/shard_map/concatenate | solution.py:669
  9.2 13.4 %collective-permute-done.far.refs_2_ = bf16[8,192,128]{2,1,0:T(8,128)(2,1)} collective-permute-done((bf16[8,192,128]{2,1,0:T(8,128)(2,1)}, bf16[8,192,128]{2,1,0:T(8,128)(2,1)}, u32[]{:S(2)}, u32[]{:S(2)}) %collective-permute-start) | collective-permute-done | bytes 393248 | tf_op jit(solution)/shard_map/ppermute | solution.py:18
  22.7 1.7 collective-permute-start.6
  26.3 1.1 collective-permute-done.5.diagonal.refs_3_
  27.5 3.7 %row_front.2 = (bf16[8,192,128]{2,1,0:T(8,128)(2,1)S(1)}, f32[12,128,128]{2,1,0:T(8,128)S(1)}) custom-call(s32[4]{0:T(128)S(1)} %pad_add_fusion.me_ref, s32[128]{0:T(128)S(1)} %copy-done.14, s32[5]{0:T(128)S(1)} %convert_reduce_fusion.1.starts_ref, s32[4]{0:T(128)S(1)} %copy-done.15, bf16[8,192,128]{2,1,0:T(8,128)(2,1)} %get-tuple-element.68.own.refs_0_, ...), custom_call_target="tpu_custom_call" | custom-call | tf_op jit(solution)/shard_map/row_front/pallas_call | solution.py:167
  31.2 4.8 %row_front.3 = (bf16[8,6,16,128]{3,2,1,0:T(8,128)(2,1)S(1)}, bf16[6,128,128]{2,1,0:T(8,128)(2,1)S(1)}, bf16[8,192,128]{2,1,0:T(8,128)(2,1)S(1)}) custom-call(s32[4]{0:T(128)S(1)} %pad_add_fusion.me_ref, s32[128]{0:T(128)S(1)} %copy-done.14, s32[5]{0:T(128)S(1)} %convert_reduce_fusion.1.starts_ref, s32[4]{0:T(128)S(1)} %copy-done.15, ...), custom_call_target="tpu_custom_call" | custom-call | tf_op jit(solution)/shard_map/row_front/pallas_call | solution.py:178
  36.0 13.9 %all_to_all.20.parts = bf16[8,6,16,128]{3,2,1,0:T(8,128)(2,1)S(1)} all-to-all(bf16[8,6,16,128]{3,2,1,0:T(8,128)(2,1)S(1)} %get-tuple-element.39), channel_id=1, replica_groups=mesh['plane'=4,'pair'=2,'chip'=2,'core'=2] {'plane','pair'}, dimensions={0} | all-to-all | bytes 393216 | tf_op jit(solution)/shard_map/all_to_all | solution.py:698
  50.8 10.7 %all_to_all.21.shared = bf16[8,6,16,128]{3,2,1,0:T(8,128)(2,1)S(1)} all-to-all(bf16[8,6,16,128]{3,2,1,0:T(8,128)(2,1)S(1)} %tie.1), channel_id=1, replica_groups=mesh['plane'=4,'pair'=2,'chip'=2,'core'=2] {'plane','pair'}, dimensions={0} | all-to-all | bytes 393216 | tf_op jit(solution)/shard_map/all_to_all | solution.py:699
  61.5 1.8 mix.1
  63.4 1.1 collective-permute-start.8
  65.5 7.3 %collective-permute-done.7.got = bf16[8,192,128]{2,1,0:T(8,128)(2,1)S(1)} collective-permute-done((bf16[8,192,128]{2,1,0:T(8,128)(2,1)S(1)}, bf16[8,192,128]{2,1,0:T(8,128)(2,1)S(1)}, u32[]{:S(2)}, u32[]{:S(2)}) %collective-permute-start.7) | collective-permute-done | bytes 393248 | tf_op jit(solution)/shard_map/ppermute | solution.py:18
  72.8 4.1 %collective-permute-done.8.rest = bf16[384,768]{1,0:T(8,128)(2,1)S(1)} collective-permute-done((bf16[384,768]{1,0:T(8,128)(2,1)S(1)}, bf16[384,768]{1,0:T(8,128)(2,1)S(1)}, u32[]{:S(2)}, u32[]{:S(2)}) %collective-permute-start.8) | collective-permute-done | bytes 589856 | tf_op jit(solution)/shard_map/ppermute | solution.py:22
  77.7 2.3 %project.1 = (f32[4,128,768]{2,1,0:T(8,128)S(1)}, bf16[4,128,768]{2,1,0:T(8,128)(2,1)S(1)}) custom-call(s32[4]{0:T(128)S(1)} %pad_add_fusion.me_ref, bf16[8,192,128]{2,1,0:T(8,128)(2,1)S(1)} %get-tuple-element.43.mixed, bf16[8,192,128]{2,1,0:T(8,128)(2,1)S(1)} %collective-permute-done.7.got, bf16[192,768]{1,0:T(8,128)(2,1)S(1)} %copy-done.10, ...), custom_call_target="tpu_custom_call" | custom-call | tf_op jit(solution)/shard_map/project/pallas_call | solution.py:355
  80.0 2.3 %collective-permute-done.9.got = bf16[4,128,768]{2,1,0:T(8,128)(2,1)S(1)} collective-permute-done((bf16[4,128,768]{2,1,0:T(8,128)(2,1)S(1)}, bf16[4,128,768]{2,1,0:T(8,128)(2,1)S(1)}, u32[]{:S(2)}, u32[]{:S(2)}) %collective-permute-start.9) | collective-permute-done | bytes 786464 | tf_op jit(solution)/shard_map/ppermute | solution.py:26
  83.3 5.9 %all-to-all-start.2 = ((bf16[16,32,768]{2,1,0:T(8,128)(2,1)}), bf16[16,32,768]{2,1,0:T(8,128)(2,1)}, u32[]{:S(2)}, u32[]{:S(2)}) async-start(bf16[16,32,768]{2,1,0:T(8,128)(2,1)} %copy-done.8), calls=%async_computation.2 | async-start | bytes 1572864 | tf_op jit(solution)/shard_map/all_to_all | solution.py:717
  90.2 1.9 %collective-permute-start.10 = (bf16[576,768]{1,0:T(8,128)(2,1)}, bf16[576,768]{1,0:T(8,128)(2,1)}, u32[]{:S(2)}, u32[]{:S(2)}) collective-permute-start(bf16[576,768]{1,0:T(8,128)(2,1)} %slice.48), channel_id=1, source_target_pairs={{0,4},{4,0},{1,5},{5,1},{2,6},{6,2},{3,7},{7,3},{8,12},{12,8},{9,1... | collective-permute-start | bytes 2654216 | tf_op jit(solution)/shard_map/ppermute | solution.py:22
  92.0 1.5 collective-permute-start.11
  93.5 15.7 %all-to-all-done.2.blocks = bf16[16,32,768]{2,1,0:T(8,128)(2,1)} async-done(((bf16[16,32,768]{2,1,0:T(8,128)(2,1)}), bf16[16,32,768]{2,1,0:T(8,128)(2,1)}, u32[]{:S(2)}, u32[]{:S(2)}) %all-to-all-start.2) | async-done | bytes 786464 | tf_op jit(solution)/shard_map/all_to_all | solution.py:717
  109.2 1.9 %arrive.1 = (bf16[8,64,768]{2,1,0:T(8,128)(2,1)S(1)}, bf16[8,64,768]{2,1,0:T(8,128)(2,1)S(1)}) custom-call(bf16[16,32,768]{2,1,0:T(8,128)(2,1)} %all-to-all-done.2.blocks), custom_call_target="tpu_custom_call" | custom-call | tf_op jit(solution)/shard_map/arrive/pallas_call | solution.py:419
  111.2 1.9 %collective-permute-done.11.late = bf16[384,768]{1,0:T(8,128)(2,1)S(1)} collective-permute-done((bf16[384,768]{1,0:T(8,128)(2,1)}, bf16[384,768]{1,0:T(8,128)(2,1)S(1)}, u32[]{:S(2)}, u32[]{:S(2)}) %collective-permute-start.11) | collective-permute-done | bytes 589856 | tf_op jit(solution)/shard_map/ppermute | solution.py:18
  113.1 6.4 %collective-permute-done.10.rest = bf16[576,768]{1,0:T(8,128)(2,1)} collective-permute-done((bf16[576,768]{1,0:T(8,128)(2,1)}, bf16[576,768]{1,0:T(8,128)(2,1)}, u32[]{:S(2)}, u32[]{:S(2)}) %collective-permute-start.10) | collective-permute-done | bytes 884768 | tf_op jit(solution)/shard_map/ppermute | solution.py:22
  119.6 2.3 %collective-permute-done.12.other = bf16[8,64,768]{2,1,0:T(8,128)(2,1)S(1)} collective-permute-done((bf16[8,64,768]{2,1,0:T(8,128)(2,1)S(1)}, bf16[8,64,768]{2,1,0:T(8,128)(2,1)S(1)}, u32[]{:S(2)}, u32[]{:S(2)}) %collective-permute-start.12) | collective-permute-done | bytes 786464 | tf_op jit(solution)/shard_map/ppermute | solution.py:26
  121.8 1.2 copy-done.7
  125.0 12.5 %column.1 = (f32[8,64,768]{2,1,0:T(8,128)S(1)}, bf16[8,64,768]{2,1,0:T(8,128)(2,1)S(1)}) custom-call(s32[4]{0:T(128)S(1)} %pad_add_fusion.me_ref, s32[5]{0:T(128)S(1)} %convert_reduce_fusion.1.starts_ref, bf16[8,64,768]{2,1,0:T(8,128)(2,1)S(1)} %get-tuple-element.55.own, bf16[8,64,768]{2,1,0:T(8,128)(2,1)S(1)} %collective-permute-done.12.other, ...), custom_call_target="tpu_custom_call" | custom-call | tf_op jit(solution)/shard_map/column/pallas_call | solution.py:509
  137.7 2.2 %collective-permute-done.13 = bf16[8,64,768]{2,1,0:T(8,128)(2,1)S(1)} collective-permute-done((bf16[8,64,768]{2,1,0:T(8,128)(2,1)S(1)}, bf16[8,64,768]{2,1,0:T(8,128)(2,1)S(1)}, u32[]{:S(2)}, u32[]{:S(2)}) %collective-permute-start.13) | collective-permute-done | bytes 786464 | tf_op jit(solution)/shard_map/ppermute | solution.py:26
  141.1 2.1 %collective-permute-done.14 = bf16[8,64,768]{2,1,0:T(8,128)(2,1)S(1)} collective-permute-done((bf16[8,64,768]{2,1,0:T(8,128)(2,1)S(1)}, bf16[8,64,768]{2,1,0:T(8,128)(2,1)S(1)}, u32[]{:S(2)}, u32[]{:S(2)}) %collective-permute-start.14) | collective-permute-done | bytes 786464 | tf_op jit(solution)/shard_map/ppermute | solution.py:26
  143.2 4.7 %feed_forward.3 = bf16[512,768]{1,0:T(8,128)(2,1)S(1)} custom-call(s32[4]{0:T(128)S(1)} %pad_add_fusion.me_ref, bf16[512,768]{1,0:T(8,128)(2,1)S(1)} %bitcast.24, bf16[768,768]{1,0:T(8,128)(2,1)S(1)} %copy-done, bf16[768,768]{1,0:T(8,128)(2,1)S(1)} %copy-done.2, bf16[1152,768]{1,0:T(8,128)(2,1)S(1)} %collective-permute-done.6.piece, ...), custom_call_target="tpu_custom_call" | custom-call | tf_op jit(solution)/shard_map/feed_forward/pallas_call | solution.py:611
  148.1 4.7 %feed_forward.2 = f32[512,768]{1,0:T(8,128)S(1)} custom-call(s32[4]{0:T(128)S(1)} %pad_add_fusion.me_ref, bf16[512,768]{1,0:T(8,128)(2,1)S(1)} %bitcast.22, bf16[768,768]{1,0:T(8,128)(2,1)S(1)} %copy-done, bf16[768,768]{1,0:T(8,128)(2,1)S(1)} %copy-done.2, bf16[1152,768]{1,0:T(8,128)(2,1)S(1)} %collective-permute-done.6.piece, ...), custom_call_target="tpu_custom_call" | custom-call | tf_op jit(solution)/shard_map/feed_forward/pallas_call | solution.py:611
  155.0 24.6 %all_to_all.22 = bf16[32,96,128]{2,1,0:T(8,128)(2,1)S(1)} all-to-all(bf16[32,96,128]{2,1,0:T(8,128)(2,1)S(1)} %maximum_maximum_fusion.1), channel_id=1, replica_groups=mesh['plane'=4,'pair'=2,'chip'=2,'core'=2] {'plane','pair','chip','core'}, dimensions={0} | all-to-all | bytes 1572864 | tf_op jit(solution)/shard_map/all_to_all | solution.py:749
  180.2 1.3 copy.15
  (78 shorter events, 15.2 us)
Async XLA Ops:
  0.0 5.1 %copy-start.14 = (s32[128]{0:T(128)S(1)}, s32[128]{0:T(128)}, u32[]{:S(2)}) copy-start(s32[128]{0:T(128)} %label_ref.7) | copy-start | bytes 1540
  0.0 5.2 %copy-start = (bf16[768,768]{1,0:T(8,128)(2,1)S(1)}, bf16[768,768]{1,0:T(8,128)(2,1)}, u32[]{:S(2)}) copy-start(bf16[768,768]{1,0:T(8,128)(2,1)} %expand.3) | copy-start | bytes 3538948
  0.0 5.2 %copy-start.1 = (bf16[768,768]{1,0:T(8,128)(2,1)S(1)}, bf16[768,768]{1,0:T(8,128)(2,1)}, u32[]{:S(2)}) copy-start(bf16[768,768]{1,0:T(8,128)(2,1)} %contract.3) | copy-start | bytes 3538948
  2.1 5.2 %copy-start.4 = (bf16[8,192,128]{2,1,0:T(8,128)(2,1)}, bf16[8,192,128]{2,1,0:T(8,128)(2,1)S(1)}, u32[]{:S(2)}) copy-start(bf16[8,192,128]{2,1,0:T(8,128)(2,1)S(1)} %get-tuple-element.67.own.refs_4_) | copy-start | bytes 1179652
  2.1 20.6 %collective-permute-start.2 = (bf16[8,192,128]{2,1,0:T(8,128)(2,1)S(1)}, bf16[8,192,128]{2,1,0:T(8,128)(2,1)}, u32[]{:S(2)}, u32[]{:S(2)}) collective-permute-start(bf16[8,192,128]{2,1,0:T(8,128)(2,1)S(1)} %get-tuple-element.67.own.refs_4_), channel_id=1, source_target_pairs={{0,2},{2,0},{1,3},{3,1},{4,6},{6,4},{5,7},{7,5},{8,10},{10,8},{9,1... | collective-permute-start | bytes 1179656 | tf_op jit(solution)/shard_map/ppermute | solution.py:18
  5.0 17.6 %collective-permute-start = (bf16[8,192,128]{2,1,0:T(8,128)(2,1)}, bf16[8,192,128]{2,1,0:T(8,128)(2,1)}, u32[]{:S(2)}, u32[]{:S(2)}) collective-permute-start(bf16[8,192,128]{2,1,0:T(8,128)(2,1)} %get-tuple-element.68.own.refs_0_), channel_id=1, source_target_pairs={{0,2},{2,0},{1,3},{3,1},{4,6},{6,4},{5,7},{7,5},{8,10},{10,8},{9,1... | collective-permute-start | bytes 1179656 | tf_op jit(solution)/shard_map/ppermute | solution.py:18
  5.2 2.1 %slice-start = ((bf16[768,768]{1,0:T(8,128)(2,1)}), bf16[192,768]{1,0:T(8,128)(2,1)S(1)}, s32[]{:S(2)}) async-start(bf16[768,768]{1,0:T(8,128)(2,1)} %expand.3), calls=%async_computation.4 | async-start | bytes 589824 | tf_op jit(solution)/shard_map/slice | solution.py:674
  5.2 2.1 %slice-start.1 = ((bf16[768,768]{1,0:T(8,128)(2,1)}), bf16[192,768]{1,0:T(8,128)(2,1)S(1)}, s32[]{:S(2)}) async-start(bf16[768,768]{1,0:T(8,128)(2,1)} %contract.3), calls=%async_computation.5 | async-start | bytes 589824 | tf_op jit(solution)/shard_map/slice | solution.py:674
  7.3 1.4 copy-start.6
  7.3 1.8 copy-start.9
  7.3 1.8 copy-start.16
  9.1 15.8 %copy-start.5 = (bf16[8,192,128]{2,1,0:T(8,128)(2,1)S(1)}, bf16[8,192,128]{2,1,0:T(8,128)(2,1)}, u32[]{:S(2)}) copy-start(bf16[8,192,128]{2,1,0:T(8,128)(2,1)} %copy-done.4) | copy-start | bytes 1179652
  9.1 18.4 %copy-start.3 = (bf16[3,192,768]{2,1,0:T(8,128)(2,1)S(1)}, bf16[3,192,768]{2,1,0:T(8,128)(2,1)}, u32[]{:S(2)}) copy-start(bf16[3,192,768]{2,1,0:T(8,128)(2,1)} %param.12) | copy-start | bytes 2654212
  9.1 18.4 %copy-start.15 = (s32[4]{0:T(128)S(1)}, s32[4]{0:T(128)}, u32[]{:S(2)}) copy-start(s32[4]{0:T(128)} %tally_ref.7) | copy-start | bytes 52
  22.7 40.7 %collective-permute-start.6 = (bf16[1152,768]{1,0:T(8,128)(2,1)S(1)}, bf16[1152,768]{1,0:T(8,128)(2,1)S(1)}, u32[]{:S(2)}, u32[]{:S(2)}) collective-permute-start(bf16[1152,768]{1,0:T(8,128)(2,1)S(1)} %pad_maximum_fusion), channel_id=1, source_target_pairs={{0,2},{2,0},{1,3},{3,1},{4,6},{6,4},{5,7},{7,5},{8,10},{10,8},{9,1... | collective-permute-start | bytes 5308424 | tf_op jit(solution)/shard_map/ppermute | solution.py:18
  24.4 1.9 %collective-permute-start.4 = (bf16[8,192,128]{2,1,0:T(8,128)(2,1)}, bf16[8,192,128]{2,1,0:T(8,128)(2,1)S(1)}, u32[]{:S(2)}, u32[]{:S(2)}) collective-permute-start(bf16[8,192,128]{2,1,0:T(8,128)(2,1)} %get-tuple-element.68.own.refs_0_), channel_id=1, source_target_pairs={{0,1},{1,0},{2,3},{3,2},{4,5},{5,4},{6,7},{7,6},{8,9},{9,8},{10,11... | collective-permute-start | bytes 1179656 | tf_op jit(solution)/shard_map/ppermute | solution.py:26
  24.4 3.1 %collective-permute-start.5 = (bf16[8,192,128]{2,1,0:T(8,128)(2,1)}, bf16[8,192,128]{2,1,0:T(8,128)(2,1)S(1)}, u32[]{:S(2)}, u32[]{:S(2)}) collective-permute-start(bf16[8,192,128]{2,1,0:T(8,128)(2,1)} %collective-permute-done.far.refs_2_), channel_id=1, source_target_pairs={{0,1},{1,0},{2,3},{3,2},{4,5},{5,4},{6,7},{7,6},{8,9},{9,8},{10,11... | collective-permute-start | bytes 1179656 | tf_op jit(solution)/shard_map/ppermute | solution.py:26
  24.9 6.3 %collective-permute-start.1 = (bf16[8,192,128]{2,1,0:T(8,128)(2,1)S(1)}, bf16[8,192,128]{2,1,0:T(8,128)(2,1)S(1)}, u32[]{:S(2)}, u32[]{:S(2)}) collective-permute-start(bf16[8,192,128]{2,1,0:T(8,128)(2,1)S(1)} %copy-done.5), channel_id=1, source_target_pairs={{0,1},{1,0},{2,3},{3,2},{4,5},{5,4},{6,7},{7,6},{8,9},{9,8},{10,11... | collective-permute-start | bytes 1179656 | tf_op jit(solution)/shard_map/ppermute | solution.py:26
  24.9 6.3 %collective-permute-start.3 = (bf16[8,192,128]{2,1,0:T(8,128)(2,1)}, bf16[8,192,128]{2,1,0:T(8,128)(2,1)S(1)}, u32[]{:S(2)}, u32[]{:S(2)}) collective-permute-start(bf16[8,192,128]{2,1,0:T(8,128)(2,1)} %collective-permute-done.2.far.refs_6_), channel_id=1, source_target_pairs={{0,1},{1,0},{2,3},{3,2},{4,5},{5,4},{6,7},{7,6},{8,9},{9,8},{10,11... | collective-permute-start | bytes 1179656 | tf_op jit(solution)/shard_map/ppermute | solution.py:26
  49.9 27.8 %copy-start.10 = (bf16[192,768]{1,0:T(8,128)(2,1)S(1)}, bf16[192,768]{1,0:T(8,128)(2,1)}, u32[]{:S(2)}) copy-start(bf16[192,768]{1,0:T(8,128)(2,1)} %mixing.2) | copy-start | bytes 884740
  63.4 13.5 %collective-permute-start.8 = (bf16[384,768]{1,0:T(8,128)(2,1)S(1)}, bf16[384,768]{1,0:T(8,128)(2,1)S(1)}, u32[]{:S(2)}, u32[]{:S(2)}) collective-permute-start(bf16[384,768]{1,0:T(8,128)(2,1)S(1)} %slice.47), channel_id=1, source_target_pairs={{0,4},{4,0},{1,5},{5,1},{2,6},{6,2},{3,7},{7,3},{8,12},{12,8},{9,1... | collective-permute-start | bytes 1769480 | tf_op jit(solution)/shard_map/ppermute | solution.py:22
  64.5 8.3 %collective-permute-start.7 = (bf16[8,192,128]{2,1,0:T(8,128)(2,1)S(1)}, bf16[8,192,128]{2,1,0:T(8,128)(2,1)S(1)}, u32[]{:S(2)}, u32[]{:S(2)}) collective-permute-start(bf16[8,192,128]{2,1,0:T(8,128)(2,1)S(1)} %get-tuple-element.47), channel_id=1, source_target_pairs={{0,2},{2,0},{1,3},{3,1},{4,6},{6,4},{5,7},{7,5},{8,10},{10,8},{9,1... | collective-permute-start | bytes 1179656 | tf_op jit(solution)/shard_map/ppermute | solution.py:18
  80.0 2.4 %collective-permute-start.9 = (bf16[4,128,768]{2,1,0:T(8,128)(2,1)S(1)}, bf16[4,128,768]{2,1,0:T(8,128)(2,1)S(1)}, u32[]{:S(2)}, u32[]{:S(2)}) collective-permute-start(bf16[4,128,768]{2,1,0:T(8,128)(2,1)S(1)} %get-tuple-element.51), channel_id=1, source_target_pairs={{0,1},{1,0},{2,3},{3,2},{4,5},{5,4},{6,7},{7,6},{8,9},{9,8},{10,11... | collective-permute-start | bytes 2359304 | tf_op jit(solution)/shard_map/ppermute | solution.py:26
  83.3 25.9 %all-to-all-start.2 = ((bf16[16,32,768]{2,1,0:T(8,128)(2,1)}), bf16[16,32,768]{2,1,0:T(8,128)(2,1)}, u32[]{:S(2)}, u32[]{:S(2)}) async-start(bf16[16,32,768]{2,1,0:T(8,128)(2,1)} %copy-done.8), calls=%async_computation.2 | async-start | bytes 1572864 | tf_op jit(solution)/shard_map/all_to_all | solution.py:717
  90.2 29.4 %collective-permute-start.10 = (bf16[576,768]{1,0:T(8,128)(2,1)}, bf16[576,768]{1,0:T(8,128)(2,1)}, u32[]{:S(2)}, u32[]{:S(2)}) collective-permute-start(bf16[576,768]{1,0:T(8,128)(2,1)} %slice.48), channel_id=1, source_target_pairs={{0,4},{4,0},{1,5},{5,1},{2,6},{6,2},{3,7},{7,3},{8,12},{12,8},{9,1... | collective-permute-start | bytes 2654216 | tf_op jit(solution)/shard_map/ppermute | solution.py:22
  92.0 21.1 %collective-permute-start.11 = (bf16[384,768]{1,0:T(8,128)(2,1)}, bf16[384,768]{1,0:T(8,128)(2,1)S(1)}, u32[]{:S(2)}, u32[]{:S(2)}) collective-permute-start(bf16[384,768]{1,0:T(8,128)(2,1)} %pad_maximum_fusion.1), channel_id=1, source_target_pairs={{0,2},{2,0},{1,3},{3,1},{4,6},{6,4},{5,7},{7,5},{8,10},{10,8},{9,1... | collective-permute-start | bytes 1769480 | tf_op jit(solution)/shard_map/ppermute | solution.py:18
  119.5 2.3 %collective-permute-start.12 = (bf16[8,64,768]{2,1,0:T(8,128)(2,1)S(1)}, bf16[8,64,768]{2,1,0:T(8,128)(2,1)S(1)}, u32[]{:S(2)}, u32[]{:S(2)}) collective-permute-start(bf16[8,64,768]{2,1,0:T(8,128)(2,1)S(1)} %get-tuple-element.55.own), channel_id=1, source_target_pairs={{0,1},{1,0},{2,3},{3,2},{4,5},{5,4},{6,7},{7,6},{8,9},{9,8},{10,11... | collective-permute-start | bytes 2359304 | tf_op jit(solution)/shard_map/ppermute | solution.py:26
  121.8 1.2 copy-start.7
  137.5 2.4 %collective-permute-start.13 = (bf16[8,64,768]{2,1,0:T(8,128)(2,1)S(1)}, bf16[8,64,768]{2,1,0:T(8,128)(2,1)S(1)}, u32[]{:S(2)}, u32[]{:S(2)}) collective-permute-start(bf16[8,64,768]{2,1,0:T(8,128)(2,1)S(1)} %get-tuple-element.58), channel_id=1, source_target_pairs={{0,1},{1,0},{2,3},{3,2},{4,5},{5,4},{6,7},{7,6},{8,9},{9,8},{10,11... | collective-permute-start | bytes 2359304 | tf_op jit(solution)/shard_map/ppermute | solution.py:26
  140.2 3.0 %copy-start.2 = (bf16[768,768]{1,0:T(8,128)(2,1)S(1)}, bf16[768,768]{1,0:T(8,128)(2,1)}, u32[]{:S(2)}) copy-start(bf16[768,768]{1,0:T(8,128)(2,1)} %contract.3) | copy-start | bytes 3538948
  140.9 2.4 %collective-permute-start.14 = (bf16[8,64,768]{2,1,0:T(8,128)(2,1)S(1)}, bf16[8,64,768]{2,1,0:T(8,128)(2,1)S(1)}, u32[]{:S(2)}, u32[]{:S(2)}) collective-permute-start(bf16[8,64,768]{2,1,0:T(8,128)(2,1)S(1)} %fusion.3), channel_id=1, source_target_pairs={{0,1},{1,0},{2,3},{3,2},{4,5},{5,4},{6,7},{7,6},{8,9},{9,8},{10,11... | collective-permute-start | bytes 2359304 | tf_op jit(solution)/shard_map/ppermute | solution.py:26
  147.9 4.9 %collective-permute-start.15 = (bf16[8,64,768]{2,1,0:T(8,128)(2,1)S(1)}, bf16[8,64,768]{2,1,0:T(8,128)(2,1)S(1)}, u32[]{:S(2)}, u32[]{:S(2)}) collective-permute-start(bf16[8,64,768]{2,1,0:T(8,128)(2,1)S(1)} %bitcast.23), channel_id=1, source_target_pairs={{0,1},{1,0},{2,3},{3,2},{4,5},{5,4},{6,7},{7,6},{8,9},{9,8},{10,11... | collective-permute-start | bytes 2359304 | tf_op jit(solution)/shard_map/ppermute | solution.py:26
  (4 other events, 3.7 us)

commit v3 on v2

v3 whole, which is shorter than its diff:
```python
import functools

import jax
import jax.numpy as jnp
from jax import lax
from jax.experimental import pallas as pl
from jax.experimental.pallas import tpu as pltpu
from jax.sharding import Mesh, PartitionSpec as P

HEAD_SIZE = 64
SWAP = [(0, 1), (1, 0)]
ROWS = ("far", "plane", "pair")
BF16 = jnp.bfloat16
F32 = jnp.float32


def other_chip(value):
    return lax.ppermute(value, "chip", SWAP)


def other_pair(value):
    return lax.ppermute(value, "pair", SWAP)


def other_plane(value):
    return lax.ppermute(value, "plane", SWAP)


def other_core(value):
    return lax.ppermute(value, "core", SWAP)


def in_order(first, second, index, axis):
    forward = jnp.concatenate([first, second], axis=axis)
    backward = jnp.concatenate([second, first], axis=axis)
    return jnp.where(index == 0, forward, backward)


def half_rows(value, index):
    rows = value.shape[0] // 2
    return lax.dynamic_slice_in_dim(value, index * rows, rows)


def own_norm(values, axis):
    values = values.astype(F32)
    average = jnp.mean(values, axis=axis, keepdims=True)
    centred = values - average
    variance = jnp.mean(centred * centred, axis=axis, keepdims=True)
    return (centred * lax.rsqrt(variance + 1e-05)).astype(BF16)


def masked_softmax(tables, tally):
    live = jnp.arange(tables.shape[-1])[None, :] < tally[:, None]
    tables = jnp.where(live[:, None, None, :], tables, -jnp.inf)
    return jax.nn.softmax(tables, axis=-1).astype(BF16)


CONTRACT_FIRST = (((0,), (0,)), ((), ()))
CONTRACT_LAST = (((1,), (1,)), ((), ()))
IN_VMEM = pl.BlockSpec(memory_space=pltpu.VMEM)
IN_SMEM = pl.BlockSpec(memory_space=pltpu.SMEM)
IN_HBM = pl.BlockSpec(memory_space=pltpu.HBM)
GRANT = pltpu.CompilerParams(vmem_limit_bytes=40 * 2**20)


def slot_of(label_ref, start, lines, line):
    first, last = label_ref[start], label_ref[start + lines - 1]
    family = label_ref[start + line]
    return jnp.where(family == first, 0, jnp.where(family == last, 1, family - first + 1))


def quarter_spots(me_ref):
    chip, core = me_ref[1], me_ref[2]
    return (
        2 * chip + core, 2 * chip + 1 - core, 2 * (1 - chip) + core, 2 * (1 - chip) + 1 - core
    )


def row_front_kernel(
    lines, me_ref, label_ref, starts_ref, tally_ref, own, near, far, diagonal, triple,
    table_ref, inner_ref, value_ref, tables, normed,
):
    step = pl.program_id(0)
    group, quarter, sites = own.shape
    heads = quarter // HEAD_SIZE

    @pl.when(step == 0)
    def _():
        tables[...] = jnp.zeros_like(tables)

    pieces = []
    for ref in (own, near, far, diagonal):
        lanes = jnp.concatenate([ref[line] for line in range(group)], axis=-1)
        pieces.append(lanes.astype(F32))
    size = 4 * quarter
    average = sum(jnp.sum(piece, axis=0, keepdims=True) for piece in pieces) / size
    pieces = [piece - average for piece in pieces]
    variance = sum(jnp.sum(piece * piece, axis=0, keepdims=True) for piece in pieces) / size
    inverse = lax.rsqrt(variance + 1e-05)
    for spot, piece in zip(quarter_spots(me_ref), pieces):
        spot = pl.multiple_of(spot * quarter, quarter)
        normed[pl.ds(spot, quarter), :] = (piece * inverse).astype(BF16)
    projected = jnp.dot(triple[...], normed[...], preferred_element_type=F32).astype(BF16)
    base = me_ref[0] * lines
    jobs = []
    for line in range(group):
        part = projected[:, line * sites : (line + 1) * sites]
        value_ref[line] = part[2 * quarter :]
        place = step * group + line
        slot = slot_of(label_ref, base, lines, place)
        family = label_ref[base + place]
        members = jnp.full((1, sites), starts_ref[family + 1] - starts_ref[family], jnp.int32)
        scale = HEAD_SIZE**-0.5 * lax.rsqrt(members.astype(F32))
        for head in range(heads):
            lower = head * HEAD_SIZE
            queries = part[lower : lower + HEAD_SIZE]
            keys = part[quarter + lower : quarter + lower + HEAD_SIZE]
            logits = lax.dot_general(queries, keys, CONTRACT_FIRST, preferred_element_type=F32)
            jobs.append((slot * heads + head, logits, scale))
    for index, logits, scale in jobs:
        tables[index] += logits * scale

    @pl.when(step == pl.num_programs(0) - 1)
    def _():
        for index in range(2 * heads):
            table = tables[index].astype(BF16)
            if len(table_ref.shape) == 4:
                groups, _, rows, _ = table_ref.shape
                table_ref[:, index] = table.reshape(groups, rows, sites)
            else:
                table_ref[index] = table
        site = lax.broadcasted_iota(jnp.int32, (sites, sites), 1)

        def inner(index, carry):
            table = tables[2 * heads + index]
            family = label_ref[base] + 1 + index // heads
            family = jnp.minimum(family, tally_ref.shape[0] - 1)
            table = jnp.where(site < tally_ref[family], table, -jnp.inf)
            table = jnp.exp(table - jnp.max(table, axis=-1, keepdims=True))
            table = table / jnp.sum(table, axis=-1, keepdims=True)
            inner_ref[index] = table.astype(BF16)
            return carry

        lax.fori_loop(0, inner_ref.shape[0], inner, 0)


def row_front(pieces, triple, plan, slots, row_groups):
    lines, quarter, sites = pieces[0].shape
    group = 4
    heads = quarter // HEAD_SIZE
    inner = slots - 2
    rows = sites // row_groups
    shape = (row_groups, 2 * heads, rows, sites) if rows % 16 == 0 else (2 * heads, sites, sites)
    block = pl.BlockSpec((group, quarter, sites), lambda step: (step, 0, 0))

    def whole(shape):
        return pl.BlockSpec(shape, lambda step: (0,) * len(shape))

    tables, inner_weights, values = pl.pallas_call(
        functools.partial(row_front_kernel, lines),
        grid=(lines // group,),
        out_shape=(
            jax.ShapeDtypeStruct(shape, BF16),
            jax.ShapeDtypeStruct((inner * heads, sites, sites), BF16),
            jax.ShapeDtypeStruct((lines, quarter, sites), BF16),
        ),
        in_specs=[IN_SMEM] * 4 + [block] * 4 + [whole((3 * quarter, 4 * quarter))],
        out_specs=(whole(shape), whole((inner * heads, sites, sites)), block),
        scratch_shapes=[
            pltpu.VMEM((slots * heads, sites, sites), F32),
            pltpu.VMEM((4 * quarter, group * sites), BF16),
        ],
        compiler_params=GRANT,
        name="row_front",
    )(*plan, *pieces, triple.reshape(3 * quarter, 4 * quarter))
    if rows % 16:
        tables = jnp.transpose(tables.reshape(-1, row_groups, rows, sites), (1, 0, 2, 3))
    return tables, inner_weights, values


def tie_kernel(me_ref, label_ref, starts_ref, tally_ref, parts, out, weights):
    groups, pairs, rows, sites = parts.shape
    lines = label_ref.shape[0] // groups
    ends = [label_ref[g * lines + e * (lines - 1)] for g in range(groups) for e in range(2)]
    heads = pairs // 2
    site = lax.broadcasted_iota(jnp.int32, (heads, rows, sites), 2)
    for family in range(weights.shape[0]):
        total = jnp.zeros((heads, rows, sites), F32)
        for group in range(groups):
            for end in range(2):
                part = parts[group, end * heads : (end + 1) * heads].astype(F32)
                total += jnp.where(ends[2 * group + end] == family, part, 0.0)
        total = jnp.where(site < tally_ref[family], total, -jnp.inf)
        total = jnp.exp(total - jnp.max(total, axis=-1, keepdims=True))
        total = total / jnp.sum(total, axis=-1, keepdims=True)
        weights[family] = total.astype(BF16)
    for group in range(groups):
        for end in range(2):
            chosen = weights[ends[2 * group + end]]
            out[group, end * heads : (end + 1) * heads] = chosen


def tie(parts, plan):
    groups, pairs, rows, sites = parts.shape
    _, label, _, tally = plan
    if rows % 16 == 0:
        return pl.pallas_call(
            tie_kernel,
            out_shape=jax.ShapeDtypeStruct(parts.shape, BF16),
            in_specs=[IN_SMEM] * 4 + [IN_VMEM],
            out_specs=IN_VMEM,
            scratch_shapes=[pltpu.VMEM((tally.shape[0], pairs // 2, rows, sites), BF16)],
            compiler_params=GRANT,
            name="tie",
        )(*plan, parts)
    ends = jnp.stack([label.reshape(groups, -1)[:, 0], label.reshape(groups, -1)[:, -1]], axis=1)
    parts = parts.astype(F32).reshape(groups, 2, -1, rows, sites)
    member = (ends[:, :, None] == jnp.arange(tally.shape[0])).astype(F32)
    totals = jnp.einsum("stf,sthij->fhij", member, parts, precision=lax.Precision.HIGHEST)
    return masked_softmax(totals, tally)[ends].reshape(groups, pairs, rows, sites)


def mix_kernel(
    me_ref, label_ref, starts_ref, tally_ref, shared, inner, values, kept, sent, weights
):
    heads, sites = shared.shape[1] // 2, values.shape[2]
    half = kept.shape[0]
    for index in range(2 * heads):
        weights[index] = shared[:, index].reshape(sites, sites)
    weights[2 * heads :] = inner[...]
    for target, chip in ((sent, 1 - me_ref[1]), (kept, me_ref[1])):
        jobs = []
        for line in range(half):
            row = chip * half + line
            slot = slot_of(label_ref, me_ref[0] * 2 * half, 2 * half, row)
            value = values[row]
            for head in range(heads):
                features = slice(head * HEAD_SIZE, (head + 1) * HEAD_SIZE)
                result = lax.dot_general(
                    value[features],
                    weights[slot * heads + head],
                    CONTRACT_LAST,
                    preferred_element_type=F32,
                )
                jobs.append((line, features, result))
        for line, features, result in jobs:
            target[line, features] = result.astype(BF16)


def mix(shared, inner, values, plan):
    groups, pairs, rows, sites = shared.shape
    lines, quarter, _ = values.shape
    if rows % 16 == 0:
        half = jax.ShapeDtypeStruct((lines // 2, quarter, sites), BF16)
        return pl.pallas_call(
            mix_kernel,
            out_shape=(half, half),
            in_specs=[IN_SMEM] * 4 + [IN_VMEM] * 3,
            out_specs=(IN_VMEM, IN_VMEM),
            scratch_shapes=[pltpu.VMEM((pairs + inner.shape[0], sites, sites), BF16)],
            compiler_params=GRANT,
            name="mix",
        )(*plan, shared, inner, values)
    me, label = plan[:2]
    chip = me[1]
    label = lax.dynamic_slice_in_dim(label, me[0] * lines, lines)
    slot = slot_of(label, 0, lines, jnp.arange(lines))
    ends = jnp.transpose(shared, (1, 0, 2, 3)).reshape(2, pairs // 2, sites, sites)
    weights = jnp.concatenate([ends, inner.reshape(-1, *ends.shape[1:])])[slot]
    values = values.reshape(lines, -1, HEAD_SIZE, sites)
    mixed = jnp.einsum("rhdj,rhij->rhdi", values, weights, preferred_element_type=F32)
    mixed = mixed.astype(BF16).reshape(lines, quarter, sites)
    return half_rows(mixed, chip), half_rows(mixed, 1 - chip)


def project_kernel(
    me_ref, mixed, got, mixing, piece, *refs
):
    pieces = refs[:4]
    kept, sent, stream, far, semaphores = refs[4:]
    lines, _, sites = stream.shape
    quarter = mixing.shape[0]
    chip, core = me_ref[1], me_ref[2]
    copies = []
    for index, (spot, source) in enumerate(zip(quarter_spots(me_ref), pieces)):
        spot = pl.multiple_of(spot * quarter, quarter)
        copies.append(
            pltpu.make_async_copy(
                source.at[pl.ds((2 * chip + core) * lines, lines)],
                stream.at[:, pl.ds(spot, quarter)],
                semaphores.at[index],
            )
        )
    for copy in copies:
        copy.start()
    fetch = pltpu.make_async_copy(piece.at[pl.ds(7 * quarter // 2, quarter)], far, semaphores.at[4])
    fetch.start()

    def partial(row):
        near_part = lax.dot_general(
            mixed[row], mixing[...], CONTRACT_FIRST, preferred_element_type=F32
        )
        return near_part + lax.dot_general(
            got[row], far[...], CONTRACT_FIRST, preferred_element_type=F32
        )

    fetch.wait()
    for line in range(lines):
        sent[line] = partial((1 - core) * lines + line).astype(BF16)
    for copy in copies:
        copy.wait()
    for line in range(lines):
        kept[line] = partial(core * lines + line) + stream[line].astype(F32).T


def project(mixed, got, mixing, piece, pieces, me):
    half, quarter, sites = mixed.shape
    lines, model = half // 2, mixing.shape[1]
    out = (lines, sites, model)
    return pl.pallas_call(
        project_kernel,
        out_shape=(jax.ShapeDtypeStruct(out, F32), jax.ShapeDtypeStruct(out, BF16)),
        in_specs=[IN_SMEM] + [IN_VMEM] * 3 + [IN_HBM] * 5,
        out_specs=(IN_VMEM, IN_VMEM),
        scratch_shapes=[
            pltpu.VMEM((lines, model, sites), BF16),
            pltpu.VMEM((quarter, model), BF16),
            pltpu.SemaphoreType.DMA((5,)),
        ],
        compiler_params=GRANT,
        name="project",
    )(me, mixed, got, mixing, piece, *pieces)


def settle_kernel(kept, got, out):
    lines, sites, model = kept.shape
    chips = out.shape[0]
    parts = []
    for line in range(lines):
        total = kept[line] + got[line].astype(F32)
        parts.append(total.reshape(chips, sites // chips, model))
    out[...] = jnp.concatenate(parts, axis=1).astype(BF16)


def settle(kept, got, chips):
    lines, sites, model = kept.shape
    place = sites // chips
    if place % 8 == 0:
        return pl.pallas_call(
            settle_kernel,
            out_shape=jax.ShapeDtypeStruct((chips, lines * place, model), BF16),
            in_specs=[IN_VMEM, IN_VMEM],
            out_specs=IN_VMEM,
            compiler_params=GRANT,
            name="settle",
        )(kept, got)
    total = (kept + got.astype(F32)).astype(BF16).reshape(lines, chips, place, model)
    return jnp.transpose(total, (1, 0, 2, 3)).reshape(chips, lines * place, model)


def arrive_kernel(blocks, normed, stream, tokens):
    chips, count, model = blocks.shape
    places, rows, _ = normed.shape
    lanes = tokens.shape[-1]
    flat = blocks[...].reshape(chips * count, model).astype(F32)
    for index in range(tokens.shape[0]):
        tokens[index] = flat[:, index * lanes : (index + 1) * lanes]
    for place in range(places):
        values = [
            tokens[index, pl.ds(place, rows, stride=places), :] for index in range(tokens.shape[0])
        ]
        values = jnp.concatenate(values, axis=-1)
        stream[place] = values.astype(BF16)
        centred = values - jnp.mean(values, axis=-1, keepdims=True)
        variance = jnp.mean(centred * centred, axis=-1, keepdims=True)
        normed[place] = (centred * lax.rsqrt(variance + 1e-05)).astype(BF16)


def arrive(blocks, place):
    chips, count, model = blocks.shape
    rows = chips * count // place
    if place % 8 == 0:
        shape = jax.ShapeDtypeStruct((place, rows, model), BF16)
        return pl.pallas_call(
            arrive_kernel,
            out_shape=(shape, shape),
            in_specs=[IN_VMEM],
            out_specs=(IN_VMEM, IN_VMEM),
            scratch_shapes=[pltpu.VMEM((model // 128, chips * count, 128), F32)],
            compiler_params=GRANT,
            name="arrive",
        )(blocks)
    stream = jnp.transpose(blocks.reshape(rows, place, model), (1, 0, 2))
    return own_norm(stream, -1), stream


def column_kernel(
    lines, me_ref, starts_ref, own, other, triple, mixing, piece, pair_rest, plane_rest,
    kept, sent, normed, near, far, projected, mixed, semaphores,
):
    quarter = mixing.shape[0]
    eighth = quarter // 2
    core, pair, plane = me_ref[2], me_ref[3], me_ref[4]

    def rows_of(ref, start):
        return ref.at[pl.ds(start, quarter)]

    def spot(index):
        return pl.multiple_of(index * quarter, quarter)

    moves = (
        (triple, near.at[pl.ds(0, 3 * quarter)]),
        (mixing, near.at[pl.ds(3 * quarter, quarter)]),
        (rows_of(piece, 5 * eighth), rows_of(far, spot(pair))),
        (rows_of(piece, 9 * eighth), rows_of(far, spot(2 + plane))),
        (rows_of(pair_rest, eighth), rows_of(far, spot(1 - pair))),
        (rows_of(plane_rest, 0), rows_of(far, spot(3 - plane))),
    )
    copies = [
        pltpu.make_async_copy(source, target, semaphores.at[index])
        for index, (source, target) in enumerate(moves)
    ]
    for copy in copies:
        copy.start()
    places, rows, model = own.shape
    both = 2 * rows
    normed[:, :rows] = own[...]
    normed[:, rows:] = other[...]
    flat = normed[...].reshape(places * both, model)

    def families(axis):
        shape = (both, 1) if axis == 0 else (1, both)
        index = lax.broadcasted_iota(jnp.int32, shape, axis)
        line = jnp.where(index < rows, core * lines, (1 - core) * lines)
        index = jnp.where(index < rows, index, index - rows)
        line += index // lines * (2 * lines) + index % lines
        return sum(
            (line >= starts_ref[family]).astype(jnp.int32)
            for family in range(1, starts_ref.shape[0] - 1)
        )

    same = families(0) == families(1)
    scale = HEAD_SIZE**-0.5

    def attend(weights, lower):
        projected[...] = lax.dot_general(
            weights, flat, CONTRACT_LAST, preferred_element_type=F32
        ).astype(BF16)
        heads = quarter // HEAD_SIZE
        jobs = [(place, head) for place in range(places) for head in range(heads)]
        group = min(len(jobs), max(1, 12 * 128 // both))
        for first in range(0, len(jobs), group):
            batch = jobs[first : first + group]
            scores = []
            for place, head in batch:
                lanes = slice(place * both, (place + 1) * both)
                features = slice(head * HEAD_SIZE, (head + 1) * HEAD_SIZE)
                queries = projected[:quarter, lanes][features]
                keys = projected[quarter : 2 * quarter, lanes][features]
                scores.append(
                    lax.dot_general(keys, queries, CONTRACT_FIRST, preferred_element_type=F32)
                )
            scores = [jnp.where(same, part * scale, -jnp.inf) for part in scores]
            scores = [jnp.exp(part - jnp.max(part, axis=0, keepdims=True)) for part in scores]
            totals = [jnp.sum(part, axis=0, keepdims=True) for part in scores]
            scores = [part.astype(BF16) for part in scores]
            results = []
            for (place, head), part in zip(batch, scores):
                lanes = slice(place * both, (place + 1) * both)
                features = slice(head * HEAD_SIZE, (head + 1) * HEAD_SIZE)
                values = projected[2 * quarter :, lanes][features]
                results.append(jnp.dot(values, part, preferred_element_type=F32))
            for (place, head), part, total in zip(batch, results, totals):
                lanes = slice(place * both, (place + 1) * both)
                target = slice(lower + head * HEAD_SIZE, lower + (head + 1) * HEAD_SIZE)
                mixed[target, lanes] = (part / total).astype(BF16)

    copies[0].wait()
    attend(near[: 3 * quarter], 0)
    for copy in copies[1:]:
        copy.wait()
    attend(far[: 3 * quarter], quarter)
    for place in range(places):
        lanes = slice(place * both, (place + 1) * both)
        partial = lax.dot_general(
            mixed[:quarter, lanes], near[3 * quarter :], CONTRACT_FIRST, preferred_element_type=F32
        )
        partial += lax.dot_general(
            mixed[quarter:, lanes], far[3 * quarter :], CONTRACT_FIRST, preferred_element_type=F32
        )
        kept[place] = partial[:rows]
        sent[place] = partial[rows:].astype(BF16)


def column(own, other, triple, mixing, piece, pair_rest, plane_rest, plan, lines):
    places, rows, model = own.shape
    quarter = mixing.shape[0]
    tokens = 2 * places * rows
    return pl.pallas_call(
        functools.partial(column_kernel, lines),
        out_shape=(
            jax.ShapeDtypeStruct(own.shape, F32),
            jax.ShapeDtypeStruct(own.shape, BF16),
        ),
        in_specs=[IN_SMEM] * 2 + [IN_VMEM] * 2 + [IN_HBM] * 5,
        out_specs=(IN_VMEM, IN_VMEM),
        scratch_shapes=[
            pltpu.VMEM((places, 2 * rows, model), BF16),
            pltpu.VMEM((4 * quarter, model), BF16),
            pltpu.VMEM((4 * quarter, model), BF16),
            pltpu.VMEM((3 * quarter, tokens), BF16),
            pltpu.VMEM((2 * quarter, tokens), BF16),
            pltpu.SemaphoreType.DMA((6,)),
        ],
        compiler_params=GRANT,
        name="column",
    )(plan[0], plan[2], own, other, triple.reshape(-1, model), mixing, piece, pair_rest, plane_rest)


def finish_kernel(stream, kept, got, out):
    places, rows, model = stream.shape
    parts, wide = out.shape[1] // 3, out.shape[2]
    quarter = wide // 2 * 3
    heads = model // quarter
    groups = out.shape[0] // heads
    lines = rows // groups
    for group in range(groups):
        these = slice(group * lines, (group + 1) * lines)
        total = stream[:, these].astype(F32) + kept[:, these] + got[:, these].astype(F32)
        total = total.reshape(places * lines, model)
        for head in range(heads):
            block = total[:, head * quarter : (head + 1) * quarter]
            narrow = jnp.concatenate([block[:parts, wide:], block[parts:, wide:]], axis=1)
            block = jnp.concatenate([block[:, :wide], narrow], axis=0)
            out[group * heads + head] = block.astype(BF16)


def finish(stream, kept, got, groups, quarter):
    places, rows, model = stream.shape
    heads, lines = model // quarter, rows // groups
    parts, wide = places * lines // 2, quarter // 3 * 2
    shape = (groups * heads, 3 * parts, wide)
    if parts % 16 == 0 and lines % 8 == 0:
        return pl.pallas_call(
            finish_kernel,
            out_shape=jax.ShapeDtypeStruct(shape, BF16),
            in_specs=[IN_VMEM] * 3,
            out_specs=IN_VMEM,
            compiler_params=GRANT,
            name="finish",
        )(stream, kept, got)
    total = (stream.astype(F32) + kept + got.astype(F32)).astype(BF16)
    total = total.reshape(places, groups, lines, heads, quarter)
    total = jnp.transpose(total, (1, 3, 0, 2, 4)).reshape(-1, places * lines, quarter)
    narrow = jnp.concatenate([total[:, :parts, wide:], total[:, parts:, wide:]], axis=2)
    return jnp.concatenate([total[:, :, :wide], narrow], axis=1)


def feed_forward_kernel(
    me_ref, normed, expand, contract, piece, pair_rest, column_rest, plane_rest, late, out,
    near_expand, near_contract, far_expand, far_contract, hidden, semaphores,
):
    width = near_expand.shape[1]
    quarter = late.shape[0] // 2
    pair, plane = me_ref[3], me_ref[4]
    eighth = quarter // 2

    def move(source, start, count, target, place, index):
        return pltpu.make_async_copy(
            source.at[pl.ds(start, count)], target.at[pl.ds(place, count)], semaphores.at[index]
        )

    def own_weights():
        return [
            move(expand, 0, width, near_expand, 0, 0),
            move(contract, 0, width, near_contract, 0, 1),
            move(late, 0, quarter, far_expand, 3 * quarter, 2),
            move(late, quarter, quarter, far_contract, 3 * quarter, 3),
        ]

    def by_pair(first, second):
        return [
            move(piece, 0, 5 * eighth, first, 0, 4),
            move(pair_rest, 0, 4 * eighth, second, 0, 5),
            move(column_rest, 0, eighth, second, 4 * eighth, 8),
        ]

    def by_plane(first, second):
        return [
            move(piece, 11 * eighth, eighth, first, 5 * eighth, 6),
            move(plane_rest, 2 * eighth, eighth, second, 5 * eighth, 7),
        ]

    for copy in own_weights():
        copy.start()
    for index, moves in ((pair, by_pair), (plane, by_plane)):

        @pl.when(index == 0)
        def _(moves=moves):
            for copy in moves(far_expand, far_contract):
                copy.start()

        @pl.when(index != 0)
        def _(moves=moves):
            for copy in moves(far_contract, far_expand):
                copy.start()

    tile = width // 3
    values = normed[...]

    def raise_by(weights, lower):
        for start in range(0, width, tile):
            up = jnp.dot(values, weights[:, start : start + tile], preferred_element_type=F32)
            up = 0.5 * up * (1.0 + lax.erf(up * 2.0**-0.5))
            hidden[:, lower + start : lower + start + tile] = up.astype(BF16)

    copies = own_weights() + by_pair(far_expand, far_contract) + by_plane(far_expand, far_contract)
    copies[0].wait()
    raise_by(near_expand, 0)
    for copy in copies[1:]:
        copy.wait()
    raise_by(far_expand, width)
    down = jnp.dot(hidden[:, :width], near_contract[...], preferred_element_type=F32)
    down += jnp.dot(hidden[:, width:], far_contract[...], preferred_element_type=F32)
    out[...] = down.astype(out.dtype)


def feed_forward(normed, expand, contract, pieces, me, kind):
    places, rows, model = normed.shape
    tokens, width = places * rows, expand.shape[1]
    result = pl.pallas_call(
        feed_forward_kernel,
        out_shape=jax.ShapeDtypeStruct((tokens, model), kind),
        in_specs=[IN_SMEM, IN_VMEM] + [IN_HBM] * 7,
        out_specs=IN_VMEM,
        scratch_shapes=[
            pltpu.VMEM((model, width), BF16),
            pltpu.VMEM((width, model), BF16),
            pltpu.VMEM((model, width), BF16),
            pltpu.VMEM((model, width), BF16),
            pltpu.VMEM((tokens, 2 * width), BF16),
            pltpu.SemaphoreType.DMA((9,)),
        ],
        compiler_params=GRANT,
        name="feed_forward",
    )(me, normed.reshape(tokens, model), expand, contract, *pieces)
    return result.reshape(normed.shape)


def core_sum(stream, kept, sent):
    return (stream.astype(F32) + kept + other_core(sent).astype(F32)).astype(BF16)


def shards(
    alignment_embedding,
    line_group_label,
    group_site_tally,
    horizontal_triple_matrix,
    horizontal_mixing_matrix,
    vertical_triple_matrix,
    vertical_mixing_matrix,
    expand_matrix,
    contract_matrix,
):
    lines, quarter, sites = alignment_embedding.shape
    row_groups = lax.axis_size(ROWS)
    own = lines // 4
    chips = 2 * row_groups
    place = sites // chips
    pair = lax.axis_index("pair")
    chip = lax.axis_index("chip")
    core = lax.axis_index("core")
    label = line_group_label
    tally = group_site_tally
    families = tally.shape[0]

    starts = jnp.sum(label[:, None] < jnp.arange(families + 1), axis=0, dtype=jnp.int32)
    plane = lax.axis_index("plane")
    me = jnp.stack([lax.axis_index(ROWS), chip, core, pair, plane]).astype(jnp.int32)

    across = other_chip(alignment_embedding)
    near = other_core(alignment_embedding)
    width, eighth = expand_matrix.shape[0], quarter // 2
    column_pack = jnp.concatenate(
        [
            vertical_triple_matrix.reshape(-1, vertical_triple_matrix.shape[-1]),
            vertical_mixing_matrix,
        ]
    )
    feed = jnp.stack([expand_matrix, contract_matrix])

    def chosen(options, index):
        return lax.dynamic_index_in_dim(options, index, 0, False)

    quarters = column_pack.reshape(4, quarter, -1)
    pack = jnp.concatenate(
        [
            chosen(feed[:, : 5 * eighth], pair),
            chosen(quarters, pair),
            horizontal_mixing_matrix,
            chosen(quarters, 2 + plane),
            chosen(feed[:, 5 * eighth : 6 * eighth], plane),
        ]
    )
    late_pack = feed[:, 6 * eighth :].reshape(2 * (width - 6 * eighth), -1)
    across, near, pack, late_pack, starts, me = lax.optimization_barrier(
        (across, near, pack, late_pack, starts, me)
    )
    plan = (me, label, starts, tally)
    streams = (alignment_embedding, near, across, other_core(across))
    piece = other_chip(pack)

    shared, inner_weights, values = row_front(
        streams,
        horizontal_triple_matrix,
        plan,
        2 + max(min(families, lines) - 2, 1),
        row_groups,
    )
    parts = lax.all_to_all(shared, ROWS, 0, 0, tiled=True)
    shared = lax.all_to_all(tie(parts, plan), ROWS, 0, 0, tiled=True)
    mixed, sent = mix(shared, inner_weights, values, plan)
    sent, piece, late_pack = lax.optimization_barrier((sent, piece, late_pack))
    column_rest = other_pair(piece[4 * eighth : 7 * eighth])
    plane_rest = other_plane(piece[9 * eighth :])
    feed_rest = other_pair(piece[: 4 * eighth])
    late_piece = other_chip(late_pack)

    got, column_rest, plane_rest = lax.optimization_barrier(
        (other_chip(sent), column_rest, plane_rest)
    )
    kept, sent = project(
        mixed,
        got,
        horizontal_mixing_matrix,
        piece,
        streams,
        me,
    )

    blocks = settle(kept, other_core(sent), chips)
    blocks = lax.all_to_all(blocks, ROWS + ("chip",), 0, 0, tiled=True)
    normed, after_row = arrive(blocks, place)
    normed, feed_rest, late_piece = lax.optimization_barrier((normed, feed_rest, late_piece))
    kept, sent = column(
        normed,
        other_core(normed),
        vertical_triple_matrix,
        vertical_mixing_matrix,
        piece,
        column_rest,
        plane_rest,
        plan,
        lines // 4,
    )
    after_col = core_sum(after_row, kept, sent)

    normed = own_norm(after_col, -1)
    pieces = (piece, feed_rest, column_rest, plane_rest, late_piece)
    weights = (expand_matrix, contract_matrix, pieces, me)
    kept = feed_forward(normed, *weights, F32)
    sent = feed_forward(other_core(normed), *weights, BF16)
    blocks = finish(after_col, kept, other_core(sent), row_groups, quarter)

    blocks = lax.all_to_all(blocks, ROWS + ("chip", "core"), 0, 0, tiled=True)
    parts, wide = 2 * own * place // 2, quarter // 3 * 2
    narrow = blocks[:, 2 * parts :]
    narrow = jnp.concatenate([narrow[:, :, : wide // 2], narrow[:, :, wide // 2 :]], axis=1)
    finished = jnp.concatenate([blocks[:, : 2 * parts], narrow], axis=2)
    finished = finished.reshape(chips, 2, place, 2, own, quarter)
    finished = jnp.transpose(finished, (3, 1, 4, 5, 0, 2))
    return finished.reshape(lines, quarter, sites)


def solution(mesh):
    far = mesh.shape["rows"] // 4
    split = Mesh(mesh.devices.reshape(far, 2, 2, 2, 2), ROWS + ("chip", "core"))
    heads = ("chip", "core")
    placed = (
        P(ROWS, heads, None),
        P(),
        P(),
        P(None, heads, None),
        P(heads, None),
        P(None, heads, None),
        P(heads, None),
        P(None, heads),
        P(heads, None),
    )
    return jax.shard_map(
        shards, mesh=split, in_specs=placed, out_specs=P(ROWS, heads, None), check_vma=False
    )
```

time: 182 us -> 166 us (0.912)
  waiting for transfers between devices: 59.8 us -> 41.1 us
  local copies, waits for them, and re-layouts: 11.8 us -> 16.7 us
  Pallas kernels: 37.3 us -> 32.8 us
    ppermute x5 -> x4, waiting for transfers between devices: 22.6 us -> 11.8 us  [other_chip(): return lax.ppermute(value, 'chip', SWAP)]
    ppermute x2, waiting for transfers between devices: 10.5 us -> 2.05 us  [other_pair(): return lax.ppermute(value, 'pair', SWAP)]
    pallas_call x1, Pallas kernels: 12.5 us -> 6.04 us  [column(): pl.pallas_call(functools.partial(column_kernel, lines), out_shape=(jax.Sh...]
    unnamed x34 -> x39, local copies, waits for them, and re-layouts: 5.42 us -> 10.4 us
    concatenate x5 -> x2, other arithmetic: 3.5 us -> 0.3 us  [the longest x1 0.26 us: shards(): finished = jnp.concatenate([blocks[:, :2 * parts], narrow], axis=2)]
    unnamed x0 -> x1, other arithmetic: none -> 2.54 us
    slice x10 -> x5, local copies, waits for them, and re-layouts: 3.36 us -> 4.24 us  [the longest x1 3.23 us: shards(): feed[:, :5 * eighth]]
    ppermute x9 -> x7, waiting for transfers between devices: 10.9 us -> 11.3 us  [other_core(): return lax.ppermute(value, 'core', SWAP)]
  transfers between devices with their start and end apart: 17 -> 15, of which waited for: 12 -> 10; matrix products, arithmetic and copies ran while one was open for 3% -> 8% of each run, Pallas kernels for 10% -> 11%
where the time goes in v3:
time: 166 us; the launch traced here: 165 us
  blocking collectives  49.2 us (30%)
  waiting for transfers between devices  41.1 us (25%)
  Pallas kernels  32.8 us (20%)
  starting transfers between devices  19 us (11%)
  local copies, waits for them, and re-layouts  16.7 us (10%)
  other arithmetic  5.94 us (4%)
    all_to_all x1, blocking collectives, shards(): blocks = lax.all_to_all(blocks, ROWS + ('chip', 'core'), 0, 0, tiled=True)  24.6 us
    all_to_all x1, waiting for transfers between devices, shards(): blocks = lax.all_to_all(blocks, ROWS + ('chip',), 0, 0, tiled=True)  15.9 us
    all_to_all x1, blocking collectives, shards(): parts = lax.all_to_all(shared, ROWS, 0, 0, tiled=True)  13.9 us
    ppermute x4, waiting for transfers between devices, other_chip(): return lax.ppermute(value, 'chip', SWAP)  11.8 us
    ppermute x7, waiting for transfers between devices, other_core(): return lax.ppermute(value, 'core', SWAP)  11.3 us
    pallas_call x2, Pallas kernels, feed_forward(): pl.pallas_call(feed_forward_kernel, out_shape=jax.ShapeDtypeStruct((token...  10.9 us
    all_to_all x1, blocking collectives, shards(): shared = lax.all_to_all(tie(parts, plan), ROWS, 0, 0, tiled=True)  10.7 us
    unnamed x39, local copies, waits for them, and re-layouts  10.4 us
  transfers between devices with their start and end apart: 15, of which 10 were waited for; matrix products, arithmetic and copies ran while one was open for 8% of the time, Pallas kernels for 11%

profile of v3, /device:TPU:0, one launch (start us, length us, event | category | flops | bytes accessed | tf_op | source)
XLA Modules:
  0.0 165.1 jit_solution(17636073332193468105)
XLA Ops:
  0.0 2.9 %collective-permute-start = (bf16[16,192,128]{2,1,0:T(8,128)(2,1)}, bf16[16,192,128]{2,1,0:T(8,128)(2,1)}, u32[]{:S(2)}, u32[]{:S(2)}) collective-permute-start(bf16[16,192,128]{2,1,0:T(8,128)(2,1)} %refs_0_.1), channel_id=1, source_target_pairs={{0,2},{2,0},{1,3},{3,1},{4,6},{6,4},{5,7},{7,5},{8,10},{10,8},{9,1... | collective-permute-start | bytes 2359304 | tf_op jit(solution)/shard_map/ppermute | solution.py:18
  2.9 3.2 %pad_slice_fusion = (bf16[2,480,768]{2,1,0:T(8,128)(2,1)}, bf16[2,480,768]{2,1,0:T(8,128)(2,1)}) fusion(bf16[1,768,768]{2,1,0:T(8,128)(2,1)} %bitcast.30, bf16[1,768,768]{2,1,0:T(8,128)(2,1)} %bitcast.33), kind=kLoop, calls=%fused_computation | loop fusion | bytes 5308416 | tf_op jit(solution)/shard_map/slice | solution.py:698
  7.3 2.5 %fusion.5 = bf16[1152,768]{1,0:T(8,128)(2,1)} fusion(bf16[2,480,768]{2,1,0:T(8,128)(2,1)} %get-tuple-element.63, s32[]{:T(128)S(6)} %select_n.15, bf16[2,480,768]{2,1,0:T(8,128)(2,1)} %get-tuple-element.64), kind=kLoop, calls=%fused_computation.15 | loop fusion | flops 1474559 | bytes 2211844
  10.1 1.7 %bitcast_dynamic-update-slice_fusion.1 = bf16[1152,768]{1,0:T(8,128)(2,1)} fusion(bf16[1152,768]{1,0:T(8,128)(2,1)} %fusion.5, bf16[4,192,768]{2,1,0:T(8,128)(2,1)} %bitcast.44, s32[]{:T(128)S(6)} %select_n.16), kind=kLoop, calls=%fused_computation.18 | loop fusion | bytes 589828
  12.5 1.7 %bitcast_dynamic-update-slice_fusion = bf16[1152,768]{1,0:T(8,128)(2,1)} fusion(bf16[1152,768]{1,0:T(8,128)(2,1)} %constant_dynamic-update-slice_fusion, bf16[4,192,768]{2,1,0:T(8,128)(2,1)} %bitcast.45, s32[]{:T(128)S(6)} %select_n.17), kind=kLoop, calls=%fused_computation.17 | loop fusion | bytes 589828
  14.2 1.4 copy-done.17
  16.7 4.1 %collective-permute-done.far.refs_2_ = bf16[16,192,128]{2,1,0:T(8,128)(2,1)} collective-permute-done((bf16[16,192,128]{2,1,0:T(8,128)(2,1)}, bf16[16,192,128]{2,1,0:T(8,128)(2,1)}, u32[]{:S(2)}, u32[]{:S(2)}) %collective-permute-start) | collective-permute-done | bytes 786464 | tf_op jit(solution)/shard_map/ppermute | solution.py:18
  20.8 1.7 %collective-permute-start.3 = (bf16[1152,768]{1,0:T(8,128)(2,1)S(1)}, bf16[1152,768]{1,0:T(8,128)(2,1)S(1)}, u32[]{:S(2)}, u32[]{:S(2)}) collective-permute-start(bf16[1152,768]{1,0:T(8,128)(2,1)S(1)} %fusion.7), channel_id=1, source_target_pairs={{0,2},{2,0},{1,3},{3,1},{4,6},{6,4},{5,7},{7,5},{8,10},{10,8},{9,1... | collective-permute-start | bytes 5308424 | tf_op jit(solution)/shard_map/ppermute | solution.py:18
  22.5 2.5 %collective-permute-done.2.diagonal.refs_3_ = bf16[16,192,128]{2,1,0:T(8,128)(2,1)S(1)} collective-permute-done((bf16[16,192,128]{2,1,0:T(8,128)(2,1)}, bf16[16,192,128]{2,1,0:T(8,128)(2,1)S(1)}, u32[]{:S(2)}, u32[]{:S(2)}) %collective-permute-start.2) | collective-permute-done | bytes 786464 | tf_op jit(solution)/shard_map/ppermute | solution.py:30
  25.0 7.5 %row_front.1 = (bf16[8,6,16,128]{3,2,1,0:T(8,128)(2,1)S(1)}, bf16[6,128,128]{2,1,0:T(8,128)(2,1)S(1)}, bf16[16,192,128]{2,1,0:T(8,128)(2,1)S(1)}) custom-call(s32[5]{0:T(128)S(1)} %stack.35.me_ref, s32[128]{0:T(128)S(1)} %copy-done.15, s32[5]{0:T(128)S(1)} %convert_reduce_fusion.1.starts_ref, s32[4]{0:T(128)S(1)} %copy-done.16, ...), custom_call_target="tpu_custom_call" | custom-call | tf_op jit(solution)/shard_map/row_front/pallas_call | solution.py:159
  32.6 13.9 %all_to_all.20.parts = bf16[8,6,16,128]{3,2,1,0:T(8,128)(2,1)S(1)} all-to-all(bf16[8,6,16,128]{3,2,1,0:T(8,128)(2,1)S(1)} %get-tuple-element.35), channel_id=1, replica_groups=mesh['far'=2,'plane'=2,'pair'=2,'chip'=2,'core'=2] {'far','plane','pair'}, dimensions={0} | all-to-all | bytes 393216 | tf_op jit(solution)/shard_map/all_to_all | solution.py:720
  47.4 10.7 %all_to_all.21.shared = bf16[8,6,16,128]{3,2,1,0:T(8,128)(2,1)S(1)} all-to-all(bf16[8,6,16,128]{3,2,1,0:T(8,128)(2,1)S(1)} %tie.1), channel_id=1, replica_groups=mesh['far'=2,'plane'=2,'pair'=2,'chip'=2,'core'=2] {'far','plane','pair'}, dimensions={0} | all-to-all | bytes 393216 | tf_op jit(solution)/shard_map/all_to_all | solution.py:721
  58.1 1.8 %mix.1 = (bf16[8,192,128]{2,1,0:T(8,128)(2,1)S(1)}, bf16[8,192,128]{2,1,0:T(8,128)(2,1)S(1)}) custom-call(s32[5]{0:T(128)S(1)} %stack.35.me_ref, s32[128]{0:T(128)S(1)} %copy-done.15, s32[5]{0:T(128)S(1)} %convert_reduce_fusion.1.starts_ref, s32[4]{0:T(128)S(1)} %copy-done.16, bf16[8,6,16,128]{3,2,1,0:T(8,128)(2,1)S(1)} %all_to_all.21.shared, ...), custom_call_target="tpu_custom_call" | custom-call | tf_op jit(solution)/shard_map/mix/pallas_call | solution.py:255
  60.7 1.5 collective-permute-start.5
  62.2 1.6 collective-permute-start.6
  63.7 1.5 collective-permute-start.4
  65.2 7.0 %collective-permute-done.4.got = bf16[8,192,128]{2,1,0:T(8,128)(2,1)S(1)} collective-permute-done((bf16[8,192,128]{2,1,0:T(8,128)(2,1)S(1)}, bf16[8,192,128]{2,1,0:T(8,128)(2,1)S(1)}, u32[]{:S(2)}, u32[]{:S(2)}) %collective-permute-start.4) | collective-permute-done | bytes 393248 | tf_op jit(solution)/shard_map/ppermute | solution.py:18
  73.1 2.3 %project.1 = (f32[4,128,768]{2,1,0:T(8,128)S(1)}, bf16[4,128,768]{2,1,0:T(8,128)(2,1)S(1)}) custom-call(s32[5]{0:T(128)S(1)} %stack.35.me_ref, bf16[8,192,128]{2,1,0:T(8,128)(2,1)S(1)} %get-tuple-element.38.mixed, bf16[8,192,128]{2,1,0:T(8,128)(2,1)S(1)} %collective-permute-done.4.got, bf16[192,768]{1,0:T(8,128)(2,1)S(1)} %copy-done.13, ...), custom_call_target="tpu_custom_call" | custom-call | tf_op jit(solution)/shard_map/project/pallas_call | solution.py:320
  75.5 2.3 %collective-permute-done.7.got = bf16[4,128,768]{2,1,0:T(8,128)(2,1)S(1)} collective-permute-done((bf16[4,128,768]{2,1,0:T(8,128)(2,1)S(1)}, bf16[4,128,768]{2,1,0:T(8,128)(2,1)S(1)}, u32[]{:S(2)}, u32[]{:S(2)}) %collective-permute-start.7) | collective-permute-done | bytes 786464 | tf_op jit(solution)/shard_map/ppermute | solution.py:30
  78.8 5.7 %all-to-all-start.2 = ((bf16[16,32,768]{2,1,0:T(8,128)(2,1)}), bf16[16,32,768]{2,1,0:T(8,128)(2,1)}, u32[]{:S(2)}, u32[]{:S(2)}) async-start(bf16[16,32,768]{2,1,0:T(8,128)(2,1)} %copy-done.9), calls=%async_computation.2 | async-start | bytes 1572864 | tf_op jit(solution)/shard_map/all_to_all | solution.py:742
  85.4 1.9 %collective-permute-start.8 = (bf16[384,768]{1,0:T(8,128)(2,1)}, bf16[384,768]{1,0:T(8,128)(2,1)}, u32[]{:S(2)}, u32[]{:S(2)}) collective-permute-start(bf16[384,768]{1,0:T(8,128)(2,1)} %slice.35), channel_id=1, source_target_pairs={{0,4},{4,0},{1,5},{5,1},{2,6},{6,2},{3,7},{7,3},{8,12},{12,8},{9,1... | collective-permute-start | bytes 1769480 | tf_op jit(solution)/shard_map/ppermute | solution.py:22
  87.2 1.5 collective-permute-start.9
  88.7 15.9 %all-to-all-done.2.blocks = bf16[16,32,768]{2,1,0:T(8,128)(2,1)} async-done(((bf16[16,32,768]{2,1,0:T(8,128)(2,1)}), bf16[16,32,768]{2,1,0:T(8,128)(2,1)}, u32[]{:S(2)}, u32[]{:S(2)}) %all-to-all-start.2) | async-done | bytes 786464 | tf_op jit(solution)/shard_map/all_to_all | solution.py:742
  104.6 1.9 %arrive.1 = (bf16[8,64,768]{2,1,0:T(8,128)(2,1)S(1)}, bf16[8,64,768]{2,1,0:T(8,128)(2,1)S(1)}) custom-call(bf16[16,32,768]{2,1,0:T(8,128)(2,1)} %all-to-all-done.2.blocks), custom_call_target="tpu_custom_call" | custom-call | tf_op jit(solution)/shard_map/arrive/pallas_call | solution.py:384
  106.5 2.1 %collective-permute-done.8.pair_rest = bf16[384,768]{1,0:T(8,128)(2,1)} collective-permute-done((bf16[384,768]{1,0:T(8,128)(2,1)}, bf16[384,768]{1,0:T(8,128)(2,1)}, u32[]{:S(2)}, u32[]{:S(2)}) %collective-permute-start.8) | collective-permute-done | bytes 589856 | tf_op jit(solution)/shard_map/ppermute | solution.py:22
  108.6 2.3 %collective-permute-done.10.other = bf16[8,64,768]{2,1,0:T(8,128)(2,1)S(1)} collective-permute-done((bf16[8,64,768]{2,1,0:T(8,128)(2,1)S(1)}, bf16[8,64,768]{2,1,0:T(8,128)(2,1)S(1)}, u32[]{:S(2)}, u32[]{:S(2)}) %collective-permute-start.10) | collective-permute-done | bytes 786464 | tf_op jit(solution)/shard_map/ppermute | solution.py:30
  114.0 6.0 %column.1 = (f32[8,64,768]{2,1,0:T(8,128)S(1)}, bf16[8,64,768]{2,1,0:T(8,128)(2,1)S(1)}) custom-call(s32[5]{0:T(128)S(1)} %stack.35.me_ref, s32[5]{0:T(128)S(1)} %convert_reduce_fusion.1.starts_ref, bf16[8,64,768]{2,1,0:T(8,128)(2,1)S(1)} %get-tuple-element.50.own, bf16[8,64,768]{2,1,0:T(8,128)(2,1)S(1)} %collective-permute-done.10.other, ...), custom_call_target="tpu_custom_call" | custom-call | tf_op jit(solution)/shard_map/column/pallas_call | solution.py:499
  120.2 2.1 %collective-permute-done.11 = bf16[8,64,768]{2,1,0:T(8,128)(2,1)S(1)} collective-permute-done((bf16[8,64,768]{2,1,0:T(8,128)(2,1)S(1)}, bf16[8,64,768]{2,1,0:T(8,128)(2,1)S(1)}, u32[]{:S(2)}, u32[]{:S(2)}) %collective-permute-start.11) | collective-permute-done | bytes 786464 | tf_op jit(solution)/shard_map/ppermute | solution.py:30
  123.6 2.1 %collective-permute-done.12 = bf16[8,64,768]{2,1,0:T(8,128)(2,1)S(1)} collective-permute-done((bf16[8,64,768]{2,1,0:T(8,128)(2,1)S(1)}, bf16[8,64,768]{2,1,0:T(8,128)(2,1)S(1)}, u32[]{:S(2)}, u32[]{:S(2)}) %collective-permute-start.12) | collective-permute-done | bytes 786464 | tf_op jit(solution)/shard_map/ppermute | solution.py:30
  125.8 5.6 %feed_forward.3 = bf16[512,768]{1,0:T(8,128)(2,1)S(1)} custom-call(s32[5]{0:T(128)S(1)} %stack.35.me_ref, bf16[512,768]{1,0:T(8,128)(2,1)S(1)} %bitcast.42, bf16[768,768]{1,0:T(8,128)(2,1)S(1)} %copy-done.2, bf16[768,768]{1,0:T(8,128)(2,1)S(1)} %copy-done, bf16[1152,768]{1,0:T(8,128)(2,1)S(1)} %collective-permute-done.3.piece, ...), custom_call_target="tpu_custom_call" | custom-call | tf_op jit(solution)/shard_map/feed_forward/pallas_call | solution.py:631
  131.5 5.4 %feed_forward.2 = f32[512,768]{1,0:T(8,128)S(1)} custom-call(s32[5]{0:T(128)S(1)} %stack.35.me_ref, bf16[512,768]{1,0:T(8,128)(2,1)S(1)} %bitcast.39, bf16[768,768]{1,0:T(8,128)(2,1)S(1)} %copy-done.2, bf16[768,768]{1,0:T(8,128)(2,1)S(1)} %copy-done, bf16[1152,768]{1,0:T(8,128)(2,1)S(1)} %collective-permute-done.3.piece, ...), custom_call_target="tpu_custom_call" | custom-call | tf_op jit(solution)/shard_map/feed_forward/pallas_call | solution.py:631
  138.1 24.6 %all_to_all.22 = bf16[32,96,128]{2,1,0:T(8,128)(2,1)S(1)} all-to-all(bf16[32,96,128]{2,1,0:T(8,128)(2,1)S(1)} %finish.1), channel_id=1, replica_groups=mesh['far'=2,'plane'=2,'pair'=2,'chip'=2,'core'=2] {'far','plane','pair'..., dimensions={0} | all-to-all | bytes 1572864 | tf_op jit(solution)/shard_map/all_to_all | solution.py:765
  (71 shorter events, 15.8 us)
Async XLA Ops:
  0.0 20.8 %collective-permute-start = (bf16[16,192,128]{2,1,0:T(8,128)(2,1)}, bf16[16,192,128]{2,1,0:T(8,128)(2,1)}, u32[]{:S(2)}, u32[]{:S(2)}) collective-permute-start(bf16[16,192,128]{2,1,0:T(8,128)(2,1)} %refs_0_.1), channel_id=1, source_target_pairs={{0,2},{2,0},{1,3},{3,1},{4,6},{6,4},{5,7},{7,5},{8,10},{10,8},{9,1... | collective-permute-start | bytes 2359304 | tf_op jit(solution)/shard_map/ppermute | solution.py:18
  2.9 17.9 %collective-permute-start.1 = (bf16[16,192,128]{2,1,0:T(8,128)(2,1)}, bf16[16,192,128]{2,1,0:T(8,128)(2,1)}, u32[]{:S(2)}, u32[]{:S(2)}) collective-permute-start(bf16[16,192,128]{2,1,0:T(8,128)(2,1)} %refs_0_.1), channel_id=1, source_target_pairs={{0,1},{1,0},{2,3},{3,2},{4,5},{5,4},{6,7},{7,6},{8,9},{9,8},{10,11... | collective-permute-start | bytes 2359304 | tf_op jit(solution)/shard_map/ppermute | solution.py:30
  2.9 3.2 %copy-start.6 = (bf16[3,192,768]{2,1,0:T(8,128)(2,1)S(1)}, bf16[3,192,768]{2,1,0:T(8,128)(2,1)}, u32[]{:S(2)}) copy-start(bf16[3,192,768]{2,1,0:T(8,128)(2,1)} %param.14) | copy-start | bytes 2654212
  2.9 3.2 %copy-start.10 = (bf16[192,768]{1,0:T(8,128)(2,1)S(1)}, bf16[192,768]{1,0:T(8,128)(2,1)}, u32[]{:S(2)}) copy-start(bf16[192,768]{1,0:T(8,128)(2,1)} %mixing.3) | copy-start | bytes 884740
  7.3 2.6 %copy-start.15 = (s32[128]{0:T(128)S(1)}, s32[128]{0:T(128)}, u32[]{:S(2)}) copy-start(s32[128]{0:T(128)} %label_ref.5) | copy-start | bytes 1540
  7.3 4.5 %copy-start.12 = (bf16[192,768]{1,0:T(8,128)(2,1)S(1)}, bf16[192,768]{1,0:T(8,128)(2,1)}, u32[]{:S(2)}) copy-start(bf16[192,768]{1,0:T(8,128)(2,1)} %mixing.2) | copy-start | bytes 884740
  7.3 6.9 %copy-start = (bf16[768,768]{1,0:T(8,128)(2,1)S(1)}, bf16[768,768]{1,0:T(8,128)(2,1)}, u32[]{:S(2)}) copy-start(bf16[768,768]{1,0:T(8,128)(2,1)} %contract.3) | copy-start | bytes 3538948
  7.3 6.9 %copy-start.1 = (bf16[768,768]{1,0:T(8,128)(2,1)S(1)}, bf16[768,768]{1,0:T(8,128)(2,1)}, u32[]{:S(2)}) copy-start(bf16[768,768]{1,0:T(8,128)(2,1)} %expand.3) | copy-start | bytes 3538948
  14.2 1.5 copy-start.17
  15.7 9.3 %copy-start.8 = (bf16[16,192,128]{2,1,0:T(8,128)(2,1)S(1)}, bf16[16,192,128]{2,1,0:T(8,128)(2,1)}, u32[]{:S(2)}) copy-start(bf16[16,192,128]{2,1,0:T(8,128)(2,1)} %refs_0_.1) | copy-start | bytes 2359300
  15.7 9.3 %copy-start.14 = (bf16[3,192,768]{2,1,0:T(8,128)(2,1)S(1)}, bf16[3,192,768]{2,1,0:T(8,128)(2,1)}, u32[]{:S(2)}) copy-start(bf16[3,192,768]{2,1,0:T(8,128)(2,1)} %param.12) | copy-start | bytes 2654212
  15.7 9.3 %copy-start.16 = (s32[4]{0:T(128)S(1)}, s32[4]{0:T(128)}, u32[]{:S(2)}) copy-start(s32[4]{0:T(128)} %tally_ref.5) | copy-start | bytes 52
  20.8 39.8 %collective-permute-start.3 = (bf16[1152,768]{1,0:T(8,128)(2,1)S(1)}, bf16[1152,768]{1,0:T(8,128)(2,1)S(1)}, u32[]{:S(2)}, u32[]{:S(2)}) collective-permute-start(bf16[1152,768]{1,0:T(8,128)(2,1)S(1)} %fusion.7), channel_id=1, source_target_pairs={{0,2},{2,0},{1,3},{3,1},{4,6},{6,4},{5,7},{7,5},{8,10},{10,8},{9,1... | collective-permute-start | bytes 5308424 | tf_op jit(solution)/shard_map/ppermute | solution.py:18
  22.5 2.5 %collective-permute-start.2 = (bf16[16,192,128]{2,1,0:T(8,128)(2,1)}, bf16[16,192,128]{2,1,0:T(8,128)(2,1)S(1)}, u32[]{:S(2)}, u32[]{:S(2)}) collective-permute-start(bf16[16,192,128]{2,1,0:T(8,128)(2,1)} %collective-permute-done.far.refs_2_), channel_id=1, source_target_pairs={{0,1},{1,0},{2,3},{3,2},{4,5},{5,4},{6,7},{7,6},{8,9},{9,8},{10,11... | collective-permute-start | bytes 2359304 | tf_op jit(solution)/shard_map/ppermute | solution.py:30
  58.1 14.9 %copy-start.13 = (bf16[192,768]{1,0:T(8,128)(2,1)S(1)}, bf16[192,768]{1,0:T(8,128)(2,1)}, u32[]{:S(2)}) copy-start(bf16[192,768]{1,0:T(8,128)(2,1)} %mixing.2) | copy-start | bytes 884740
  60.7 11.6 %collective-permute-start.5 = (bf16[288,768]{1,0:T(8,128)(2,1)S(1)}, bf16[288,768]{1,0:T(8,128)(2,1)S(1)}, u32[]{:S(2)}, u32[]{:S(2)}) collective-permute-start(bf16[288,768]{1,0:T(8,128)(2,1)S(1)} %get-tuple-element.60), channel_id=1, source_target_pairs={{0,4},{4,0},{1,5},{5,1},{2,6},{6,2},{3,7},{7,3},{8,12},{12,8},{9,1... | collective-permute-start | bytes 1327112 | tf_op jit(solution)/shard_map/ppermute | solution.py:22
  62.2 10.1 %collective-permute-start.6 = (bf16[288,768]{1,0:T(8,128)(2,1)S(1)}, bf16[288,768]{1,0:T(8,128)(2,1)S(1)}, u32[]{:S(2)}, u32[]{:S(2)}) collective-permute-start(bf16[288,768]{1,0:T(8,128)(2,1)S(1)} %get-tuple-element.59), channel_id=1, source_target_pairs={{0,8},{8,0},{1,9},{9,1},{2,10},{10,2},{3,11},{11,3},{4,12},{12,4},... | collective-permute-start | bytes 1327112 | tf_op jit(solution)/shard_map/ppermute | solution.py:26
  63.7 8.5 %collective-permute-start.4 = (bf16[8,192,128]{2,1,0:T(8,128)(2,1)S(1)}, bf16[8,192,128]{2,1,0:T(8,128)(2,1)S(1)}, u32[]{:S(2)}, u32[]{:S(2)}) collective-permute-start(bf16[8,192,128]{2,1,0:T(8,128)(2,1)S(1)} %get-tuple-element.42), channel_id=1, source_target_pairs={{0,2},{2,0},{1,3},{3,1},{4,6},{6,4},{5,7},{7,5},{8,10},{10,8},{9,1... | collective-permute-start | bytes 1179656 | tf_op jit(solution)/shard_map/ppermute | solution.py:18
  75.4 2.4 %collective-permute-start.7 = (bf16[4,128,768]{2,1,0:T(8,128)(2,1)S(1)}, bf16[4,128,768]{2,1,0:T(8,128)(2,1)S(1)}, u32[]{:S(2)}, u32[]{:S(2)}) collective-permute-start(bf16[4,128,768]{2,1,0:T(8,128)(2,1)S(1)} %get-tuple-element.46), channel_id=1, source_target_pairs={{0,1},{1,0},{2,3},{3,2},{4,5},{5,4},{6,7},{7,6},{8,9},{9,8},{10,11... | collective-permute-start | bytes 2359304 | tf_op jit(solution)/shard_map/ppermute | solution.py:30
  77.9 0.9 copy-start.9
  78.8 25.8 %all-to-all-start.2 = ((bf16[16,32,768]{2,1,0:T(8,128)(2,1)}), bf16[16,32,768]{2,1,0:T(8,128)(2,1)}, u32[]{:S(2)}, u32[]{:S(2)}) async-start(bf16[16,32,768]{2,1,0:T(8,128)(2,1)} %copy-done.9), calls=%async_computation.2 | async-start | bytes 1572864 | tf_op jit(solution)/shard_map/all_to_all | solution.py:742
  85.4 23.2 %collective-permute-start.8 = (bf16[384,768]{1,0:T(8,128)(2,1)}, bf16[384,768]{1,0:T(8,128)(2,1)}, u32[]{:S(2)}, u32[]{:S(2)}) collective-permute-start(bf16[384,768]{1,0:T(8,128)(2,1)} %slice.35), channel_id=1, source_target_pairs={{0,4},{4,0},{1,5},{5,1},{2,6},{6,2},{3,7},{7,3},{8,12},{12,8},{9,1... | collective-permute-start | bytes 1769480 | tf_op jit(solution)/shard_map/ppermute | solution.py:22
  87.2 21.3 %collective-permute-start.9 = (bf16[384,768]{1,0:T(8,128)(2,1)}, bf16[384,768]{1,0:T(8,128)(2,1)}, u32[]{:S(2)}, u32[]{:S(2)}) collective-permute-start(bf16[384,768]{1,0:T(8,128)(2,1)} %bitcast.46), channel_id=1, source_target_pairs={{0,2},{2,0},{1,3},{3,1},{4,6},{6,4},{5,7},{7,5},{8,10},{10,8},{9,1... | collective-permute-start | bytes 1769480 | tf_op jit(solution)/shard_map/ppermute | solution.py:18
  108.6 2.3 %collective-permute-start.10 = (bf16[8,64,768]{2,1,0:T(8,128)(2,1)S(1)}, bf16[8,64,768]{2,1,0:T(8,128)(2,1)S(1)}, u32[]{:S(2)}, u32[]{:S(2)}) collective-permute-start(bf16[8,64,768]{2,1,0:T(8,128)(2,1)S(1)} %get-tuple-element.50.own), channel_id=1, source_target_pairs={{0,1},{1,0},{2,3},{3,2},{4,5},{5,4},{6,7},{7,6},{8,9},{9,8},{10,11... | collective-permute-start | bytes 2359304 | tf_op jit(solution)/shard_map/ppermute | solution.py:30
  110.9 1.0 copy-start.4
  111.9 1.2 copy-start.7
  113.0 1.0 copy-start.11
  120.0 2.4 %collective-permute-start.11 = (bf16[8,64,768]{2,1,0:T(8,128)(2,1)S(1)}, bf16[8,64,768]{2,1,0:T(8,128)(2,1)S(1)}, u32[]{:S(2)}, u32[]{:S(2)}) collective-permute-start(bf16[8,64,768]{2,1,0:T(8,128)(2,1)S(1)} %get-tuple-element.54), channel_id=1, source_target_pairs={{0,1},{1,0},{2,3},{3,2},{4,5},{5,4},{6,7},{7,6},{8,9},{9,8},{10,11... | collective-permute-start | bytes 2359304 | tf_op jit(solution)/shard_map/ppermute | solution.py:30
  122.7 3.0 %copy-start.2 = (bf16[768,768]{1,0:T(8,128)(2,1)S(1)}, bf16[768,768]{1,0:T(8,128)(2,1)}, u32[]{:S(2)}) copy-start(bf16[768,768]{1,0:T(8,128)(2,1)} %expand.3) | copy-start | bytes 3538948
  122.7 3.0 %copy-start.5 = (bf16[288,768]{1,0:T(8,128)(2,1)S(1)}, bf16[288,768]{1,0:T(8,128)(2,1)}, u32[]{:S(2)}) copy-start(bf16[288,768]{1,0:T(8,128)(2,1)} %copy-done.3) | copy-start | bytes 1327108
  123.4 2.4 %collective-permute-start.12 = (bf16[8,64,768]{2,1,0:T(8,128)(2,1)S(1)}, bf16[8,64,768]{2,1,0:T(8,128)(2,1)S(1)}, u32[]{:S(2)}, u32[]{:S(2)}) collective-permute-start(bf16[8,64,768]{2,1,0:T(8,128)(2,1)S(1)} %fusion.3), channel_id=1, source_target_pairs={{0,1},{1,0},{2,3},{3,2},{4,5},{5,4},{6,7},{7,6},{8,9},{9,8},{10,11... | collective-permute-start | bytes 2359304 | tf_op jit(solution)/shard_map/ppermute | solution.py:30
  131.3 5.6 %collective-permute-start.13 = (bf16[8,64,768]{2,1,0:T(8,128)(2,1)S(1)}, bf16[8,64,768]{2,1,0:T(8,128)(2,1)S(1)}, u32[]{:S(2)}, u32[]{:S(2)}) collective-permute-start(bf16[8,64,768]{2,1,0:T(8,128)(2,1)S(1)} %bitcast.41), channel_id=1, source_target_pairs={{0,1},{1,0},{2,3},{3,2},{4,5},{5,4},{6,7},{7,6},{8,9},{9,8},{10,11... | collective-permute-start | bytes 2359304 | tf_op jit(solution)/shard_map/ppermute | solution.py:30
  (1 other events, 0.8 us)

commit v4 on v3

--- a/solution.py
+++ b/solution.py
@@ -9,7 +9,7 @@
 
 HEAD_SIZE = 64
 SWAP = [(0, 1), (1, 0)]
-ROWS = ("far", "plane", "pair")
+ROWS = ("plane", "pair")
 BF16 = jnp.bfloat16
 F32 = jnp.float32
 
@@ -20,10 +20,6 @@
 
 def other_pair(value):
     return lax.ppermute(value, "pair", SWAP)
-
-
-def other_plane(value):
-    return lax.ppermute(value, "plane", SWAP)
 
 
 def other_core(value):
@@ -74,6 +70,94 @@
     return (
         2 * chip + core, 2 * chip + 1 - core, 2 * (1 - chip) + core, 2 * (1 - chip) + 1 - core
     )
+
+
+def pack_kernel(me_ref, mixing, triple, vertical, expand, contract, pack, late, semaphores):
+    quarter = mixing.shape[0]
+    half, pair = 2 * quarter, me_ref[3]
+
+    def move(index, source, start, count, target, place):
+        return pltpu.make_async_copy(
+            source.at[pl.ds(start, count)], target.at[pl.ds(place, count)], semaphores.at[index]
+        )
+
+    fixed = [
+        move(0, mixing, 0, quarter, pack, 2 * half),
+        move(1, expand, half, half, late, 0),
+        move(2, contract, half, half, late, half),
+    ]
+    options = (
+        [
+            move(3, expand, 0, half, pack, 0),
+            move(4, triple, 0, quarter, pack, half),
+            move(5, triple, quarter, quarter, pack, half + quarter),
+        ],
+        [
+            move(3, contract, 0, half, pack, 0),
+            move(4, triple, half, quarter, pack, half),
+            move(5, vertical, 0, quarter, pack, half + quarter),
+        ],
+    )
+    for copy in fixed:
+        copy.start()
+    for index, copies in enumerate(options):
+
+        @pl.when(pair == index)
+        def _(copies=copies):
+            for copy in copies:
+                copy.start()
+
+    for copy in fixed + options[0]:
+        copy.wait()
+
+
+def pack_weights(me, mixing, triple, vertical, expand, contract):
+    quarter, model = mixing.shape
+    return pl.pallas_call(
+        pack_kernel,
+        out_shape=(
+            jax.ShapeDtypeStruct((5 * quarter, model), BF16),
+            jax.ShapeDtypeStruct((4 * quarter, model), BF16),
+        ),
+        in_specs=[IN_SMEM] + [IN_HBM] * 5,
+        out_specs=(IN_HBM, IN_HBM),
+        scratch_shapes=[pltpu.SemaphoreType.DMA((6,))],
+        compiler_params=GRANT,
+        name="pack",
+    )(me, mixing, triple.reshape(-1, model), vertical, expand, contract)
+
+
+def spread_kernel(stream, out):
+    lines, quarter, sites = stream.shape
+    chips = out.shape[0] // 2
+    place, own = sites // chips, lines // 2
+    wide = out.shape[2]
+    for core in range(2):
+        values = [stream[core * own + line].astype(F32).T for line in range(own)]
+        values = [value.reshape(chips, place, quarter) for value in values]
+        values = jnp.concatenate(values, axis=1)
+        parts = own * place // 2
+        narrow = jnp.concatenate([values[:, :parts, wide:], values[:, parts:, wide:]], axis=2)
+        values = jnp.concatenate([values[:, :, :wide], narrow], axis=1).astype(BF16)
+        for chip in range(chips):
+            out[2 * chip + core] = values[chip]
+
+
+def spread(stream, chips):
+    lines, quarter, sites = stream.shape
+    place, own = sites // chips, lines // 2
+    if place % 8 == 0:
+        shape = (2 * chips, 3 * own * place // 2, quarter // 3 * 2)
+        return pl.pallas_call(
+            spread_kernel,
+            out_shape=jax.ShapeDtypeStruct(shape, BF16),
+            in_specs=[IN_VMEM],
+            out_specs=IN_VMEM,
+            compiler_params=GRANT,
+            name="spread",
+        )(stream)
+    stream = jnp.transpose(stream.reshape(2, own, quarter, chips, place), (3, 0, 1, 4, 2))
+    return stream.reshape(2 * chips, own * place, quarter)
 
 
 def row_front_kernel(
@@ -220,201 +304,202 @@
     return masked_softmax(totals, tally)[ends].reshape(groups, pairs, rows, sites)
 
 
-def mix_kernel(
-    me_ref, label_ref, starts_ref, tally_ref, shared, inner, values, kept, sent, weights
-):
+def mix_kernel(me_ref, label_ref, starts_ref, tally_ref, shared, inner, values, out, weights):
     heads, sites = shared.shape[1] // 2, values.shape[2]
-    half = kept.shape[0]
+    lines, chips = values.shape[0], out.shape[0]
+    place = sites // chips
     for index in range(2 * heads):
         weights[index] = shared[:, index].reshape(sites, sites)
     weights[2 * heads :] = inner[...]
-    for target, chip in ((sent, 1 - me_ref[1]), (kept, me_ref[1])):
-        jobs = []
-        for line in range(half):
-            row = chip * half + line
-            slot = slot_of(label_ref, me_ref[0] * 2 * half, 2 * half, row)
-            value = values[row]
-            for head in range(heads):
-                features = slice(head * HEAD_SIZE, (head + 1) * HEAD_SIZE)
-                result = lax.dot_general(
-                    value[features],
+    mixed = []
+    for line in range(lines):
+        slot = slot_of(label_ref, me_ref[0] * lines, lines, line)
+        value = values[line]
+        mixed.append(
+            [
+                lax.dot_general(
                     weights[slot * heads + head],
+                    value[head * HEAD_SIZE : (head + 1) * HEAD_SIZE],
                     CONTRACT_LAST,
                     preferred_element_type=F32,
                 )
-                jobs.append((line, features, result))
-        for line, features, result in jobs:
-            target[line, features] = result.astype(BF16)
-
-
-def mix(shared, inner, values, plan):
+                for head in range(heads)
+            ]
+        )
+    pairs = [(part[0], part[1]) for part in mixed]
+    pairs += [(mixed[line][2], mixed[line + lines // 2][2]) for line in range(lines // 2)]
+    for index in range(0, len(pairs), 2):
+        block = [
+            jnp.concatenate(pair, axis=1).reshape(chips, place, 2 * HEAD_SIZE)
+            for pair in pairs[index : index + 2]
+        ]
+        out[:, index * place : (index + 2) * place] = jnp.concatenate(block, axis=1).astype(BF16)
+
+
+def mix(shared, inner, values, plan, chips):
     groups, pairs, rows, sites = shared.shape
     lines, quarter, _ = values.shape
-    if rows % 16 == 0:
-        half = jax.ShapeDtypeStruct((lines // 2, quarter, sites), BF16)
+    place = sites // chips
+    if rows % 16 == 0 and place % 8 == 0:
+        shape = (chips, 3 * lines * place // 2, 2 * HEAD_SIZE)
         return pl.pallas_call(
             mix_kernel,
-            out_shape=(half, half),
+            out_shape=jax.ShapeDtypeStruct(shape, BF16),
             in_specs=[IN_SMEM] * 4 + [IN_VMEM] * 3,
-            out_specs=(IN_VMEM, IN_VMEM),
+            out_specs=IN_VMEM,
             scratch_shapes=[pltpu.VMEM((pairs + inner.shape[0], sites, sites), BF16)],
             compiler_params=GRANT,
             name="mix",
         )(*plan, shared, inner, values)
     me, label = plan[:2]
-    chip = me[1]
     label = lax.dynamic_slice_in_dim(label, me[0] * lines, lines)
     slot = slot_of(label, 0, lines, jnp.arange(lines))
     ends = jnp.transpose(shared, (1, 0, 2, 3)).reshape(2, pairs // 2, sites, sites)
     weights = jnp.concatenate([ends, inner.reshape(-1, *ends.shape[1:])])[slot]
     values = values.reshape(lines, -1, HEAD_SIZE, sites)
-    mixed = jnp.einsum("rhdj,rhij->rhdi", values, weights, preferred_element_type=F32)
-    mixed = mixed.astype(BF16).reshape(lines, quarter, sites)
-    return half_rows(mixed, chip), half_rows(mixed, 1 - chip)
-
-
-def project_kernel(
-    me_ref, mixed, got, mixing, piece, *refs
-):
-    pieces = refs[:4]
-    kept, sent, stream, far, semaphores = refs[4:]
-    lines, _, sites = stream.shape
-    quarter = mixing.shape[0]
+    mixed = jnp.einsum("rhdj,rhij->rihd", values, weights, preferred_element_type=F32)
+    mixed = mixed.astype(BF16).reshape(lines, chips, place, quarter)
+    return jnp.transpose(mixed, (1, 0, 2, 3)).reshape(chips, lines * place, quarter)
+
+
+def project_kernel(me_ref, blocks, mixing, piece, kept, sent, wide, first, second, semaphores):
+    chips, count, lanes = blocks.shape
+    quarter, model = mixing.shape
+    tokens = count * 2 // 3
+    groups, own = chips // 2, tokens // 2
     chip, core = me_ref[1], me_ref[2]
+    start = piece.shape[0] - quarter
+    tail = quarter - lanes
+    first[...] = jnp.zeros_like(first)
+    second[...] = jnp.zeros_like(second)
     copies = []
-    for index, (spot, source) in enumerate(zip(quarter_spots(me_ref), pieces)):
-        spot = pl.multiple_of(spot * quarter, quarter)
-        copies.append(
-            pltpu.make_async_copy(
-                source.at[pl.ds((2 * chip + core) * lines, lines)],
-                stream.at[:, pl.ds(spot, quarter)],
-                semaphores.at[index],
+    for index, (source, place, side) in enumerate(((mixing, 0, chip), (piece, start, 1 - chip))):
+        spot = pl.multiple_of(side * lanes, lanes)
+        end = source.at[pl.ds(place + lanes, tail)]
+        moves = (
+            (source.at[pl.ds(place, lanes)], wide.at[pl.ds(spot, lanes)]),
+            (end, first.at[pl.ds(spot, tail)]),
+            (end, second.at[pl.ds(pl.multiple_of(spot + tail, tail), tail)]),
+        )
+        for number, (origin, target) in enumerate(moves):
+            copies.append(
+                pltpu.make_async_copy(origin, target, semaphores.at[3 * index + number])
             )
-        )
     for copy in copies:
         copy.start()
-    fetch = pltpu.make_async_copy(piece.at[pl.ds(7 * quarter // 2, quarter)], far, semaphores.at[4])
-    fetch.start()
-
-    def partial(row):
-        near_part = lax.dot_general(
-            mixed[row], mixing[...], CONTRACT_FIRST, preferred_element_type=F32
-        )
-        return near_part + lax.dot_general(
-            got[row], far[...], CONTRACT_FIRST, preferred_element_type=F32
-        )
-
-    fetch.wait()
-    for line in range(lines):
-        sent[line] = partial((1 - core) * lines + line).astype(BF16)
+    values = blocks[...].reshape(groups, 2, count, lanes)
+    values = jnp.concatenate([values[:, 0], values[:, 1]], axis=-1)
+    whole = values[:, :tokens].reshape(groups * tokens, 2 * lanes)
+    narrow = values[:, tokens:].reshape(groups * own, 2 * lanes)
     for copy in copies:
         copy.wait()
-    for line in range(lines):
-        kept[line] = partial(core * lines + line) + stream[line].astype(F32).T
-
-
-def project(mixed, got, mixing, piece, pieces, me):
-    half, quarter, sites = mixed.shape
-    lines, model = half // 2, mixing.shape[1]
-    out = (lines, sites, model)
-    return pl.pallas_call(
-        project_kernel,
-        out_shape=(jax.ShapeDtypeStruct(out, F32), jax.ShapeDtypeStruct(out, BF16)),
-        in_specs=[IN_SMEM] + [IN_VMEM] * 3 + [IN_HBM] * 5,
-        out_specs=(IN_VMEM, IN_VMEM),
-        scratch_shapes=[
-            pltpu.VMEM((lines, model, sites), BF16),
-            pltpu.VMEM((quarter, model), BF16),
-            pltpu.SemaphoreType.DMA((5,)),
-        ],
-        compiler_params=GRANT,
-        name="project",
-    )(me, mixed, got, mixing, piece, *pieces)
-
-
-def settle_kernel(kept, got, out):
-    lines, sites, model = kept.shape
-    chips = out.shape[0]
-    parts = []
-    for line in range(lines):
-        total = kept[line] + got[line].astype(F32)
-        parts.append(total.reshape(chips, sites // chips, model))
-    out[...] = jnp.concatenate(parts, axis=1).astype(BF16)
-
-
-def settle(kept, got, chips):
-    lines, sites, model = kept.shape
-    place = sites // chips
-    if place % 8 == 0:
+    total = jnp.dot(whole, wide[...], preferred_element_type=F32)
+    total = total.reshape(groups, tokens, model)
+    ends = [
+        jnp.dot(narrow, weights[...], preferred_element_type=F32).reshape(groups, own, model)
+        for weights in (first, second)
+    ]
+    halves = [total[:, :own] + ends[0], total[:, own:] + ends[1]]
+    for index in range(2):
+
+        @pl.when(core == index)
+        def _(index=index):
+            kept[...] = halves[index]
+            sent[...] = halves[1 - index].astype(BF16)
+
+
+def project(blocks, mixing, piece, me, lines):
+    chips, count, lanes = blocks.shape
+    quarter, model = mixing.shape
+    groups = chips // 2
+    if lanes != quarter:
+        out = (groups, count // 3, model)
         return pl.pallas_call(
-            settle_kernel,
-            out_shape=jax.ShapeDtypeStruct((chips, lines * place, model), BF16),
-            in_specs=[IN_VMEM, IN_VMEM],
-            out_specs=IN_VMEM,
+            project_kernel,
+            out_shape=(jax.ShapeDtypeStruct(out, F32), jax.ShapeDtypeStruct(out, BF16)),
+            in_specs=[IN_SMEM, IN_VMEM, IN_HBM, IN_HBM],
+            out_specs=(IN_VMEM, IN_VMEM),
+            scratch_shapes=[pltpu.VMEM((2 * lanes, model), BF16)] * 3
+            + [pltpu.SemaphoreType.DMA((6,))],
             compiler_params=GRANT,
-            name="settle",
-        )(kept, got)
-    total = (kept + got.astype(F32)).astype(BF16).reshape(lines, chips, place, model)
-    return jnp.transpose(total, (1, 0, 2, 3)).reshape(chips, lines * place, model)
-
-
-def arrive_kernel(blocks, normed, stream, tokens):
-    chips, count, model = blocks.shape
+            name="project",
+        )(me, blocks, mixing, piece)
+    weights = in_order(mixing[None], piece[None, -quarter:], me[1], 0)
+    values = blocks.reshape(groups, 2, 2, count // 2, quarter)
+    partial = jnp.einsum("gxctd,xde->cgte", values, weights, preferred_element_type=F32)
+    kept = lax.dynamic_index_in_dim(partial, me[2], 0, False)
+    sent = lax.dynamic_index_in_dim(partial, 1 - me[2], 0, False)
+    return kept, sent.astype(BF16)
+
+
+def arrive_kernel(kept, got, blocks, normed, stream, tokens):
+    groups, own, model = kept.shape
     places, rows, _ = normed.shape
-    lanes = tokens.shape[-1]
-    flat = blocks[...].reshape(chips * count, model).astype(F32)
-    for index in range(tokens.shape[0]):
-        tokens[index] = flat[:, index * lanes : (index + 1) * lanes]
+    count, lanes = blocks.shape[1], blocks.shape[2]
+    heads = blocks.shape[0] // groups
+    parts = count // 3
+    total = kept[...] + got[...].astype(F32)
+    for group in range(groups):
+        features = []
+        for head in range(heads):
+            block = blocks[group * heads + head].astype(F32)
+            narrow = block[2 * parts :]
+            narrow = jnp.concatenate([narrow[:, : lanes // 2], narrow[:, lanes // 2 :]], axis=0)
+            features += [block[: 2 * parts], narrow]
+        values = total[group] + jnp.concatenate(features, axis=1)
+        for index in range(tokens.shape[0]):
+            lower = index * tokens.shape[2]
+            part = values[:, lower : lower + tokens.shape[2]]
+            tokens[index, group * own : (group + 1) * own] = part
     for place in range(places):
         values = [
             tokens[index, pl.ds(place, rows, stride=places), :] for index in range(tokens.shape[0])
         ]
-        values = jnp.concatenate(values, axis=-1)
-        stream[place] = values.astype(BF16)
+        values = jnp.concatenate(values, axis=-1).astype(BF16)
+        stream[place] = values
+        values = values.astype(F32)
         centred = values - jnp.mean(values, axis=-1, keepdims=True)
         variance = jnp.mean(centred * centred, axis=-1, keepdims=True)
         normed[place] = (centred * lax.rsqrt(variance + 1e-05)).astype(BF16)
 
 
-def arrive(blocks, place):
-    chips, count, model = blocks.shape
-    rows = chips * count // place
+def arrive(kept, got, blocks, place):
+    groups, own, model = kept.shape
+    rows = groups * own // place
     if place % 8 == 0:
         shape = jax.ShapeDtypeStruct((place, rows, model), BF16)
         return pl.pallas_call(
             arrive_kernel,
             out_shape=(shape, shape),
-            in_specs=[IN_VMEM],
+            in_specs=[IN_VMEM] * 3,
             out_specs=(IN_VMEM, IN_VMEM),
-            scratch_shapes=[pltpu.VMEM((model // 128, chips * count, 128), F32)],
+            scratch_shapes=[pltpu.VMEM((model // 128, groups * own, 128), F32)],
             compiler_params=GRANT,
             name="arrive",
-        )(blocks)
-    stream = jnp.transpose(blocks.reshape(rows, place, model), (1, 0, 2))
+        )(kept, got, blocks)
+    heads = blocks.shape[0] // groups
+    stream = jnp.transpose(blocks.reshape(groups, heads, own, -1), (0, 2, 1, 3))
+    stream = stream.reshape(groups, own, model).astype(F32) + kept + got.astype(F32)
+    stream = jnp.transpose(stream.reshape(rows, place, model), (1, 0, 2)).astype(BF16)
     return own_norm(stream, -1), stream
 
 
 def column_kernel(
-    lines, me_ref, starts_ref, own, other, triple, mixing, piece, pair_rest, plane_rest,
+    lines, me_ref, starts_ref, own, other, triple, mixing, piece, rest,
     kept, sent, normed, near, far, projected, mixed, semaphores,
 ):
     quarter = mixing.shape[0]
-    eighth = quarter // 2
-    core, pair, plane = me_ref[2], me_ref[3], me_ref[4]
-
-    def rows_of(ref, start):
-        return ref.at[pl.ds(start, quarter)]
+    core, pair = me_ref[2], me_ref[3]
+    half = rest.shape[0] // 2
 
     def spot(index):
-        return pl.multiple_of(index * quarter, quarter)
+        return far.at[pl.ds(pl.multiple_of(index * half, half), half)]
 
     moves = (
         (triple, near.at[pl.ds(0, 3 * quarter)]),
         (mixing, near.at[pl.ds(3 * quarter, quarter)]),
-        (rows_of(piece, 5 * eighth), rows_of(far, spot(pair))),
-        (rows_of(piece, 9 * eighth), rows_of(far, spot(2 + plane))),
-        (rows_of(pair_rest, eighth), rows_of(far, spot(1 - pair))),
-        (rows_of(plane_rest, 0), rows_of(far, spot(3 - plane))),
+        (piece.at[pl.ds(half, half)], spot(pair)),
+        (rest.at[pl.ds(half, half)], spot(1 - pair)),
     )
     copies = [
         pltpu.make_async_copy(source, target, semaphores.at[index])
@@ -492,7 +577,7 @@
         sent[place] = partial[rows:].astype(BF16)
 
 
-def column(own, other, triple, mixing, piece, pair_rest, plane_rest, plan, lines):
+def column(own, other, triple, mixing, piece, rest, plan, lines):
     places, rows, model = own.shape
     quarter = mixing.shape[0]
     tokens = 2 * places * rows
@@ -502,7 +587,7 @@
             jax.ShapeDtypeStruct(own.shape, F32),
             jax.ShapeDtypeStruct(own.shape, BF16),
         ),
-        in_specs=[IN_SMEM] * 2 + [IN_VMEM] * 2 + [IN_HBM] * 5,
+        in_specs=[IN_SMEM] * 2 + [IN_VMEM] * 2 + [IN_HBM] * 4,
         out_specs=(IN_VMEM, IN_VMEM),
         scratch_shapes=[
             pltpu.VMEM((places, 2 * rows, model), BF16),
@@ -510,11 +595,11 @@
             pltpu.VMEM((4 * quarter, model), BF16),
             pltpu.VMEM((3 * quarter, tokens), BF16),
             pltpu.VMEM((2 * quarter, tokens), BF16),
-            pltpu.SemaphoreType.DMA((6,)),
+            pltpu.SemaphoreType.DMA((4,)),
         ],
         compiler_params=GRANT,
         name="column",
-    )(plan[0], plan[2], own, other, triple.reshape(-1, model), mixing, piece, pair_rest, plane_rest)
+    )(plan[0], plan[2], own, other, triple.reshape(-1, model), mixing, piece, rest)
 
 
 def finish_kernel(stream, kept, got, out):
@@ -557,53 +642,41 @@
 
 
 def feed_forward_kernel(
-    me_ref, normed, expand, contract, piece, pair_rest, column_rest, plane_rest, late, out,
+    me_ref, normed, expand, contract, piece, rest, late, out,
     near_expand, near_contract, far_expand, far_contract, hidden, semaphores,
 ):
     width = near_expand.shape[1]
-    quarter = late.shape[0] // 2
-    pair, plane = me_ref[3], me_ref[4]
-    eighth = quarter // 2
+    half, pair = rest.shape[0] // 2, me_ref[3]
 
     def move(source, start, count, target, place, index):
         return pltpu.make_async_copy(
             source.at[pl.ds(start, count)], target.at[pl.ds(place, count)], semaphores.at[index]
         )
 
-    def own_weights():
+    def shared(first, second):
         return [
-            move(expand, 0, width, near_expand, 0, 0),
-            move(contract, 0, width, near_contract, 0, 1),
-            move(late, 0, quarter, far_expand, 3 * quarter, 2),
-            move(late, quarter, quarter, far_contract, 3 * quarter, 3),
+            move(piece, 0, half, first, 0, 4),
+            move(rest, 0, half, second, 0, 5),
         ]
 
-    def by_pair(first, second):
-        return [
-            move(piece, 0, 5 * eighth, first, 0, 4),
-            move(pair_rest, 0, 4 * eighth, second, 0, 5),
-            move(column_rest, 0, eighth, second, 4 * eighth, 8),
-        ]
-
-    def by_plane(first, second):
-        return [
-            move(piece, 11 * eighth, eighth, first, 5 * eighth, 6),
-            move(plane_rest, 2 * eighth, eighth, second, 5 * eighth, 7),
-        ]
-
-    for copy in own_weights():
+    copies = [
+        move(expand, 0, width, near_expand, 0, 0),
+        move(contract, 0, width, near_contract, 0, 1),
+        move(late, 0, half, far_expand, half, 2),
+        move(late, half, half, far_contract, half, 3),
+    ]
+    for copy in copies:
         copy.start()
-    for index, moves in ((pair, by_pair), (plane, by_plane)):
-
-        @pl.when(index == 0)
-        def _(moves=moves):
-            for copy in moves(far_expand, far_contract):
-                copy.start()
-
-        @pl.when(index != 0)
-        def _(moves=moves):
-            for copy in moves(far_contract, far_expand):
-                copy.start()
+
+    @pl.when(pair == 0)
+    def _():
+        for copy in shared(far_expand, far_contract):
+            copy.start()
+
+    @pl.when(pair != 0)
+    def _():
+        for copy in shared(far_contract, far_expand):
+            copy.start()
 
     tile = width // 3
     values = normed[...]
@@ -614,7 +687,7 @@
             up = 0.5 * up * (1.0 + lax.erf(up * 2.0**-0.5))
             hidden[:, lower + start : lower + start + tile] = up.astype(BF16)
 
-    copies = own_weights() + by_pair(far_expand, far_contract) + by_plane(far_expand, far_contract)
+    copies += shared(far_expand, far_contract)
     copies[0].wait()
     raise_by(near_expand, 0)
     for copy in copies[1:]:
@@ -631,7 +704,7 @@
     result = pl.pallas_call(
         feed_forward_kernel,
         out_shape=jax.ShapeDtypeStruct((tokens, model), kind),
-        in_specs=[IN_SMEM, IN_VMEM] + [IN_HBM] * 7,
+        in_specs=[IN_SMEM, IN_VMEM] + [IN_HBM] * 5,
         out_specs=IN_VMEM,
         scratch_shapes=[
             pltpu.VMEM((model, width), BF16),
@@ -639,7 +712,7 @@
             pltpu.VMEM((model, width), BF16),
             pltpu.VMEM((model, width), BF16),
             pltpu.VMEM((tokens, 2 * width), BF16),
-            pltpu.SemaphoreType.DMA((9,)),
+            pltpu.SemaphoreType.DMA((6,)),
         ],
         compiler_params=GRANT,
         name="feed_forward",
@@ -664,117 +737,88 @@
 ):
     lines, quarter, sites = alignment_embedding.shape
     row_groups = lax.axis_size(ROWS)
-    own = lines // 4
+    own = lines // 2
     chips = 2 * row_groups
     place = sites // chips
     pair = lax.axis_index("pair")
     chip = lax.axis_index("chip")
     core = lax.axis_index("core")
-    label = line_group_label
-    tally = group_site_tally
+    label, tally = line_group_label, group_site_tally
     families = tally.shape[0]
-
     starts = jnp.sum(label[:, None] < jnp.arange(families + 1), axis=0, dtype=jnp.int32)
-    plane = lax.axis_index("plane")
-    me = jnp.stack([lax.axis_index(ROWS), chip, core, pair, plane]).astype(jnp.int32)
+    me = jnp.stack([lax.axis_index(ROWS), chip, core, pair]).astype(jnp.int32)
 
     across = other_chip(alignment_embedding)
     near = other_core(alignment_embedding)
-    width, eighth = expand_matrix.shape[0], quarter // 2
-    column_pack = jnp.concatenate(
-        [
-            vertical_triple_matrix.reshape(-1, vertical_triple_matrix.shape[-1]),
-            vertical_mixing_matrix,
-        ]
+    pack, late = pack_weights(
+        me,
+        horizontal_mixing_matrix,
+        vertical_triple_matrix,
+        vertical_mixing_matrix,
+        expand_matrix,
+        contract_matrix,
     )
-    feed = jnp.stack([expand_matrix, contract_matrix])
-
-    def chosen(options, index):
-        return lax.dynamic_index_in_dim(options, index, 0, False)
-
-    quarters = column_pack.reshape(4, quarter, -1)
-    pack = jnp.concatenate(
-        [
-            chosen(feed[:, : 5 * eighth], pair),
-            chosen(quarters, pair),
-            horizontal_mixing_matrix,
-            chosen(quarters, 2 + plane),
-            chosen(feed[:, 5 * eighth : 6 * eighth], plane),
-        ]
-    )
-    late_pack = feed[:, 6 * eighth :].reshape(2 * (width - 6 * eighth), -1)
-    across, near, pack, late_pack, starts, me = lax.optimization_barrier(
-        (across, near, pack, late_pack, starts, me)
+    stream, pack, late = lax.optimization_barrier((alignment_embedding, pack, late))
+    stream = spread(stream, chips)
+    stream = lax.all_to_all(stream, ROWS + ("chip", "core"), 0, 0, tiled=True)
+    across, near, pack, late, starts, me = lax.optimization_barrier(
+        (across, near, pack, late, starts, me)
     )
     plan = (me, label, starts, tally)
-    streams = (alignment_embedding, near, across, other_core(across))
     piece = other_chip(pack)
 
     shared, inner_weights, values = row_front(
-        streams,
+        (alignment_embedding, near, across, other_core(across)),
         horizontal_triple_matrix,
         plan,
         2 + max(min(families, lines) - 2, 1),
         row_groups,
     )
+    shared, stream = lax.optimization_barrier((shared, stream))
     parts = lax.all_to_all(shared, ROWS, 0, 0, tiled=True)
     shared = lax.all_to_all(tie(parts, plan), ROWS, 0, 0, tiled=True)
-    mixed, sent = mix(shared, inner_weights, values, plan)
-    sent, piece, late_pack = lax.optimization_barrier((sent, piece, late_pack))
-    column_rest = other_pair(piece[4 * eighth : 7 * eighth])
-    plane_rest = other_plane(piece[9 * eighth :])
-    feed_rest = other_pair(piece[: 4 * eighth])
-    late_piece = other_chip(late_pack)
-
-    got, column_rest, plane_rest = lax.optimization_barrier(
-        (other_chip(sent), column_rest, plane_rest)
-    )
-    kept, sent = project(
-        mixed,
-        got,
-        horizontal_mixing_matrix,
-        piece,
-        streams,
-        me,
-    )
-
-    blocks = settle(kept, other_core(sent), chips)
+    blocks = mix(shared, inner_weights, values, plan, chips)
+
+    blocks, piece, late = lax.optimization_barrier((blocks, piece, late))
+    half = expand_matrix.shape[0] // 2
+    rest = other_pair(piece[: 2 * half])
+    late = other_chip(late)
     blocks = lax.all_to_all(blocks, ROWS + ("chip",), 0, 0, tiled=True)
-    normed, after_row = arrive(blocks, place)
-    normed, feed_rest, late_piece = lax.optimization_barrier((normed, feed_rest, late_piece))
+    kept, sent = project(blocks, horizontal_mixing_matrix, piece, me, lines)
+    normed, after_row = arrive(kept, other_core(sent), stream, place)
+    normed, rest, late = lax.optimization_barrier((normed, rest, late))
+
     kept, sent = column(
         normed,
         other_core(normed),
         vertical_triple_matrix,
         vertical_mixing_matrix,
         piece,
-        column_rest,
-        plane_rest,
+        rest,
         plan,
-        lines // 4,
+        own,
     )
     after_col = core_sum(after_row, kept, sent)
 
     normed = own_norm(after_col, -1)
-    pieces = (piece, feed_rest, column_rest, plane_rest, late_piece)
-    weights = (expand_matrix, contract_matrix, pieces, me)
+    weights = (expand_matrix, contract_matrix, (piece, rest, late), me)
     kept = feed_forward(normed, *weights, F32)
     sent = feed_forward(other_core(normed), *weights, BF16)
     blocks = finish(after_col, kept, other_core(sent), row_groups, quarter)
 
     blocks = lax.all_to_all(blocks, ROWS + ("chip", "core"), 0, 0, tiled=True)
-    parts, wide = 2 * own * place // 2, quarter // 3 * 2
+    parts, wide = own * place // 2, quarter // 3 * 2
     narrow = blocks[:, 2 * parts :]
     narrow = jnp.concatenate([narrow[:, :, : wide // 2], narrow[:, :, wide // 2 :]], axis=1)
     finished = jnp.concatenate([blocks[:, : 2 * parts], narrow], axis=2)
-    finished = finished.reshape(chips, 2, place, 2, own, quarter)
-    finished = jnp.transpose(finished, (3, 1, 4, 5, 0, 2))
+    finished = finished.reshape(chips, 2, place, own, quarter)
+    finished = jnp.transpose(finished, (1, 3, 4, 0, 2))
     return finished.reshape(lines, quarter, sites)
 
 
 def solution(mesh):
-    far = mesh.shape["rows"] // 4
-    split = Mesh(mesh.devices.reshape(far, 2, 2, 2, 2), ROWS + ("chip", "core"))
+    planes = mesh.shape["rows"] // 2
+    split = Mesh(mesh.devices.reshape(planes, 2, 2, 2), ROWS + ("chip", "core"))
     heads = ("chip", "core")
     placed = (
         P(ROWS, heads, None),

time: 166 us -> 159 us (0.958)
  other arithmetic: 5.94 us -> 1.42 us
  waiting for transfers between devices: 41.1 us -> 38.9 us
  local copies, waits for them, and re-layouts: 16.7 us -> 14.6 us
  Pallas kernels: 32.8 us -> 34.7 us
    ppermute x4 -> x3, waiting for transfers between devices: 11.8 us -> 3.41 us  [other_chip(): return lax.ppermute(value, 'chip', SWAP)]
    ppermute x2 -> x1, waiting for transfers between devices: 2.05 us -> 8.4 us  [other_pair(): return lax.ppermute(value, 'pair', SWAP)]
    all_to_all x0 -> x1, starting transfers between devices: none -> 4.92 us  [shards(): stream = lax.all_to_all(stream, ROWS + ('chip', 'core'), 0, 0, tiled=True)]
    all_to_all x0 -> x1, waiting for transfers between devices: none -> 3.25 us  [shards(): stream = lax.all_to_all(stream, ROWS + ('chip', 'core'), 0, 0, tiled=True)]
    pallas_call x2 -> x3, Pallas kernels: 1.95 us -> 5.07 us  [the longest x1 2.08 us: mix(): pl.pallas_call(mix_kernel, out_shape=jax.ShapeDtypeStruct(shape, BF16), i...]
    slice x4 -> x1, local copies, waits for them, and re-layouts: 4.18 us -> 1.1 us  [shards(): rest = other_pair(piece[:2 * half])]
    unnamed x1 -> x0, other arithmetic: 2.54 us -> none
    ppermute x7, waiting for transfers between devices: 11.3 us -> 8.84 us  [other_core(): return lax.ppermute(value, 'core', SWAP)]
  transfers between devices with their start and end apart: 15 -> 13, of which waited for: 10 -> 9; matrix products, arithmetic and copies ran while one was open for 8% -> 1% of each run, Pallas kernels for 11% -> 14%
where the time goes in v4:
time: 159 us; the launch traced here: 158 us
  blocking collectives  48.7 us (31%)
  waiting for transfers between devices  38.9 us (24%)
  Pallas kernels  34.7 us (22%)
  starting transfers between devices  19.8 us (12%)
  local copies, waits for them, and re-layouts  14.6 us (9%)
    all_to_all x1, blocking collectives, shards(): blocks = lax.all_to_all(blocks, ROWS + ('chip', 'core'), 0, 0, tiled=True)  24.3 us
    all_to_all x1, waiting for transfers between devices, shards(): blocks = lax.all_to_all(blocks, ROWS + ('chip',), 0, 0, tiled=True)  15 us
    all_to_all x1, blocking collectives, shards(): parts = lax.all_to_all(shared, ROWS, 0, 0, tiled=True)  13.7 us
    unnamed x38, local copies, waits for them, and re-layouts  11.8 us
    all_to_all x1, blocking collectives, shards(): shared = lax.all_to_all(tie(parts, plan), ROWS, 0, 0, tiled=True)  10.7 us
    pallas_call x2, Pallas kernels, feed_forward(): pl.pallas_call(feed_forward_kernel, out_shape=jax.ShapeDtypeStruct((token...  9.37 us
    ppermute x7, waiting for transfers between devices, other_core(): return lax.ppermute(value, 'core', SWAP)  8.84 us
    ppermute x1, waiting for transfers between devices, other_pair(): return lax.ppermute(value, 'pair', SWAP)  8.4 us
  transfers between devices with their start and end apart: 13, of which 9 were waited for; matrix products, arithmetic and copies ran while one was open for 1% of the time, Pallas kernels for 14%

profile of v4, /device:TPU:0, one launch (start us, length us, event | category | flops | bytes accessed | tf_op | source)
XLA Modules:
  0.0 158.4 jit_solution(9620077724633763989)
XLA Ops:
  0.5 2.5 %collective-permute-start = (bf16[16,192,128]{2,1,0:T(8,128)(2,1)}, bf16[16,192,128]{2,1,0:T(8,128)(2,1)}, u32[]{:S(2)}, u32[]{:S(2)}) collective-permute-start(bf16[16,192,128]{2,1,0:T(8,128)(2,1)} %stream), channel_id=1, source_target_pairs={{0,2},{2,0},{1,3},{3,1},{4,6},{6,4},{5,7},{7,5},{8,10},{10,8},{9,1... | collective-permute-start | bytes 2359304 | tf_op jit(solution)/shard_map/ppermute | solution.py:18
  3.0 1.3 copy-done
  4.3 1.3 copy-done.2
  5.6 1.2 copy-done.4
  8.7 1.7 %pack.1 = (bf16[960,768]{1,0:T(8,128)(2,1)S(1)}, bf16[768,768]{1,0:T(8,128)(2,1)}) custom-call(s32[4]{0:T(128)S(1)} %pad_add_fusion.me_ref, bf16[192,768]{1,0:T(8,128)(2,1)S(1)} %copy-done.9, bf16[576,768]{1,0:T(8,128)(2,1)S(1)} %bitcast.15, bf16[192,768]{1,0:T(8,128)(2,1)S(1)} %copy-done.7, bf16[768,768]{1,0:T(8,128)(2,1)S(1)} %copy-done, ...), custom_call_target="tpu_custom_call" | custom-call | tf_op jit(solution)/shard_map/pack/pallas_call | solution.py:116
  11.5 1.3 spread.1
  12.8 4.9 %all-to-all-start = ((bf16[32,96,128]{2,1,0:T(8,128)(2,1)}), bf16[32,96,128]{2,1,0:T(8,128)(2,1)S(1)}, u32[]{:S(2)}, u32[]{:S(2)}) async-start(bf16[32,96,128]{2,1,0:T(8,128)(2,1)} %spread.1), calls=%async_computation | async-start | bytes 1572864 | tf_op jit(solution)/shard_map/all_to_all | solution.py:763
  18.7 2.9 %collective-permute-done.far = bf16[16,192,128]{2,1,0:T(8,128)(2,1)} collective-permute-done((bf16[16,192,128]{2,1,0:T(8,128)(2,1)}, bf16[16,192,128]{2,1,0:T(8,128)(2,1)}, u32[]{:S(2)}, u32[]{:S(2)}) %collective-permute-start) | collective-permute-done | bytes 786464 | tf_op jit(solution)/shard_map/ppermute | solution.py:18
  21.7 2.8 %collective-permute-start.3 = (bf16[960,768]{1,0:T(8,128)(2,1)}, bf16[960,768]{1,0:T(8,128)(2,1)S(1)}, u32[]{:S(2)}, u32[]{:S(2)}) collective-permute-start(bf16[960,768]{1,0:T(8,128)(2,1)} %copy-done.18), channel_id=1, source_target_pairs={{0,2},{2,0},{1,3},{3,1},{4,6},{6,4},{5,7},{7,5},{8,10},{10,8},{9,1... | collective-permute-start | bytes 4423688 | tf_op jit(solution)/shard_map/ppermute | solution.py:18
  24.5 1.2 copy-done.11
  25.7 1.1 copy-done.13
  26.8 7.4 %row_front.1 = (bf16[8,6,16,128]{3,2,1,0:T(8,128)(2,1)S(1)}, bf16[6,128,128]{2,1,0:T(8,128)(2,1)S(1)}, bf16[16,192,128]{2,1,0:T(8,128)(2,1)S(1)}) custom-call(s32[4]{0:T(128)S(1)} %pad_add_fusion.me_ref, s32[128]{0:T(128)S(1)} %copy-done.16, s32[5]{0:T(128)S(1)} %convert_reduce_fusion.1.starts_ref, s32[4]{0:T(128)S(1)} %copy-done.17, ...), custom_call_target="tpu_custom_call" | custom-call | tf_op jit(solution)/shard_map/row_front/pallas_call | solution.py:243
  35.1 3.2 %all-to-all-done.blocks = bf16[32,96,128]{2,1,0:T(8,128)(2,1)S(1)} async-done(((bf16[32,96,128]{2,1,0:T(8,128)(2,1)}), bf16[32,96,128]{2,1,0:T(8,128)(2,1)S(1)}, u32[]{:S(2)}, u32[]{:S(2)}) %all-to-all-start) | async-done | bytes 786464 | tf_op jit(solution)/shard_map/all_to_all | solution.py:763
  38.3 13.7 %all_to_all.25.parts = bf16[8,6,16,128]{3,2,1,0:T(8,128)(2,1)S(1)} all-to-all(bf16[8,6,16,128]{3,2,1,0:T(8,128)(2,1)S(1)} %get-tuple-element.43), channel_id=1, replica_groups=mesh['plane'=4,'pair'=2,'chip'=2,'core'=2] {'plane','pair'}, dimensions={0} | all-to-all | bytes 393216 | tf_op jit(solution)/shard_map/all_to_all | solution.py:778
  53.0 10.7 %all_to_all.26.shared = bf16[8,6,16,128]{3,2,1,0:T(8,128)(2,1)S(1)} all-to-all(bf16[8,6,16,128]{3,2,1,0:T(8,128)(2,1)S(1)} %tie.1), channel_id=1, replica_groups=mesh['plane'=4,'pair'=2,'chip'=2,'core'=2] {'plane','pair'}, dimensions={0} | all-to-all | bytes 393216 | tf_op jit(solution)/shard_map/all_to_all | solution.py:779
  63.7 2.1 %mix.1 = bf16[16,192,128]{2,1,0:T(8,128)(2,1)} custom-call(s32[4]{0:T(128)S(1)} %pad_add_fusion.me_ref, s32[128]{0:T(128)S(1)} %copy-done.16, s32[5]{0:T(128)S(1)} %convert_reduce_fusion.1.starts_ref, s32[4]{0:T(128)S(1)} %copy-done.17, bf16[8,6,16,128]{3,2,1,0:T(8,128)(2,1)S(1)} %all_to_all.26.shared, bf16[6,128,128]{2,1,0:T(8,128)(2,1)S(1)} %get-tuple-element.44.inner, ...), custom_call_target="tpu_custom_call" | custom-call | tf_op jit(solution)/shard_map/mix/pallas_call | solution.py:345
  65.8 5.1 %all-to-all-start.3 = ((bf16[16,192,128]{2,1,0:T(8,128)(2,1)}), bf16[16,192,128]{2,1,0:T(8,128)(2,1)}, u32[]{:S(2)}, u32[]{:S(2)}) async-start(bf16[16,192,128]{2,1,0:T(8,128)(2,1)} %mix.1), calls=%async_computation.3 | async-start | bytes 1572864 | tf_op jit(solution)/shard_map/all_to_all | solution.py:786
  72.0 1.9 %collective-permute-start.5 = (bf16[768,768]{1,0:T(8,128)(2,1)}, bf16[768,768]{1,0:T(8,128)(2,1)S(1)}, u32[]{:S(2)}, u32[]{:S(2)}) collective-permute-start(bf16[768,768]{1,0:T(8,128)(2,1)} %slice.15), channel_id=1, source_target_pairs={{0,4},{4,0},{1,5},{5,1},{2,6},{6,2},{3,7},{7,3},{8,12},{12,8},{9,1... | collective-permute-start | bytes 3538952 | tf_op jit(solution)/shard_map/ppermute | solution.py:22
  73.9 1.5 collective-permute-start.6
  75.3 15.0 %all-to-all-done.3.blocks = bf16[16,192,128]{2,1,0:T(8,128)(2,1)} async-done(((bf16[16,192,128]{2,1,0:T(8,128)(2,1)}), bf16[16,192,128]{2,1,0:T(8,128)(2,1)}, u32[]{:S(2)}, u32[]{:S(2)}) %all-to-all-start.3) | async-done | bytes 786464 | tf_op jit(solution)/shard_map/all_to_all | solution.py:786
  91.3 3.6 %project.1 = (f32[8,64,768]{2,1,0:T(8,128)S(1)}, bf16[8,64,768]{2,1,0:T(8,128)(2,1)S(1)}) custom-call(s32[4]{0:T(128)S(1)} %pad_add_fusion.me_ref, bf16[16,192,128]{2,1,0:T(8,128)(2,1)} %all-to-all-done.3.blocks, bf16[192,768]{1,0:T(8,128)(2,1)S(1)} %copy-done.10, bf16[960,768]{1,0:T(8,128)(2,1)S(1)} %collective-permute-done.3.piece), custom_call_target="tpu_custom_call" | custom-call | tf_op jit(solution)/shard_map/project/pallas_call | solution.py:417
  95.0 2.3 %collective-permute-done.4.got = bf16[8,64,768]{2,1,0:T(8,128)(2,1)S(1)} collective-permute-done((bf16[8,64,768]{2,1,0:T(8,128)(2,1)S(1)}, bf16[8,64,768]{2,1,0:T(8,128)(2,1)S(1)}, u32[]{:S(2)}, u32[]{:S(2)}) %collective-permute-start.4) | collective-permute-done | bytes 786464 | tf_op jit(solution)/shard_map/ppermute | solution.py:26
  98.4 8.4 %collective-permute-done.5.rest = bf16[768,768]{1,0:T(8,128)(2,1)S(1)} collective-permute-done((bf16[768,768]{1,0:T(8,128)(2,1)}, bf16[768,768]{1,0:T(8,128)(2,1)S(1)}, u32[]{:S(2)}, u32[]{:S(2)}) %collective-permute-start.5) | collective-permute-done | bytes 1179680 | tf_op jit(solution)/shard_map/ppermute | solution.py:22
  107.3 2.3 %collective-permute-done.7.other = bf16[8,64,768]{2,1,0:T(8,128)(2,1)S(1)} collective-permute-done((bf16[8,64,768]{2,1,0:T(8,128)(2,1)S(1)}, bf16[8,64,768]{2,1,0:T(8,128)(2,1)S(1)}, u32[]{:S(2)}, u32[]{:S(2)}) %collective-permute-start.7) | collective-permute-done | bytes 786464 | tf_op jit(solution)/shard_map/ppermute | solution.py:26
  109.6 6.0 %column.1 = (f32[8,64,768]{2,1,0:T(8,128)S(1)}, bf16[8,64,768]{2,1,0:T(8,128)(2,1)S(1)}) custom-call(s32[4]{0:T(128)S(1)} %pad_add_fusion.me_ref, s32[5]{0:T(128)S(1)} %convert_reduce_fusion.1.starts_ref, bf16[8,64,768]{2,1,0:T(8,128)(2,1)S(1)} %get-tuple-element.56.own, bf16[8,64,768]{2,1,0:T(8,128)(2,1)S(1)} %collective-permute-done.7.other, ...), custom_call_target="tpu_custom_call" | custom-call | tf_op jit(solution)/shard_map/column/pallas_call | solution.py:584
  115.8 2.1 %collective-permute-done.8 = bf16[8,64,768]{2,1,0:T(8,128)(2,1)S(1)} collective-permute-done((bf16[8,64,768]{2,1,0:T(8,128)(2,1)S(1)}, bf16[8,64,768]{2,1,0:T(8,128)(2,1)S(1)}, u32[]{:S(2)}, u32[]{:S(2)}) %collective-permute-start.8) | collective-permute-done | bytes 786464 | tf_op jit(solution)/shard_map/ppermute | solution.py:26
  119.1 2.1 %collective-permute-done.9 = bf16[8,64,768]{2,1,0:T(8,128)(2,1)S(1)} collective-permute-done((bf16[8,64,768]{2,1,0:T(8,128)(2,1)S(1)}, bf16[8,64,768]{2,1,0:T(8,128)(2,1)S(1)}, u32[]{:S(2)}, u32[]{:S(2)}) %collective-permute-start.9) | collective-permute-done | bytes 786464 | tf_op jit(solution)/shard_map/ppermute | solution.py:26
  121.3 4.7 %feed_forward.3 = bf16[512,768]{1,0:T(8,128)(2,1)S(1)} custom-call(s32[4]{0:T(128)S(1)} %pad_add_fusion.me_ref, bf16[512,768]{1,0:T(8,128)(2,1)S(1)} %bitcast.20, bf16[768,768]{1,0:T(8,128)(2,1)S(1)} %copy-done.1, bf16[768,768]{1,0:T(8,128)(2,1)S(1)} %copy-done.3, bf16[960,768]{1,0:T(8,128)(2,1)S(1)} %collective-permute-done.3.piece, ...), custom_call_target="tpu_custom_call" | custom-call | tf_op jit(solution)/shard_map/feed_forward/pallas_call | solution.py:704
  126.2 4.7 %feed_forward.2 = f32[512,768]{1,0:T(8,128)S(1)} custom-call(s32[4]{0:T(128)S(1)} %pad_add_fusion.me_ref, bf16[512,768]{1,0:T(8,128)(2,1)S(1)} %bitcast.17, bf16[768,768]{1,0:T(8,128)(2,1)S(1)} %copy-done.1, bf16[768,768]{1,0:T(8,128)(2,1)S(1)} %copy-done.3, bf16[960,768]{1,0:T(8,128)(2,1)S(1)} %collective-permute-done.3.piece, ...), custom_call_target="tpu_custom_call" | custom-call | tf_op jit(solution)/shard_map/feed_forward/pallas_call | solution.py:704
  130.9 1.2 finish.1
  132.1 24.3 %all_to_all.27 = bf16[32,96,128]{2,1,0:T(8,128)(2,1)S(1)} all-to-all(bf16[32,96,128]{2,1,0:T(8,128)(2,1)S(1)} %finish.1), channel_id=1, replica_groups=mesh['plane'=4,'pair'=2,'chip'=2,'core'=2] {'plane','pair','chip','core'}, dimensions={0} | all-to-all | bytes 1572864 | tf_op jit(solution)/shard_map/all_to_all | solution.py:809
  157.1 1.3 copy.14
  (59 shorter events, 12.4 us)
Async XLA Ops:
  0.0 17.8 %collective-permute-start.1 = (bf16[16,192,128]{2,1,0:T(8,128)(2,1)}, bf16[16,192,128]{2,1,0:T(8,128)(2,1)S(1)}, u32[]{:S(2)}, u32[]{:S(2)}) collective-permute-start(bf16[16,192,128]{2,1,0:T(8,128)(2,1)} %stream), channel_id=1, source_target_pairs={{0,1},{1,0},{2,3},{3,2},{4,5},{5,4},{6,7},{7,6},{8,9},{9,8},{10,11... | collective-permute-start | bytes 2359304 | tf_op jit(solution)/shard_map/ppermute | solution.py:26
  0.5 21.2 %collective-permute-start = (bf16[16,192,128]{2,1,0:T(8,128)(2,1)}, bf16[16,192,128]{2,1,0:T(8,128)(2,1)}, u32[]{:S(2)}, u32[]{:S(2)}) collective-permute-start(bf16[16,192,128]{2,1,0:T(8,128)(2,1)} %stream), channel_id=1, source_target_pairs={{0,2},{2,0},{1,3},{3,1},{4,6},{6,4},{5,7},{7,5},{8,10},{10,8},{9,1... | collective-permute-start | bytes 2359304 | tf_op jit(solution)/shard_map/ppermute | solution.py:18
  3.0 1.3 copy-start
  4.3 1.3 copy-start.2
  5.6 1.2 copy-start.4
  6.7 1.0 copy-start.7
  7.7 1.0 copy-start.9
  8.7 2.8 %copy-start.6 = (bf16[16,192,128]{2,1,0:T(8,128)(2,1)S(1)}, bf16[16,192,128]{2,1,0:T(8,128)(2,1)}, u32[]{:S(2)}) copy-start(bf16[16,192,128]{2,1,0:T(8,128)(2,1)} %stream) | copy-start | bytes 2359300
  10.3 1.1 copy-start.18
  11.5 6.3 %copy-start.16 = (s32[128]{0:T(128)S(1)}, s32[128]{0:T(128)}, u32[]{:S(2)}) copy-start(s32[128]{0:T(128)} %label_ref.5) | copy-start | bytes 1540
  11.5 13.0 %copy-start.17 = (s32[4]{0:T(128)S(1)}, s32[4]{0:T(128)}, u32[]{:S(2)}) copy-start(s32[4]{0:T(128)} %tally_ref.5) | copy-start | bytes 52
  12.8 25.5 %all-to-all-start = ((bf16[32,96,128]{2,1,0:T(8,128)(2,1)}), bf16[32,96,128]{2,1,0:T(8,128)(2,1)S(1)}, u32[]{:S(2)}, u32[]{:S(2)}) async-start(bf16[32,96,128]{2,1,0:T(8,128)(2,1)} %spread.1), calls=%async_computation | async-start | bytes 1572864 | tf_op jit(solution)/shard_map/all_to_all | solution.py:763
  17.8 0.9 copy-start.12
  21.6 2.9 %collective-permute-start.2 = (bf16[16,192,128]{2,1,0:T(8,128)(2,1)}, bf16[16,192,128]{2,1,0:T(8,128)(2,1)S(1)}, u32[]{:S(2)}, u32[]{:S(2)}) collective-permute-start(bf16[16,192,128]{2,1,0:T(8,128)(2,1)} %collective-permute-done.far), channel_id=1, source_target_pairs={{0,1},{1,0},{2,3},{3,2},{4,5},{5,4},{6,7},{7,6},{8,9},{9,8},{10,11... | collective-permute-start | bytes 2359304 | tf_op jit(solution)/shard_map/ppermute | solution.py:26
  21.7 44.2 %collective-permute-start.3 = (bf16[960,768]{1,0:T(8,128)(2,1)}, bf16[960,768]{1,0:T(8,128)(2,1)S(1)}, u32[]{:S(2)}, u32[]{:S(2)}) collective-permute-start(bf16[960,768]{1,0:T(8,128)(2,1)} %copy-done.18), channel_id=1, source_target_pairs={{0,2},{2,0},{1,3},{3,1},{4,6},{6,4},{5,7},{7,5},{8,10},{10,8},{9,1... | collective-permute-start | bytes 4423688 | tf_op jit(solution)/shard_map/ppermute | solution.py:18
  24.5 1.2 copy-start.11
  25.7 1.1 copy-start.13
  34.2 0.9 copy-start.14
  38.3 25.4 %copy-start.15 = (bf16[16,192,128]{2,1,0:T(8,128)(2,1)S(1)}, bf16[16,192,128]{2,1,0:T(8,128)(2,1)}, u32[]{:S(2)}) copy-start(bf16[16,192,128]{2,1,0:T(8,128)(2,1)} %copy-done.14) | copy-start | bytes 2359300
  65.8 24.5 %all-to-all-start.3 = ((bf16[16,192,128]{2,1,0:T(8,128)(2,1)}), bf16[16,192,128]{2,1,0:T(8,128)(2,1)}, u32[]{:S(2)}, u32[]{:S(2)}) async-start(bf16[16,192,128]{2,1,0:T(8,128)(2,1)} %mix.1), calls=%async_computation.3 | async-start | bytes 1572864 | tf_op jit(solution)/shard_map/all_to_all | solution.py:786
  72.0 34.8 %collective-permute-start.5 = (bf16[768,768]{1,0:T(8,128)(2,1)}, bf16[768,768]{1,0:T(8,128)(2,1)S(1)}, u32[]{:S(2)}, u32[]{:S(2)}) collective-permute-start(bf16[768,768]{1,0:T(8,128)(2,1)} %slice.15), channel_id=1, source_target_pairs={{0,4},{4,0},{1,5},{5,1},{2,6},{6,2},{3,7},{7,3},{8,12},{12,8},{9,1... | collective-permute-start | bytes 3538952 | tf_op jit(solution)/shard_map/ppermute | solution.py:22
  73.9 33.4 %collective-permute-start.6 = (bf16[768,768]{1,0:T(8,128)(2,1)}, bf16[768,768]{1,0:T(8,128)(2,1)}, u32[]{:S(2)}, u32[]{:S(2)}) collective-permute-start(bf16[768,768]{1,0:T(8,128)(2,1)} %get-tuple-element.55), channel_id=1, source_target_pairs={{0,2},{2,0},{1,3},{3,1},{4,6},{6,4},{5,7},{7,5},{8,10},{10,8},{9,1... | collective-permute-start | bytes 3538952 | tf_op jit(solution)/shard_map/ppermute | solution.py:18
  90.3 1.0 copy-start.10
  94.9 2.4 %collective-permute-start.4 = (bf16[8,64,768]{2,1,0:T(8,128)(2,1)S(1)}, bf16[8,64,768]{2,1,0:T(8,128)(2,1)S(1)}, u32[]{:S(2)}, u32[]{:S(2)}) collective-permute-start(bf16[8,64,768]{2,1,0:T(8,128)(2,1)S(1)} %get-tuple-element.51), channel_id=1, source_target_pairs={{0,1},{1,0},{2,3},{3,2},{4,5},{5,4},{6,7},{7,6},{8,9},{9,8},{10,11... | collective-permute-start | bytes 2359304 | tf_op jit(solution)/shard_map/ppermute | solution.py:26
  97.3 12.3 %copy-start.5 = (bf16[3,192,768]{2,1,0:T(8,128)(2,1)S(1)}, bf16[3,192,768]{2,1,0:T(8,128)(2,1)}, u32[]{:S(2)}) copy-start(bf16[3,192,768]{2,1,0:T(8,128)(2,1)} %param.14) | copy-start | bytes 2654212
  97.3 12.3 %copy-start.8 = (bf16[192,768]{1,0:T(8,128)(2,1)S(1)}, bf16[192,768]{1,0:T(8,128)(2,1)}, u32[]{:S(2)}) copy-start(bf16[192,768]{1,0:T(8,128)(2,1)} %mixing.5) | copy-start | bytes 884740
  107.3 2.3 %collective-permute-start.7 = (bf16[8,64,768]{2,1,0:T(8,128)(2,1)S(1)}, bf16[8,64,768]{2,1,0:T(8,128)(2,1)S(1)}, u32[]{:S(2)}, u32[]{:S(2)}) collective-permute-start(bf16[8,64,768]{2,1,0:T(8,128)(2,1)S(1)} %get-tuple-element.56.own), channel_id=1, source_target_pairs={{0,1},{1,0},{2,3},{3,2},{4,5},{5,4},{6,7},{7,6},{8,9},{9,8},{10,11... | collective-permute-start | bytes 2359304 | tf_op jit(solution)/shard_map/ppermute | solution.py:26
  115.6 2.4 %collective-permute-start.8 = (bf16[8,64,768]{2,1,0:T(8,128)(2,1)S(1)}, bf16[8,64,768]{2,1,0:T(8,128)(2,1)S(1)}, u32[]{:S(2)}, u32[]{:S(2)}) collective-permute-start(bf16[8,64,768]{2,1,0:T(8,128)(2,1)S(1)} %get-tuple-element.59), channel_id=1, source_target_pairs={{0,1},{1,0},{2,3},{3,2},{4,5},{5,4},{6,7},{7,6},{8,9},{9,8},{10,11... | collective-permute-start | bytes 2359304 | tf_op jit(solution)/shard_map/ppermute | solution.py:26
  118.3 3.0 %copy-start.1 = (bf16[768,768]{1,0:T(8,128)(2,1)S(1)}, bf16[768,768]{1,0:T(8,128)(2,1)}, u32[]{:S(2)}) copy-start(bf16[768,768]{1,0:T(8,128)(2,1)} %expand.5) | copy-start | bytes 3538948
  118.3 3.0 %copy-start.3 = (bf16[768,768]{1,0:T(8,128)(2,1)S(1)}, bf16[768,768]{1,0:T(8,128)(2,1)}, u32[]{:S(2)}) copy-start(bf16[768,768]{1,0:T(8,128)(2,1)} %contract.5) | copy-start | bytes 3538948
  118.9 2.4 %collective-permute-start.9 = (bf16[8,64,768]{2,1,0:T(8,128)(2,1)S(1)}, bf16[8,64,768]{2,1,0:T(8,128)(2,1)S(1)}, u32[]{:S(2)}, u32[]{:S(2)}) collective-permute-start(bf16[8,64,768]{2,1,0:T(8,128)(2,1)S(1)} %fusion.3), channel_id=1, source_target_pairs={{0,1},{1,0},{2,3},{3,2},{4,5},{5,4},{6,7},{7,6},{8,9},{9,8},{10,11... | collective-permute-start | bytes 2359304 | tf_op jit(solution)/shard_map/ppermute | solution.py:26
  126.0 4.9 %collective-permute-start.10 = (bf16[8,64,768]{2,1,0:T(8,128)(2,1)S(1)}, bf16[8,64,768]{2,1,0:T(8,128)(2,1)S(1)}, u32[]{:S(2)}, u32[]{:S(2)}) collective-permute-start(bf16[8,64,768]{2,1,0:T(8,128)(2,1)S(1)} %bitcast.19), channel_id=1, source_target_pairs={{0,1},{1,0},{2,3},{3,2},{4,5},{5,4},{6,7},{7,6},{8,9},{9,8},{10,11... | collective-permute-start | bytes 2359304 | tf_op jit(solution)/shard_map/ppermute | solution.py:26

commit v5 on v4

--- a/solution.py
+++ b/solution.py
@@ -362,7 +362,9 @@
     return jnp.transpose(mixed, (1, 0, 2, 3)).reshape(chips, lines * place, quarter)
 
 
-def project_kernel(me_ref, blocks, mixing, piece, kept, sent, wide, first, second, semaphores):
+def project_kernel(
+    me_ref, blocks, mixing, piece, kept, sent, more, wide, first, second, semaphores
+):
     chips, count, lanes = blocks.shape
     quarter, model = mixing.shape
     tokens = count * 2 // 3
@@ -405,7 +407,8 @@
         @pl.when(core == index)
         def _(index=index):
             kept[...] = halves[index]
-            sent[...] = halves[1 - index].astype(BF16)
+            sent[...] = halves[1 - index][: groups // 2].astype(BF16)
+            more[...] = halves[1 - index][groups // 2 :].astype(BF16)
 
 
 def project(blocks, mixing, piece, me, lines):
@@ -416,9 +419,13 @@
         out = (groups, count // 3, model)
         return pl.pallas_call(
             project_kernel,
-            out_shape=(jax.ShapeDtypeStruct(out, F32), jax.ShapeDtypeStruct(out, BF16)),
+            out_shape=(
+                jax.ShapeDtypeStruct(out, F32),
+                jax.ShapeDtypeStruct((groups // 2, *out[1:]), BF16),
+                jax.ShapeDtypeStruct((groups // 2, *out[1:]), BF16),
+            ),
             in_specs=[IN_SMEM, IN_VMEM, IN_HBM, IN_HBM],
-            out_specs=(IN_VMEM, IN_VMEM),
+            out_specs=(IN_VMEM, IN_VMEM, IN_VMEM),
             scratch_shapes=[pltpu.VMEM((2 * lanes, model), BF16)] * 3
             + [pltpu.SemaphoreType.DMA((6,))],
             compiler_params=GRANT,
@@ -429,24 +436,26 @@
     partial = jnp.einsum("gxctd,xde->cgte", values, weights, preferred_element_type=F32)
     kept = lax.dynamic_index_in_dim(partial, me[2], 0, False)
     sent = lax.dynamic_index_in_dim(partial, 1 - me[2], 0, False)
-    return kept, sent.astype(BF16)
-
-
-def arrive_kernel(kept, got, blocks, normed, stream, tokens):
+    sent = sent.astype(BF16)
+    return kept, sent[: groups // 2], sent[groups // 2 :]
+
+
+def arrive_kernel(kept, got, more, blocks, normed, later, stream, tokens):
     groups, own, model = kept.shape
-    places, rows, _ = normed.shape
+    places, rows, _ = stream.shape
     count, lanes = blocks.shape[1], blocks.shape[2]
     heads = blocks.shape[0] // groups
     parts = count // 3
-    total = kept[...] + got[...].astype(F32)
     for group in range(groups):
+        source = got if group < groups // 2 else more
+        total = kept[group] + source[group % (groups // 2)].astype(F32)
         features = []
         for head in range(heads):
             block = blocks[group * heads + head].astype(F32)
             narrow = block[2 * parts :]
             narrow = jnp.concatenate([narrow[:, : lanes // 2], narrow[:, lanes // 2 :]], axis=0)
             features += [block[: 2 * parts], narrow]
-        values = total[group] + jnp.concatenate(features, axis=1)
+        values = total + jnp.concatenate(features, axis=1)
         for index in range(tokens.shape[0]):
             lower = index * tokens.shape[2]
             part = values[:, lower : lower + tokens.shape[2]]
@@ -460,32 +469,38 @@
         values = values.astype(F32)
         centred = values - jnp.mean(values, axis=-1, keepdims=True)
         variance = jnp.mean(centred * centred, axis=-1, keepdims=True)
-        normed[place] = (centred * lax.rsqrt(variance + 1e-05)).astype(BF16)
-
-
-def arrive(kept, got, blocks, place):
+        target = normed if place < places // 2 else later
+        target[place % (places // 2)] = (centred * lax.rsqrt(variance + 1e-05)).astype(BF16)
+
+
+def arrive(kept, got, more, blocks, place):
     groups, own, model = kept.shape
     rows = groups * own // place
     if place % 8 == 0:
         shape = jax.ShapeDtypeStruct((place, rows, model), BF16)
+        half = jax.ShapeDtypeStruct((place // 2, rows, model), BF16)
         return pl.pallas_call(
             arrive_kernel,
-            out_shape=(shape, shape),
-            in_specs=[IN_VMEM] * 3,
-            out_specs=(IN_VMEM, IN_VMEM),
+            out_shape=(half, half, shape),
+            in_specs=[IN_VMEM] * 4,
+            out_specs=(IN_VMEM, IN_VMEM, IN_VMEM),
             scratch_shapes=[pltpu.VMEM((model // 128, groups * own, 128), F32)],
             compiler_params=GRANT,
             name="arrive",
-        )(kept, got, blocks)
+        )(kept, got, more, blocks)
     heads = blocks.shape[0] // groups
     stream = jnp.transpose(blocks.reshape(groups, heads, own, -1), (0, 2, 1, 3))
-    stream = stream.reshape(groups, own, model).astype(F32) + kept + got.astype(F32)
+    stream = stream.reshape(groups, own, model).astype(F32) + kept
+    stream += jnp.concatenate([got, more]).astype(F32)
     stream = jnp.transpose(stream.reshape(rows, place, model), (1, 0, 2)).astype(BF16)
-    return own_norm(stream, -1), stream
+    normed = own_norm(stream, -1)
+    if place == 1:
+        return normed[:, : rows // 2], normed[:, rows // 2 :], stream
+    return normed[: place // 2], normed[place // 2 :], stream
 
 
 def column_kernel(
-    lines, me_ref, starts_ref, own, other, triple, mixing, piece, rest,
+    lines, me_ref, starts_ref, own, own_later, other, other_later, triple, mixing, piece, rest,
     kept, sent, normed, near, far, projected, mixed, semaphores,
 ):
     quarter = mixing.shape[0]
@@ -507,10 +522,13 @@
     ]
     for copy in copies:
         copy.start()
-    places, rows, model = own.shape
-    both = 2 * rows
-    normed[:, :rows] = own[...]
-    normed[:, rows:] = other[...]
+    places, both, model = normed.shape
+    rows = both // 2
+    count, width = own.shape[:2]
+    for index, values in enumerate((own, own_later, other, other_later)):
+        start = index % 2 * count if count < places else 0
+        lower = index // 2 * rows + (0 if count < places else index % 2 * width)
+        normed[start : start + count, lower : lower + width] = values[...]
     flat = normed[...].reshape(places * both, model)
 
     def families(axis):
@@ -577,17 +595,17 @@
         sent[place] = partial[rows:].astype(BF16)
 
 
-def column(own, other, triple, mixing, piece, rest, plan, lines):
-    places, rows, model = own.shape
+def column(own, other, triple, mixing, piece, rest, plan, lines, shape):
+    places, rows, model = shape
     quarter = mixing.shape[0]
     tokens = 2 * places * rows
     return pl.pallas_call(
         functools.partial(column_kernel, lines),
         out_shape=(
-            jax.ShapeDtypeStruct(own.shape, F32),
-            jax.ShapeDtypeStruct(own.shape, BF16),
+            jax.ShapeDtypeStruct(shape, F32),
+            jax.ShapeDtypeStruct(shape, BF16),
         ),
-        in_specs=[IN_SMEM] * 2 + [IN_VMEM] * 2 + [IN_HBM] * 4,
+        in_specs=[IN_SMEM] * 2 + [IN_VMEM] * 4 + [IN_HBM] * 4,
         out_specs=(IN_VMEM, IN_VMEM),
         scratch_shapes=[
             pltpu.VMEM((places, 2 * rows, model), BF16),
@@ -599,7 +617,7 @@
         ],
         compiler_params=GRANT,
         name="column",
-    )(plan[0], plan[2], own, other, triple.reshape(-1, model), mixing, piece, rest)
+    )(plan[0], plan[2], *own, *other, triple.reshape(-1, model), mixing, piece, rest)
 
 
 def finish_kernel(stream, kept, got, out):
@@ -784,19 +802,22 @@
     rest = other_pair(piece[: 2 * half])
     late = other_chip(late)
     blocks = lax.all_to_all(blocks, ROWS + ("chip",), 0, 0, tiled=True)
-    kept, sent = project(blocks, horizontal_mixing_matrix, piece, me, lines)
-    normed, after_row = arrive(kept, other_core(sent), stream, place)
-    normed, rest, late = lax.optimization_barrier((normed, rest, late))
+    kept, *sent = project(blocks, horizontal_mixing_matrix, piece, me, lines)
+    got = [other_core(part) for part in sent]
+    *normed, after_row = arrive(kept, *got, stream, place)
+    other = [other_core(part) for part in normed]
+    other, rest, late = lax.optimization_barrier((other, rest, late))
 
     kept, sent = column(
         normed,
-        other_core(normed),
+        other,
         vertical_triple_matrix,
         vertical_mixing_matrix,
         piece,
         rest,
         plan,
         own,
+        after_row.shape,
     )
     after_col = core_sum(after_row, kept, sent)
 

time: 159 us -> 157 us (0.987)
  waiting for transfers between devices: 38.9 us -> 35.7 us
    ppermute x7 -> x9, waiting for transfers between devices: 8.84 us -> 6.21 us  [other_core(): return lax.ppermute(value, 'core', SWAP)]
  transfers between devices with their start and end apart: 13 -> 15, of which waited for: 9 -> 9; matrix products, arithmetic and copies ran while one was open for 1% -> 1% of each run, Pallas kernels for 14% -> 15%
where the time goes in v5:
time: 157 us; the launch traced here: 156 us
  blocking collectives  48.7 us (31%)
  waiting for transfers between devices  35.7 us (23%)
  Pallas kernels  35 us (22%)
  starting transfers between devices  20.7 us (13%)
  local copies, waits for them, and re-layouts  14.6 us (9%)
    all_to_all x1, blocking collectives, shards(): blocks = lax.all_to_all(blocks, ROWS + ('chip', 'core'), 0, 0, tiled=True)  24.3 us
    all_to_all x1, waiting for transfers between devices, shards(): blocks = lax.all_to_all(blocks, ROWS + ('chip',), 0, 0, tiled=True)  15 us
    all_to_all x1, blocking collectives, shards(): parts = lax.all_to_all(shared, ROWS, 0, 0, tiled=True)  13.7 us
    unnamed x38, local copies, waits for them, and re-layouts  11.8 us
    all_to_all x1, blocking collectives, shards(): shared = lax.all_to_all(tie(parts, plan), ROWS, 0, 0, tiled=True)  10.7 us
    pallas_call x2, Pallas kernels, feed_forward(): pl.pallas_call(feed_forward_kernel, out_shape=jax.ShapeDtypeStruct((token...  9.6 us
    ppermute x1, waiting for transfers between devices, other_pair(): return lax.ppermute(value, 'pair', SWAP)  7.8 us
    pallas_call x1, Pallas kernels, row_front(): pl.pallas_call(functools.partial(row_front_kernel, lines), grid=(lines //...  7.39 us
  transfers between devices with their start and end apart: 15, of which 9 were waited for; matrix products, arithmetic and copies ran while one was open for 1% of the time, Pallas kernels for 15%

profile of v5, /device:TPU:0, one launch (start us, length us, event | category | flops | bytes accessed | tf_op | source)
XLA Modules:
  0.0 156.3 jit_solution(14627861904434787564)
XLA Ops:
  0.5 2.5 %collective-permute-start = (bf16[16,192,128]{2,1,0:T(8,128)(2,1)}, bf16[16,192,128]{2,1,0:T(8,128)(2,1)}, u32[]{:S(2)}, u32[]{:S(2)}) collective-permute-start(bf16[16,192,128]{2,1,0:T(8,128)(2,1)} %stream), channel_id=1, source_target_pairs={{0,2},{2,0},{1,3},{3,1},{4,6},{6,4},{5,7},{7,5},{8,10},{10,8},{9,1... | collective-permute-start | bytes 2359304 | tf_op jit(solution)/shard_map/ppermute | solution.py:18
  3.0 1.3 copy-done
  4.3 1.3 copy-done.2
  5.6 1.2 copy-done.4
  8.7 1.7 %pack.1 = (bf16[960,768]{1,0:T(8,128)(2,1)S(1)}, bf16[768,768]{1,0:T(8,128)(2,1)}) custom-call(s32[4]{0:T(128)S(1)} %pad_add_fusion.me_ref, bf16[192,768]{1,0:T(8,128)(2,1)S(1)} %copy-done.9, bf16[576,768]{1,0:T(8,128)(2,1)S(1)} %bitcast.15, bf16[192,768]{1,0:T(8,128)(2,1)S(1)} %copy-done.7, bf16[768,768]{1,0:T(8,128)(2,1)S(1)} %copy-done, ...), custom_call_target="tpu_custom_call" | custom-call | tf_op jit(solution)/shard_map/pack/pallas_call | solution.py:116
  11.5 1.3 spread.1
  12.8 4.9 %all-to-all-start = ((bf16[32,96,128]{2,1,0:T(8,128)(2,1)}), bf16[32,96,128]{2,1,0:T(8,128)(2,1)S(1)}, u32[]{:S(2)}, u32[]{:S(2)}) async-start(bf16[32,96,128]{2,1,0:T(8,128)(2,1)} %spread.1), calls=%async_computation | async-start | bytes 1572864 | tf_op jit(solution)/shard_map/all_to_all | solution.py:781
  18.7 2.9 %collective-permute-done.far = bf16[16,192,128]{2,1,0:T(8,128)(2,1)} collective-permute-done((bf16[16,192,128]{2,1,0:T(8,128)(2,1)}, bf16[16,192,128]{2,1,0:T(8,128)(2,1)}, u32[]{:S(2)}, u32[]{:S(2)}) %collective-permute-start) | collective-permute-done | bytes 786464 | tf_op jit(solution)/shard_map/ppermute | solution.py:18
  21.7 2.8 %collective-permute-start.3 = (bf16[960,768]{1,0:T(8,128)(2,1)}, bf16[960,768]{1,0:T(8,128)(2,1)S(1)}, u32[]{:S(2)}, u32[]{:S(2)}) collective-permute-start(bf16[960,768]{1,0:T(8,128)(2,1)} %copy-done.18), channel_id=1, source_target_pairs={{0,2},{2,0},{1,3},{3,1},{4,6},{6,4},{5,7},{7,5},{8,10},{10,8},{9,1... | collective-permute-start | bytes 4423688 | tf_op jit(solution)/shard_map/ppermute | solution.py:18
  24.5 1.2 copy-done.11
  25.7 1.1 copy-done.13
  26.8 7.4 %row_front.1 = (bf16[8,6,16,128]{3,2,1,0:T(8,128)(2,1)S(1)}, bf16[6,128,128]{2,1,0:T(8,128)(2,1)S(1)}, bf16[16,192,128]{2,1,0:T(8,128)(2,1)S(1)}) custom-call(s32[4]{0:T(128)S(1)} %pad_add_fusion.me_ref, s32[128]{0:T(128)S(1)} %copy-done.16, s32[5]{0:T(128)S(1)} %convert_reduce_fusion.1.starts_ref, s32[4]{0:T(128)S(1)} %copy-done.17, ...), custom_call_target="tpu_custom_call" | custom-call | tf_op jit(solution)/shard_map/row_front/pallas_call | solution.py:243
  35.1 3.3 %all-to-all-done.blocks = bf16[32,96,128]{2,1,0:T(8,128)(2,1)S(1)} async-done(((bf16[32,96,128]{2,1,0:T(8,128)(2,1)}), bf16[32,96,128]{2,1,0:T(8,128)(2,1)S(1)}, u32[]{:S(2)}, u32[]{:S(2)}) %all-to-all-start) | async-done | bytes 786464 | tf_op jit(solution)/shard_map/all_to_all | solution.py:781
  38.4 13.7 %all_to_all.25.parts = bf16[8,6,16,128]{3,2,1,0:T(8,128)(2,1)S(1)} all-to-all(bf16[8,6,16,128]{3,2,1,0:T(8,128)(2,1)S(1)} %get-tuple-element.46), channel_id=1, replica_groups=mesh['plane'=4,'pair'=2,'chip'=2,'core'=2] {'plane','pair'}, dimensions={0} | all-to-all | bytes 393216 | tf_op jit(solution)/shard_map/all_to_all | solution.py:796
  53.0 10.7 %all_to_all.26.shared = bf16[8,6,16,128]{3,2,1,0:T(8,128)(2,1)S(1)} all-to-all(bf16[8,6,16,128]{3,2,1,0:T(8,128)(2,1)S(1)} %tie.1), channel_id=1, replica_groups=mesh['plane'=4,'pair'=2,'chip'=2,'core'=2] {'plane','pair'}, dimensions={0} | all-to-all | bytes 393216 | tf_op jit(solution)/shard_map/all_to_all | solution.py:797
  63.7 2.1 %mix.1 = bf16[16,192,128]{2,1,0:T(8,128)(2,1)} custom-call(s32[4]{0:T(128)S(1)} %pad_add_fusion.me_ref, s32[128]{0:T(128)S(1)} %copy-done.16, s32[5]{0:T(128)S(1)} %convert_reduce_fusion.1.starts_ref, s32[4]{0:T(128)S(1)} %copy-done.17, bf16[8,6,16,128]{3,2,1,0:T(8,128)(2,1)S(1)} %all_to_all.26.shared, bf16[6,128,128]{2,1,0:T(8,128)(2,1)S(1)} %get-tuple-element.47.inner, ...), custom_call_target="tpu_custom_call" | custom-call | tf_op jit(solution)/shard_map/mix/pallas_call | solution.py:345
  65.8 5.1 %all-to-all-start.3 = ((bf16[16,192,128]{2,1,0:T(8,128)(2,1)}), bf16[16,192,128]{2,1,0:T(8,128)(2,1)}, u32[]{:S(2)}, u32[]{:S(2)}) async-start(bf16[16,192,128]{2,1,0:T(8,128)(2,1)} %mix.1), calls=%async_computation.3 | async-start | bytes 1572864 | tf_op jit(solution)/shard_map/all_to_all | solution.py:804
  72.0 1.9 %collective-permute-start.8 = (bf16[768,768]{1,0:T(8,128)(2,1)}, bf16[768,768]{1,0:T(8,128)(2,1)S(1)}, u32[]{:S(2)}, u32[]{:S(2)}) collective-permute-start(bf16[768,768]{1,0:T(8,128)(2,1)} %slice.15), channel_id=1, source_target_pairs={{0,4},{4,0},{1,5},{5,1},{2,6},{6,2},{3,7},{7,3},{8,12},{12,8},{9,1... | collective-permute-start | bytes 3538952 | tf_op jit(solution)/shard_map/ppermute | solution.py:22
  73.9 1.5 collective-permute-start.9
  75.3 15.0 %all-to-all-done.3.blocks = bf16[16,192,128]{2,1,0:T(8,128)(2,1)} async-done(((bf16[16,192,128]{2,1,0:T(8,128)(2,1)}), bf16[16,192,128]{2,1,0:T(8,128)(2,1)}, u32[]{:S(2)}, u32[]{:S(2)}) %all-to-all-start.3) | async-done | bytes 786464 | tf_op jit(solution)/shard_map/all_to_all | solution.py:804
  91.3 3.6 %project.1 = (f32[8,64,768]{2,1,0:T(8,128)S(1)}, bf16[4,64,768]{2,1,0:T(8,128)(2,1)S(1)}, bf16[4,64,768]{2,1,0:T(8,128)(2,1)S(1)}) custom-call(s32[4]{0:T(128)S(1)} %pad_add_fusion.me_ref, bf16[16,192,128]{2,1,0:T(8,128)(2,1)} %all-to-all-done.3.blocks, bf16[192,768]{1,0:T(8,128)(2,1)S(1)} %copy-done.10, bf16[960,768]{1,0:T(8,128)(2,1)S(1)} %collective-permute-done.3.piece), custom_call_target="tpu_custom_call" | custom-call | tf_op jit(solution)/shard_map/project/pallas_call | solution.py:420
  95.5 1.2 collective-permute-done.4.got
  97.3 1.1 arrive.1
  99.0 7.8 %collective-permute-done.8.rest = bf16[768,768]{1,0:T(8,128)(2,1)S(1)} collective-permute-done((bf16[768,768]{1,0:T(8,128)(2,1)}, bf16[768,768]{1,0:T(8,128)(2,1)S(1)}, u32[]{:S(2)}, u32[]{:S(2)}) %collective-permute-start.8) | collective-permute-done | bytes 1179680 | tf_op jit(solution)/shard_map/ppermute | solution.py:22
  107.3 6.0 %column.1 = (f32[8,64,768]{2,1,0:T(8,128)S(1)}, bf16[8,64,768]{2,1,0:T(8,128)(2,1)S(1)}) custom-call(s32[4]{0:T(128)S(1)} %pad_add_fusion.me_ref, s32[5]{0:T(128)S(1)} %convert_reduce_fusion.1.starts_ref, bf16[4,64,768]{2,1,0:T(8,128)(2,1)S(1)} %get-tuple-element.58.own, bf16[4,64,768]{2,1,0:T(8,128)(2,1)S(1)} %get-tuple-element.59.own_later, ...), custom_call_target="tpu_custom_call" | custom-call | tf_op jit(solution)/shard_map/column/pallas_call | solution.py:602
  113.4 2.3 %collective-permute-done.10 = bf16[8,64,768]{2,1,0:T(8,128)(2,1)S(1)} collective-permute-done((bf16[8,64,768]{2,1,0:T(8,128)(2,1)S(1)}, bf16[8,64,768]{2,1,0:T(8,128)(2,1)S(1)}, u32[]{:S(2)}, u32[]{:S(2)}) %collective-permute-start.10) | collective-permute-done | bytes 786464 | tf_op jit(solution)/shard_map/ppermute | solution.py:26
  116.9 2.1 %collective-permute-done.11 = bf16[8,64,768]{2,1,0:T(8,128)(2,1)S(1)} collective-permute-done((bf16[8,64,768]{2,1,0:T(8,128)(2,1)S(1)}, bf16[8,64,768]{2,1,0:T(8,128)(2,1)S(1)}, u32[]{:S(2)}, u32[]{:S(2)}) %collective-permute-start.11) | collective-permute-done | bytes 786464 | tf_op jit(solution)/shard_map/ppermute | solution.py:26
  119.0 4.7 %feed_forward.3 = bf16[512,768]{1,0:T(8,128)(2,1)S(1)} custom-call(s32[4]{0:T(128)S(1)} %pad_add_fusion.me_ref, bf16[512,768]{1,0:T(8,128)(2,1)S(1)} %bitcast.20, bf16[768,768]{1,0:T(8,128)(2,1)S(1)} %copy-done.1, bf16[768,768]{1,0:T(8,128)(2,1)S(1)} %copy-done.3, bf16[960,768]{1,0:T(8,128)(2,1)S(1)} %collective-permute-done.3.piece, ...), custom_call_target="tpu_custom_call" | custom-call | tf_op jit(solution)/shard_map/feed_forward/pallas_call | solution.py:722
  123.9 4.9 %feed_forward.2 = f32[512,768]{1,0:T(8,128)S(1)} custom-call(s32[4]{0:T(128)S(1)} %pad_add_fusion.me_ref, bf16[512,768]{1,0:T(8,128)(2,1)S(1)} %bitcast.17, bf16[768,768]{1,0:T(8,128)(2,1)S(1)} %copy-done.1, bf16[768,768]{1,0:T(8,128)(2,1)S(1)} %copy-done.3, bf16[960,768]{1,0:T(8,128)(2,1)S(1)} %collective-permute-done.3.piece, ...), custom_call_target="tpu_custom_call" | custom-call | tf_op jit(solution)/shard_map/feed_forward/pallas_call | solution.py:722
  128.9 1.2 finish.1
  130.1 24.3 %all_to_all.27 = bf16[32,96,128]{2,1,0:T(8,128)(2,1)S(1)} all-to-all(bf16[32,96,128]{2,1,0:T(8,128)(2,1)S(1)} %finish.1), channel_id=1, replica_groups=mesh['plane'=4,'pair'=2,'chip'=2,'core'=2] {'plane','pair','chip','core'}, dimensions={0} | all-to-all | bytes 1572864 | tf_op jit(solution)/shard_map/all_to_all | solution.py:830
  155.1 1.3 copy.14
  (63 shorter events, 12.8 us)
Async XLA Ops:
  0.0 17.9 %collective-permute-start.1 = (bf16[16,192,128]{2,1,0:T(8,128)(2,1)}, bf16[16,192,128]{2,1,0:T(8,128)(2,1)S(1)}, u32[]{:S(2)}, u32[]{:S(2)}) collective-permute-start(bf16[16,192,128]{2,1,0:T(8,128)(2,1)} %stream), channel_id=1, source_target_pairs={{0,1},{1,0},{2,3},{3,2},{4,5},{5,4},{6,7},{7,6},{8,9},{9,8},{10,11... | collective-permute-start | bytes 2359304 | tf_op jit(solution)/shard_map/ppermute | solution.py:26
  0.5 21.2 %collective-permute-start = (bf16[16,192,128]{2,1,0:T(8,128)(2,1)}, bf16[16,192,128]{2,1,0:T(8,128)(2,1)}, u32[]{:S(2)}, u32[]{:S(2)}) collective-permute-start(bf16[16,192,128]{2,1,0:T(8,128)(2,1)} %stream), channel_id=1, source_target_pairs={{0,2},{2,0},{1,3},{3,1},{4,6},{6,4},{5,7},{7,5},{8,10},{10,8},{9,1... | collective-permute-start | bytes 2359304 | tf_op jit(solution)/shard_map/ppermute | solution.py:18
  3.0 1.3 copy-start
  4.3 1.3 copy-start.2
  5.6 1.2 copy-start.4
  6.7 1.0 copy-start.7
  7.7 1.0 copy-start.9
  8.7 2.8 %copy-start.6 = (bf16[16,192,128]{2,1,0:T(8,128)(2,1)S(1)}, bf16[16,192,128]{2,1,0:T(8,128)(2,1)}, u32[]{:S(2)}) copy-start(bf16[16,192,128]{2,1,0:T(8,128)(2,1)} %stream) | copy-start | bytes 2359300
  10.4 1.1 copy-start.18
  11.5 6.3 %copy-start.16 = (s32[128]{0:T(128)S(1)}, s32[128]{0:T(128)}, u32[]{:S(2)}) copy-start(s32[128]{0:T(128)} %label_ref.5) | copy-start | bytes 1540
  11.5 13.0 %copy-start.17 = (s32[4]{0:T(128)S(1)}, s32[4]{0:T(128)}, u32[]{:S(2)}) copy-start(s32[4]{0:T(128)} %tally_ref.5) | copy-start | bytes 52
  12.8 25.5 %all-to-all-start = ((bf16[32,96,128]{2,1,0:T(8,128)(2,1)}), bf16[32,96,128]{2,1,0:T(8,128)(2,1)S(1)}, u32[]{:S(2)}, u32[]{:S(2)}) async-start(bf16[32,96,128]{2,1,0:T(8,128)(2,1)} %spread.1), calls=%async_computation | async-start | bytes 1572864 | tf_op jit(solution)/shard_map/all_to_all | solution.py:781
  21.6 2.9 %collective-permute-start.2 = (bf16[16,192,128]{2,1,0:T(8,128)(2,1)}, bf16[16,192,128]{2,1,0:T(8,128)(2,1)S(1)}, u32[]{:S(2)}, u32[]{:S(2)}) collective-permute-start(bf16[16,192,128]{2,1,0:T(8,128)(2,1)} %collective-permute-done.far), channel_id=1, source_target_pairs={{0,1},{1,0},{2,3},{3,2},{4,5},{5,4},{6,7},{7,6},{8,9},{9,8},{10,11... | collective-permute-start | bytes 2359304 | tf_op jit(solution)/shard_map/ppermute | solution.py:26
  21.7 44.2 %collective-permute-start.3 = (bf16[960,768]{1,0:T(8,128)(2,1)}, bf16[960,768]{1,0:T(8,128)(2,1)S(1)}, u32[]{:S(2)}, u32[]{:S(2)}) collective-permute-start(bf16[960,768]{1,0:T(8,128)(2,1)} %copy-done.18), channel_id=1, source_target_pairs={{0,2},{2,0},{1,3},{3,1},{4,6},{6,4},{5,7},{7,5},{8,10},{10,8},{9,1... | collective-permute-start | bytes 4423688 | tf_op jit(solution)/shard_map/ppermute | solution.py:18
  24.5 1.2 copy-start.11
  25.7 1.1 copy-start.13
  38.4 25.4 %copy-start.15 = (bf16[16,192,128]{2,1,0:T(8,128)(2,1)S(1)}, bf16[16,192,128]{2,1,0:T(8,128)(2,1)}, u32[]{:S(2)}) copy-start(bf16[16,192,128]{2,1,0:T(8,128)(2,1)} %copy-done.14) | copy-start | bytes 2359300
  65.8 24.5 %all-to-all-start.3 = ((bf16[16,192,128]{2,1,0:T(8,128)(2,1)}), bf16[16,192,128]{2,1,0:T(8,128)(2,1)}, u32[]{:S(2)}, u32[]{:S(2)}) async-start(bf16[16,192,128]{2,1,0:T(8,128)(2,1)} %mix.1), calls=%async_computation.3 | async-start | bytes 1572864 | tf_op jit(solution)/shard_map/all_to_all | solution.py:804
  72.0 34.8 %collective-permute-start.8 = (bf16[768,768]{1,0:T(8,128)(2,1)}, bf16[768,768]{1,0:T(8,128)(2,1)S(1)}, u32[]{:S(2)}, u32[]{:S(2)}) collective-permute-start(bf16[768,768]{1,0:T(8,128)(2,1)} %slice.15), channel_id=1, source_target_pairs={{0,4},{4,0},{1,5},{5,1},{2,6},{6,2},{3,7},{7,3},{8,12},{12,8},{9,1... | collective-permute-start | bytes 3538952 | tf_op jit(solution)/shard_map/ppermute | solution.py:22
  73.9 33.4 %collective-permute-start.9 = (bf16[768,768]{1,0:T(8,128)(2,1)}, bf16[768,768]{1,0:T(8,128)(2,1)}, u32[]{:S(2)}, u32[]{:S(2)}) collective-permute-start(bf16[768,768]{1,0:T(8,128)(2,1)} %get-tuple-element.60), channel_id=1, source_target_pairs={{0,2},{2,0},{1,3},{3,1},{4,6},{6,4},{5,7},{7,5},{8,10},{10,8},{9,1... | collective-permute-start | bytes 3538952 | tf_op jit(solution)/shard_map/ppermute | solution.py:18
  90.3 1.0 copy-start.10
  94.9 1.8 %collective-permute-start.4 = (bf16[4,64,768]{2,1,0:T(8,128)(2,1)S(1)}, bf16[4,64,768]{2,1,0:T(8,128)(2,1)S(1)}, u32[]{:S(2)}, u32[]{:S(2)}) collective-permute-start(bf16[4,64,768]{2,1,0:T(8,128)(2,1)S(1)} %get-tuple-element.54), channel_id=1, source_target_pairs={{0,1},{1,0},{2,3},{3,2},{4,5},{5,4},{6,7},{7,6},{8,9},{9,8},{10,11... | collective-permute-start | bytes 1179656 | tf_op jit(solution)/shard_map/ppermute | solution.py:26
  95.0 2.3 %collective-permute-start.5 = (bf16[4,64,768]{2,1,0:T(8,128)(2,1)S(1)}, bf16[4,64,768]{2,1,0:T(8,128)(2,1)S(1)}, u32[]{:S(2)}, u32[]{:S(2)}) collective-permute-start(bf16[4,64,768]{2,1,0:T(8,128)(2,1)S(1)} %get-tuple-element.55), channel_id=1, source_target_pairs={{0,1},{1,0},{2,3},{3,2},{4,5},{5,4},{6,7},{7,6},{8,9},{9,8},{10,11... | collective-permute-start | bytes 1179656 | tf_op jit(solution)/shard_map/ppermute | solution.py:26
  97.3 10.0 %copy-start.5 = (bf16[3,192,768]{2,1,0:T(8,128)(2,1)S(1)}, bf16[3,192,768]{2,1,0:T(8,128)(2,1)}, u32[]{:S(2)}) copy-start(bf16[3,192,768]{2,1,0:T(8,128)(2,1)} %param.14) | copy-start | bytes 2654212
  97.3 10.0 %copy-start.8 = (bf16[192,768]{1,0:T(8,128)(2,1)S(1)}, bf16[192,768]{1,0:T(8,128)(2,1)}, u32[]{:S(2)}) copy-start(bf16[192,768]{1,0:T(8,128)(2,1)} %mixing.5) | copy-start | bytes 884740
  98.4 8.9 %collective-permute-start.6 = (bf16[4,64,768]{2,1,0:T(8,128)(2,1)S(1)}, bf16[4,64,768]{2,1,0:T(8,128)(2,1)S(1)}, u32[]{:S(2)}, u32[]{:S(2)}) collective-permute-start(bf16[4,64,768]{2,1,0:T(8,128)(2,1)S(1)} %get-tuple-element.58.own), channel_id=1, source_target_pairs={{0,1},{1,0},{2,3},{3,2},{4,5},{5,4},{6,7},{7,6},{8,9},{9,8},{10,11... | collective-permute-start | bytes 1179656 | tf_op jit(solution)/shard_map/ppermute | solution.py:26
  98.6 8.7 %collective-permute-start.7 = (bf16[4,64,768]{2,1,0:T(8,128)(2,1)S(1)}, bf16[4,64,768]{2,1,0:T(8,128)(2,1)S(1)}, u32[]{:S(2)}, u32[]{:S(2)}) collective-permute-start(bf16[4,64,768]{2,1,0:T(8,128)(2,1)S(1)} %get-tuple-element.59.own_later), channel_id=1, source_target_pairs={{0,1},{1,0},{2,3},{3,2},{4,5},{5,4},{6,7},{7,6},{8,9},{9,8},{10,11... | collective-permute-start | bytes 1179656 | tf_op jit(solution)/shard_map/ppermute | solution.py:26
  113.3 2.4 %collective-permute-start.10 = (bf16[8,64,768]{2,1,0:T(8,128)(2,1)S(1)}, bf16[8,64,768]{2,1,0:T(8,128)(2,1)S(1)}, u32[]{:S(2)}, u32[]{:S(2)}) collective-permute-start(bf16[8,64,768]{2,1,0:T(8,128)(2,1)S(1)} %get-tuple-element.65), channel_id=1, source_target_pairs={{0,1},{1,0},{2,3},{3,2},{4,5},{5,4},{6,7},{7,6},{8,9},{9,8},{10,11... | collective-permute-start | bytes 2359304 | tf_op jit(solution)/shard_map/ppermute | solution.py:26
  116.0 3.0 %copy-start.1 = (bf16[768,768]{1,0:T(8,128)(2,1)S(1)}, bf16[768,768]{1,0:T(8,128)(2,1)}, u32[]{:S(2)}) copy-start(bf16[768,768]{1,0:T(8,128)(2,1)} %expand.5) | copy-start | bytes 3538948
  116.0 3.0 %copy-start.3 = (bf16[768,768]{1,0:T(8,128)(2,1)S(1)}, bf16[768,768]{1,0:T(8,128)(2,1)}, u32[]{:S(2)}) copy-start(bf16[768,768]{1,0:T(8,128)(2,1)} %contract.5) | copy-start | bytes 3538948
  116.7 2.4 %collective-permute-start.11 = (bf16[8,64,768]{2,1,0:T(8,128)(2,1)S(1)}, bf16[8,64,768]{2,1,0:T(8,128)(2,1)S(1)}, u32[]{:S(2)}, u32[]{:S(2)}) collective-permute-start(bf16[8,64,768]{2,1,0:T(8,128)(2,1)S(1)} %fusion.3), channel_id=1, source_target_pairs={{0,1},{1,0},{2,3},{3,2},{4,5},{5,4},{6,7},{7,6},{8,9},{9,8},{10,11... | collective-permute-start | bytes 2359304 | tf_op jit(solution)/shard_map/ppermute | solution.py:26
  123.7 5.1 %collective-permute-start.12 = (bf16[8,64,768]{2,1,0:T(8,128)(2,1)S(1)}, bf16[8,64,768]{2,1,0:T(8,128)(2,1)S(1)}, u32[]{:S(2)}, u32[]{:S(2)}) collective-permute-start(bf16[8,64,768]{2,1,0:T(8,128)(2,1)S(1)} %bitcast.19), channel_id=1, source_target_pairs={{0,1},{1,0},{2,3},{3,2},{4,5},{5,4},{6,7},{7,6},{8,9},{9,8},{10,11... | collective-permute-start | bytes 2359304 | tf_op jit(solution)/shard_map/ppermute | solution.py:26
  (2 other events, 1.8 us)

commit v6 on v5

--- a/solution.py
+++ b/solution.py
@@ -9,7 +9,8 @@
 
 HEAD_SIZE = 64
 SWAP = [(0, 1), (1, 0)]
-ROWS = ("plane", "pair")
+ROWS = ("far", "plane", "pair")
+PARTS = 4
 BF16 = jnp.bfloat16
 F32 = jnp.float32
 
@@ -20,6 +21,10 @@
 
 def other_pair(value):
     return lax.ppermute(value, "pair", SWAP)
+
+
+def other_plane(value):
+    return lax.ppermute(value, "plane", SWAP)
 
 
 def other_core(value):
@@ -74,7 +79,7 @@
 
 def pack_kernel(me_ref, mixing, triple, vertical, expand, contract, pack, late, semaphores):
     quarter = mixing.shape[0]
-    half, pair = 2 * quarter, me_ref[3]
+    half, pair, plane = 2 * quarter, me_ref[3], me_ref[4]
 
     def move(index, source, start, count, target, place):
         return pltpu.make_async_copy(
@@ -86,28 +91,33 @@
         move(1, expand, half, half, late, 0),
         move(2, contract, half, half, late, half),
     ]
-    options = (
+    by_pair = (
         [
-            move(3, expand, 0, half, pack, 0),
+            move(3, expand, 0, quarter, pack, 0),
             move(4, triple, 0, quarter, pack, half),
             move(5, triple, quarter, quarter, pack, half + quarter),
         ],
         [
-            move(3, contract, 0, half, pack, 0),
+            move(3, contract, 0, quarter, pack, 0),
             move(4, triple, half, quarter, pack, half),
             move(5, vertical, 0, quarter, pack, half + quarter),
         ],
     )
+    by_plane = (
+        [move(6, expand, quarter, quarter, pack, quarter)],
+        [move(6, contract, quarter, quarter, pack, quarter)],
+    )
     for copy in fixed:
         copy.start()
-    for index, copies in enumerate(options):
-
-        @pl.when(pair == index)
-        def _(copies=copies):
-            for copy in copies:
-                copy.start()
-
-    for copy in fixed + options[0]:
+    for index in range(2):
+        for place, options in ((pair, by_pair), (plane, by_plane)):
+
+            @pl.when(place == index)
+            def _(copies=options[index]):
+                for copy in copies:
+                    copy.start()
+
+    for copy in fixed + by_pair[0] + by_plane[0]:
         copy.wait()
 
 
@@ -121,7 +131,7 @@
         ),
         in_specs=[IN_SMEM] + [IN_HBM] * 5,
         out_specs=(IN_HBM, IN_HBM),
-        scratch_shapes=[pltpu.SemaphoreType.DMA((6,))],
+        scratch_shapes=[pltpu.SemaphoreType.DMA((7,))],
         compiler_params=GRANT,
         name="pack",
     )(me, mixing, triple.reshape(-1, model), vertical, expand, contract)
@@ -362,9 +372,9 @@
     return jnp.transpose(mixed, (1, 0, 2, 3)).reshape(chips, lines * place, quarter)
 
 
-def project_kernel(
-    me_ref, blocks, mixing, piece, kept, sent, more, wide, first, second, semaphores
-):
+def project_kernel(me_ref, blocks, mixing, piece, kept, *refs):
+    sent = refs[:PARTS]
+    wide, first, second, semaphores = refs[PARTS:]
     chips, count, lanes = blocks.shape
     quarter, model = mixing.shape
     tokens = count * 2 // 3
@@ -407,8 +417,9 @@
         @pl.when(core == index)
         def _(index=index):
             kept[...] = halves[index]
-            sent[...] = halves[1 - index][: groups // 2].astype(BF16)
-            more[...] = halves[1 - index][groups // 2 :].astype(BF16)
+            for number, part in enumerate(sent):
+                lower = number * groups // PARTS
+                part[...] = halves[1 - index][lower : lower + groups // PARTS].astype(BF16)
 
 
 def project(blocks, mixing, piece, me, lines):
@@ -419,13 +430,10 @@
         out = (groups, count // 3, model)
         return pl.pallas_call(
             project_kernel,
-            out_shape=(
-                jax.ShapeDtypeStruct(out, F32),
-                jax.ShapeDtypeStruct((groups // 2, *out[1:]), BF16),
-                jax.ShapeDtypeStruct((groups // 2, *out[1:]), BF16),
-            ),
+            out_shape=(jax.ShapeDtypeStruct(out, F32),)
+            + (jax.ShapeDtypeStruct((groups // PARTS, *out[1:]), BF16),) * PARTS,
             in_specs=[IN_SMEM, IN_VMEM, IN_HBM, IN_HBM],
-            out_specs=(IN_VMEM, IN_VMEM, IN_VMEM),
+            out_specs=(IN_VMEM,) * (1 + PARTS),
             scratch_shapes=[pltpu.VMEM((2 * lanes, model), BF16)] * 3
             + [pltpu.SemaphoreType.DMA((6,))],
             compiler_params=GRANT,
@@ -436,19 +444,20 @@
     partial = jnp.einsum("gxctd,xde->cgte", values, weights, preferred_element_type=F32)
     kept = lax.dynamic_index_in_dim(partial, me[2], 0, False)
     sent = lax.dynamic_index_in_dim(partial, 1 - me[2], 0, False)
-    sent = sent.astype(BF16)
-    return kept, sent[: groups // 2], sent[groups // 2 :]
-
-
-def arrive_kernel(kept, got, more, blocks, normed, later, stream, tokens):
+    return kept, *jnp.split(sent.astype(BF16), PARTS)
+
+
+def arrive_kernel(kept, *refs):
+    got, blocks = refs[:PARTS], refs[PARTS]
+    normed, (stream, tokens) = refs[PARTS + 1 : 2 * PARTS + 1], refs[2 * PARTS + 1 :]
     groups, own, model = kept.shape
     places, rows, _ = stream.shape
     count, lanes = blocks.shape[1], blocks.shape[2]
     heads = blocks.shape[0] // groups
     parts = count // 3
     for group in range(groups):
-        source = got if group < groups // 2 else more
-        total = kept[group] + source[group % (groups // 2)].astype(F32)
+        each = groups // PARTS
+        total = kept[group] + got[group // each][group % each].astype(F32)
         features = []
         for head in range(heads):
             block = blocks[group * heads + head].astype(F32)
@@ -469,43 +478,43 @@
         values = values.astype(F32)
         centred = values - jnp.mean(values, axis=-1, keepdims=True)
         variance = jnp.mean(centred * centred, axis=-1, keepdims=True)
-        target = normed if place < places // 2 else later
-        target[place % (places // 2)] = (centred * lax.rsqrt(variance + 1e-05)).astype(BF16)
-
-
-def arrive(kept, got, more, blocks, place):
+        each = places // PARTS
+        normed[place // each][place % each] = (centred * lax.rsqrt(variance + 1e-05)).astype(BF16)
+
+
+def arrive(kept, got, blocks, place):
     groups, own, model = kept.shape
     rows = groups * own // place
     if place % 8 == 0:
         shape = jax.ShapeDtypeStruct((place, rows, model), BF16)
-        half = jax.ShapeDtypeStruct((place // 2, rows, model), BF16)
+        part = jax.ShapeDtypeStruct((place // PARTS, rows, model), BF16)
         return pl.pallas_call(
             arrive_kernel,
-            out_shape=(half, half, shape),
-            in_specs=[IN_VMEM] * 4,
-            out_specs=(IN_VMEM, IN_VMEM, IN_VMEM),
+            out_shape=(part,) * PARTS + (shape,),
+            in_specs=[IN_VMEM] * (2 + PARTS),
+            out_specs=(IN_VMEM,) * (1 + PARTS),
             scratch_shapes=[pltpu.VMEM((model // 128, groups * own, 128), F32)],
             compiler_params=GRANT,
             name="arrive",
-        )(kept, got, more, blocks)
+        )(kept, *got, blocks)
     heads = blocks.shape[0] // groups
     stream = jnp.transpose(blocks.reshape(groups, heads, own, -1), (0, 2, 1, 3))
     stream = stream.reshape(groups, own, model).astype(F32) + kept
-    stream += jnp.concatenate([got, more]).astype(F32)
+    stream += jnp.concatenate(got).astype(F32)
     stream = jnp.transpose(stream.reshape(rows, place, model), (1, 0, 2)).astype(BF16)
     normed = own_norm(stream, -1)
-    if place == 1:
-        return normed[:, : rows // 2], normed[:, rows // 2 :], stream
-    return normed[: place // 2], normed[place // 2 :], stream
+    return *jnp.split(normed, PARTS, axis=0 if place % PARTS == 0 else 1), stream
 
 
 def column_kernel(
-    lines, me_ref, starts_ref, own, own_later, other, other_later, triple, mixing, piece, rest,
-    kept, sent, normed, near, far, projected, mixed, semaphores,
+    lines, me_ref, starts_ref, *refs
 ):
+    tokens = refs[: 2 * PARTS]
+    triple, mixing, piece, rest, kept, sent = refs[2 * PARTS : 2 * PARTS + 6]
+    normed, near, far, projected, mixed, semaphores = refs[2 * PARTS + 6 :]
     quarter = mixing.shape[0]
     core, pair = me_ref[2], me_ref[3]
-    half = rest.shape[0] // 2
+    half = rest.shape[0]
 
     def spot(index):
         return far.at[pl.ds(pl.multiple_of(index * half, half), half)]
@@ -514,7 +523,7 @@
         (triple, near.at[pl.ds(0, 3 * quarter)]),
         (mixing, near.at[pl.ds(3 * quarter, quarter)]),
         (piece.at[pl.ds(half, half)], spot(pair)),
-        (rest.at[pl.ds(half, half)], spot(1 - pair)),
+        (rest, spot(1 - pair)),
     )
     copies = [
         pltpu.make_async_copy(source, target, semaphores.at[index])
@@ -524,10 +533,11 @@
         copy.start()
     places, both, model = normed.shape
     rows = both // 2
-    count, width = own.shape[:2]
-    for index, values in enumerate((own, own_later, other, other_later)):
-        start = index % 2 * count if count < places else 0
-        lower = index // 2 * rows + (0 if count < places else index % 2 * width)
+    count, width = tokens[0].shape[:2]
+    for index, values in enumerate(tokens):
+        part, lower = index % PARTS, index // PARTS * rows
+        start = part * count if count < places else 0
+        lower += 0 if count < places else part * width
         normed[start : start + count, lower : lower + width] = values[...]
     flat = normed[...].reshape(places * both, model)
 
@@ -605,7 +615,7 @@
             jax.ShapeDtypeStruct(shape, F32),
             jax.ShapeDtypeStruct(shape, BF16),
         ),
-        in_specs=[IN_SMEM] * 2 + [IN_VMEM] * 4 + [IN_HBM] * 4,
+        in_specs=[IN_SMEM] * 2 + [IN_VMEM] * (2 * PARTS) + [IN_HBM] * 4,
         out_specs=(IN_VMEM, IN_VMEM),
         scratch_shapes=[
             pltpu.VMEM((places, 2 * rows, model), BF16),
@@ -660,21 +670,28 @@
 
 
 def feed_forward_kernel(
-    me_ref, normed, expand, contract, piece, rest, late, out,
+    me_ref, normed, expand, contract, piece, pair_rest, plane_rest, late, out,
     near_expand, near_contract, far_expand, far_contract, hidden, semaphores,
 ):
     width = near_expand.shape[1]
-    half, pair = rest.shape[0] // 2, me_ref[3]
+    count, half = pair_rest.shape[0], width // 2
+    pair, plane = me_ref[3], me_ref[4]
 
     def move(source, start, count, target, place, index):
         return pltpu.make_async_copy(
             source.at[pl.ds(start, count)], target.at[pl.ds(place, count)], semaphores.at[index]
         )
 
-    def shared(first, second):
+    def by_pair(first, second):
         return [
-            move(piece, 0, half, first, 0, 4),
-            move(rest, 0, half, second, 0, 5),
+            move(piece, 0, count, first, 0, 4),
+            move(pair_rest, 0, count, second, 0, 5),
+        ]
+
+    def by_plane(first, second):
+        return [
+            move(piece, count, count, first, count, 6),
+            move(plane_rest, 0, count, second, count, 7),
         ]
 
     copies = [
@@ -685,16 +702,17 @@
     ]
     for copy in copies:
         copy.start()
-
-    @pl.when(pair == 0)
-    def _():
-        for copy in shared(far_expand, far_contract):
-            copy.start()
-
-    @pl.when(pair != 0)
-    def _():
-        for copy in shared(far_contract, far_expand):
-            copy.start()
+    for place, moves in ((pair, by_pair), (plane, by_plane)):
+
+        @pl.when(place == 0)
+        def _(moves=moves):
+            for copy in moves(far_expand, far_contract):
+                copy.start()
+
+        @pl.when(place != 0)
+        def _(moves=moves):
+            for copy in moves(far_contract, far_expand):
+                copy.start()
 
     tile = width // 3
     values = normed[...]
@@ -705,7 +723,7 @@
             up = 0.5 * up * (1.0 + lax.erf(up * 2.0**-0.5))
             hidden[:, lower + start : lower + start + tile] = up.astype(BF16)
 
-    copies += shared(far_expand, far_contract)
+    copies += by_pair(far_expand, far_contract) + by_plane(far_expand, far_contract)
     copies[0].wait()
     raise_by(near_expand, 0)
     for copy in copies[1:]:
@@ -722,7 +740,7 @@
     result = pl.pallas_call(
         feed_forward_kernel,
         out_shape=jax.ShapeDtypeStruct((tokens, model), kind),
-        in_specs=[IN_SMEM, IN_VMEM] + [IN_HBM] * 5,
+        in_specs=[IN_SMEM, IN_VMEM] + [IN_HBM] * 6,
         out_specs=IN_VMEM,
         scratch_shapes=[
             pltpu.VMEM((model, width), BF16),
@@ -730,7 +748,7 @@
             pltpu.VMEM((model, width), BF16),
             pltpu.VMEM((model, width), BF16),
             pltpu.VMEM((tokens, 2 * width), BF16),
-            pltpu.SemaphoreType.DMA((6,)),
+            pltpu.SemaphoreType.DMA((8,)),
         ],
         compiler_params=GRANT,
         name="feed_forward",
@@ -764,7 +782,8 @@
     label, tally = line_group_label, group_site_tally
     families = tally.shape[0]
     starts = jnp.sum(label[:, None] < jnp.arange(families + 1), axis=0, dtype=jnp.int32)
-    me = jnp.stack([lax.axis_index(ROWS), chip, core, pair]).astype(jnp.int32)
+    plane = lax.axis_index("plane")
+    me = jnp.stack([lax.axis_index(ROWS), chip, core, pair, plane]).astype(jnp.int32)
 
     across = other_chip(alignment_embedding)
     near = other_core(alignment_embedding)
@@ -799,14 +818,15 @@
 
     blocks, piece, late = lax.optimization_barrier((blocks, piece, late))
     half = expand_matrix.shape[0] // 2
-    rest = other_pair(piece[: 2 * half])
+    column_rest = other_pair(piece[half : 2 * half])
+    feed_rest = (other_pair(piece[:quarter]), other_plane(piece[quarter:half]))
     late = other_chip(late)
     blocks = lax.all_to_all(blocks, ROWS + ("chip",), 0, 0, tiled=True)
     kept, *sent = project(blocks, horizontal_mixing_matrix, piece, me, lines)
     got = [other_core(part) for part in sent]
-    *normed, after_row = arrive(kept, *got, stream, place)
+    got, column_rest = lax.optimization_barrier((got, column_rest))
+    *normed, after_row = arrive(kept, got, stream, place)
     other = [other_core(part) for part in normed]
-    other, rest, late = lax.optimization_barrier((other, rest, late))
 
     kept, sent = column(
         normed,
@@ -814,15 +834,16 @@
         vertical_triple_matrix,
         vertical_mixing_matrix,
         piece,
-        rest,
+        column_rest,
         plan,
         own,
         after_row.shape,
     )
+    sent, feed_rest, late = lax.optimization_barrier((sent, feed_rest, late))
     after_col = core_sum(after_row, kept, sent)
 
     normed = own_norm(after_col, -1)
-    weights = (expand_matrix, contract_matrix, (piece, rest, late), me)
+    weights = (expand_matrix, contract_matrix, (piece, *feed_rest, late), me)
     kept = feed_forward(normed, *weights, F32)
     sent = feed_forward(other_core(normed), *weights, BF16)
     blocks = finish(after_col, kept, other_core(sent), row_groups, quarter)
@@ -838,8 +859,8 @@
 
 
 def solution(mesh):
-    planes = mesh.shape["rows"] // 2
-    split = Mesh(mesh.devices.reshape(planes, 2, 2, 2), ROWS + ("chip", "core"))
+    far = mesh.shape["rows"] // 4
+    split = Mesh(mesh.devices.reshape(far, 2, 2, 2, 2), ROWS + ("chip", "core"))
     heads = ("chip", "core")
     placed = (
         P(ROWS, heads, None),

time: 157 us -> 154 us (0.981)
  waiting for transfers between devices: 35.7 us -> 26.9 us
  starting transfers between devices: 20.7 us -> 26.9 us
    ppermute x1 -> x2, waiting for transfers between devices: 7.8 us -> 0.01 us  [other_pair(): return lax.ppermute(value, 'pair', SWAP)]
    all_to_all x1, waiting for transfers between devices: 3.26 us -> 0.58 us  [shards(): stream = lax.all_to_all(stream, ROWS + ('chip', 'core'), 0, 0, tiled=True)]
    ppermute x1 -> x2, starting transfers between devices: 1.88 us -> 3.65 us  [other_pair(): return lax.ppermute(value, 'pair', SWAP)]
    ppermute x0 -> x1, starting transfers between devices: none -> 1.72 us  [other_plane(): return lax.ppermute(value, 'plane', SWAP)]
    ppermute x9 -> x13, waiting for transfers between devices: 6.21 us -> 6.59 us  [other_core(): return lax.ppermute(value, 'core', SWAP)]
    unnamed x38 -> x40, local copies, waits for them, and re-layouts: 11.8 us -> 11.8 us
  transfers between devices with their start and end apart: 15 -> 21, of which waited for: 9 -> 11; matrix products, arithmetic and copies ran while one was open for 1% -> 1% of each run, Pallas kernels for 15% -> 19%
where the time goes in v6:
time: 154 us
  blocking collectives  48.9 us (32%)
  Pallas kernels  34.9 us (23%)
  starting transfers between devices  26.9 us (17%)
  waiting for transfers between devices  26.9 us (17%)
  local copies, waits for them, and re-layouts  14.5 us (9%)
    all_to_all x1, blocking collectives, shards(): blocks = lax.all_to_all(blocks, ROWS + ('chip', 'core'), 0, 0, tiled=True)  23 us
    all_to_all x1, waiting for transfers between devices, shards(): blocks = lax.all_to_all(blocks, ROWS + ('chip',), 0, 0, tiled=True)  15.2 us
    all_to_all x1, blocking collectives, shards(): parts = lax.all_to_all(shared, ROWS, 0, 0, tiled=True)  15.1 us
    unnamed x40, local copies, waits for them, and re-layouts  11.8 us
    all_to_all x1, blocking collectives, shards(): shared = lax.all_to_all(tie(parts, plan), ROWS, 0, 0, tiled=True)  10.7 us
    pallas_call x2, Pallas kernels, feed_forward(): pl.pallas_call(feed_forward_kernel, out_shape=jax.ShapeDtypeStruct((token...  10.1 us
    ppermute x3, starting transfers between devices, other_chip(): return lax.ppermute(value, 'chip', SWAP)  8.35 us
    pallas_call x1, Pallas kernels, row_front(): pl.pallas_call(functools.partial(row_front_kernel, lines), grid=(lines //...  7.39 us
  transfers between devices with their start and end apart: 21, of which 11 were waited for; matrix products, arithmetic and copies ran while one was open for 1% of the time, Pallas kernels for 19%

profile of v6, /device:TPU:0, one launch (start us, length us, event | category | flops | bytes accessed | tf_op | source)
XLA Modules:
  0.0 153.6 jit_solution(12964190320119073890)
XLA Ops:
  0.0 2.9 %collective-permute-start = (bf16[16,192,128]{2,1,0:T(8,128)(2,1)}, bf16[16,192,128]{2,1,0:T(8,128)(2,1)}, u32[]{:S(2)}, u32[]{:S(2)}) collective-permute-start(bf16[16,192,128]{2,1,0:T(8,128)(2,1)} %stream), channel_id=1, source_target_pairs={{0,2},{2,0},{1,3},{3,1},{4,6},{6,4},{5,7},{7,5},{8,10},{10,8},{9,1... | collective-permute-start | bytes 2359304 | tf_op jit(solution)/shard_map/ppermute | solution.py:19
  3.0 1.3 copy-done
  4.3 1.3 copy-done.2
  5.6 1.2 copy-done.4
  8.7 1.2 pack.1
  9.9 1.1 copy-done.18
  11.0 1.3 spread.1
  12.3 5.0 %all-to-all-start = ((bf16[32,96,128]{2,1,0:T(8,128)(2,1)}), bf16[32,96,128]{2,1,0:T(8,128)(2,1)S(1)}, u32[]{:S(2)}, u32[]{:S(2)}) async-start(bf16[32,96,128]{2,1,0:T(8,128)(2,1)} %spread.1), calls=%async_computation | async-start | bytes 1572864 | tf_op jit(solution)/shard_map/all_to_all | solution.py:800
  17.5 4.5 %collective-permute-done.far = bf16[16,192,128]{2,1,0:T(8,128)(2,1)} collective-permute-done((bf16[16,192,128]{2,1,0:T(8,128)(2,1)}, bf16[16,192,128]{2,1,0:T(8,128)(2,1)}, u32[]{:S(2)}, u32[]{:S(2)}) %collective-permute-start) | collective-permute-done | bytes 786464 | tf_op jit(solution)/shard_map/ppermute | solution.py:19
  22.8 4.0 %collective-permute-start.3 = (bf16[960,768]{1,0:T(8,128)(2,1)}, bf16[960,768]{1,0:T(8,128)(2,1)S(1)}, u32[]{:S(2)}, u32[]{:S(2)}) collective-permute-start(bf16[960,768]{1,0:T(8,128)(2,1)} %copy-done.18), channel_id=1, source_target_pairs={{0,2},{2,0},{1,3},{3,1},{4,6},{6,4},{5,7},{7,5},{8,10},{10,8},{9,1... | collective-permute-start | bytes 4423688 | tf_op jit(solution)/shard_map/ppermute | solution.py:19
  26.8 1.2 copy-done.11
  28.0 1.1 copy-done.13
  29.1 7.4 %row_front.1 = (bf16[8,6,16,128]{3,2,1,0:T(8,128)(2,1)S(1)}, bf16[6,128,128]{2,1,0:T(8,128)(2,1)S(1)}, bf16[16,192,128]{2,1,0:T(8,128)(2,1)S(1)}) custom-call(s32[5]{0:T(128)S(1)} %stack.23.me_ref, s32[128]{0:T(128)S(1)} %copy-done.16, s32[5]{0:T(128)S(1)} %convert_reduce_fusion.1.starts_ref, s32[4]{0:T(128)S(1)} %copy-done.17, ...), custom_call_target="tpu_custom_call" | custom-call | tf_op jit(solution)/shard_map/row_front/pallas_call | solution.py:253
  38.0 15.1 %all_to_all.25.parts = bf16[8,6,16,128]{3,2,1,0:T(8,128)(2,1)S(1)} all-to-all(bf16[8,6,16,128]{3,2,1,0:T(8,128)(2,1)S(1)} %get-tuple-element.55), channel_id=1, replica_groups=mesh['far'=2,'plane'=2,'pair'=2,'chip'=2,'core'=2] {'far','plane','pair'}, dimensions={0} | all-to-all | bytes 393216 | tf_op jit(solution)/shard_map/all_to_all | solution.py:815
  54.0 10.7 %all_to_all.26.shared = bf16[8,6,16,128]{3,2,1,0:T(8,128)(2,1)S(1)} all-to-all(bf16[8,6,16,128]{3,2,1,0:T(8,128)(2,1)S(1)} %tie.1), channel_id=1, replica_groups=mesh['far'=2,'plane'=2,'pair'=2,'chip'=2,'core'=2] {'far','plane','pair'}, dimensions={0} | all-to-all | bytes 393216 | tf_op jit(solution)/shard_map/all_to_all | solution.py:816
  64.8 2.1 %mix.1 = bf16[16,192,128]{2,1,0:T(8,128)(2,1)} custom-call(s32[5]{0:T(128)S(1)} %stack.23.me_ref, s32[128]{0:T(128)S(1)} %copy-done.16, s32[5]{0:T(128)S(1)} %convert_reduce_fusion.1.starts_ref, s32[4]{0:T(128)S(1)} %copy-done.17, bf16[8,6,16,128]{3,2,1,0:T(8,128)(2,1)S(1)} %all_to_all.26.shared, bf16[6,128,128]{2,1,0:T(8,128)(2,1)S(1)} %get-tuple-element.56.inner, ...), custom_call_target="tpu_custom_call" | custom-call | tf_op jit(solution)/shard_map/mix/pallas_call | solution.py:355
  66.9 5.1 %all-to-all-start.3 = ((bf16[16,192,128]{2,1,0:T(8,128)(2,1)}), bf16[16,192,128]{2,1,0:T(8,128)(2,1)}, u32[]{:S(2)}, u32[]{:S(2)}) async-start(bf16[16,192,128]{2,1,0:T(8,128)(2,1)} %mix.1), calls=%async_computation.3 | async-start | bytes 1572864 | tf_op jit(solution)/shard_map/all_to_all | solution.py:824
  72.8 1.9 %collective-permute-start.8 = (bf16[384,768]{1,0:T(8,128)(2,1)}, bf16[384,768]{1,0:T(8,128)(2,1)}, u32[]{:S(2)}, u32[]{:S(2)}) collective-permute-start(bf16[384,768]{1,0:T(8,128)(2,1)} %slice.21), channel_id=1, source_target_pairs={{0,4},{4,0},{1,5},{5,1},{2,6},{6,2},{3,7},{7,3},{8,12},{12,8},{9,1... | collective-permute-start | bytes 1769480 | tf_op jit(solution)/shard_map/ppermute | solution.py:23
  74.7 1.5 collective-permute-start.15
  76.2 15.2 %all-to-all-done.3.blocks = bf16[16,192,128]{2,1,0:T(8,128)(2,1)} async-done(((bf16[16,192,128]{2,1,0:T(8,128)(2,1)}), bf16[16,192,128]{2,1,0:T(8,128)(2,1)}, u32[]{:S(2)}, u32[]{:S(2)}) %all-to-all-start.3) | async-done | bytes 786464 | tf_op jit(solution)/shard_map/all_to_all | solution.py:824
  92.3 3.6 %project.1 = (f32[8,64,768]{2,1,0:T(8,128)S(1)}, bf16[2,64,768]{2,1,0:T(8,128)(2,1)S(1)}, bf16[2,64,768]{2,1,0:T(8,128)(2,1)S(1)}, bf16[2,64,768]{2,1,0:T(8,128)(2,1)S(1)}, bf16[2,64,768]{2,1,0:T(8,128)(2,1)S(1)}) custom-call(s32[5]{0:T(128)S(1)} %stack.23.me_ref, bf16[16,192,128]{2,1,0:T(8,128)(2,1)} %all-to-all-done.3.blocks, ...), custom_call_target="tpu_custom_call" | custom-call | tf_op jit(solution)/shard_map/project/pallas_call | solution.py:431
  98.3 1.1 arrive.1
  100.0 1.8 %collective-permute-start.13 = (bf16[192,768]{1,0:T(8,128)(2,1)S(1)}, bf16[192,768]{1,0:T(8,128)(2,1)S(1)}, u32[]{:S(2)}, u32[]{:S(2)}) collective-permute-start(bf16[192,768]{1,0:T(8,128)(2,1)S(1)} %get-tuple-element.88), channel_id=1, source_target_pairs={{0,4},{4,0},{1,5},{5,1},{2,6},{6,2},{3,7},{7,3},{8,12},{12,8},{9,1... | collective-permute-start | bytes 884744 | tf_op jit(solution)/shard_map/ppermute | solution.py:23
  101.8 1.7 %collective-permute-start.14 = (bf16[192,768]{1,0:T(8,128)(2,1)S(1)}, bf16[192,768]{1,0:T(8,128)(2,1)S(1)}, u32[]{:S(2)}, u32[]{:S(2)}) collective-permute-start(bf16[192,768]{1,0:T(8,128)(2,1)S(1)} %get-tuple-element.87), channel_id=1, source_target_pairs={{0,8},{8,0},{1,9},{9,1},{2,10},{10,2},{3,11},{11,3},{4,12},{12,4},... | collective-permute-start | bytes 884744 | tf_op jit(solution)/shard_map/ppermute | solution.py:27
  105.3 5.9 %column.1 = (f32[8,64,768]{2,1,0:T(8,128)S(1)}, bf16[8,64,768]{2,1,0:T(8,128)(2,1)S(1)}) custom-call(s32[5]{0:T(128)S(1)} %stack.23.me_ref, s32[5]{0:T(128)S(1)} %convert_reduce_fusion.1.starts_ref, bf16[2,64,768]{2,1,0:T(8,128)(2,1)S(1)} %get-tuple-element.73.refs_0_, bf16[2,64,768]{2,1,0:T(8,128)(2,1)S(1)} %get-tuple-element.74.refs_1_, ...), custom_call_target="tpu_custom_call" | custom-call | tf_op jit(solution)/shard_map/column/pallas_call | solution.py:612
  111.5 2.1 %collective-permute-done.16 = bf16[8,64,768]{2,1,0:T(8,128)(2,1)S(1)} collective-permute-done((bf16[8,64,768]{2,1,0:T(8,128)(2,1)S(1)}, bf16[8,64,768]{2,1,0:T(8,128)(2,1)S(1)}, u32[]{:S(2)}, u32[]{:S(2)}) %collective-permute-start.16) | collective-permute-done | bytes 786464 | tf_op jit(solution)/shard_map/ppermute | solution.py:31
  114.9 2.1 %collective-permute-done.17 = bf16[8,64,768]{2,1,0:T(8,128)(2,1)S(1)} collective-permute-done((bf16[8,64,768]{2,1,0:T(8,128)(2,1)S(1)}, bf16[8,64,768]{2,1,0:T(8,128)(2,1)S(1)}, u32[]{:S(2)}, u32[]{:S(2)}) %collective-permute-start.17) | collective-permute-done | bytes 786464 | tf_op jit(solution)/shard_map/ppermute | solution.py:31
  116.9 5.0 %feed_forward.3 = bf16[512,768]{1,0:T(8,128)(2,1)S(1)} custom-call(s32[5]{0:T(128)S(1)} %stack.23.me_ref, bf16[512,768]{1,0:T(8,128)(2,1)S(1)} %bitcast.21, bf16[768,768]{1,0:T(8,128)(2,1)S(1)} %copy-done.1, bf16[768,768]{1,0:T(8,128)(2,1)S(1)} %copy-done.3, bf16[960,768]{1,0:T(8,128)(2,1)S(1)} %collective-permute-done.3.piece.refs_10_, ...), custom_call_target="tpu_custom_call" | custom-call | tf_op jit(solution)/shard_map/feed_forward/pallas_call | solution.py:740
  122.2 5.2 %feed_forward.2 = f32[512,768]{1,0:T(8,128)S(1)} custom-call(s32[5]{0:T(128)S(1)} %stack.23.me_ref, bf16[512,768]{1,0:T(8,128)(2,1)S(1)} %bitcast.18, bf16[768,768]{1,0:T(8,128)(2,1)S(1)} %copy-done.1, bf16[768,768]{1,0:T(8,128)(2,1)S(1)} %copy-done.3, bf16[960,768]{1,0:T(8,128)(2,1)S(1)} %collective-permute-done.3.piece.refs_10_, ...), custom_call_target="tpu_custom_call" | custom-call | tf_op jit(solution)/shard_map/feed_forward/pallas_call | solution.py:740
  127.4 1.2 finish.1
  128.6 23.0 %all_to_all.27 = bf16[32,96,128]{2,1,0:T(8,128)(2,1)S(1)} all-to-all(bf16[32,96,128]{2,1,0:T(8,128)(2,1)S(1)} %finish.1), channel_id=1, replica_groups=mesh['far'=2,'plane'=2,'pair'=2,'chip'=2,'core'=2] {'far','plane','pair'..., dimensions={0} | all-to-all | bytes 1572864 | tf_op jit(solution)/shard_map/all_to_all | solution.py:851
  152.3 1.3 copy.14
  (78 shorter events, 14.5 us)
Async XLA Ops:
  0.0 22.0 %collective-permute-start = (bf16[16,192,128]{2,1,0:T(8,128)(2,1)}, bf16[16,192,128]{2,1,0:T(8,128)(2,1)}, u32[]{:S(2)}, u32[]{:S(2)}) collective-permute-start(bf16[16,192,128]{2,1,0:T(8,128)(2,1)} %stream), channel_id=1, source_target_pairs={{0,2},{2,0},{1,3},{3,1},{4,6},{6,4},{5,7},{7,5},{8,10},{10,8},{9,1... | collective-permute-start | bytes 2359304 | tf_op jit(solution)/shard_map/ppermute | solution.py:19
  2.9 19.0 %collective-permute-start.1 = (bf16[16,192,128]{2,1,0:T(8,128)(2,1)}, bf16[16,192,128]{2,1,0:T(8,128)(2,1)S(1)}, u32[]{:S(2)}, u32[]{:S(2)}) collective-permute-start(bf16[16,192,128]{2,1,0:T(8,128)(2,1)} %stream), channel_id=1, source_target_pairs={{0,1},{1,0},{2,3},{3,2},{4,5},{5,4},{6,7},{7,6},{8,9},{9,8},{10,11... | collective-permute-start | bytes 2359304 | tf_op jit(solution)/shard_map/ppermute | solution.py:31
  3.0 1.3 copy-start
  4.3 1.3 copy-start.2
  8.7 2.3 %copy-start.6 = (bf16[16,192,128]{2,1,0:T(8,128)(2,1)S(1)}, bf16[16,192,128]{2,1,0:T(8,128)(2,1)}, u32[]{:S(2)}) copy-start(bf16[16,192,128]{2,1,0:T(8,128)(2,1)} %stream) | copy-start | bytes 2359300
  9.9 2.5 %copy-start.19 = (bf16[768,768]{1,0:T(8,128)(2,1)}, bf16[768,768]{1,0:T(8,128)(2,1)S(1)}, u32[]{:S(2)}) copy-start(bf16[768,768]{1,0:T(8,128)(2,1)S(1)} %get-tuple-element.80) | copy-start | bytes 3538948
  11.0 6.4 %copy-start.16 = (s32[128]{0:T(128)S(1)}, s32[128]{0:T(128)}, u32[]{:S(2)}) copy-start(s32[128]{0:T(128)} %label_ref.5) | copy-start | bytes 1540
  11.0 15.8 %copy-start.17 = (s32[4]{0:T(128)S(1)}, s32[4]{0:T(128)}, u32[]{:S(2)}) copy-start(s32[4]{0:T(128)} %tally_ref.5) | copy-start | bytes 52
  12.3 25.7 %all-to-all-start = ((bf16[32,96,128]{2,1,0:T(8,128)(2,1)}), bf16[32,96,128]{2,1,0:T(8,128)(2,1)S(1)}, u32[]{:S(2)}, u32[]{:S(2)}) async-start(bf16[32,96,128]{2,1,0:T(8,128)(2,1)} %spread.1), calls=%async_computation | async-start | bytes 1572864 | tf_op jit(solution)/shard_map/all_to_all | solution.py:800
  22.8 4.0 %collective-permute-start.2 = (bf16[16,192,128]{2,1,0:T(8,128)(2,1)}, bf16[16,192,128]{2,1,0:T(8,128)(2,1)S(1)}, u32[]{:S(2)}, u32[]{:S(2)}) collective-permute-start(bf16[16,192,128]{2,1,0:T(8,128)(2,1)} %collective-permute-done.far), channel_id=1, source_target_pairs={{0,1},{1,0},{2,3},{3,2},{4,5},{5,4},{6,7},{7,6},{8,9},{9,8},{10,11... | collective-permute-start | bytes 2359304 | tf_op jit(solution)/shard_map/ppermute | solution.py:31
  22.8 44.0 %collective-permute-start.3 = (bf16[960,768]{1,0:T(8,128)(2,1)}, bf16[960,768]{1,0:T(8,128)(2,1)S(1)}, u32[]{:S(2)}, u32[]{:S(2)}) collective-permute-start(bf16[960,768]{1,0:T(8,128)(2,1)} %copy-done.18), channel_id=1, source_target_pairs={{0,2},{2,0},{1,3},{3,1},{4,6},{6,4},{5,7},{7,5},{8,10},{10,8},{9,1... | collective-permute-start | bytes 4423688 | tf_op jit(solution)/shard_map/ppermute | solution.py:19
  38.0 26.8 %copy-start.15 = (bf16[16,192,128]{2,1,0:T(8,128)(2,1)S(1)}, bf16[16,192,128]{2,1,0:T(8,128)(2,1)}, u32[]{:S(2)}) copy-start(bf16[16,192,128]{2,1,0:T(8,128)(2,1)} %copy-done.14) | copy-start | bytes 2359300
  66.9 24.5 %all-to-all-start.3 = ((bf16[16,192,128]{2,1,0:T(8,128)(2,1)}), bf16[16,192,128]{2,1,0:T(8,128)(2,1)}, u32[]{:S(2)}, u32[]{:S(2)}) async-start(bf16[16,192,128]{2,1,0:T(8,128)(2,1)} %mix.1), calls=%async_computation.3 | async-start | bytes 1572864 | tf_op jit(solution)/shard_map/all_to_all | solution.py:824
  72.8 23.8 %collective-permute-start.8 = (bf16[384,768]{1,0:T(8,128)(2,1)}, bf16[384,768]{1,0:T(8,128)(2,1)}, u32[]{:S(2)}, u32[]{:S(2)}) collective-permute-start(bf16[384,768]{1,0:T(8,128)(2,1)} %slice.21), channel_id=1, source_target_pairs={{0,4},{4,0},{1,5},{5,1},{2,6},{6,2},{3,7},{7,3},{8,12},{12,8},{9,1... | collective-permute-start | bytes 1769480 | tf_op jit(solution)/shard_map/ppermute | solution.py:23
  74.7 36.5 %collective-permute-start.15 = (bf16[768,768]{1,0:T(8,128)(2,1)}, bf16[768,768]{1,0:T(8,128)(2,1)S(1)}, u32[]{:S(2)}, u32[]{:S(2)}) collective-permute-start(bf16[768,768]{1,0:T(8,128)(2,1)} %copy-done.19), channel_id=1, source_target_pairs={{0,2},{2,0},{1,3},{3,1},{4,6},{6,4},{5,7},{7,5},{8,10},{10,8},{9,1... | collective-permute-start | bytes 3538952 | tf_op jit(solution)/shard_map/ppermute | solution.py:19
  96.0 1.5 collective-permute-start.4
  96.0 1.7 %collective-permute-start.5 = (bf16[2,64,768]{2,1,0:T(8,128)(2,1)S(1)}, bf16[2,64,768]{2,1,0:T(8,128)(2,1)S(1)}, u32[]{:S(2)}, u32[]{:S(2)}) collective-permute-start(bf16[2,64,768]{2,1,0:T(8,128)(2,1)S(1)} %get-tuple-element.64), channel_id=1, source_target_pairs={{0,1},{1,0},{2,3},{3,2},{4,5},{5,4},{6,7},{7,6},{8,9},{9,8},{10,11... | collective-permute-start | bytes 589832 | tf_op jit(solution)/shard_map/ppermute | solution.py:31
  96.5 1.5 collective-permute-start.6
  96.6 1.7 %collective-permute-start.7 = (bf16[2,64,768]{2,1,0:T(8,128)(2,1)S(1)}, bf16[2,64,768]{2,1,0:T(8,128)(2,1)S(1)}, u32[]{:S(2)}, u32[]{:S(2)}) collective-permute-start(bf16[2,64,768]{2,1,0:T(8,128)(2,1)S(1)} %get-tuple-element.66), channel_id=1, source_target_pairs={{0,1},{1,0},{2,3},{3,2},{4,5},{5,4},{6,7},{7,6},{8,9},{9,8},{10,11... | collective-permute-start | bytes 589832 | tf_op jit(solution)/shard_map/ppermute | solution.py:31
  98.3 6.9 %copy-start.5 = (bf16[3,192,768]{2,1,0:T(8,128)(2,1)S(1)}, bf16[3,192,768]{2,1,0:T(8,128)(2,1)}, u32[]{:S(2)}) copy-start(bf16[3,192,768]{2,1,0:T(8,128)(2,1)} %param.14) | copy-start | bytes 2654212
  98.3 6.9 %copy-start.10 = (bf16[192,768]{1,0:T(8,128)(2,1)S(1)}, bf16[192,768]{1,0:T(8,128)(2,1)}, u32[]{:S(2)}) copy-start(bf16[192,768]{1,0:T(8,128)(2,1)} %refs_9_.1) | copy-start | bytes 884740
  99.4 4.1 %collective-permute-start.10 = (bf16[2,64,768]{2,1,0:T(8,128)(2,1)S(1)}, bf16[2,64,768]{2,1,0:T(8,128)(2,1)S(1)}, u32[]{:S(2)}, u32[]{:S(2)}) collective-permute-start(bf16[2,64,768]{2,1,0:T(8,128)(2,1)S(1)} %get-tuple-element.74.refs_1_), channel_id=1, source_target_pairs={{0,1},{1,0},{2,3},{3,2},{4,5},{5,4},{6,7},{7,6},{8,9},{9,8},{10,11... | collective-permute-start | bytes 589832 | tf_op jit(solution)/shard_map/ppermute | solution.py:31
  99.7 3.8 %collective-permute-start.11 = (bf16[2,64,768]{2,1,0:T(8,128)(2,1)S(1)}, bf16[2,64,768]{2,1,0:T(8,128)(2,1)S(1)}, u32[]{:S(2)}, u32[]{:S(2)}) collective-permute-start(bf16[2,64,768]{2,1,0:T(8,128)(2,1)S(1)} %get-tuple-element.75.refs_2_), channel_id=1, source_target_pairs={{0,1},{1,0},{2,3},{3,2},{4,5},{5,4},{6,7},{7,6},{8,9},{9,8},{10,11... | collective-permute-start | bytes 589832 | tf_op jit(solution)/shard_map/ppermute | solution.py:31
  100.0 11.1 %collective-permute-start.13 = (bf16[192,768]{1,0:T(8,128)(2,1)S(1)}, bf16[192,768]{1,0:T(8,128)(2,1)S(1)}, u32[]{:S(2)}, u32[]{:S(2)}) collective-permute-start(bf16[192,768]{1,0:T(8,128)(2,1)S(1)} %get-tuple-element.88), channel_id=1, source_target_pairs={{0,4},{4,0},{1,5},{5,1},{2,6},{6,2},{3,7},{7,3},{8,12},{12,8},{9,1... | collective-permute-start | bytes 884744 | tf_op jit(solution)/shard_map/ppermute | solution.py:23
  101.8 9.4 %collective-permute-start.14 = (bf16[192,768]{1,0:T(8,128)(2,1)S(1)}, bf16[192,768]{1,0:T(8,128)(2,1)S(1)}, u32[]{:S(2)}, u32[]{:S(2)}) collective-permute-start(bf16[192,768]{1,0:T(8,128)(2,1)S(1)} %get-tuple-element.87), channel_id=1, source_target_pairs={{0,8},{8,0},{1,9},{9,1},{2,10},{10,2},{3,11},{11,3},{4,12},{12,4},... | collective-permute-start | bytes 884744 | tf_op jit(solution)/shard_map/ppermute | solution.py:27
  103.5 1.4 collective-permute-start.12
  103.5 1.7 %collective-permute-start.9 = (bf16[2,64,768]{2,1,0:T(8,128)(2,1)S(1)}, bf16[2,64,768]{2,1,0:T(8,128)(2,1)S(1)}, u32[]{:S(2)}, u32[]{:S(2)}) collective-permute-start(bf16[2,64,768]{2,1,0:T(8,128)(2,1)S(1)} %get-tuple-element.73.refs_0_), channel_id=1, source_target_pairs={{0,1},{1,0},{2,3},{3,2},{4,5},{5,4},{6,7},{7,6},{8,9},{9,8},{10,11... | collective-permute-start | bytes 589832 | tf_op jit(solution)/shard_map/ppermute | solution.py:31
  111.2 2.4 %collective-permute-start.16 = (bf16[8,64,768]{2,1,0:T(8,128)(2,1)S(1)}, bf16[8,64,768]{2,1,0:T(8,128)(2,1)S(1)}, u32[]{:S(2)}, u32[]{:S(2)}) collective-permute-start(bf16[8,64,768]{2,1,0:T(8,128)(2,1)S(1)} %get-tuple-element.81), channel_id=1, source_target_pairs={{0,1},{1,0},{2,3},{3,2},{4,5},{5,4},{6,7},{7,6},{8,9},{9,8},{10,11... | collective-permute-start | bytes 2359304 | tf_op jit(solution)/shard_map/ppermute | solution.py:31
  113.9 3.0 %copy-start.1 = (bf16[768,768]{1,0:T(8,128)(2,1)S(1)}, bf16[768,768]{1,0:T(8,128)(2,1)}, u32[]{:S(2)}) copy-start(bf16[768,768]{1,0:T(8,128)(2,1)} %expand.5) | copy-start | bytes 3538948
  113.9 3.0 %copy-start.3 = (bf16[768,768]{1,0:T(8,128)(2,1)S(1)}, bf16[768,768]{1,0:T(8,128)(2,1)}, u32[]{:S(2)}) copy-start(bf16[768,768]{1,0:T(8,128)(2,1)} %contract.5) | copy-start | bytes 3538948
  114.6 2.4 %collective-permute-start.17 = (bf16[8,64,768]{2,1,0:T(8,128)(2,1)S(1)}, bf16[8,64,768]{2,1,0:T(8,128)(2,1)S(1)}, u32[]{:S(2)}, u32[]{:S(2)}) collective-permute-start(bf16[8,64,768]{2,1,0:T(8,128)(2,1)S(1)} %fusion.3), channel_id=1, source_target_pairs={{0,1},{1,0},{2,3},{3,2},{4,5},{5,4},{6,7},{7,6},{8,9},{9,8},{10,11... | collective-permute-start | bytes 2359304 | tf_op jit(solution)/shard_map/ppermute | solution.py:31
  121.9 5.5 %collective-permute-start.18 = (bf16[8,64,768]{2,1,0:T(8,128)(2,1)S(1)}, bf16[8,64,768]{2,1,0:T(8,128)(2,1)S(1)}, u32[]{:S(2)}, u32[]{:S(2)}) collective-permute-start(bf16[8,64,768]{2,1,0:T(8,128)(2,1)S(1)} %bitcast.20), channel_id=1, source_target_pairs={{0,1},{1,0},{2,3},{3,2},{4,5},{5,4},{6,7},{7,6},{8,9},{9,8},{10,11... | collective-permute-start | bytes 2359304 | tf_op jit(solution)/shard_map/ppermute | solution.py:31
  (9 other events, 9.3 us)

commit v7 on v6

--- a/solution.py
+++ b/solution.py
@@ -511,7 +511,7 @@
 ):
     tokens = refs[: 2 * PARTS]
     triple, mixing, piece, rest, kept, sent = refs[2 * PARTS : 2 * PARTS + 6]
-    normed, near, far, projected, mixed, semaphores = refs[2 * PARTS + 6 :]
+    normed, far, projected, mixed, semaphores = refs[2 * PARTS + 6 :]
     quarter = mixing.shape[0]
     core, pair = me_ref[2], me_ref[3]
     half = rest.shape[0]
@@ -520,8 +520,6 @@
         return far.at[pl.ds(pl.multiple_of(index * half, half), half)]
 
     moves = (
-        (triple, near.at[pl.ds(0, 3 * quarter)]),
-        (mixing, near.at[pl.ds(3 * quarter, quarter)]),
         (piece.at[pl.ds(half, half)], spot(pair)),
         (rest, spot(1 - pair)),
     )
@@ -588,15 +586,14 @@
                 target = slice(lower + head * HEAD_SIZE, lower + (head + 1) * HEAD_SIZE)
                 mixed[target, lanes] = (part / total).astype(BF16)
 
-    copies[0].wait()
-    attend(near[: 3 * quarter], 0)
-    for copy in copies[1:]:
+    attend(triple[...], 0)
+    for copy in copies:
         copy.wait()
     attend(far[: 3 * quarter], quarter)
     for place in range(places):
         lanes = slice(place * both, (place + 1) * both)
         partial = lax.dot_general(
-            mixed[:quarter, lanes], near[3 * quarter :], CONTRACT_FIRST, preferred_element_type=F32
+            mixed[:quarter, lanes], mixing[...], CONTRACT_FIRST, preferred_element_type=F32
         )
         partial += lax.dot_general(
             mixed[quarter:, lanes], far[3 * quarter :], CONTRACT_FIRST, preferred_element_type=F32
@@ -615,15 +612,14 @@
             jax.ShapeDtypeStruct(shape, F32),
             jax.ShapeDtypeStruct(shape, BF16),
         ),
-        in_specs=[IN_SMEM] * 2 + [IN_VMEM] * (2 * PARTS) + [IN_HBM] * 4,
+        in_specs=[IN_SMEM] * 2 + [IN_VMEM] * (2 * PARTS + 2) + [IN_HBM] * 2,
         out_specs=(IN_VMEM, IN_VMEM),
         scratch_shapes=[
             pltpu.VMEM((places, 2 * rows, model), BF16),
             pltpu.VMEM((4 * quarter, model), BF16),
-            pltpu.VMEM((4 * quarter, model), BF16),
             pltpu.VMEM((3 * quarter, tokens), BF16),
             pltpu.VMEM((2 * quarter, tokens), BF16),
-            pltpu.SemaphoreType.DMA((4,)),
+            pltpu.SemaphoreType.DMA((2,)),
         ],
         compiler_params=GRANT,
         name="column",
@@ -671,9 +667,9 @@
 
 def feed_forward_kernel(
     me_ref, normed, expand, contract, piece, pair_rest, plane_rest, late, out,
-    near_expand, near_contract, far_expand, far_contract, hidden, semaphores,
+    far_expand, far_contract, hidden, semaphores,
 ):
-    width = near_expand.shape[1]
+    width = expand.shape[1]
     count, half = pair_rest.shape[0], width // 2
     pair, plane = me_ref[3], me_ref[4]
 
@@ -684,21 +680,19 @@
 
     def by_pair(first, second):
         return [
-            move(piece, 0, count, first, 0, 4),
-            move(pair_rest, 0, count, second, 0, 5),
+            move(piece, 0, count, first, 0, 2),
+            move(pair_rest, 0, count, second, 0, 3),
         ]
 
     def by_plane(first, second):
         return [
-            move(piece, count, count, first, count, 6),
-            move(plane_rest, 0, count, second, count, 7),
+            move(piece, count, count, first, count, 4),
+            move(plane_rest, 0, count, second, count, 5),
         ]
 
     copies = [
-        move(expand, 0, width, near_expand, 0, 0),
-        move(contract, 0, width, near_contract, 0, 1),
-        move(late, 0, half, far_expand, half, 2),
-        move(late, half, half, far_contract, half, 3),
+        move(late, 0, half, far_expand, half, 0),
+        move(late, half, half, far_contract, half, 1),
     ]
     for copy in copies:
         copy.start()
@@ -724,12 +718,11 @@
             hidden[:, lower + start : lower + start + tile] = up.astype(BF16)
 
     copies += by_pair(far_expand, far_contract) + by_plane(far_expand, far_contract)
-    copies[0].wait()
-    raise_by(near_expand, 0)
-    for copy in copies[1:]:
+    raise_by(expand, 0)
+    for copy in copies:
         copy.wait()
     raise_by(far_expand, width)
-    down = jnp.dot(hidden[:, :width], near_contract[...], preferred_element_type=F32)
+    down = jnp.dot(hidden[:, :width], contract[...], preferred_element_type=F32)
     down += jnp.dot(hidden[:, width:], far_contract[...], preferred_element_type=F32)
     out[...] = down.astype(out.dtype)
 
@@ -740,15 +733,13 @@
     result = pl.pallas_call(
         feed_forward_kernel,
         out_shape=jax.ShapeDtypeStruct((tokens, model), kind),
-        in_specs=[IN_SMEM, IN_VMEM] + [IN_HBM] * 6,
+        in_specs=[IN_SMEM] + [IN_VMEM] * 3 + [IN_HBM] * 4,
         out_specs=IN_VMEM,
         scratch_shapes=[
             pltpu.VMEM((model, width), BF16),
             pltpu.VMEM((width, model), BF16),
-            pltpu.VMEM((model, width), BF16),
-            pltpu.VMEM((model, width), BF16),
             pltpu.VMEM((tokens, 2 * width), BF16),
-            pltpu.SemaphoreType.DMA((8,)),
+            pltpu.SemaphoreType.DMA((6,)),
         ],
         compiler_params=GRANT,
         name="feed_forward",
@@ -756,8 +747,24 @@
     return result.reshape(normed.shape)
 
 
-def core_sum(stream, kept, sent):
-    return (stream.astype(F32) + kept + other_core(sent).astype(F32)).astype(BF16)
+def renew_kernel(stream, kept, got, after, normed):
+    total = (stream[...].astype(F32) + kept[...] + got[...].astype(F32)).astype(BF16)
+    after[...] = total
+    values = total.astype(F32)
+    centred = values - jnp.mean(values, axis=-1, keepdims=True)
+    variance = jnp.mean(centred * centred, axis=-1, keepdims=True)
+    normed[...] = (centred * lax.rsqrt(variance + 1e-05)).astype(BF16)
+
+
+def renew(stream, kept, got):
+    return pl.pallas_call(
+        renew_kernel,
+        out_shape=(jax.ShapeDtypeStruct(stream.shape, BF16),) * 2,
+        in_specs=[IN_VMEM] * 3,
+        out_specs=(IN_VMEM, IN_VMEM),
+        compiler_params=GRANT,
+        name="renew",
+    )(stream, kept, got)
 
 
 def shards(
@@ -840,9 +847,8 @@
         after_row.shape,
     )
     sent, feed_rest, late = lax.optimization_barrier((sent, feed_rest, late))
-    after_col = core_sum(after_row, kept, sent)
-
-    normed = own_norm(after_col, -1)
+    after_col, normed = renew(after_row, kept, other_core(sent))
+
     weights = (expand_matrix, contract_matrix, (piece, *feed_rest, late), me)
     kept = feed_forward(normed, *weights, F32)
     sent = feed_forward(other_core(normed), *weights, BF16)

time: 154 us -> 153 us (level)
  transfers between devices with their start and end apart: 21 -> 21, of which waited for: 11 -> 11; matrix products, arithmetic and copies ran while one was open for 1% -> 1% of each run, Pallas kernels for 19% -> 18%
where the time goes in v7:
time: 153 us; the launch traced here: 152 us
  blocking collectives  48.9 us (32%)
  Pallas kernels  34.2 us (22%)
  waiting for transfers between devices  27 us (18%)
  starting transfers between devices  26.8 us (18%)
  local copies, waits for them, and re-layouts  14.5 us (9%)
    all_to_all x1, blocking collectives, shards(): blocks = lax.all_to_all(blocks, ROWS + ('chip', 'core'), 0, 0, tiled=True)  23 us
    all_to_all x1, waiting for transfers between devices, shards(): blocks = lax.all_to_all(blocks, ROWS + ('chip',), 0, 0, tiled=True)  15.2 us
    all_to_all x1, blocking collectives, shards(): parts = lax.all_to_all(shared, ROWS, 0, 0, tiled=True)  15.1 us
    unnamed x40, local copies, waits for them, and re-layouts  11.8 us
    all_to_all x1, blocking collectives, shards(): shared = lax.all_to_all(tie(parts, plan), ROWS, 0, 0, tiled=True)  10.7 us
    pallas_call x2, Pallas kernels, feed_forward(): pl.pallas_call(feed_forward_kernel, out_shape=jax.ShapeDtypeStruct((token...  9.08 us
    ppermute x3, starting transfers between devices, other_chip(): return lax.ppermute(value, 'chip', SWAP)  8.27 us
    pallas_call x1, Pallas kernels, row_front(): pl.pallas_call(functools.partial(row_front_kernel, lines), grid=(lines //...  7.39 us
  transfers between devices with their start and end apart: 21, of which 11 were waited for; matrix products, arithmetic and copies ran while one was open for 1% of the time, Pallas kernels for 18%

profile of v7, /device:TPU:0, one launch (start us, length us, event | category | flops | bytes accessed | tf_op | source)
XLA Modules:
  0.0 151.9 jit_solution(10811017048124866185)
XLA Ops:
  0.0 2.9 %collective-permute-start = (bf16[16,192,128]{2,1,0:T(8,128)(2,1)}, bf16[16,192,128]{2,1,0:T(8,128)(2,1)}, u32[]{:S(2)}, u32[]{:S(2)}) collective-permute-start(bf16[16,192,128]{2,1,0:T(8,128)(2,1)} %stream), channel_id=1, source_target_pairs={{0,2},{2,0},{1,3},{3,1},{4,6},{6,4},{5,7},{7,5},{8,10},{10,8},{9,1... | collective-permute-start | bytes 2359304 | tf_op jit(solution)/shard_map/ppermute | solution.py:19
  3.0 1.3 copy-done
  4.3 1.3 copy-done.2
  5.6 1.2 copy-done.4
  8.7 1.2 pack.1
  9.9 1.1 copy-done.18
  11.0 1.3 spread.1
  12.3 5.0 %all-to-all-start = ((bf16[32,96,128]{2,1,0:T(8,128)(2,1)}), bf16[32,96,128]{2,1,0:T(8,128)(2,1)S(1)}, u32[]{:S(2)}, u32[]{:S(2)}) async-start(bf16[32,96,128]{2,1,0:T(8,128)(2,1)} %spread.1), calls=%async_computation | async-start | bytes 1572864 | tf_op jit(solution)/shard_map/all_to_all | solution.py:807
  17.5 4.5 %collective-permute-done.far = bf16[16,192,128]{2,1,0:T(8,128)(2,1)} collective-permute-done((bf16[16,192,128]{2,1,0:T(8,128)(2,1)}, bf16[16,192,128]{2,1,0:T(8,128)(2,1)}, u32[]{:S(2)}, u32[]{:S(2)}) %collective-permute-start) | collective-permute-done | bytes 786464 | tf_op jit(solution)/shard_map/ppermute | solution.py:19
  22.8 3.9 %collective-permute-start.3 = (bf16[960,768]{1,0:T(8,128)(2,1)}, bf16[960,768]{1,0:T(8,128)(2,1)S(1)}, u32[]{:S(2)}, u32[]{:S(2)}) collective-permute-start(bf16[960,768]{1,0:T(8,128)(2,1)} %copy-done.18), channel_id=1, source_target_pairs={{0,2},{2,0},{1,3},{3,1},{4,6},{6,4},{5,7},{7,5},{8,10},{10,8},{9,1... | collective-permute-start | bytes 4423688 | tf_op jit(solution)/shard_map/ppermute | solution.py:19
  26.7 1.2 copy-done.11
  27.9 1.1 copy-done.13
  29.0 7.4 %row_front.1 = (bf16[8,6,16,128]{3,2,1,0:T(8,128)(2,1)S(1)}, bf16[6,128,128]{2,1,0:T(8,128)(2,1)S(1)}, bf16[16,192,128]{2,1,0:T(8,128)(2,1)S(1)}) custom-call(s32[5]{0:T(128)S(1)} %stack.23.me_ref, s32[128]{0:T(128)S(1)} %copy-done.16, s32[5]{0:T(128)S(1)} %convert_reduce_fusion.starts_ref, s32[4]{0:T(128)S(1)} %copy-done.17, ...), custom_call_target="tpu_custom_call" | custom-call | tf_op jit(solution)/shard_map/row_front/pallas_call | solution.py:253
  38.0 15.1 %all_to_all.25.parts = bf16[8,6,16,128]{3,2,1,0:T(8,128)(2,1)S(1)} all-to-all(bf16[8,6,16,128]{3,2,1,0:T(8,128)(2,1)S(1)} %get-tuple-element.57), channel_id=1, replica_groups=mesh['far'=2,'plane'=2,'pair'=2,'chip'=2,'core'=2] {'far','plane','pair'}, dimensions={0} | all-to-all | bytes 393216 | tf_op jit(solution)/shard_map/all_to_all | solution.py:822
  54.0 10.7 %all_to_all.26.shared = bf16[8,6,16,128]{3,2,1,0:T(8,128)(2,1)S(1)} all-to-all(bf16[8,6,16,128]{3,2,1,0:T(8,128)(2,1)S(1)} %tie.1), channel_id=1, replica_groups=mesh['far'=2,'plane'=2,'pair'=2,'chip'=2,'core'=2] {'far','plane','pair'}, dimensions={0} | all-to-all | bytes 393216 | tf_op jit(solution)/shard_map/all_to_all | solution.py:823
  64.8 2.1 %mix.1 = bf16[16,192,128]{2,1,0:T(8,128)(2,1)} custom-call(s32[5]{0:T(128)S(1)} %stack.23.me_ref, s32[128]{0:T(128)S(1)} %copy-done.16, s32[5]{0:T(128)S(1)} %convert_reduce_fusion.starts_ref, s32[4]{0:T(128)S(1)} %copy-done.17, bf16[8,6,16,128]{3,2,1,0:T(8,128)(2,1)S(1)} %all_to_all.26.shared, bf16[6,128,128]{2,1,0:T(8,128)(2,1)S(1)} %get-tuple-element.58.inner, ...), custom_call_target="tpu_custom_call" | custom-call | tf_op jit(solution)/shard_map/mix/pallas_call | solution.py:355
  66.9 5.1 %all-to-all-start.3 = ((bf16[16,192,128]{2,1,0:T(8,128)(2,1)}), bf16[16,192,128]{2,1,0:T(8,128)(2,1)}, u32[]{:S(2)}, u32[]{:S(2)}) async-start(bf16[16,192,128]{2,1,0:T(8,128)(2,1)} %mix.1), calls=%async_computation.3 | async-start | bytes 1572864 | tf_op jit(solution)/shard_map/all_to_all | solution.py:831
  72.8 1.9 %collective-permute-start.8 = (bf16[384,768]{1,0:T(8,128)(2,1)}, bf16[384,768]{1,0:T(8,128)(2,1)}, u32[]{:S(2)}, u32[]{:S(2)}) collective-permute-start(bf16[384,768]{1,0:T(8,128)(2,1)} %slice.21), channel_id=1, source_target_pairs={{0,4},{4,0},{1,5},{5,1},{2,6},{6,2},{3,7},{7,3},{8,12},{12,8},{9,1... | collective-permute-start | bytes 1769480 | tf_op jit(solution)/shard_map/ppermute | solution.py:23
  74.7 1.5 collective-permute-start.15
  76.1 15.2 %all-to-all-done.3.blocks = bf16[16,192,128]{2,1,0:T(8,128)(2,1)} async-done(((bf16[16,192,128]{2,1,0:T(8,128)(2,1)}), bf16[16,192,128]{2,1,0:T(8,128)(2,1)}, u32[]{:S(2)}, u32[]{:S(2)}) %all-to-all-start.3) | async-done | bytes 786464 | tf_op jit(solution)/shard_map/all_to_all | solution.py:831
  92.3 3.6 %project.1 = (f32[8,64,768]{2,1,0:T(8,128)S(1)}, bf16[2,64,768]{2,1,0:T(8,128)(2,1)S(1)}, bf16[2,64,768]{2,1,0:T(8,128)(2,1)S(1)}, bf16[2,64,768]{2,1,0:T(8,128)(2,1)S(1)}, bf16[2,64,768]{2,1,0:T(8,128)(2,1)S(1)}) custom-call(s32[5]{0:T(128)S(1)} %stack.23.me_ref, bf16[16,192,128]{2,1,0:T(8,128)(2,1)} %all-to-all-done.3.blocks, ...), custom_call_target="tpu_custom_call" | custom-call | tf_op jit(solution)/shard_map/project/pallas_call | solution.py:431
  98.3 1.1 arrive.1
  100.0 1.8 %collective-permute-start.13 = (bf16[192,768]{1,0:T(8,128)(2,1)S(1)}, bf16[192,768]{1,0:T(8,128)(2,1)S(1)}, u32[]{:S(2)}, u32[]{:S(2)}) collective-permute-start(bf16[192,768]{1,0:T(8,128)(2,1)S(1)} %get-tuple-element.90), channel_id=1, source_target_pairs={{0,4},{4,0},{1,5},{5,1},{2,6},{6,2},{3,7},{7,3},{8,12},{12,8},{9,1... | collective-permute-start | bytes 884744 | tf_op jit(solution)/shard_map/ppermute | solution.py:23
  101.8 1.7 %collective-permute-start.14 = (bf16[192,768]{1,0:T(8,128)(2,1)S(1)}, bf16[192,768]{1,0:T(8,128)(2,1)S(1)}, u32[]{:S(2)}, u32[]{:S(2)}) collective-permute-start(bf16[192,768]{1,0:T(8,128)(2,1)S(1)} %get-tuple-element.89), channel_id=1, source_target_pairs={{0,8},{8,0},{1,9},{9,1},{2,10},{10,2},{3,11},{11,3},{4,12},{12,4},... | collective-permute-start | bytes 884744 | tf_op jit(solution)/shard_map/ppermute | solution.py:27
  105.3 5.6 %column.1 = (f32[8,64,768]{2,1,0:T(8,128)S(1)}, bf16[8,64,768]{2,1,0:T(8,128)(2,1)S(1)}) custom-call(s32[5]{0:T(128)S(1)} %stack.23.me_ref, s32[5]{0:T(128)S(1)} %convert_reduce_fusion.starts_ref, bf16[2,64,768]{2,1,0:T(8,128)(2,1)S(1)} %get-tuple-element.75.refs_0_, bf16[2,64,768]{2,1,0:T(8,128)(2,1)S(1)} %get-tuple-element.76.refs_1_, ...), custom_call_target="tpu_custom_call" | custom-call | tf_op jit(solution)/shard_map/column/pallas_call | solution.py:609
  111.2 2.1 %collective-permute-done.16.got = bf16[8,64,768]{2,1,0:T(8,128)(2,1)S(1)} collective-permute-done((bf16[8,64,768]{2,1,0:T(8,128)(2,1)S(1)}, bf16[8,64,768]{2,1,0:T(8,128)(2,1)S(1)}, u32[]{:S(2)}, u32[]{:S(2)}) %collective-permute-start.16) | collective-permute-done | bytes 786464 | tf_op jit(solution)/shard_map/ppermute | solution.py:31
  114.2 2.1 %collective-permute-done.17 = bf16[8,64,768]{2,1,0:T(8,128)(2,1)S(1)} collective-permute-done((bf16[8,64,768]{2,1,0:T(8,128)(2,1)S(1)}, bf16[8,64,768]{2,1,0:T(8,128)(2,1)S(1)}, u32[]{:S(2)}, u32[]{:S(2)}) %collective-permute-start.17) | collective-permute-done | bytes 786464 | tf_op jit(solution)/shard_map/ppermute | solution.py:31
  116.3 4.4 %feed_forward.3 = bf16[512,768]{1,0:T(8,128)(2,1)S(1)} custom-call(s32[5]{0:T(128)S(1)} %stack.23.me_ref, bf16[512,768]{1,0:T(8,128)(2,1)S(1)} %bitcast.20, bf16[768,768]{1,0:T(8,128)(2,1)S(1)} %copy-done.1, bf16[768,768]{1,0:T(8,128)(2,1)S(1)} %copy-done.3, bf16[960,768]{1,0:T(8,128)(2,1)S(1)} %collective-permute-done.3.piece.refs_10_, ...), custom_call_target="tpu_custom_call" | custom-call | tf_op jit(solution)/shard_map/feed_forward/pallas_call | solution.py:733
  121.0 4.7 %feed_forward.2 = f32[512,768]{1,0:T(8,128)S(1)} custom-call(s32[5]{0:T(128)S(1)} %stack.23.me_ref, bf16[512,768]{1,0:T(8,128)(2,1)S(1)} %bitcast.21, bf16[768,768]{1,0:T(8,128)(2,1)S(1)} %copy-done.1, bf16[768,768]{1,0:T(8,128)(2,1)S(1)} %copy-done.3, bf16[960,768]{1,0:T(8,128)(2,1)S(1)} %collective-permute-done.3.piece.refs_10_, ...), custom_call_target="tpu_custom_call" | custom-call | tf_op jit(solution)/shard_map/feed_forward/pallas_call | solution.py:733
  125.7 1.2 finish.1
  126.9 23.0 %all_to_all.27 = bf16[32,96,128]{2,1,0:T(8,128)(2,1)S(1)} all-to-all(bf16[32,96,128]{2,1,0:T(8,128)(2,1)S(1)} %finish.1), channel_id=1, replica_groups=mesh['far'=2,'plane'=2,'pair'=2,'chip'=2,'core'=2] {'far','plane','pair'..., dimensions={0} | all-to-all | bytes 1572864 | tf_op jit(solution)/shard_map/all_to_all | solution.py:857
  150.7 1.3 copy.14
  (74 shorter events, 14.3 us)
Async XLA Ops:
  0.0 22.0 %collective-permute-start = (bf16[16,192,128]{2,1,0:T(8,128)(2,1)}, bf16[16,192,128]{2,1,0:T(8,128)(2,1)}, u32[]{:S(2)}, u32[]{:S(2)}) collective-permute-start(bf16[16,192,128]{2,1,0:T(8,128)(2,1)} %stream), channel_id=1, source_target_pairs={{0,2},{2,0},{1,3},{3,1},{4,6},{6,4},{5,7},{7,5},{8,10},{10,8},{9,1... | collective-permute-start | bytes 2359304 | tf_op jit(solution)/shard_map/ppermute | solution.py:19
  2.9 19.0 %collective-permute-start.1 = (bf16[16,192,128]{2,1,0:T(8,128)(2,1)}, bf16[16,192,128]{2,1,0:T(8,128)(2,1)S(1)}, u32[]{:S(2)}, u32[]{:S(2)}) collective-permute-start(bf16[16,192,128]{2,1,0:T(8,128)(2,1)} %stream), channel_id=1, source_target_pairs={{0,1},{1,0},{2,3},{3,2},{4,5},{5,4},{6,7},{7,6},{8,9},{9,8},{10,11... | collective-permute-start | bytes 2359304 | tf_op jit(solution)/shard_map/ppermute | solution.py:31
  3.0 1.3 copy-start
  4.3 1.3 copy-start.2
  8.7 2.3 %copy-start.6 = (bf16[16,192,128]{2,1,0:T(8,128)(2,1)S(1)}, bf16[16,192,128]{2,1,0:T(8,128)(2,1)}, u32[]{:S(2)}) copy-start(bf16[16,192,128]{2,1,0:T(8,128)(2,1)} %stream) | copy-start | bytes 2359300
  9.9 2.5 %copy-start.19 = (bf16[768,768]{1,0:T(8,128)(2,1)}, bf16[768,768]{1,0:T(8,128)(2,1)S(1)}, u32[]{:S(2)}) copy-start(bf16[768,768]{1,0:T(8,128)(2,1)S(1)} %get-tuple-element.82) | copy-start | bytes 3538948
  11.0 6.4 %copy-start.16 = (s32[128]{0:T(128)S(1)}, s32[128]{0:T(128)}, u32[]{:S(2)}) copy-start(s32[128]{0:T(128)} %label_ref.5) | copy-start | bytes 1540
  11.0 15.7 %copy-start.17 = (s32[4]{0:T(128)S(1)}, s32[4]{0:T(128)}, u32[]{:S(2)}) copy-start(s32[4]{0:T(128)} %tally_ref.5) | copy-start | bytes 52
  12.3 25.7 %all-to-all-start = ((bf16[32,96,128]{2,1,0:T(8,128)(2,1)}), bf16[32,96,128]{2,1,0:T(8,128)(2,1)S(1)}, u32[]{:S(2)}, u32[]{:S(2)}) async-start(bf16[32,96,128]{2,1,0:T(8,128)(2,1)} %spread.1), calls=%async_computation | async-start | bytes 1572864 | tf_op jit(solution)/shard_map/all_to_all | solution.py:807
  22.8 3.9 %collective-permute-start.2 = (bf16[16,192,128]{2,1,0:T(8,128)(2,1)}, bf16[16,192,128]{2,1,0:T(8,128)(2,1)S(1)}, u32[]{:S(2)}, u32[]{:S(2)}) collective-permute-start(bf16[16,192,128]{2,1,0:T(8,128)(2,1)} %collective-permute-done.far), channel_id=1, source_target_pairs={{0,1},{1,0},{2,3},{3,2},{4,5},{5,4},{6,7},{7,6},{8,9},{9,8},{10,11... | collective-permute-start | bytes 2359304 | tf_op jit(solution)/shard_map/ppermute | solution.py:31
  22.8 44.0 %collective-permute-start.3 = (bf16[960,768]{1,0:T(8,128)(2,1)}, bf16[960,768]{1,0:T(8,128)(2,1)S(1)}, u32[]{:S(2)}, u32[]{:S(2)}) collective-permute-start(bf16[960,768]{1,0:T(8,128)(2,1)} %copy-done.18), channel_id=1, source_target_pairs={{0,2},{2,0},{1,3},{3,1},{4,6},{6,4},{5,7},{7,5},{8,10},{10,8},{9,1... | collective-permute-start | bytes 4423688 | tf_op jit(solution)/shard_map/ppermute | solution.py:19
  38.0 26.8 %copy-start.15 = (bf16[16,192,128]{2,1,0:T(8,128)(2,1)S(1)}, bf16[16,192,128]{2,1,0:T(8,128)(2,1)}, u32[]{:S(2)}) copy-start(bf16[16,192,128]{2,1,0:T(8,128)(2,1)} %copy-done.14) | copy-start | bytes 2359300
  66.9 24.5 %all-to-all-start.3 = ((bf16[16,192,128]{2,1,0:T(8,128)(2,1)}), bf16[16,192,128]{2,1,0:T(8,128)(2,1)}, u32[]{:S(2)}, u32[]{:S(2)}) async-start(bf16[16,192,128]{2,1,0:T(8,128)(2,1)} %mix.1), calls=%async_computation.3 | async-start | bytes 1572864 | tf_op jit(solution)/shard_map/all_to_all | solution.py:831
  72.8 23.9 %collective-permute-start.8 = (bf16[384,768]{1,0:T(8,128)(2,1)}, bf16[384,768]{1,0:T(8,128)(2,1)}, u32[]{:S(2)}, u32[]{:S(2)}) collective-permute-start(bf16[384,768]{1,0:T(8,128)(2,1)} %slice.21), channel_id=1, source_target_pairs={{0,4},{4,0},{1,5},{5,1},{2,6},{6,2},{3,7},{7,3},{8,12},{12,8},{9,1... | collective-permute-start | bytes 1769480 | tf_op jit(solution)/shard_map/ppermute | solution.py:23
  74.7 36.2 %collective-permute-start.15 = (bf16[768,768]{1,0:T(8,128)(2,1)}, bf16[768,768]{1,0:T(8,128)(2,1)S(1)}, u32[]{:S(2)}, u32[]{:S(2)}) collective-permute-start(bf16[768,768]{1,0:T(8,128)(2,1)} %copy-done.19), channel_id=1, source_target_pairs={{0,2},{2,0},{1,3},{3,1},{4,6},{6,4},{5,7},{7,5},{8,10},{10,8},{9,1... | collective-permute-start | bytes 3538952 | tf_op jit(solution)/shard_map/ppermute | solution.py:19
  96.0 1.5 collective-permute-start.4
  96.0 1.7 %collective-permute-start.5 = (bf16[2,64,768]{2,1,0:T(8,128)(2,1)S(1)}, bf16[2,64,768]{2,1,0:T(8,128)(2,1)S(1)}, u32[]{:S(2)}, u32[]{:S(2)}) collective-permute-start(bf16[2,64,768]{2,1,0:T(8,128)(2,1)S(1)} %get-tuple-element.66), channel_id=1, source_target_pairs={{0,1},{1,0},{2,3},{3,2},{4,5},{5,4},{6,7},{7,6},{8,9},{9,8},{10,11... | collective-permute-start | bytes 589832 | tf_op jit(solution)/shard_map/ppermute | solution.py:31
  96.5 1.5 collective-permute-start.6
  96.6 1.7 %collective-permute-start.7 = (bf16[2,64,768]{2,1,0:T(8,128)(2,1)S(1)}, bf16[2,64,768]{2,1,0:T(8,128)(2,1)S(1)}, u32[]{:S(2)}, u32[]{:S(2)}) collective-permute-start(bf16[2,64,768]{2,1,0:T(8,128)(2,1)S(1)} %get-tuple-element.68), channel_id=1, source_target_pairs={{0,1},{1,0},{2,3},{3,2},{4,5},{5,4},{6,7},{7,6},{8,9},{9,8},{10,11... | collective-permute-start | bytes 589832 | tf_op jit(solution)/shard_map/ppermute | solution.py:31
  98.3 6.9 %copy-start.5 = (bf16[3,192,768]{2,1,0:T(8,128)(2,1)S(1)}, bf16[3,192,768]{2,1,0:T(8,128)(2,1)}, u32[]{:S(2)}) copy-start(bf16[3,192,768]{2,1,0:T(8,128)(2,1)} %param.14) | copy-start | bytes 2654212
  98.3 6.9 %copy-start.10 = (bf16[192,768]{1,0:T(8,128)(2,1)S(1)}, bf16[192,768]{1,0:T(8,128)(2,1)}, u32[]{:S(2)}) copy-start(bf16[192,768]{1,0:T(8,128)(2,1)} %refs_9_.1) | copy-start | bytes 884740
  99.4 4.1 %collective-permute-start.10 = (bf16[2,64,768]{2,1,0:T(8,128)(2,1)S(1)}, bf16[2,64,768]{2,1,0:T(8,128)(2,1)S(1)}, u32[]{:S(2)}, u32[]{:S(2)}) collective-permute-start(bf16[2,64,768]{2,1,0:T(8,128)(2,1)S(1)} %get-tuple-element.76.refs_1_), channel_id=1, source_target_pairs={{0,1},{1,0},{2,3},{3,2},{4,5},{5,4},{6,7},{7,6},{8,9},{9,8},{10,11... | collective-permute-start | bytes 589832 | tf_op jit(solution)/shard_map/ppermute | solution.py:31
  99.7 3.8 %collective-permute-start.11 = (bf16[2,64,768]{2,1,0:T(8,128)(2,1)S(1)}, bf16[2,64,768]{2,1,0:T(8,128)(2,1)S(1)}, u32[]{:S(2)}, u32[]{:S(2)}) collective-permute-start(bf16[2,64,768]{2,1,0:T(8,128)(2,1)S(1)} %get-tuple-element.77.refs_2_), channel_id=1, source_target_pairs={{0,1},{1,0},{2,3},{3,2},{4,5},{5,4},{6,7},{7,6},{8,9},{9,8},{10,11... | collective-permute-start | bytes 589832 | tf_op jit(solution)/shard_map/ppermute | solution.py:31
  100.0 10.8 %collective-permute-start.13 = (bf16[192,768]{1,0:T(8,128)(2,1)S(1)}, bf16[192,768]{1,0:T(8,128)(2,1)S(1)}, u32[]{:S(2)}, u32[]{:S(2)}) collective-permute-start(bf16[192,768]{1,0:T(8,128)(2,1)S(1)} %get-tuple-element.90), channel_id=1, source_target_pairs={{0,4},{4,0},{1,5},{5,1},{2,6},{6,2},{3,7},{7,3},{8,12},{12,8},{9,1... | collective-permute-start | bytes 884744 | tf_op jit(solution)/shard_map/ppermute | solution.py:23
  101.8 9.0 %collective-permute-start.14 = (bf16[192,768]{1,0:T(8,128)(2,1)S(1)}, bf16[192,768]{1,0:T(8,128)(2,1)S(1)}, u32[]{:S(2)}, u32[]{:S(2)}) collective-permute-start(bf16[192,768]{1,0:T(8,128)(2,1)S(1)} %get-tuple-element.89), channel_id=1, source_target_pairs={{0,8},{8,0},{1,9},{9,1},{2,10},{10,2},{3,11},{11,3},{4,12},{12,4},... | collective-permute-start | bytes 884744 | tf_op jit(solution)/shard_map/ppermute | solution.py:27
  103.5 1.4 collective-permute-start.12
  103.5 1.7 %collective-permute-start.9 = (bf16[2,64,768]{2,1,0:T(8,128)(2,1)S(1)}, bf16[2,64,768]{2,1,0:T(8,128)(2,1)S(1)}, u32[]{:S(2)}, u32[]{:S(2)}) collective-permute-start(bf16[2,64,768]{2,1,0:T(8,128)(2,1)S(1)} %get-tuple-element.75.refs_0_), channel_id=1, source_target_pairs={{0,1},{1,0},{2,3},{3,2},{4,5},{5,4},{6,7},{7,6},{8,9},{9,8},{10,11... | collective-permute-start | bytes 589832 | tf_op jit(solution)/shard_map/ppermute | solution.py:31
  110.9 2.4 %collective-permute-start.16 = (bf16[8,64,768]{2,1,0:T(8,128)(2,1)S(1)}, bf16[8,64,768]{2,1,0:T(8,128)(2,1)S(1)}, u32[]{:S(2)}, u32[]{:S(2)}) collective-permute-start(bf16[8,64,768]{2,1,0:T(8,128)(2,1)S(1)} %get-tuple-element.83), channel_id=1, source_target_pairs={{0,1},{1,0},{2,3},{3,2},{4,5},{5,4},{6,7},{7,6},{8,9},{9,8},{10,11... | collective-permute-start | bytes 2359304 | tf_op jit(solution)/shard_map/ppermute | solution.py:31
  113.2 3.1 %copy-start.1 = (bf16[768,768]{1,0:T(8,128)(2,1)S(1)}, bf16[768,768]{1,0:T(8,128)(2,1)}, u32[]{:S(2)}) copy-start(bf16[768,768]{1,0:T(8,128)(2,1)} %expand.5) | copy-start | bytes 3538948
  113.2 3.1 %copy-start.3 = (bf16[768,768]{1,0:T(8,128)(2,1)S(1)}, bf16[768,768]{1,0:T(8,128)(2,1)}, u32[]{:S(2)}) copy-start(bf16[768,768]{1,0:T(8,128)(2,1)} %contract.5) | copy-start | bytes 3538948
  113.9 2.4 %collective-permute-start.17 = (bf16[8,64,768]{2,1,0:T(8,128)(2,1)S(1)}, bf16[8,64,768]{2,1,0:T(8,128)(2,1)S(1)}, u32[]{:S(2)}, u32[]{:S(2)}) collective-permute-start(bf16[8,64,768]{2,1,0:T(8,128)(2,1)S(1)} %get-tuple-element.85), channel_id=1, source_target_pairs={{0,1},{1,0},{2,3},{3,2},{4,5},{5,4},{6,7},{7,6},{8,9},{9,8},{10,11... | collective-permute-start | bytes 2359304 | tf_op jit(solution)/shard_map/ppermute | solution.py:31
  120.7 5.0 %collective-permute-start.18 = (bf16[8,64,768]{2,1,0:T(8,128)(2,1)S(1)}, bf16[8,64,768]{2,1,0:T(8,128)(2,1)S(1)}, u32[]{:S(2)}, u32[]{:S(2)}) collective-permute-start(bf16[8,64,768]{2,1,0:T(8,128)(2,1)S(1)} %bitcast.19), channel_id=1, source_target_pairs={{0,1},{1,0},{2,3},{3,2},{4,5},{5,4},{6,7},{7,6},{8,9},{9,8},{10,11... | collective-permute-start | bytes 2359304 | tf_op jit(solution)/shard_map/ppermute | solution.py:31
  (9 other events, 9.3 us)

commit v8 on v7

--- a/solution.py
+++ b/solution.py
@@ -493,7 +493,7 @@
             out_shape=(part,) * PARTS + (shape,),
             in_specs=[IN_VMEM] * (2 + PARTS),
             out_specs=(IN_VMEM,) * (1 + PARTS),
-            scratch_shapes=[pltpu.VMEM((model // 128, groups * own, 128), F32)],
+            scratch_shapes=[pltpu.VMEM((model // 128, groups * own + place, 128), F32)],
             compiler_params=GRANT,
             name="arrive",
         )(kept, *got, blocks)
@@ -626,7 +626,7 @@
     )(plan[0], plan[2], *own, *other, triple.reshape(-1, model), mixing, piece, rest)
 
 
-def finish_kernel(stream, kept, got, out):
+def finish_kernel(stream, first, second, got, out):
     places, rows, model = stream.shape
     parts, wide = out.shape[1] // 3, out.shape[2]
     quarter = wide // 2 * 3
@@ -635,7 +635,8 @@
     lines = rows // groups
     for group in range(groups):
         these = slice(group * lines, (group + 1) * lines)
-        total = stream[:, these].astype(F32) + kept[:, these] + got[:, these].astype(F32)
+        total = jnp.concatenate([first[:, these], second[:, these]], axis=0)
+        total += stream[:, these].astype(F32) + got[:, these].astype(F32)
         total = total.reshape(places * lines, model)
         for head in range(heads):
             block = total[:, head * quarter : (head + 1) * quarter]
@@ -644,20 +645,24 @@
             out[group * heads + head] = block.astype(BF16)
 
 
-def finish(stream, kept, got, groups, quarter):
+def finish(stream, first, second, got, groups, quarter):
     places, rows, model = stream.shape
     heads, lines = model // quarter, rows // groups
     parts, wide = places * lines // 2, quarter // 3 * 2
     shape = (groups * heads, 3 * parts, wide)
-    if parts % 16 == 0 and lines % 8 == 0:
+    got = got.reshape(stream.shape)
+    if parts % 16 == 0 and lines % 8 == 0 and places % 2 == 0:
+        half = (places // 2, rows, model)
+        first, second = first.reshape(half), second.reshape(half)
         return pl.pallas_call(
             finish_kernel,
             out_shape=jax.ShapeDtypeStruct(shape, BF16),
-            in_specs=[IN_VMEM] * 3,
+            in_specs=[IN_VMEM] * 4,
             out_specs=IN_VMEM,
             compiler_params=GRANT,
             name="finish",
-        )(stream, kept, got)
+        )(stream, first, second, got)
+    kept = jnp.concatenate([first, second]).reshape(stream.shape)
     total = (stream.astype(F32) + kept + got.astype(F32)).astype(BF16)
     total = total.reshape(places, groups, lines, heads, quarter)
     total = jnp.transpose(total, (1, 3, 0, 2, 4)).reshape(-1, places * lines, quarter)
@@ -728,9 +733,9 @@
 
 
 def feed_forward(normed, expand, contract, pieces, me, kind):
-    places, rows, model = normed.shape
-    tokens, width = places * rows, expand.shape[1]
-    result = pl.pallas_call(
+    tokens, model = normed.shape
+    width = expand.shape[1]
+    return pl.pallas_call(
         feed_forward_kernel,
         out_shape=jax.ShapeDtypeStruct((tokens, model), kind),
         in_specs=[IN_SMEM] + [IN_VMEM] * 3 + [IN_HBM] * 4,
@@ -743,25 +748,30 @@
         ],
         compiler_params=GRANT,
         name="feed_forward",
-    )(me, normed.reshape(tokens, model), expand, contract, *pieces)
-    return result.reshape(normed.shape)
-
-
-def renew_kernel(stream, kept, got, after, normed):
+    )(me, normed, expand, contract, *pieces)
+
+
+def renew_kernel(stream, kept, got, after, normed, first, second):
     total = (stream[...].astype(F32) + kept[...] + got[...].astype(F32)).astype(BF16)
     after[...] = total
     values = total.astype(F32)
     centred = values - jnp.mean(values, axis=-1, keepdims=True)
     variance = jnp.mean(centred * centred, axis=-1, keepdims=True)
-    normed[...] = (centred * lax.rsqrt(variance + 1e-05)).astype(BF16)
+    values = (centred * lax.rsqrt(variance + 1e-05)).astype(BF16)
+    normed[...] = values
+    values = values.reshape(2 * first.shape[0], first.shape[1])
+    first[...] = values[: first.shape[0]]
+    second[...] = values[first.shape[0] :]
 
 
 def renew(stream, kept, got):
+    half = (stream.shape[0] * stream.shape[1] // 2, stream.shape[2])
     return pl.pallas_call(
         renew_kernel,
-        out_shape=(jax.ShapeDtypeStruct(stream.shape, BF16),) * 2,
+        out_shape=(jax.ShapeDtypeStruct(stream.shape, BF16),) * 2
+        + (jax.ShapeDtypeStruct(half, BF16),) * 2,
         in_specs=[IN_VMEM] * 3,
-        out_specs=(IN_VMEM, IN_VMEM),
+        out_specs=(IN_VMEM,) * 4,
         compiler_params=GRANT,
         name="renew",
     )(stream, kept, got)
@@ -847,12 +857,15 @@
         after_row.shape,
     )
     sent, feed_rest, late = lax.optimization_barrier((sent, feed_rest, late))
-    after_col, normed = renew(after_row, kept, other_core(sent))
+    after_col, normed, first, second = renew(after_row, kept, other_core(sent))
 
     weights = (expand_matrix, contract_matrix, (piece, *feed_rest, late), me)
-    kept = feed_forward(normed, *weights, F32)
-    sent = feed_forward(other_core(normed), *weights, BF16)
-    blocks = finish(after_col, kept, other_core(sent), row_groups, quarter)
+    first = feed_forward(first, *weights, F32)
+    other = other_core(normed).reshape(-1, normed.shape[-1])
+    other, first = lax.optimization_barrier((other, first))
+    sent = feed_forward(other, *weights, BF16)
+    second = feed_forward(second, *weights, F32)
+    blocks = finish(after_col, first, second, other_core(sent), row_groups, quarter)
 
     blocks = lax.all_to_all(blocks, ROWS + ("chip", "core"), 0, 0, tiled=True)
     parts, wide = own * place // 2, quarter // 3 * 2

time: 153 us -> 152 us (level)
  waiting for transfers between devices: 27 us -> 25.3 us
  Pallas kernels: 34.2 us -> 35.8 us
    ppermute x13, waiting for transfers between devices: 6.6 us -> 4.77 us  [other_core(): return lax.ppermute(value, 'core', SWAP)]
    pallas_call x2 -> x3, Pallas kernels: 9.08 us -> 10.7 us  [feed_forward(): pl.pallas_call(feed_forward_kernel, out_shape=jax.ShapeDtypeStruct((token...]
  transfers between devices with their start and end apart: 21 -> 21, of which waited for: 11 -> 11; matrix products, arithmetic and copies ran while one was open for 1% -> 1% of each run, Pallas kernels for 18% -> 19%
where the time goes in v8:
time: 152 us; the launch traced here: 151 us
  blocking collectives  48.4 us (32%)
  Pallas kernels  35.8 us (24%)
  starting transfers between devices  25.9 us (17%)
  waiting for transfers between devices  25.3 us (17%)
  local copies, waits for them, and re-layouts  15.2 us (10%)
    all_to_all x1, blocking collectives, shards(): blocks = lax.all_to_all(blocks, ROWS + ('chip', 'core'), 0, 0, tiled=True)  22.8 us
    all_to_all x1, waiting for transfers between devices, shards(): blocks = lax.all_to_all(blocks, ROWS + ('chip',), 0, 0, tiled=True)  15.2 us
    all_to_all x1, blocking collectives, shards(): parts = lax.all_to_all(shared, ROWS, 0, 0, tiled=True)  14.9 us
    unnamed x40, local copies, waits for them, and re-layouts  12.5 us
    all_to_all x1, blocking collectives, shards(): shared = lax.all_to_all(tie(parts, plan), ROWS, 0, 0, tiled=True)  10.7 us
    pallas_call x3, Pallas kernels, feed_forward(): pl.pallas_call(feed_forward_kernel, out_shape=jax.ShapeDtypeStruct((token...  10.7 us
    ppermute x3, starting transfers between devices, other_chip(): return lax.ppermute(value, 'chip', SWAP)  8.04 us
    pallas_call x1, Pallas kernels, row_front(): pl.pallas_call(functools.partial(row_front_kernel, lines), grid=(lines //...  7.4 us
  transfers between devices with their start and end apart: 21, of which 11 were waited for; matrix products, arithmetic and copies ran while one was open for 1% of the time, Pallas kernels for 19%

profile of v8, /device:TPU:0, one launch (start us, length us, event | category | flops | bytes accessed | tf_op | source)
XLA Modules:
  0.0 151.3 jit_solution(7113795326311285112)
XLA Ops:
  0.5 2.5 %collective-permute-start = (bf16[16,192,128]{2,1,0:T(8,128)(2,1)}, bf16[16,192,128]{2,1,0:T(8,128)(2,1)}, u32[]{:S(2)}, u32[]{:S(2)}) collective-permute-start(bf16[16,192,128]{2,1,0:T(8,128)(2,1)} %stream), channel_id=1, source_target_pairs={{0,2},{2,0},{1,3},{3,1},{4,6},{6,4},{5,7},{7,5},{8,10},{10,8},{9,1... | collective-permute-start | bytes 2359304 | tf_op jit(solution)/shard_map/ppermute | solution.py:19
  3.0 1.3 copy-done
  4.3 1.3 copy-done.2
  5.6 1.2 copy-done.4
  8.7 1.2 pack.1
  9.9 1.1 copy-done.18
  11.0 1.3 spread.1
  12.3 4.9 %all-to-all-start = ((bf16[32,96,128]{2,1,0:T(8,128)(2,1)}), bf16[32,96,128]{2,1,0:T(8,128)(2,1)S(1)}, u32[]{:S(2)}, u32[]{:S(2)}) async-start(bf16[32,96,128]{2,1,0:T(8,128)(2,1)} %spread.1), calls=%async_computation | async-start | bytes 1572864 | tf_op jit(solution)/shard_map/all_to_all | solution.py:817
  18.3 3.6 %collective-permute-done.far = bf16[16,192,128]{2,1,0:T(8,128)(2,1)} collective-permute-done((bf16[16,192,128]{2,1,0:T(8,128)(2,1)}, bf16[16,192,128]{2,1,0:T(8,128)(2,1)}, u32[]{:S(2)}, u32[]{:S(2)}) %collective-permute-start) | collective-permute-done | bytes 786464 | tf_op jit(solution)/shard_map/ppermute | solution.py:19
  21.9 4.1 %collective-permute-start.3 = (bf16[960,768]{1,0:T(8,128)(2,1)}, bf16[960,768]{1,0:T(8,128)(2,1)S(1)}, u32[]{:S(2)}, u32[]{:S(2)}) collective-permute-start(bf16[960,768]{1,0:T(8,128)(2,1)} %copy-done.18), channel_id=1, source_target_pairs={{0,2},{2,0},{1,3},{3,1},{4,6},{6,4},{5,7},{7,5},{8,10},{10,8},{9,1... | collective-permute-start | bytes 4423688 | tf_op jit(solution)/shard_map/ppermute | solution.py:19
  26.0 1.2 copy-done.11
  27.1 1.1 copy-done.13
  28.3 7.4 %row_front.1 = (bf16[8,6,16,128]{3,2,1,0:T(8,128)(2,1)S(1)}, bf16[6,128,128]{2,1,0:T(8,128)(2,1)S(1)}, bf16[16,192,128]{2,1,0:T(8,128)(2,1)S(1)}) custom-call(s32[5]{0:T(128)S(1)} %stack.23.me_ref, s32[128]{0:T(128)S(1)} %copy-done.16, s32[5]{0:T(128)S(1)} %convert_reduce_fusion.starts_ref, s32[4]{0:T(128)S(1)} %copy-done.17, ...), custom_call_target="tpu_custom_call" | custom-call | tf_op jit(solution)/shard_map/row_front/pallas_call | solution.py:253
  36.6 1.3 all-to-all-done.refs_4_
  37.9 14.9 %all_to_all.25.parts = bf16[8,6,16,128]{3,2,1,0:T(8,128)(2,1)S(1)} all-to-all(bf16[8,6,16,128]{3,2,1,0:T(8,128)(2,1)S(1)} %get-tuple-element.61), channel_id=1, replica_groups=mesh['far'=2,'plane'=2,'pair'=2,'chip'=2,'core'=2] {'far','plane','pair'}, dimensions={0} | all-to-all | bytes 393216 | tf_op jit(solution)/shard_map/all_to_all | solution.py:832
  53.7 10.7 %all_to_all.26.shared = bf16[8,6,16,128]{3,2,1,0:T(8,128)(2,1)S(1)} all-to-all(bf16[8,6,16,128]{3,2,1,0:T(8,128)(2,1)S(1)} %tie.1), channel_id=1, replica_groups=mesh['far'=2,'plane'=2,'pair'=2,'chip'=2,'core'=2] {'far','plane','pair'}, dimensions={0} | all-to-all | bytes 393216 | tf_op jit(solution)/shard_map/all_to_all | solution.py:833
  64.4 2.1 %mix.1 = bf16[16,192,128]{2,1,0:T(8,128)(2,1)} custom-call(s32[5]{0:T(128)S(1)} %stack.23.me_ref, s32[128]{0:T(128)S(1)} %copy-done.16, s32[5]{0:T(128)S(1)} %convert_reduce_fusion.starts_ref, s32[4]{0:T(128)S(1)} %copy-done.17, bf16[8,6,16,128]{3,2,1,0:T(8,128)(2,1)S(1)} %all_to_all.26.shared, bf16[6,128,128]{2,1,0:T(8,128)(2,1)S(1)} %get-tuple-element.62.inner, ...), custom_call_target="tpu_custom_call" | custom-call | tf_op jit(solution)/shard_map/mix/pallas_call | solution.py:355
  66.5 4.5 %all-to-all-start.3 = ((bf16[16,192,128]{2,1,0:T(8,128)(2,1)}), bf16[16,192,128]{2,1,0:T(8,128)(2,1)}, u32[]{:S(2)}, u32[]{:S(2)}) async-start(bf16[16,192,128]{2,1,0:T(8,128)(2,1)} %mix.1), calls=%async_computation.3 | async-start | bytes 1572864 | tf_op jit(solution)/shard_map/all_to_all | solution.py:841
  71.9 1.9 %collective-permute-start.8 = (bf16[384,768]{1,0:T(8,128)(2,1)}, bf16[384,768]{1,0:T(8,128)(2,1)}, u32[]{:S(2)}, u32[]{:S(2)}) collective-permute-start(bf16[384,768]{1,0:T(8,128)(2,1)} %slice.21), channel_id=1, source_target_pairs={{0,4},{4,0},{1,5},{5,1},{2,6},{6,2},{3,7},{7,3},{8,12},{12,8},{9,1... | collective-permute-start | bytes 1769480 | tf_op jit(solution)/shard_map/ppermute | solution.py:23
  73.8 1.5 collective-permute-start.15
  75.2 15.2 %all-to-all-done.3.blocks = bf16[16,192,128]{2,1,0:T(8,128)(2,1)} async-done(((bf16[16,192,128]{2,1,0:T(8,128)(2,1)}), bf16[16,192,128]{2,1,0:T(8,128)(2,1)}, u32[]{:S(2)}, u32[]{:S(2)}) %all-to-all-start.3) | async-done | bytes 786464 | tf_op jit(solution)/shard_map/all_to_all | solution.py:841
  91.4 3.6 %project.1 = (f32[8,64,768]{2,1,0:T(8,128)S(1)}, bf16[2,64,768]{2,1,0:T(8,128)(2,1)S(1)}, bf16[2,64,768]{2,1,0:T(8,128)(2,1)S(1)}, bf16[2,64,768]{2,1,0:T(8,128)(2,1)S(1)}, bf16[2,64,768]{2,1,0:T(8,128)(2,1)S(1)}) custom-call(s32[5]{0:T(128)S(1)} %stack.23.me_ref, bf16[16,192,128]{2,1,0:T(8,128)(2,1)} %all-to-all-done.3.blocks, ...), custom_call_target="tpu_custom_call" | custom-call | tf_op jit(solution)/shard_map/project/pallas_call | solution.py:431
  99.2 2.4 %collective-permute-start.14 = (bf16[192,768]{1,0:T(8,128)(2,1)S(1)}, bf16[192,768]{1,0:T(8,128)(2,1)S(1)}, u32[]{:S(2)}, u32[]{:S(2)}) collective-permute-start(bf16[192,768]{1,0:T(8,128)(2,1)S(1)} %get-tuple-element.97), channel_id=1, source_target_pairs={{0,8},{8,0},{1,9},{9,1},{2,10},{10,2},{3,11},{11,3},{4,12},{12,4},... | collective-permute-start | bytes 884744 | tf_op jit(solution)/shard_map/ppermute | solution.py:27
  101.5 1.1 collective-permute-start.13
  104.4 5.6 %column.1 = (f32[8,64,768]{2,1,0:T(8,128)S(1)}, bf16[8,64,768]{2,1,0:T(8,128)(2,1)S(1)}) custom-call(s32[5]{0:T(128)S(1)} %stack.23.me_ref, s32[5]{0:T(128)S(1)} %convert_reduce_fusion.starts_ref, bf16[2,64,768]{2,1,0:T(8,128)(2,1)S(1)} %get-tuple-element.79.refs_0_, bf16[2,64,768]{2,1,0:T(8,128)(2,1)S(1)} %get-tuple-element.80.refs_1_, ...), custom_call_target="tpu_custom_call" | custom-call | tf_op jit(solution)/shard_map/column/pallas_call | solution.py:609
  110.4 2.3 %collective-permute-done.16.got = bf16[8,64,768]{2,1,0:T(8,128)(2,1)S(1)} collective-permute-done((bf16[8,64,768]{2,1,0:T(8,128)(2,1)S(1)}, bf16[8,64,768]{2,1,0:T(8,128)(2,1)S(1)}, u32[]{:S(2)}, u32[]{:S(2)}) %collective-permute-start.16) | collective-permute-done | bytes 786464 | tf_op jit(solution)/shard_map/ppermute | solution.py:31
  114.3 3.0 %feed_forward.3 = f32[256,768]{1,0:T(8,128)S(1)} custom-call(s32[5]{0:T(128)S(1)} %stack.23.me_ref, bf16[256,768]{1,0:T(8,128)(2,1)S(1)} %get-tuple-element.90.normed, bf16[768,768]{1,0:T(8,128)(2,1)S(1)} %copy-done.1, bf16[768,768]{1,0:T(8,128)(2,1)S(1)} %copy-done.3, bf16[960,768]{1,0:T(8,128)(2,1)S(1)} %collective-permute-done.3.piece.refs_10_, ...), custom_call_target="tpu_custom_call" | custom-call | tf_op jit(solution)/shard_map/feed_forward/pallas_call | solution.py:738
  117.3 4.4 %feed_forward.5 = bf16[512,768]{1,0:T(8,128)(2,1)S(1)} custom-call(s32[5]{0:T(128)S(1)} %stack.23.me_ref, bf16[512,768]{1,0:T(8,128)(2,1)S(1)} %bitcast.20, bf16[768,768]{1,0:T(8,128)(2,1)S(1)} %copy-done.1, bf16[768,768]{1,0:T(8,128)(2,1)S(1)} %copy-done.3, bf16[960,768]{1,0:T(8,128)(2,1)S(1)} %collective-permute-done.3.piece.refs_10_, ...), custom_call_target="tpu_custom_call" | custom-call | tf_op jit(solution)/shard_map/feed_forward/pallas_call | solution.py:738
  122.0 3.2 %feed_forward.4 = f32[256,768]{1,0:T(8,128)S(1)} custom-call(s32[5]{0:T(128)S(1)} %stack.23.me_ref, bf16[256,768]{1,0:T(8,128)(2,1)S(1)} %get-tuple-element.95.normed, bf16[768,768]{1,0:T(8,128)(2,1)S(1)} %copy-done.1, bf16[768,768]{1,0:T(8,128)(2,1)S(1)} %copy-done.3, bf16[960,768]{1,0:T(8,128)(2,1)S(1)} %collective-permute-done.3.piece.refs_10_, ...), custom_call_target="tpu_custom_call" | custom-call | tf_op jit(solution)/shard_map/feed_forward/pallas_call | solution.py:738
  125.2 1.2 finish.1
  126.5 22.8 %all_to_all.27 = bf16[32,96,128]{2,1,0:T(8,128)(2,1)S(1)} all-to-all(bf16[32,96,128]{2,1,0:T(8,128)(2,1)S(1)} %finish.1), channel_id=1, replica_groups=mesh['far'=2,'plane'=2,'pair'=2,'chip'=2,'core'=2] {'far','plane','pair'..., dimensions={0} | all-to-all | bytes 1572864 | tf_op jit(solution)/shard_map/all_to_all | solution.py:870
  150.0 1.3 copy.14
  (75 shorter events, 15.8 us)
Async XLA Ops:
  0.0 17.4 %collective-permute-start.1 = (bf16[16,192,128]{2,1,0:T(8,128)(2,1)}, bf16[16,192,128]{2,1,0:T(8,128)(2,1)S(1)}, u32[]{:S(2)}, u32[]{:S(2)}) collective-permute-start(bf16[16,192,128]{2,1,0:T(8,128)(2,1)} %stream), channel_id=1, source_target_pairs={{0,1},{1,0},{2,3},{3,2},{4,5},{5,4},{6,7},{7,6},{8,9},{9,8},{10,11... | collective-permute-start | bytes 2359304 | tf_op jit(solution)/shard_map/ppermute | solution.py:31
  0.5 21.4 %collective-permute-start = (bf16[16,192,128]{2,1,0:T(8,128)(2,1)}, bf16[16,192,128]{2,1,0:T(8,128)(2,1)}, u32[]{:S(2)}, u32[]{:S(2)}) collective-permute-start(bf16[16,192,128]{2,1,0:T(8,128)(2,1)} %stream), channel_id=1, source_target_pairs={{0,2},{2,0},{1,3},{3,1},{4,6},{6,4},{5,7},{7,5},{8,10},{10,8},{9,1... | collective-permute-start | bytes 2359304 | tf_op jit(solution)/shard_map/ppermute | solution.py:19
  3.0 1.3 copy-start
  4.3 1.3 copy-start.2
  8.7 2.3 %copy-start.6 = (bf16[16,192,128]{2,1,0:T(8,128)(2,1)S(1)}, bf16[16,192,128]{2,1,0:T(8,128)(2,1)}, u32[]{:S(2)}) copy-start(bf16[16,192,128]{2,1,0:T(8,128)(2,1)} %stream) | copy-start | bytes 2359300
  9.9 2.5 %copy-start.19 = (bf16[768,768]{1,0:T(8,128)(2,1)}, bf16[768,768]{1,0:T(8,128)(2,1)S(1)}, u32[]{:S(2)}) copy-start(bf16[768,768]{1,0:T(8,128)(2,1)S(1)} %get-tuple-element.86) | copy-start | bytes 3538948
  11.0 6.3 %copy-start.16 = (s32[128]{0:T(128)S(1)}, s32[128]{0:T(128)}, u32[]{:S(2)}) copy-start(s32[128]{0:T(128)} %label_ref.5) | copy-start | bytes 1540
  11.0 15.0 %copy-start.17 = (s32[4]{0:T(128)S(1)}, s32[4]{0:T(128)}, u32[]{:S(2)}) copy-start(s32[4]{0:T(128)} %tally_ref.5) | copy-start | bytes 52
  12.3 25.5 %all-to-all-start = ((bf16[32,96,128]{2,1,0:T(8,128)(2,1)}), bf16[32,96,128]{2,1,0:T(8,128)(2,1)S(1)}, u32[]{:S(2)}, u32[]{:S(2)}) async-start(bf16[32,96,128]{2,1,0:T(8,128)(2,1)} %spread.1), calls=%async_computation | async-start | bytes 1572864 | tf_op jit(solution)/shard_map/all_to_all | solution.py:817
  21.9 4.1 %collective-permute-start.2 = (bf16[16,192,128]{2,1,0:T(8,128)(2,1)}, bf16[16,192,128]{2,1,0:T(8,128)(2,1)S(1)}, u32[]{:S(2)}, u32[]{:S(2)}) collective-permute-start(bf16[16,192,128]{2,1,0:T(8,128)(2,1)} %collective-permute-done.far), channel_id=1, source_target_pairs={{0,1},{1,0},{2,3},{3,2},{4,5},{5,4},{6,7},{7,6},{8,9},{9,8},{10,11... | collective-permute-start | bytes 2359304 | tf_op jit(solution)/shard_map/ppermute | solution.py:31
  21.9 44.6 %collective-permute-start.3 = (bf16[960,768]{1,0:T(8,128)(2,1)}, bf16[960,768]{1,0:T(8,128)(2,1)S(1)}, u32[]{:S(2)}, u32[]{:S(2)}) collective-permute-start(bf16[960,768]{1,0:T(8,128)(2,1)} %copy-done.18), channel_id=1, source_target_pairs={{0,2},{2,0},{1,3},{3,1},{4,6},{6,4},{5,7},{7,5},{8,10},{10,8},{9,1... | collective-permute-start | bytes 4423688 | tf_op jit(solution)/shard_map/ppermute | solution.py:19
  37.9 26.6 %copy-start.15 = (bf16[16,192,128]{2,1,0:T(8,128)(2,1)S(1)}, bf16[16,192,128]{2,1,0:T(8,128)(2,1)}, u32[]{:S(2)}) copy-start(bf16[16,192,128]{2,1,0:T(8,128)(2,1)} %copy-done.14) | copy-start | bytes 2359300
  66.5 24.0 %all-to-all-start.3 = ((bf16[16,192,128]{2,1,0:T(8,128)(2,1)}), bf16[16,192,128]{2,1,0:T(8,128)(2,1)}, u32[]{:S(2)}, u32[]{:S(2)}) async-start(bf16[16,192,128]{2,1,0:T(8,128)(2,1)} %mix.1), calls=%async_computation.3 | async-start | bytes 1572864 | tf_op jit(solution)/shard_map/all_to_all | solution.py:841
  71.9 23.9 %collective-permute-start.8 = (bf16[384,768]{1,0:T(8,128)(2,1)}, bf16[384,768]{1,0:T(8,128)(2,1)}, u32[]{:S(2)}, u32[]{:S(2)}) collective-permute-start(bf16[384,768]{1,0:T(8,128)(2,1)} %slice.21), channel_id=1, source_target_pairs={{0,4},{4,0},{1,5},{5,1},{2,6},{6,2},{3,7},{7,3},{8,12},{12,8},{9,1... | collective-permute-start | bytes 1769480 | tf_op jit(solution)/shard_map/ppermute | solution.py:23
  73.8 36.6 %collective-permute-start.15 = (bf16[768,768]{1,0:T(8,128)(2,1)}, bf16[768,768]{1,0:T(8,128)(2,1)S(1)}, u32[]{:S(2)}, u32[]{:S(2)}) collective-permute-start(bf16[768,768]{1,0:T(8,128)(2,1)} %copy-done.19), channel_id=1, source_target_pairs={{0,2},{2,0},{1,3},{3,1},{4,6},{6,4},{5,7},{7,5},{8,10},{10,8},{9,1... | collective-permute-start | bytes 3538952 | tf_op jit(solution)/shard_map/ppermute | solution.py:19
  95.1 1.5 collective-permute-start.4
  95.2 1.7 %collective-permute-start.5 = (bf16[2,64,768]{2,1,0:T(8,128)(2,1)S(1)}, bf16[2,64,768]{2,1,0:T(8,128)(2,1)S(1)}, u32[]{:S(2)}, u32[]{:S(2)}) collective-permute-start(bf16[2,64,768]{2,1,0:T(8,128)(2,1)S(1)} %get-tuple-element.70), channel_id=1, source_target_pairs={{0,1},{1,0},{2,3},{3,2},{4,5},{5,4},{6,7},{7,6},{8,9},{9,8},{10,11... | collective-permute-start | bytes 589832 | tf_op jit(solution)/shard_map/ppermute | solution.py:31
  95.7 1.5 collective-permute-start.6
  95.8 1.7 %collective-permute-start.7 = (bf16[2,64,768]{2,1,0:T(8,128)(2,1)S(1)}, bf16[2,64,768]{2,1,0:T(8,128)(2,1)S(1)}, u32[]{:S(2)}, u32[]{:S(2)}) collective-permute-start(bf16[2,64,768]{2,1,0:T(8,128)(2,1)S(1)} %get-tuple-element.72), channel_id=1, source_target_pairs={{0,1},{1,0},{2,3},{3,2},{4,5},{5,4},{6,7},{7,6},{8,9},{9,8},{10,11... | collective-permute-start | bytes 589832 | tf_op jit(solution)/shard_map/ppermute | solution.py:31
  97.4 6.9 %copy-start.5 = (bf16[3,192,768]{2,1,0:T(8,128)(2,1)S(1)}, bf16[3,192,768]{2,1,0:T(8,128)(2,1)}, u32[]{:S(2)}) copy-start(bf16[3,192,768]{2,1,0:T(8,128)(2,1)} %param.14) | copy-start | bytes 2654212
  97.5 6.9 %copy-start.10 = (bf16[192,768]{1,0:T(8,128)(2,1)S(1)}, bf16[192,768]{1,0:T(8,128)(2,1)}, u32[]{:S(2)}) copy-start(bf16[192,768]{1,0:T(8,128)(2,1)} %refs_9_.1) | copy-start | bytes 884740
  98.6 4.1 %collective-permute-start.9 = (bf16[2,64,768]{2,1,0:T(8,128)(2,1)S(1)}, bf16[2,64,768]{2,1,0:T(8,128)(2,1)S(1)}, u32[]{:S(2)}, u32[]{:S(2)}) collective-permute-start(bf16[2,64,768]{2,1,0:T(8,128)(2,1)S(1)} %get-tuple-element.79.refs_0_), channel_id=1, source_target_pairs={{0,1},{1,0},{2,3},{3,2},{4,5},{5,4},{6,7},{7,6},{8,9},{9,8},{10,11... | collective-permute-start | bytes 589832 | tf_op jit(solution)/shard_map/ppermute | solution.py:31
  98.8 3.8 %collective-permute-start.10 = (bf16[2,64,768]{2,1,0:T(8,128)(2,1)S(1)}, bf16[2,64,768]{2,1,0:T(8,128)(2,1)S(1)}, u32[]{:S(2)}, u32[]{:S(2)}) collective-permute-start(bf16[2,64,768]{2,1,0:T(8,128)(2,1)S(1)} %get-tuple-element.80.refs_1_), channel_id=1, source_target_pairs={{0,1},{1,0},{2,3},{3,2},{4,5},{5,4},{6,7},{7,6},{8,9},{9,8},{10,11... | collective-permute-start | bytes 589832 | tf_op jit(solution)/shard_map/ppermute | solution.py:31
  99.2 10.8 %collective-permute-start.14 = (bf16[192,768]{1,0:T(8,128)(2,1)S(1)}, bf16[192,768]{1,0:T(8,128)(2,1)S(1)}, u32[]{:S(2)}, u32[]{:S(2)}) collective-permute-start(bf16[192,768]{1,0:T(8,128)(2,1)S(1)} %get-tuple-element.97), channel_id=1, source_target_pairs={{0,8},{8,0},{1,9},{9,1},{2,10},{10,2},{3,11},{11,3},{4,12},{12,4},... | collective-permute-start | bytes 884744 | tf_op jit(solution)/shard_map/ppermute | solution.py:27
  101.5 8.9 %collective-permute-start.13 = (bf16[192,768]{1,0:T(8,128)(2,1)S(1)}, bf16[192,768]{1,0:T(8,128)(2,1)S(1)}, u32[]{:S(2)}, u32[]{:S(2)}) collective-permute-start(bf16[192,768]{1,0:T(8,128)(2,1)S(1)} %get-tuple-element.98), channel_id=1, source_target_pairs={{0,4},{4,0},{1,5},{5,1},{2,6},{6,2},{3,7},{7,3},{8,12},{12,8},{9,1... | collective-permute-start | bytes 884744 | tf_op jit(solution)/shard_map/ppermute | solution.py:23
  102.7 1.4 collective-permute-start.11
  102.7 1.7 %collective-permute-start.12 = (bf16[2,64,768]{2,1,0:T(8,128)(2,1)S(1)}, bf16[2,64,768]{2,1,0:T(8,128)(2,1)S(1)}, u32[]{:S(2)}, u32[]{:S(2)}) collective-permute-start(bf16[2,64,768]{2,1,0:T(8,128)(2,1)S(1)} %get-tuple-element.82.refs_3_), channel_id=1, source_target_pairs={{0,1},{1,0},{2,3},{3,2},{4,5},{5,4},{6,7},{7,6},{8,9},{9,8},{10,11... | collective-permute-start | bytes 589832 | tf_op jit(solution)/shard_map/ppermute | solution.py:31
  110.4 2.3 %collective-permute-start.16 = (bf16[8,64,768]{2,1,0:T(8,128)(2,1)S(1)}, bf16[8,64,768]{2,1,0:T(8,128)(2,1)S(1)}, u32[]{:S(2)}, u32[]{:S(2)}) collective-permute-start(bf16[8,64,768]{2,1,0:T(8,128)(2,1)S(1)} %get-tuple-element.87), channel_id=1, source_target_pairs={{0,1},{1,0},{2,3},{3,2},{4,5},{5,4},{6,7},{7,6},{8,9},{9,8},{10,11... | collective-permute-start | bytes 2359304 | tf_op jit(solution)/shard_map/ppermute | solution.py:31
  112.7 1.3 copy-start.1
  112.7 1.6 %copy-start.3 = (bf16[768,768]{1,0:T(8,128)(2,1)S(1)}, bf16[768,768]{1,0:T(8,128)(2,1)}, u32[]{:S(2)}) copy-start(bf16[768,768]{1,0:T(8,128)(2,1)} %contract.7) | copy-start | bytes 3538948
  113.4 3.9 %collective-permute-start.17 = (bf16[8,64,768]{2,1,0:T(8,128)(2,1)S(1)}, bf16[8,64,768]{2,1,0:T(8,128)(2,1)S(1)}, u32[]{:S(2)}, u32[]{:S(2)}) collective-permute-start(bf16[8,64,768]{2,1,0:T(8,128)(2,1)S(1)} %get-tuple-element.89), channel_id=1, source_target_pairs={{0,1},{1,0},{2,3},{3,2},{4,5},{5,4},{6,7},{7,6},{8,9},{9,8},{10,11... | collective-permute-start | bytes 2359304 | tf_op jit(solution)/shard_map/ppermute | solution.py:31
  121.8 3.4 %collective-permute-start.18 = (bf16[512,768]{1,0:T(8,128)(2,1)S(1)}, bf16[512,768]{1,0:T(8,128)(2,1)S(1)}, u32[]{:S(2)}, u32[]{:S(2)}) collective-permute-start(bf16[512,768]{1,0:T(8,128)(2,1)S(1)} %feed_forward.5), channel_id=1, source_target_pairs={{0,1},{1,0},{2,3},{3,2},{4,5},{5,4},{6,7},{7,6},{8,9},{9,8},{10,11... | collective-permute-start | bytes 2359304 | tf_op jit(solution)/shard_map/ppermute | solution.py:31
  (9 other events, 9.3 us)
